TPU v7x, 32 devices: a whole 2x2x4 slice. The times are simulated.
32 devices in a mesh: ctx: 8 (over z, x), wt: 4 (over y, core).
Axes of the slice: x: 2, y: 2, z: 4, core: 2. Of those that a mesh axis runs over, the one named last changes fastest.
Arguments:
- block_in: bfloat16 [4096, 2048], P(('ctx', 'wt')), may hold values from -6 to 6
- target: bfloat16 [4096, 2048], P(('ctx', 'wt')), may hold values from -6 to 6
- seq_lengths: int32 [3], replicated, may hold values from 1024 to 2048, as said below
- permutation: int32 [4096], replicated, may hold values from 0 to 4095, each once
- routes: int32 [4096, 2], P('ctx'), may hold values from 0 to 3, all different within a row
- attn_qkv: float32 [3, 2048, 2048], P(None, None, 'wt'), may hold values from -0.125 to 0.125
- attn_out: float32 [2048, 2048], P(None, 'wt'), may hold values from -3 to 3
- norm_gains: float32 [4, 2048], replicated, may hold values from 0.5 to 1.5
- router: float32 [2048, 4], replicated, may hold values from -0.09375 to 0.09375
- gate_up: float32 [2, 4, 2048, 1024], P(None, None, None, 'wt'), may hold values from -0.125 to 0.125
- down: float32 [4, 2048, 1024], P(None, None, 'wt'), may hold values from -0.5 to 0.5
Outputs:
- block_out: bfloat16 [4096, 2048], P(('ctx', 'wt'))
- input_grad: bfloat16 [4096, 2048], P(('ctx', 'wt'))
- qkv_grad: float32 [3, 2048, 2048], P(None, 'ctx', 'wt')
- out_grad: float32 [2048, 2048], P('ctx', 'wt')
- gains_grad: float32 [4, 2048], replicated
- router_grad: float32 [2048, 4], replicated
- gate_up_grad: float32 [2, 4, 2048, 1024], P(None, None, 'ctx', 'wt')
- down_grad: float32 [4, 2048, 1024], P(None, 'ctx', 'wt')
Inputs may be any that keep to these rules, and one draw needn't show every extreme that they name: `seq_lengths`: the lengths sum to 4096, and one of them is 2048.
All inputs are finite; a program needn't handle non-finite values.
Results may differ from a plain program's by a relative error of at most 0.025.
Values may be sent and summed in bfloat16 or wider, within the bound.
No kernel may reach another device: no remote copies, remote signals or barrier semaphores. Data moves between devices by JAX's collectives and lax.ppermute only.
A program may use at most 320 MiB of HBM per device.

v0:
```python
import math

import jax
import jax.numpy as jnp
from jax import lax
from jax.sharding import PartitionSpec as P

HEAD_DIM = 128


norm_eps = 1e-05


def token_places(seq_lengths, permutation):
    seq_ends = jnp.cumsum(seq_lengths)
    seq_starts = seq_ends - seq_lengths
    seq_id = jnp.sum((permutation[:, None] >= seq_ends[None, :]).astype(jnp.int32), axis=1)
    member = seq_id[:, None] == jnp.arange(seq_lengths.shape[0], dtype=jnp.int32)[None, :]
    positions = permutation - jnp.sum(jnp.where(member, seq_starts[None, :], 0), axis=1)
    return (seq_id, positions)


def rope_tables(positions, head_dim):
    half_dim = head_dim // 2
    frequency = jnp.exp(
        jnp.arange(half_dim, dtype=jnp.float32) * (-2.0 * math.log(10000.0) / head_dim)
    )
    angles = positions.astype(jnp.float32)[:, None] * frequency[None, :]
    return (jnp.cos(angles), jnp.sin(angles))


def rotate(vectors, cosine, sine_tab):
    half_dim = vectors.shape[-1] // 2
    lower_half = vectors[..., :half_dim]
    upper_half = vectors[..., half_dim:]
    cos_part = cosine[:, None, :]
    sin_part = sine_tab[:, None, :]
    return jnp.concatenate(
        [
            lower_half * cos_part - upper_half * sin_part,
            upper_half * cos_part + lower_half * sin_part,
        ],
        axis=-1,
    )


def rotate_back(grad_rows, cosine, sine_tab):
    half_dim = grad_rows.shape[-1] // 2
    lower_half = grad_rows[..., :half_dim]
    upper_half = grad_rows[..., half_dim:]
    cos_part = cosine[:, None, :]
    sin_part = sine_tab[:, None, :]
    return jnp.concatenate(
        [
            lower_half * cos_part + upper_half * sin_part,
            upper_half * cos_part - lower_half * sin_part,
        ],
        axis=-1,
    )


def norm_back(grad_out, hat_rows, inv_rows, gain_row):
    grad_hat = grad_out * gain_row
    return inv_rows * (grad_hat - hat_rows * jnp.mean(grad_hat * hat_rows, axis=-1, keepdims=True))


def mask_rows(q_seq, q_pos, k_seq, k_pos):
    return (q_seq[:, None] == k_seq[None, :]) & (k_pos[None, :] <= q_pos[:, None])


def key_blocks(key_all, val_all, seq_all, pos_all, heads_here):
    row_count = key_all.shape[0]
    block_len = math.gcd(row_count, 2048)
    blocks = row_count // block_len
    head_dim = key_all.shape[1] // heads_here
    seq_part = seq_all.reshape(blocks, block_len)
    pos_part = pos_all.reshape(blocks, block_len)
    return (
        key_all.reshape(blocks, block_len, heads_here, head_dim),
        val_all.reshape(blocks, block_len, heads_here, head_dim),
        seq_part,
        pos_part,
    )


def attend_keys(carry_state, queries, shard_piece, q_seq, q_pos, seq_all, pos_all, score_scale):
    heads_here = queries.shape[1]
    block_items = key_blocks(shard_piece[0], shard_piece[1], seq_all, pos_all, heads_here)

    def attend_block_step(carried, block_item):
        run_max, run_sum, run_acc = carried
        key_blk, val_blk, k_seq, k_pos = block_item
        scores = (
            jnp.einsum("qhd,khd->hqk", queries, key_blk, preferred_element_type=jnp.float32)
            * score_scale
        )
        allowed = mask_rows(q_seq, q_pos, k_seq, k_pos)[None]
        scores = jnp.where(allowed, scores, -1e30)
        new_max = jnp.maximum(run_max, jnp.max(scores, axis=-1))
        weights = jnp.where(allowed, jnp.exp(scores - new_max[..., None]), 0.0)
        shrink = jnp.exp(run_max - new_max)
        run_sum = run_sum * shrink + jnp.sum(weights, axis=-1)
        run_acc = run_acc * shrink.T[:, :, None] + jnp.einsum(
            "hqk,khd->qhd",
            weights.astype(jnp.bfloat16),
            val_blk,
            preferred_element_type=jnp.float32,
        )
        return ((new_max, run_sum, run_acc), None)

    carry_state, unused = lax.scan(attend_block_step, carry_state, block_items)
    return carry_state


def grad_keys(
    queries,
    d_attn,
    row_delta,
    row_lse,
    key_all,
    val_all,
    q_seq,
    q_pos,
    seq_all,
    pos_all,
    score_scale,
):
    heads_here = queries.shape[1]
    block_items = key_blocks(key_all, val_all, seq_all, pos_all, heads_here)
    block_len = block_items[2].shape[1]

    def grad_block_step(d_query, block_item):
        key_blk, val_blk, k_seq, k_pos = block_item
        scores = (
            jnp.einsum("qhd,khd->hqk", queries, key_blk, preferred_element_type=jnp.float32)
            * score_scale
        )
        allowed = mask_rows(q_seq, q_pos, k_seq, k_pos)[None]
        prob_blk = jnp.where(allowed, jnp.exp(scores - row_lse[..., None]), 0.0)
        d_prob = jnp.einsum("qhd,khd->hqk", d_attn, val_blk, preferred_element_type=jnp.float32)
        d_score = (prob_blk * (d_prob - row_delta[..., None])).astype(jnp.bfloat16)
        d_query = (
            d_query
            + jnp.einsum("hqk,khd->qhd", d_score, key_blk, preferred_element_type=jnp.float32)
            * score_scale
        )
        d_key = (
            jnp.einsum("hqk,qhd->khd", d_score, queries, preferred_element_type=jnp.float32)
            * score_scale
        )
        d_value = jnp.einsum(
            "hqk,qhd->khd",
            prob_blk.astype(jnp.bfloat16),
            d_attn,
            preferred_element_type=jnp.float32,
        )
        return (
            d_query,
            jnp.concatenate([d_key.reshape(block_len, -1), d_value.reshape(block_len, -1)], axis=1),
        )

    d_query, kv_terms = lax.scan(
        grad_block_step, jnp.zeros(queries.shape, jnp.float32), block_items
    )
    return (d_query, kv_terms.reshape(key_all.shape[0], -1))


def local(
    block_in,
    target,
    seq_lengths,
    permutation,
    routes,
    attn_qkv,
    attn_out,
    norm_gains,
    router,
    gate_up,
    down,
):
    wt_count = lax.axis_size("wt")
    wt_pos = lax.axis_index("wt")
    ctx_pos = lax.axis_index("ctx")
    local_rows, model_width = block_in.shape
    tok_rows = local_rows * wt_count
    head_cols = attn_qkv.shape[2]
    heads_here = head_cols // HEAD_DIM
    hidden_cols = gate_up.shape[3]
    experts = gate_up.shape[1]
    score_scale = HEAD_DIM ** (-0.5)
    seq_all, pos_all = token_places(seq_lengths, permutation)
    q_seq = lax.dynamic_slice_in_dim(seq_all, ctx_pos * tok_rows, tok_rows)
    q_pos = lax.dynamic_slice_in_dim(pos_all, ctx_pos * tok_rows, tok_rows)
    cosine, sine_tab = rope_tables(q_pos, HEAD_DIM)
    resid_in = block_in.astype(jnp.float32)
    inv_first = lax.rsqrt(jnp.mean(resid_in * resid_in, axis=-1, keepdims=True) + norm_eps)
    hat_first = resid_in * inv_first
    normed = (hat_first * norm_gains[0]).astype(jnp.bfloat16)
    normed_all = lax.all_gather(normed, "wt", axis=0, tiled=True)
    qkv_b = attn_qkv.astype(jnp.bfloat16)
    projected = jnp.einsum("td,kdc->ktc", normed_all, qkv_b, preferred_element_type=jnp.float32)
    query_raw = projected[0]
    key_raw = projected[1]
    square_q, square_k = lax.psum(
        (jnp.sum(query_raw * query_raw, axis=-1), jnp.sum(key_raw * key_raw, axis=-1)), "wt"
    )
    inv_q = lax.rsqrt(square_q / model_width + norm_eps)[:, None]
    inv_k = lax.rsqrt(square_k / model_width + norm_eps)[:, None]
    gain_q = lax.dynamic_slice_in_dim(norm_gains[2], wt_pos * head_cols, head_cols)
    gain_k = lax.dynamic_slice_in_dim(norm_gains[3], wt_pos * head_cols, head_cols)
    q_hat = query_raw * inv_q
    k_hat = key_raw * inv_k
    queries = rotate(
        (q_hat * gain_q).reshape(tok_rows, heads_here, HEAD_DIM), cosine, sine_tab
    ).astype(jnp.bfloat16)
    key_rows = (
        rotate((k_hat * gain_k).reshape(tok_rows, heads_here, HEAD_DIM), cosine, sine_tab)
        .astype(jnp.bfloat16)
        .reshape(tok_rows, head_cols)
    )
    val_rows = projected[2].astype(jnp.bfloat16)
    start_state = (
        jnp.full((heads_here, tok_rows), -1e30, jnp.float32),
        jnp.zeros((heads_here, tok_rows), jnp.float32),
        jnp.zeros((tok_rows, heads_here, HEAD_DIM), jnp.float32),
    )
    run_max, run_sum, run_acc = attend_keys(
        start_state,
        queries,
        (
            lax.all_gather(key_rows, "ctx", axis=0, tiled=True),
            lax.all_gather(val_rows, "ctx", axis=0, tiled=True),
        ),
        q_seq,
        q_pos,
        seq_all,
        pos_all,
        score_scale,
    )
    attn_f = run_acc / run_sum.T[:, :, None]
    row_lse = run_max + jnp.log(run_sum)
    attn_b = attn_f.reshape(tok_rows, head_cols).astype(jnp.bfloat16)
    out_b = attn_out.astype(jnp.bfloat16)
    row_block = attn_b
    attn_y = lax.psum_scatter(
        lax.dot_general(
            row_block, out_b, (((1,), (1,)), ((), ())), preferred_element_type=jnp.float32
        ).astype(jnp.bfloat16),
        "wt",
        scatter_dimension=0,
        tiled=True,
    ).astype(jnp.float32)
    residual = resid_in + attn_y
    inv_second = lax.rsqrt(jnp.mean(residual * residual, axis=-1, keepdims=True) + norm_eps)
    hat_second = residual * inv_second
    mixed_rows = (hat_second * norm_gains[1]).astype(jnp.bfloat16)
    mixed_all = lax.all_gather(mixed_rows, "wt", axis=0, tiled=True)
    router_b = router.astype(jnp.bfloat16)
    logits = jnp.dot(mixed_all, router_b, preferred_element_type=jnp.float32)
    prob_all = jax.nn.softmax(logits, axis=-1)
    choose = jnp.sum(
        (routes[:, :, None] == jnp.arange(experts, dtype=jnp.int32)[None, None, :]).astype(
            jnp.float32
        ),
        axis=1,
    )
    gate_w = prob_all * choose
    gu_b = gate_up.astype(jnp.bfloat16)
    pre_act = jnp.einsum("td,kedf->ketf", mixed_all, gu_b, preferred_element_type=jnp.float32)
    gate_in = pre_act[0]
    up_in = pre_act[1]
    gate_sig = jax.nn.sigmoid(gate_in)
    gate_act = gate_in * gate_sig
    hidden = (gate_w.T[:, :, None] * gate_act * up_in).astype(jnp.bfloat16)
    down_b = down.astype(jnp.bfloat16)
    row_block = hidden
    expert_y = lax.psum_scatter(
        jnp.einsum("etf,edf->td", row_block, down_b, preferred_element_type=jnp.float32).astype(
            jnp.bfloat16
        ),
        "wt",
        scatter_dimension=0,
        tiled=True,
    ).astype(jnp.float32)
    out_local = residual + expert_y
    block_out = out_local.astype(jnp.bfloat16)
    rows_at = wt_pos * local_rows
    cot_local = out_local - target.astype(jnp.float32)
    cot_all = lax.all_gather(cot_local.astype(jnp.bfloat16), "wt", axis=0, tiled=True)
    d_hidden = jnp.einsum(
        "td,edf->etf", cot_all, down_b, preferred_element_type=jnp.float32
    ).astype(jnp.bfloat16)
    down_grad = jnp.einsum("td,etf->edf", cot_all, hidden, preferred_element_type=jnp.float32)
    d_hid = d_hidden.astype(jnp.float32)
    d_gate_w = jnp.sum(d_hid * gate_act * up_in, axis=-1).T
    scaled = d_hid * gate_w.T[:, :, None]
    d_gate_in = scaled * up_in * gate_sig * (1.0 + gate_in * (1.0 - gate_sig))
    d_up_in = scaled * gate_act
    d_pre = jnp.stack([d_gate_in, d_up_in]).astype(jnp.bfloat16)
    gate_up_grad = jnp.einsum("td,ketf->kedf", mixed_all, d_pre, preferred_element_type=jnp.float32)
    d_mixed_part = jnp.einsum("ketf,kedf->td", d_pre, gu_b, preferred_element_type=jnp.float32)
    d_mixed, d_gate_loc = (
        lax.psum_scatter(
            d_mixed_part.astype(jnp.bfloat16), "wt", scatter_dimension=0, tiled=True
        ).astype(jnp.float32),
        lax.psum_scatter(
            d_gate_w.astype(jnp.bfloat16), "wt", scatter_dimension=0, tiled=True
        ).astype(jnp.float32),
    )
    prob_loc = lax.dynamic_slice_in_dim(prob_all, rows_at, local_rows, 0)
    choose_loc = lax.dynamic_slice_in_dim(choose, rows_at, local_rows, 0)
    d_prob = d_gate_loc * choose_loc
    d_logit = (prob_loc * (d_prob - jnp.sum(prob_loc * d_prob, axis=-1, keepdims=True))).astype(
        jnp.bfloat16
    )
    d_mixed = d_mixed + lax.dot_general(
        d_logit, router_b, (((1,), (1,)), ((), ())), preferred_element_type=jnp.float32
    )
    router_grad = lax.dot_general(
        mixed_rows, d_logit, (((0,), (0,)), ((), ())), preferred_element_type=jnp.float32
    )
    gain_second = jnp.sum(d_mixed * hat_second, axis=0)
    d_resid = cot_local + norm_back(d_mixed, hat_second, inv_second, norm_gains[1])
    d_resid_all = lax.all_gather(d_resid.astype(jnp.bfloat16), "wt", axis=0, tiled=True)
    out_grad = lax.dot_general(
        d_resid_all, attn_b, (((0,), (0,)), ((), ())), preferred_element_type=jnp.float32
    )
    d_attn = (
        jnp.dot(d_resid_all, out_b, preferred_element_type=jnp.float32)
        .astype(jnp.bfloat16)
        .reshape(tok_rows, heads_here, HEAD_DIM)
    )
    row_delta = jnp.einsum("qhd,qhd->hq", d_attn.astype(jnp.float32), attn_f)
    key_all, val_all = (
        lax.all_gather(key_rows, "ctx", axis=0, tiled=True),
        lax.all_gather(val_rows, "ctx", axis=0, tiled=True),
    )
    d_query, kv_terms = grad_keys(
        queries,
        d_attn,
        row_delta,
        row_lse,
        key_all,
        val_all,
        q_seq,
        q_pos,
        seq_all,
        pos_all,
        score_scale,
    )
    kv_local = lax.psum_scatter(
        kv_terms.astype(jnp.bfloat16), "ctx", scatter_dimension=0, tiled=True
    ).astype(jnp.float32)
    d_q_norm = rotate_back(d_query, cosine, sine_tab).reshape(tok_rows, head_cols)
    d_k_norm = rotate_back(
        kv_local[:, :head_cols].reshape(tok_rows, heads_here, HEAD_DIM), cosine, sine_tab
    ).reshape(tok_rows, head_cols)
    d_q_hat = d_q_norm * gain_q
    d_k_hat = d_k_norm * gain_k
    inner_q, inner_k = lax.psum(
        (jnp.sum(d_q_hat * q_hat, axis=-1), jnp.sum(d_k_hat * k_hat, axis=-1)), "wt"
    )
    d_q_raw = inv_q * (d_q_hat - q_hat * (inner_q / model_width)[:, None])
    d_k_raw = inv_k * (d_k_hat - k_hat * (inner_k / model_width)[:, None])
    zero_row = jnp.zeros((model_width,), jnp.float32)
    gain_q_full = lax.dynamic_update_slice_in_dim(
        zero_row, jnp.sum(d_q_norm * q_hat, axis=0), wt_pos * head_cols, 0
    )
    gain_k_full = lax.dynamic_update_slice_in_dim(
        zero_row, jnp.sum(d_k_norm * k_hat, axis=0), wt_pos * head_cols, 0
    )
    d_proj = jnp.stack([d_q_raw, d_k_raw, kv_local[:, head_cols:]]).astype(jnp.bfloat16)
    qkv_grad = jnp.einsum("td,ktc->kdc", normed_all, d_proj, preferred_element_type=jnp.float32)
    row_block = d_proj
    d_normed = lax.psum_scatter(
        jnp.einsum("ktc,kdc->td", row_block, qkv_b, preferred_element_type=jnp.float32).astype(
            jnp.bfloat16
        ),
        "wt",
        scatter_dimension=0,
        tiled=True,
    ).astype(jnp.float32)
    gain_first = jnp.sum(d_normed * hat_first, axis=0)
    input_grad = (d_resid + norm_back(d_normed, hat_first, inv_first, norm_gains[0])).astype(
        jnp.bfloat16
    )
    gains_grad = jnp.stack([gain_first, gain_second, gain_q_full, gain_k_full])
    gains_grad, router_grad = lax.psum((gains_grad, router_grad), ("ctx", "wt"))
    qkv_part, out_part, gate_up_part, down_part = (
        lax.psum_scatter(
            qkv_grad.astype(jnp.bfloat16), "ctx", scatter_dimension=1, tiled=True
        ).astype(jnp.float32),
        lax.psum_scatter(
            out_grad[None].astype(jnp.bfloat16), "ctx", scatter_dimension=1, tiled=True
        ).astype(jnp.float32),
        lax.psum_scatter(
            gate_up_grad.reshape(2 * experts, model_width, hidden_cols).astype(jnp.bfloat16),
            "ctx",
            scatter_dimension=1,
            tiled=True,
        ).astype(jnp.float32),
        lax.psum_scatter(
            down_grad.astype(jnp.bfloat16), "ctx", scatter_dimension=1, tiled=True
        ).astype(jnp.float32),
    )
    return (
        block_out,
        input_grad,
        qkv_part,
        out_part[0],
        gains_grad,
        router_grad,
        gate_up_part.reshape(2, experts, -1, hidden_cols),
        down_part,
    )


def solution(mesh):
    return jax.shard_map(
        local,
        mesh=mesh,
        in_specs=(
            P(("ctx", "wt"), None),
            P(("ctx", "wt"), None),
            P(),
            P(),
            P("ctx", None),
            P(None, None, "wt"),
            P(None, "wt"),
            P(),
            P(),
            P(None, None, None, "wt"),
            P(None, None, "wt"),
        ),
        out_specs=(
            P(("ctx", "wt"), None),
            P(("ctx", "wt"), None),
            P(None, "ctx", "wt"),
            P("ctx", "wt"),
            P(),
            P(),
            P(None, None, "ctx", "wt"),
            P(None, "ctx", "wt"),
        ),
        check_vma=False,
    )
```

profile of v0, /device:TPU:0, one launch (start us, length us, event | category | flops | bytes accessed | tf_op | source)
XLA Modules:
  0.0 1323.9 jit_solution(8968695081149820411)
XLA Ops:
  16.5 21.6 %all-gather.8.cloned.1.call-done = bf16[512,2048]{1,0:T(8,128)(2,1)} async-done(((bf16[128,2048]{1,0:T(8,128)(2,1)}), bf16[512,2048]{1,0:T(8,128)(2,1)}) %all-gather.8.cloned.1.call-update) | async-done | bytes 2097168 | tf_op jit(solution)/shard_map/all_gather | solution.py:199
  38.1 7.3 fusion.83
  47.2 5.8 all-reduce.2
  64.4 70.2 %all-gather.10.cloned.1.call-done = bf16[4096,512]{1,0:T(8,128)(2,1)} async-done(((bf16[512,512]{1,0:T(8,128)(2,1)}), bf16[4096,512]{1,0:T(8,128)(2,1)}) %all-gather.10.cloned.1.call-update) | async-done | bytes 4194320 | tf_op jit(solution)/shard_map/all_gather | solution.py:231
  134.6 6.9 reshape.476
  141.5 5.0 copy.100
  146.5 64.0 %all-gather.18.cloned.1.call-done = bf16[1,4096,512]{1,2,0:T(8,128)(2,1)} async-done(((bf16[1,512,512]{1,2,0:T(8,128)(2,1)}), bf16[1,4096,512]{1,2,0:T(8,128)(2,1)}) %all-gather.18.cloned.1.call-update) | async-done | bytes 4194320 | tf_op jit(solution)/shard_map/all_gather | solution.py:232
  210.5 7.8 reshape.477
  218.3 6.1 copy.102
  224.4 33.4 %while.28 = (s32[]{:T(128)}, f32[4,512]{1,0:T(4,128)S(1)}, f32[4,512]{1,0:T(4,128)S(1)}, f32[512,4,128]{0,2,1:T(8,128)S(1)}, s32[512]{0:T(512)S(1)}, /*index=5*/...) while((s32[]{:T(128)}, f32[4,512]{1,0:T(4,128)S(1)}, ...), condition=%wide.region_11.12_spmd.clone, body=%wide.region_8.11_spmd.clone.sunk | while | flops 2205954048 | bytes 61526168 | solution.py:111
  226.0 4.4 fusion.178
  234.7 6.4 fusion.182
  242.7 4.4 fusion.178
  251.4 6.4 fusion.182
  259.7 4.9 convolution_convert_fusion.2
  264.7 29.8 %reduce-scatter.13.cloned.1.call-done = bf16[128,2048]{1,0:T(8,128)(2,1)} async-done(((bf16[512,2048]{1,0:T(8,128)(2,1)}), bf16[128,2048]{1,0:T(8,128)(2,1)}) %reduce-scatter.13.cloned.1.call-update) | async-done | bytes 524304 | tf_op jit(solution)/shard_map/reduce_scatter | solution.py:245
  298.1 22.4 %all-gather.12.cloned.1.call-done = bf16[512,2048]{1,0:T(8,128)(2,1)} async-done(((bf16[128,2048]{1,0:T(8,128)(2,1)}), bf16[512,2048]{1,0:T(8,128)(2,1)}) %all-gather.12.cloned.1.call-update) | async-done | bytes 2097168 | tf_op jit(solution)/shard_map/all_gather | solution.py:257
  322.9 8.8 convolution_bitcast_fusion
  335.4 7.2 bitcast_convert_fusion.2
  342.7 31.5 %reduce-scatter.15.cloned.1.call-done = bf16[128,2048]{1,0:T(8,128)(2,1)} async-done(((bf16[512,2048]{1,0:T(8,128)(2,1)}), bf16[128,2048]{1,0:T(8,128)(2,1)}) %reduce-scatter.15.cloned.1.call-update) | async-done | bytes 524304 | tf_op jit(solution)/shard_map/reduce_scatter | solution.py:277
  376.5 22.7 %all-gather.14.cloned.1.call-done = bf16[512,2048]{1,0:T(8,128)(2,1)} async-done(((bf16[128,2048]{1,0:T(8,128)(2,1)}), bf16[512,2048]{1,0:T(8,128)(2,1)}) %all-gather.14.cloned.1.call-update) | async-done | bytes 2097168 | tf_op jit(solution)/shard_map/all_gather | solution.py:289
  399.2 9.4 fusion.111
  410.0 12.0 bitcast_convert_fusion
  422.1 7.2 reduce-scatter.31.cloned.1.call-done
  430.2 33.9 %reduce-scatter.17.cloned.1.call-done = bf16[128,2048]{1,0:T(8,128)(2,1)} async-done(((bf16[512,2048]{1,0:T(8,128)(2,1)}), bf16[128,2048]{1,0:T(8,128)(2,1)}) %reduce-scatter.17.cloned.1.call-update) | async-done | bytes 524304 | tf_op jit(solution)/shard_map/reduce_scatter | solution.py:303
  468.3 11.3 copy.109
  479.6 11.3 all-gather.16.cloned.1.call-done
  490.9 4.9 fusion.108
  495.9 67.5 %while.29 = (s32[]{:T(128)}, f32[512,4,128]{0,2,1:T(8,128)S(1)}, bf16[2,2048,1024]{1,2,0:T(8,128)(2,1)}, bf16[2,2048,4,128]{3,1,2,0:T(8,128)(2,1)}, s32[512]{0:T...) while((s32[]{:T(128)}, f32[512,4,128]{0,2,1:T(8,128)S(1)}, ...), condition=%wide.region_24.25_spmd.clone, body=%wide.region_23.24_spmd.clone.sunk | while | flops 5425070080 | bytes 191967536 | solution.py:162
  497.7 4.4 fusion.193
  502.1 5.7 copy-done
  512.0 9.6 fusion.194
  531.3 4.4 fusion.193
  535.7 5.7 copy-done
  545.6 9.6 fusion.194
  563.4 8.3 copy.140
  572.9 5.9 convert_bitcast_fusion.2
  584.2 9.7 convolution_convert_fusion
  594.1 127.2 %reduce-scatter.19.cloned.1.call-done = bf16[512,1024]{0,1:T(8,128)(2,1)} async-done(((bf16[4096,1024]{0,1:T(8,128)(2,1)}), bf16[512,1024]{0,1:T(8,128)(2,1)}) %reduce-scatter.19.cloned.1.call-update) | async-done | bytes 1048592 | tf_op jit(solution)/shard_map/reduce_scatter | solution.py:351
  726.9 6.8 all-reduce.1
  736.7 9.5 bitcast_convert_fusion.1
  746.6 6.5 convert_bitcast_fusion.1
  755.7 56.8 %reduce-scatter.29.cloned.1.call-done = bf16[4,256,256]{1,2,0:T(8,128)(2,1)} async-done(((bf16[4,2048,256]{1,2,0:T(8,128)(2,1)}), bf16[4,256,256]{1,2,0:T(8,128)(2,1)}) %reduce-scatter.29.cloned.1.call-update) | async-done | bytes 524304 | tf_op jit(solution)/shard_map/reduce_scatter | solution.py:402
  814.7 69.4 %reduce-scatter.25.cloned.1.call-done = bf16[1,256,512]{2,1,0:T(8,128)(2,1)} async-done(((bf16[1,2048,512]{2,1,0:T(8,128)(2,1)}), bf16[1,256,512]{2,1,0:T(8,128)(2,1)}) %reduce-scatter.25.cloned.1.call-update) | async-done | bytes 262160 | tf_op jit(solution)/shard_map/reduce_scatter | solution.py:393
  885.9 150.2 %reduce-scatter.27.cloned.1.call-done = bf16[8,256,256]{1,2,0:T(8,128)(2,1)} async-done(((bf16[8,2048,256]{1,2,0:T(8,128)(2,1)}), bf16[8,256,256]{1,2,0:T(8,128)(2,1)}) %reduce-scatter.27.cloned.1.call-update) | async-done | bytes 1048592 | tf_op jit(solution)/shard_map/reduce_scatter | solution.py:396
  1038.7 30.4 %reduce-scatter.21.cloned.1.call-done = bf16[128,2048]{1,0:T(8,128)(2,1)} async-done(((bf16[512,2048]{1,0:T(8,128)(2,1)}), bf16[128,2048]{1,0:T(8,128)(2,1)}) %reduce-scatter.21.cloned.1.call-update) | async-done | bytes 524304 | tf_op jit(solution)/shard_map/reduce_scatter | solution.py:375
  1073.5 117.5 %reduce-scatter.23.cloned.1.call-done = bf16[3,256,512]{1,2,0:T(8,128)(2,1)} async-done(((bf16[3,2048,512]{1,2,0:T(8,128)(2,1)}), bf16[3,256,512]{1,2,0:T(8,128)(2,1)}) %reduce-scatter.23.cloned.1.call-update) | async-done | bytes 786448 | tf_op jit(solution)/shard_map/reduce_scatter | solution.py:390
  1193.5 120.8 %all-reduce.5.cloned.1.call-done = (f32[4,2048]{1,0:T(4,128)}, f32[2048,4]{0,1:T(4,128)}) async-done(((f32[4,2048]{1,0:T(4,128)}, f32[2048,4]{0,1:T(4,128)}), (f32[4,2048]{1,0:T(4,128)}, f32[2048,4]{0,1:T(4,128)})) %all-reduce.5.cloned.1.call-update) | async-done | bytes 65552 | tf_op jit(solution)/shard_map/psum | solution.py:388
  (251 shorter events, 116.2 us)
Async XLA Ops:
  7.2 30.9 %all-gather.8.cloned.1.call-start = ((), (), s32[]{:S(2)}) async-start(), calls=%async_computation.10 | async-start | bytes 2621440 | tf_op jit(solution)/shard_map/all_gather | solution.py:199
  12.6 122.0 %all-gather.10.cloned.1.call-start = ((), (), s32[]{:S(2)}) async-start(), calls=%async_computation.11 | async-start | bytes 4718592 | tf_op jit(solution)/shard_map/all_gather | solution.py:231
  16.0 37.2 %copy-start.37 = (f32[1,512]{1,0:T(1,128)}, f32[1,512]{1,0:T(1,128)S(1)}, u32[]{:S(2)}) copy-start(f32[1,512]{1,0:T(1,128)S(1)} %get-tuple-element.459) | copy-start | bytes 6148
  16.0 38.5 %copy-start.39 = (f32[1,512]{1,0:T(1,128)}, f32[1,512]{1,0:T(1,128)S(1)}, u32[]{:S(2)}) copy-start(f32[1,512]{1,0:T(1,128)S(1)} %get-tuple-element.460) | copy-start | bytes 6148
  16.5 39.4 %copy-start.20 = (f32[512,64]{0,1:T(8,128)}, f32[512,64]{0,1:T(8,128)S(1)}, u32[]{:S(2)}) copy-start(f32[512,64]{0,1:T(8,128)S(1)} %get-tuple-element.452) | copy-start | bytes 393220
  16.5 39.4 %copy-start.22 = (f32[512,64]{0,1:T(8,128)}, f32[512,64]{0,1:T(8,128)S(1)}, u32[]{:S(2)}) copy-start(f32[512,64]{0,1:T(8,128)S(1)} %get-tuple-element.453) | copy-start | bytes 393220
  45.4 14.7 %copy-start.5 = (f32[3,512,512]{1,2,0:T(8,128)}, f32[3,512,512]{1,2,0:T(8,128)S(1)}, u32[]{:S(2)}) copy-start(f32[3,512,512]{1,2,0:T(8,128)S(1)} %fusion.83) | copy-start | bytes 9437188
  60.0 150.6 %all-gather.18.cloned.1.call-start = ((), (), s32[]{:S(2)}) async-start(), calls=%async_computation.24 | async-start | bytes 4718592 | tf_op jit(solution)/shard_map/all_gather | solution.py:232
  60.9 233.5 %reduce-scatter.13.cloned.1.call-start = ((), (), s32[]{:S(2)}) async-start(), calls=%async_computation.12 | async-start | bytes 2621440 | tf_op jit(solution)/shard_map/reduce_scatter | solution.py:245
  259.7 34.8 %copy-start.2 = (bf16[128,2048]{1,0:T(8,128)(2,1)S(1)}, bf16[128,2048]{1,0:T(8,128)(2,1)}, u32[]{:S(2)}) copy-start(bf16[128,2048]{1,0:T(8,128)(2,1)} %param.15) | copy-start | bytes 1572868
  259.7 36.1 %copy-start.34 = (f32[1,2048]{1,0:T(1,128)S(1)}, f32[1,2048]{1,0:T(1,128)}, u32[]{:S(2)}) copy-start(f32[1,2048]{1,0:T(1,128)} %get-tuple-element.448) | copy-start | bytes 24580
  264.6 33.5 %copy-start.51 = (s32[512,2]{0,1:T(2,128)S(1)}, s32[512,2]{0,1:T(2,128)}, u32[]{:S(2)}) copy-start(s32[512,2]{0,1:T(2,128)} %param.19) | copy-start | bytes 12292
  264.6 56.0 %copy-start.36 = (f32[2048,4]{0,1:T(4,128)S(1)}, f32[2048,4]{0,1:T(4,128)}, u32[]{:S(2)}) copy-start(f32[2048,4]{0,1:T(4,128)} %param.23) | copy-start | bytes 98308
  264.7 55.9 %all-gather.12.cloned.1.call-start = ((), (), s32[]{:S(2)}) async-start(), calls=%async_computation.13 | async-start | bytes 2621440 | tf_op jit(solution)/shard_map/all_gather | solution.py:257
  297.8 76.4 %reduce-scatter.15.cloned.1.call-start = ((), (), s32[]{:S(2)}) async-start(), calls=%async_computation.14 | async-start | bytes 2621440 | tf_op jit(solution)/shard_map/reduce_scatter | solution.py:277
  298.1 165.9 %copy-start.35 = (f32[512,4]{0,1:T(4,128)}, f32[512,4]{0,1:T(4,128)S(1)}, u32[]{:S(2)}) copy-start(f32[512,4]{0,1:T(4,128)S(1)} %convert_reduce_fusion.1) | copy-start | bytes 24580
  322.9 141.1 %copy-start.45 = (f32[512,4]{0,1:T(4,128)}, f32[512,4]{0,1:T(4,128)S(1)}, u32[]{:S(2)}) copy-start(f32[512,4]{0,1:T(4,128)S(1)} %get-tuple-element.417) | copy-start | bytes 24580
  335.4 38.8 %copy-start.10 = (bf16[128,2048]{1,0:T(8,128)(2,1)S(1)}, bf16[128,2048]{1,0:T(8,128)(2,1)}, u32[]{:S(2)}) copy-start(bf16[128,2048]{1,0:T(8,128)(2,1)} %reduce-scatter.13.cloned.1.call-done) | copy-start | bytes 1572868
  335.4 38.8 %copy-start.16 = (bf16[128,2048]{1,0:T(8,128)(2,1)S(1)}, bf16[128,2048]{1,0:T(8,128)(2,1)}, u32[]{:S(2)}) copy-start(bf16[128,2048]{1,0:T(8,128)(2,1)} %param.16) | copy-start | bytes 1572868
  342.6 56.5 %all-gather.14.cloned.1.call-start = ((), (), s32[]{:S(2)}) async-start(), calls=%async_computation.15 | async-start | bytes 2621440 | tf_op jit(solution)/shard_map/all_gather | solution.py:289
  376.4 52.9 %reduce-scatter.31.cloned.1.call-start = ((), (), s32[]{:S(2)}) async-start(), calls=%async_computation.25 | async-start | bytes 163840
  409.6 54.5 %reduce-scatter.17.cloned.1.call-start = ((), (), s32[]{:S(2)}) async-start(), calls=%async_computation.16 | async-start | bytes 2621440 | tf_op jit(solution)/shard_map/reduce_scatter | solution.py:303
  422.1 44.3 %copy-start.17 = (bf16[128,2048]{1,0:T(8,128)(2,1)S(1)}, bf16[128,2048]{1,0:T(8,128)(2,1)}, u32[]{:S(2)}) copy-start(bf16[128,2048]{1,0:T(8,128)(2,1)} %reduce-scatter.15.cloned.1.call-done) | copy-start | bytes 1572868
  422.1 68.9 %all-gather.16.cloned.1.call-start = ((), (), s32[]{:S(2)}) async-start(), calls=%async_computation.17 | async-start | bytes 2621440 | tf_op jit(solution)/shard_map/all_gather | solution.py:324
  430.1 38.1 %copy-start.46 = (bf16[128,4]{0,1:T(4,128)(2,1)}, bf16[128,4]{0,1:T(4,128)(2,1)S(1)}, u32[]{:S(2)}) copy-start(bf16[128,4]{0,1:T(4,128)(2,1)S(1)} %copy.139) | copy-start | bytes 3076
  430.2 38.1 %copy-start.52 = (f32[128]{0:T(128)}, f32[128]{0:T(128)S(1)}, u32[]{:S(2)}) copy-start(f32[128]{0:T(128)S(1)} %multiply_reduce_fusion.7) | copy-start | bytes 1540
  468.2 253.1 %reduce-scatter.19.cloned.1.call-start = ((), (), s32[]{:S(2)}) async-start(), calls=%async_computation.18 | async-start | bytes 9437184 | tf_op jit(solution)/shard_map/reduce_scatter | solution.py:351
  468.3 22.7 %copy-start.14 = (f32[512,4,128]{0,2,1:T(8,128)S(1)}, f32[512,4,128]{0,2,1:T(8,128)}, u32[]{:S(2)}) copy-start(f32[512,4,128]{0,2,1:T(8,128)} %copy-done.13) | copy-start | bytes 3145732
  497.7 10.1 copy-start.31
  512.0 9.7 copy-start.1
  531.3 10.1 copy-start.31
  545.6 9.7 copy-start.1
  571.7 240.8 %reduce-scatter.29.cloned.1.call-start = ((), (), s32[]{:S(2)}) async-start(), calls=%async_computation.23 | async-start | bytes 4718592 | tf_op jit(solution)/shard_map/reduce_scatter | solution.py:402
  578.8 305.3 %reduce-scatter.25.cloned.1.call-start = ((), (), s32[]{:S(2)}) async-start(), calls=%async_computation.21 | async-start | bytes 2359296 | tf_op jit(solution)/shard_map/reduce_scatter | solution.py:393
  584.2 451.9 %reduce-scatter.27.cloned.1.call-start = ((), (), s32[]{:S(2)}) async-start(), calls=%async_computation.22 | async-start | bytes 9437184 | tf_op jit(solution)/shard_map/reduce_scatter | solution.py:396
  594.0 129.5 %copy-start.21 = (f32[512,64]{0,1:T(8,128)S(1)}, f32[512,64]{0,1:T(8,128)}, u32[]{:S(2)}) copy-start(f32[512,64]{0,1:T(8,128)} %copy-done.20) | copy-start | bytes 393220
  594.0 129.5 %copy-start.23 = (f32[512,64]{0,1:T(8,128)S(1)}, f32[512,64]{0,1:T(8,128)}, u32[]{:S(2)}) copy-start(f32[512,64]{0,1:T(8,128)} %copy-done.22) | copy-start | bytes 393220
  594.0 475.1 %reduce-scatter.21.cloned.1.call-start = ((), (), s32[]{:S(2)}) async-start(), calls=%async_computation.19 | async-start | bytes 2621440 | tf_op jit(solution)/shard_map/reduce_scatter | solution.py:375
  723.8 9.9 copy-start.7
  736.7 9.9 copy-start.30
  736.7 9.9 copy-start.54
  746.3 444.7 %reduce-scatter.23.cloned.1.call-start = ((), (), s32[]{:S(2)}) async-start(), calls=%async_computation.20 | async-start | bytes 7077888 | tf_op jit(solution)/shard_map/reduce_scatter | solution.py:390
  753.2 315.9 %copy-start.3 = (bf16[128,2048]{1,0:T(8,128)(2,1)S(1)}, bf16[128,2048]{1,0:T(8,128)(2,1)}, u32[]{:S(2)}) copy-start(bf16[128,2048]{1,0:T(8,128)(2,1)} %param.15) | copy-start | bytes 1572868
  753.2 315.9 %copy-start.33 = (f32[1,2048]{1,0:T(1,128)S(1)}, f32[1,2048]{1,0:T(1,128)}, u32[]{:S(2)}) copy-start(f32[1,2048]{1,0:T(1,128)} %copy-done.32) | copy-start | bytes 24580
  753.2 315.9 %copy-start.50 = (f32[128]{0:T(128)S(1)}, f32[128]{0:T(128)}, u32[]{:S(2)}) copy-start(f32[128]{0:T(128)} %copy-done.49) | copy-start | bytes 1540
  753.2 317.4 %copy-start.48 = (f32[2048]{0:T(1024)S(1)}, f32[2048]{0:T(1024)}, u32[]{:S(2)}) copy-start(f32[2048]{0:T(1024)} %get-tuple-element.354) | copy-start | bytes 24580
  753.2 318.0 %copy-start.15 = (f32[128,2048]{1,0:T(8,128)S(1)}, f32[128,2048]{1,0:T(8,128)}, u32[]{:S(2)}) copy-start(f32[128,2048]{1,0:T(8,128)} %get-tuple-element.415) | copy-start | bytes 3145732
  753.2 561.1 %all-reduce.5.cloned.1.call-start = ((), (), s32[]{:S(2)}) async-start(), calls=%async_computation.26 | async-start | bytes 131072 | tf_op jit(solution)/shard_map/psum | solution.py:388
  (30 other events, 73.3 us)
Sparse Core Ops, SparseCore 0:
  12.8 25.3 all-gather.7
  60.1 74.4 all-gather.9
  137.2 73.2 all-gather.17
  264.8 29.6 reduce-scatter.12
  298.0 22.5 all-gather.11
  342.8 31.4 reduce-scatter.14
  376.5 22.5 all-gather.13
  409.7 19.5 reduce-scatter.30
  432.6 31.4 reduce-scatter.16
  468.3 22.5 all-gather.15
  571.8 149.4 reduce-scatter.18
  725.2 87.2 reduce-scatter.28
  816.6 67.4 reduce-scatter.24
  887.6 148.4 reduce-scatter.26
  1038.7 30.3 reduce-scatter.20
  1072.5 118.3 reduce-scatter.22
  1197.1 117.2 all-reduce.4
where the time goes:
time: 1330 us; the launch traced here: 1320 us
  waiting for transfers between devices  987 us (74%)
  matrix products  166 us (12%)
  local copies, waits for them, and re-layouts  88.3 us (7%)
  other arithmetic  52.9 us (4%)
  between operations  14.9 us (1%)
    reduce_scatter x1, waiting for transfers between devices, local(): lax.psum_scatter(gate_up_grad.reshape(2 * experts, model_width, hidden_co...  150 us
    reduce_scatter x1, waiting for transfers between devices, local(): lax.psum_scatter(kv_terms.astype(jnp.bfloat16), 'ctx', scatter_dimension=...  127 us
    psum x1, waiting for transfers between devices, local(): gains_grad, router_grad = lax.psum((gains_grad, router_grad), ('ctx', 'wt'))  121 us
    reduce_scatter x1, waiting for transfers between devices, local(): lax.psum_scatter(qkv_grad.astype(jnp.bfloat16), 'ctx', scatter_dimension=...  117 us
    all_gather x1, waiting for transfers between devices, local(): lax.all_gather(key_rows, 'ctx', axis=0, tiled=True)  70.2 us
    reduce_scatter x1, waiting for transfers between devices, local(): lax.psum_scatter(out_grad[None].astype(jnp.bfloat16), 'ctx', scatter_dime...  69.4 us
    all_gather x1, waiting for transfers between devices, local(): lax.all_gather(val_rows, 'ctx', axis=0, tiled=True)  64 us
    reduce_scatter x1, waiting for transfers between devices, local(): lax.psum_scatter(down_grad.astype(jnp.bfloat16), 'ctx', scatter_dimension...  56.8 us
  transfers between devices with their start and end apart: 17, of which 17 were waited for; matrix products, arithmetic and copies ran while one was open for 8% of the time, Pallas kernels for 0%

commit v1 on v0

v1 whole, which is shorter than its diff:
```python
import functools
import math

import jax
import jax.numpy as jnp
from jax import lax
from jax.experimental import pallas as pl
from jax.experimental.pallas import tpu as pltpu
from jax.sharding import Mesh
from jax.sharding import PartitionSpec as P

HEAD_DIM = 128
LOG2E = math.log2(math.e)
VMEM_BYTES = 56 * 1024 * 1024

norm_eps = 1e-05
f32 = jnp.float32
bf16 = jnp.bfloat16

SWAP = [(0, 1), (1, 0)]
DOT_NT = (((1,), (1,)), ((), ()))
DOT_NN = (((1,), (0,)), ((), ()))


def attend_kernel(groups, chunk, score_scale, q_ref, tok_q_ref, start_q_ref, *refs):
    key_refs = refs[: 3 * groups]
    o_ref, lse_ref = refs[3 * groups : 3 * groups + 2]
    vt_refs = refs[3 * groups + 2 :]
    rows = q_ref.shape[0]

    @pl.when(pl.program_id(0) == 0)
    def _():
        for g in range(groups):
            v_ref, vt_ref = key_refs[3 * g + 1], vt_refs[g]

            def turn(j, carry):
                r = pl.ds(pl.multiple_of(j * chunk, chunk), chunk)
                vt_ref[:, r] = v_ref[r, :].T
                return carry

            lax.fori_loop(0, v_ref.shape[0] // chunk, turn, 0)

    queries = q_ref[...]
    tok_q = tok_q_ref[...]
    start_q = start_q_ref[...]
    state = (
        jnp.full((1, rows), -1e30, f32),
        jnp.zeros((1, rows), f32),
        jnp.zeros((queries.shape[1], rows), f32),
    )
    for g in range(groups):
        k_ref, _, tok_k_ref = key_refs[3 * g : 3 * g + 3]
        vt_ref = vt_refs[g]

        def step(j, carry):
            run_max, run_sum, acc = carry
            r = pl.ds(pl.multiple_of(j * chunk, chunk), chunk)
            s = lax.dot_general(k_ref[r, :], queries, DOT_NT, preferred_element_type=f32)
            tok_k = tok_k_ref[r, :]
            s = jnp.where((tok_k <= tok_q) & (tok_k >= start_q), s * score_scale, -1e30)
            new_max = jnp.maximum(run_max, jnp.max(s, axis=0, keepdims=True))
            p = jnp.exp2(s - new_max)
            shrink = jnp.exp2(run_max - new_max)
            run_sum = run_sum * shrink + jnp.sum(p, axis=0, keepdims=True)
            acc = acc * shrink + lax.dot_general(
                vt_ref[:, r], p.astype(bf16), DOT_NN, preferred_element_type=f32
            )
            return new_max, run_sum, acc

        steps = k_ref.shape[0] // chunk
        state = lax.fori_loop(0, steps, step, state, unroll=steps <= 4)
    run_max, run_sum, acc = state
    o_ref[...] = (acc / run_sum).T
    lse_ref[...] = run_max + jnp.log2(run_sum)


def attend(packed, tok_q, start_q, key_groups):
    rows = packed.shape[0]
    block = min(1024, rows)
    chunk = 1024
    row = pl.BlockSpec((1, block), lambda i: (0, i))
    in_specs = [pl.BlockSpec((block, HEAD_DIM), lambda i: (i, 0)), row, row]
    operands = [packed, tok_q, start_q]
    scratch = []
    keys = 0
    for array, k_col, v_col, tok_k in key_groups:
        count = array.shape[0]
        keys += count
        in_specs += [
            pl.BlockSpec((count, HEAD_DIM), lambda i, col=k_col: (0, col)),
            pl.BlockSpec((count, HEAD_DIM), lambda i, col=v_col: (0, col)),
            pl.BlockSpec((count, 1), lambda i: (0, 0)),
        ]
        operands += [array, array, tok_k]
        scratch.append(pltpu.VMEM((HEAD_DIM, count), bf16))
    return pl.pallas_call(
        functools.partial(
            attend_kernel, len(key_groups), chunk, LOG2E / math.sqrt(HEAD_DIM)
        ),
        grid=(rows // block,),
        in_specs=in_specs,
        out_specs=[pl.BlockSpec((block, HEAD_DIM), lambda i: (i, 0)), row],
        out_shape=[
            jax.ShapeDtypeStruct((rows, HEAD_DIM), f32),
            jax.ShapeDtypeStruct((1, rows), f32),
        ],
        scratch_shapes=scratch,
        compiler_params=pltpu.CompilerParams(vmem_limit_bytes=VMEM_BYTES),
        cost_estimate=pl.CostEstimate(
            flops=8 * rows * keys * HEAD_DIM,
            bytes_accessed=4 * (rows + keys) * HEAD_DIM,
            transcendentals=rows * keys,
        ),
        name="attend",
    )(*operands)


def attend_grad_kernel(
    chunk,
    score_scale,
    grad_scale,
    q_ref,
    do_ref,
    lse_ref,
    delta_ref,
    tok_q_ref,
    start_q_ref,
    dq_in_ref,
    k_ref,
    v_ref,
    tok_k_ref,
    dq_ref,
    dkv_ref,
    kt_ref,
    dk_acc,
    dv_acc,
):
    steps = k_ref.shape[0] // chunk

    @pl.when(pl.program_id(0) == 0)
    def _():
        dk_acc[...] = jnp.zeros_like(dk_acc)
        dv_acc[...] = jnp.zeros_like(dv_acc)

        def turn(j, carry):
            r = pl.ds(pl.multiple_of(j * chunk, chunk), chunk)
            kt_ref[:, r] = k_ref[r, :].T
            return carry

        lax.fori_loop(0, steps, turn, 0)

    queries = q_ref[...]
    d_out = do_ref[...]
    tok_q = tok_q_ref[...]
    start_q = start_q_ref[...]
    lse = lse_ref[...]
    delta = delta_ref[...]

    def step(j, dq_t):
        r = pl.ds(pl.multiple_of(j * chunk, chunk), chunk)
        s = lax.dot_general(k_ref[r, :], queries, DOT_NT, preferred_element_type=f32)
        tok_k = tok_k_ref[r, :]
        allowed = (tok_k <= tok_q) & (tok_k >= start_q)
        p = jnp.exp2(jnp.where(allowed, s * score_scale - lse, -1e30))
        dp = lax.dot_general(v_ref[r, :], d_out, DOT_NT, preferred_element_type=f32)
        ds = (p * (dp - delta)).astype(bf16)
        dv_acc[r, :] += lax.dot_general(
            p.astype(bf16), d_out, DOT_NN, preferred_element_type=f32
        )
        dk_acc[r, :] += lax.dot_general(ds, queries, DOT_NN, preferred_element_type=f32)
        return dq_t + lax.dot_general(kt_ref[:, r], ds, DOT_NN, preferred_element_type=f32)

    dq_t = lax.fori_loop(
        0,
        steps,
        step,
        jnp.zeros((queries.shape[1], queries.shape[0]), f32),
        unroll=steps <= 4,
    )
    dq_ref[...] = dq_in_ref[...] + (dq_t * grad_scale).T

    @pl.when(pl.program_id(0) == pl.num_programs(0) - 1)
    def _():
        dkv_ref[:, :HEAD_DIM] = (dk_acc[...] * grad_scale).astype(dkv_ref.dtype)
        dkv_ref[:, HEAD_DIM:] = dv_acc[...].astype(dkv_ref.dtype)


def attend_grad(packed, d_out, lse, delta, tok_q, start_q, dq_in, key_group, out_type):
    rows = packed.shape[0]
    array, k_col, v_col, tok_k = key_group
    keys = array.shape[0]
    block = min(1024, rows)
    chunk = 1024
    row = pl.BlockSpec((1, block), lambda i: (0, i))
    head = pl.BlockSpec((block, HEAD_DIM), lambda i: (i, 0))
    return pl.pallas_call(
        functools.partial(
            attend_grad_kernel,
            chunk,
            LOG2E / math.sqrt(HEAD_DIM),
            1.0 / math.sqrt(HEAD_DIM),
        ),
        grid=(rows // block,),
        in_specs=[
            head,
            head,
            row,
            row,
            row,
            row,
            head,
            pl.BlockSpec((keys, HEAD_DIM), lambda i: (0, k_col)),
            pl.BlockSpec((keys, HEAD_DIM), lambda i: (0, v_col)),
            pl.BlockSpec((keys, 1), lambda i: (0, 0)),
        ],
        out_specs=[head, pl.BlockSpec((keys, 2 * HEAD_DIM), lambda i: (0, 0))],
        out_shape=[
            jax.ShapeDtypeStruct((rows, HEAD_DIM), f32),
            jax.ShapeDtypeStruct((keys, 2 * HEAD_DIM), out_type),
        ],
        scratch_shapes=[
            pltpu.VMEM((HEAD_DIM, keys), bf16),
            pltpu.VMEM((keys, HEAD_DIM), f32),
            pltpu.VMEM((keys, HEAD_DIM), f32),
        ],
        compiler_params=pltpu.CompilerParams(vmem_limit_bytes=VMEM_BYTES),
        cost_estimate=pl.CostEstimate(
            flops=16 * rows * keys * HEAD_DIM,
            bytes_accessed=12 * (rows + keys) * HEAD_DIM,
            transcendentals=rows * keys,
        ),
        name="attend_grad",
    )(packed, d_out, lse, delta, tok_q, start_q, dq_in, array, array, tok_k)


def pack_kernel(raw0_ref, raw1_ref, inv_ref, cos_ref, sin_ref, gain_ref, out_ref):
    half = raw0_ref.shape[1]
    for i, raw_ref in enumerate((raw0_ref, raw1_ref)):
        r = slice(i * half, (i + 1) * half)
        for j in range(2):
            u = raw_ref[j] * inv_ref[r, j : j + 1] * gain_ref[j : j + 1, :]
            turned = u * cos_ref[r, :] + pltpu.roll(u, HEAD_DIM // 2, 1) * sin_ref[r, :]
            out_ref[0, r, j * HEAD_DIM : (j + 1) * HEAD_DIM] = turned.astype(bf16)
        out_ref[0, r, 2 * HEAD_DIM :] = raw_ref[2].astype(bf16)


def pack_heads(raw0, raw1, inv, cos_tab, sin_tab, gains):
    half = raw0.shape[1]
    rows = 2 * half
    heads = raw0.shape[2] // HEAD_DIM
    raw = pl.BlockSpec((3, half, HEAD_DIM), lambda h: (0, 0, h))
    table = pl.BlockSpec((rows, HEAD_DIM), lambda h: (0, 0))
    return pl.pallas_call(
        pack_kernel,
        grid=(heads,),
        in_specs=[
            raw,
            raw,
            pl.BlockSpec((rows, 2), lambda h: (0, 0)),
            table,
            table,
            pl.BlockSpec((2, HEAD_DIM), lambda h: (0, h)),
        ],
        out_specs=pl.BlockSpec((1, rows, 3 * HEAD_DIM), lambda h: (h, 0, 0)),
        out_shape=jax.ShapeDtypeStruct((heads, rows, 3 * HEAD_DIM), bf16),
        cost_estimate=pl.CostEstimate(
            flops=20 * rows * heads * HEAD_DIM,
            bytes_accessed=18 * rows * heads * HEAD_DIM,
            transcendentals=0,
        ),
        name="pack_heads",
    )(raw0, raw1, inv, cos_tab, sin_tab, gains)


def raw_grad_kernel(dq_ref, dkv_ref, packed_ref, coef_ref, cos_ref, sin_ref, gain_ref, out_ref, sum_ref):
    @pl.when(pl.program_id(0) == 0)
    def _():
        sum_ref[...] = jnp.zeros_like(sum_ref)

    cos_tab = cos_ref[...]
    sin_tab = sin_ref[...]

    def turn_back(u):
        return u * cos_tab - pltpu.roll(u, HEAD_DIM // 2, 1) * sin_tab

    for j, grad_ref in enumerate((dq_ref, dkv_ref)):
        gain = gain_ref[j : j + 1, :]
        cols = slice(j * HEAD_DIM, (j + 1) * HEAD_DIM)
        d_norm = turn_back(grad_ref[:, :HEAD_DIM])
        hat = turn_back(packed_ref[:, cols].astype(f32)) / gain
        sum_ref[j : j + 1, :] += jnp.sum(d_norm * hat, axis=0, keepdims=True)
        inv = coef_ref[:, 2 * j : 2 * j + 1]
        inner = coef_ref[:, 2 * j + 1 : 2 * j + 2]
        out_ref[:, cols] = (inv * (d_norm * gain - hat * inner)).astype(bf16)
    out_ref[:, 2 * HEAD_DIM :] = dkv_ref[:, HEAD_DIM:].astype(bf16)


def raw_grad(d_query, d_kv, packed, coef, cos_tab, sin_tab, gains):
    rows = packed.shape[0]
    block = min(512, rows)

    def wide(cols):
        return pl.BlockSpec((block, cols), lambda i: (i, 0))

    whole = pl.BlockSpec((2, HEAD_DIM), lambda i: (0, 0))
    return pl.pallas_call(
        raw_grad_kernel,
        grid=(rows // block,),
        in_specs=[
            wide(HEAD_DIM),
            wide(2 * HEAD_DIM),
            wide(3 * HEAD_DIM),
            wide(4),
            wide(HEAD_DIM),
            wide(HEAD_DIM),
            whole,
        ],
        out_specs=[wide(3 * HEAD_DIM), whole],
        out_shape=[
            jax.ShapeDtypeStruct((rows, 3 * HEAD_DIM), bf16),
            jax.ShapeDtypeStruct((2, HEAD_DIM), f32),
        ],
        cost_estimate=pl.CostEstimate(
            flops=40 * rows * HEAD_DIM, bytes_accessed=40 * rows * HEAD_DIM, transcendentals=0
        ),
        name="raw_grad",
    )(d_query, d_kv, packed, coef, cos_tab, sin_tab, gains)


def token_places(seq_lengths, permutation):
    seq_ends = jnp.cumsum(seq_lengths)
    seq_starts = seq_ends - seq_lengths
    seq_id = jnp.sum((permutation[:, None] >= seq_ends[None, :]).astype(jnp.int32), axis=1)
    member = seq_id[:, None] == jnp.arange(seq_lengths.shape[0], dtype=jnp.int32)[None, :]
    return jnp.sum(jnp.where(member, seq_starts[None, :], 0), axis=1)


def near_first(a, axis, y_pos, c_pos):
    a = jnp.where(y_pos == 0, a, jnp.flip(a, axis))
    return jnp.where(c_pos == 0, a, jnp.flip(a, axis + 1))


def norm_back(grad_out, hat_rows, inv_rows, gain_row):
    grad_hat = grad_out * gain_row
    return inv_rows * (grad_hat - hat_rows * jnp.mean(grad_hat * hat_rows, axis=-1, keepdims=True))


def gather_halves(rows):
    core = lax.ppermute(rows, "c", SWAP)
    far = lax.ppermute(rows, "y", SWAP)
    far_core = lax.ppermute(far, "c", SWAP)
    return [jnp.concatenate([rows, core]), jnp.concatenate([far, far_core])]


def scatter_halves(parts):
    near, far = parts
    n = near.shape[0] // 2
    far_sum = far[:n].astype(f32) + lax.ppermute(far[n:], "c", SWAP).astype(f32)
    far_sum = lax.ppermute(far_sum.astype(bf16), "y", SWAP).astype(f32)
    near_sum = near[:n].astype(f32) + lax.ppermute(near[n:], "c", SWAP).astype(f32)
    return near_sum + far_sum


def sum_near(a):
    a = a + jnp.flip(lax.ppermute(a, "c", SWAP), -2)
    return a + jnp.flip(lax.ppermute(a, "y", SWAP), -3)


def sum_line(a, z_count):
    step = 1
    while step < z_count:
        a = a + lax.ppermute(a, "z", [(i, i ^ step) for i in range(z_count)])
        step *= 2
    return a


def scatter_line(part, z_pos, z_count):
    up = down = None
    last = z_count - 1
    for s in range(last):
        to_up = lax.dynamic_index_in_dim(part, jnp.clip(last - s + z_pos, 0, last), 0, False)
        to_down = lax.dynamic_index_in_dim(part, jnp.clip(z_pos + s - last, 0, last), 0, False)
        if s > 0:
            to_up = (to_up.astype(f32) + up.astype(f32)).astype(bf16)
            to_down = (to_down.astype(f32) + down.astype(f32)).astype(bf16)
        up = lax.ppermute(to_up, "z", [(i, i + 1) for i in range(s + 1)])
        down = lax.ppermute(to_down, "z", [(last - i, last - i - 1) for i in range(s + 1)])
    mine = lax.dynamic_index_in_dim(part, z_pos, 0, False).astype(f32)
    return mine + up.astype(f32) + down.astype(f32)


def local(
    z_count,
    x_count,
    block_in,
    target,
    seq_lengths,
    permutation,
    routes,
    attn_qkv,
    attn_out,
    norm_gains,
    router,
    gate_up,
    down,
):
    z_pos = lax.axis_index("z")
    x_pos = lax.axis_index("x")
    y_pos = lax.axis_index("y")
    c_pos = lax.axis_index("c")
    pair = x_count == 2
    local_rows, model_width = block_in.shape
    tok_rows = 4 * local_rows
    line_rows = z_count * tok_rows
    head_cols = attn_qkv.shape[2]
    hidden_cols = gate_up.shape[3]
    experts = gate_up.shape[1]
    wide_block = model_width // z_count
    out_block = wide_block // x_count
    wt_pos = y_pos * 2 + c_pos

    qkv_b = attn_qkv.astype(bf16)
    out_b = attn_out.astype(bf16)
    gu_b = gate_up.astype(bf16)
    down_b = down.astype(bf16)
    router_b = router.astype(bf16)

    resid_in = block_in.astype(f32)
    inv_first = lax.rsqrt(jnp.mean(resid_in * resid_in, axis=-1, keepdims=True) + norm_eps)
    hat_first = resid_in * inv_first
    normed = (hat_first * norm_gains[0]).astype(bf16)
    normed_h = gather_halves(normed)

    start_all = token_places(seq_lengths, permutation)
    shape = (z_count, x_count, 2, 2, local_rows)
    tok_all = near_first(permutation.reshape(shape), 2, y_pos, c_pos)
    start_all = near_first(start_all.reshape(shape), 2, y_pos, c_pos)

    def of_x(a, at):
        return lax.dynamic_index_in_dim(a, at, 1, False).reshape(line_rows)

    tok_own = of_x(tok_all, x_pos)
    start_own = of_x(start_all, x_pos)
    tok_q = tok_own.reshape(1, line_rows)
    start_q = start_own.reshape(1, line_rows)
    half_dim = HEAD_DIM // 2
    frequency = jnp.exp(
        jnp.arange(half_dim, dtype=f32) * (-2.0 * math.log(10000.0) / HEAD_DIM)
    )
    angles = (tok_own - start_own).astype(f32)[:, None] * frequency[None, :]
    cosine, sine = jnp.cos(angles), jnp.sin(angles)
    cos_tab = jnp.concatenate([cosine, cosine], axis=1)
    sin_tab = jnp.concatenate([-sine, sine], axis=1)

    raw_h = [
        jnp.einsum("td,kdc->ktc", n, qkv_b, preferred_element_type=f32) for n in normed_h
    ]
    squares = jnp.concatenate([jnp.sum(r[:2] * r[:2], axis=-1) for r in raw_h], axis=1)
    squares = sum_near(squares.reshape(2, 2, 2, local_rows)).reshape(2, tok_rows)
    inv_qk = lax.rsqrt(squares / model_width + norm_eps)
    inv_line = lax.all_gather(inv_qk, "z", axis=0)
    gain_qk = lax.dynamic_slice_in_dim(norm_gains[2:], wt_pos * head_cols, head_cols, 1)
    payload = pack_heads(
        raw_h[0],
        raw_h[1],
        inv_qk.T,
        lax.dynamic_slice_in_dim(cos_tab, z_pos * tok_rows, tok_rows),
        lax.dynamic_slice_in_dim(sin_tab, z_pos * tok_rows, tok_rows),
        gain_qk,
    )
    packed = lax.all_to_all(payload, "z", 0, 0, tiled=True).reshape(line_rows, 3 * HEAD_DIM)
    kv_own = packed[:, HEAD_DIM:]
    tok_col = tok_own.reshape(line_rows, 1)
    if pair:
        kv_far = lax.ppermute(kv_own, "x", SWAP)
        groups = [
            (kv_far, 0, 1, of_x(tok_all, 1 - x_pos).reshape(line_rows, 1)),
            (packed, 1, 2, tok_col),
        ]
        key_groups = groups[::-1]
    else:
        kv_all = lax.all_gather(kv_own, "x", axis=0)
        tok_x = jnp.moveaxis(tok_all, 1, 0).reshape(x_count, line_rows, 1)
        groups = [(kv_all[i], 0, 1, tok_x[i]) for i in range(x_count)]
        key_groups = [
            (kv_all.reshape(-1, 2 * HEAD_DIM), 0, 1, tok_x.reshape(-1, 1))
        ]
    attn_f, row_lse = attend(packed, tok_q, start_q, key_groups)

    def to_tokens(rows, cols):
        parts = lax.all_to_all(
            rows.reshape(z_count, tok_rows, cols), "z", 0, 0, tiled=True
        )
        return parts

    attn_parts = to_tokens(attn_f.astype(bf16), HEAD_DIM)
    attn_b = jnp.moveaxis(attn_parts, 0, 1).reshape(tok_rows, head_cols)
    half = tok_rows // 2

    def halves(a):
        return [a[:half], a[half:]]

    attn_y = scatter_halves(
        [
            lax.dot_general(a, out_b, DOT_NT, preferred_element_type=f32).astype(bf16)
            for a in halves(attn_b)
        ]
    )
    residual = resid_in + attn_y
    inv_second = lax.rsqrt(jnp.mean(residual * residual, axis=-1, keepdims=True) + norm_eps)
    hat_second = residual * inv_second
    mixed_rows = (hat_second * norm_gains[1]).astype(bf16)
    mixed_h = gather_halves(mixed_rows)

    route_rows = near_first(routes.reshape(2, 2, local_rows, -1), 0, y_pos, c_pos)
    route_rows = route_rows.reshape(tok_rows, -1)
    choose = jnp.sum(
        (route_rows[:, :, None] == jnp.arange(experts, dtype=jnp.int32)[None, None, :]).astype(f32),
        axis=1,
    )
    choose_h = halves(choose)
    prob_h = [
        jax.nn.softmax(jnp.dot(m, router_b, preferred_element_type=f32), axis=-1)
        for m in mixed_h
    ]
    gate_w_h = [p * ch for p, ch in zip(prob_h, choose_h)]
    pre_h = [
        jnp.einsum("td,kedf->ketf", m, gu_b, preferred_element_type=f32) for m in mixed_h
    ]
    hidden_h = []
    for pre, gate_w in zip(pre_h, gate_w_h):
        gate_act = pre[0] * jax.nn.sigmoid(pre[0])
        hidden_h.append((gate_w.T[:, :, None] * gate_act * pre[1]).astype(bf16))
    expert_y = scatter_halves(
        [
            jnp.einsum("etf,edf->td", h, down_b, preferred_element_type=f32).astype(bf16)
            for h in hidden_h
        ]
    )
    out_local = residual + expert_y
    block_out = out_local.astype(bf16)
    cot_local = out_local - target.astype(f32)
    cot_h = gather_halves(cot_local.astype(bf16))

    d_pre_h = []
    d_mixed_parts = []
    router_parts = []
    for cot, pre, gate_w, prob, ch, mixed in zip(
        cot_h, pre_h, gate_w_h, prob_h, choose_h, mixed_h
    ):
        d_hid = (
            jnp.einsum("td,edf->etf", cot, down_b, preferred_element_type=f32)
            .astype(bf16)
            .astype(f32)
        )
        gate_in, up_in = pre[0], pre[1]
        gate_sig = jax.nn.sigmoid(gate_in)
        gate_act = gate_in * gate_sig
        d_gate_w = jnp.sum(d_hid * gate_act * up_in, axis=-1).T
        scaled = d_hid * gate_w.T[:, :, None]
        d_gate_in = scaled * up_in * gate_sig * (1.0 + gate_in * (1.0 - gate_sig))
        d_up_in = scaled * gate_act
        d_pre = jnp.stack([d_gate_in, d_up_in]).astype(bf16)
        d_pre_h.append(d_pre)
        d_prob = d_gate_w * ch
        d_logit = (prob * (d_prob - jnp.sum(prob * d_prob, axis=-1, keepdims=True))).astype(bf16)
        d_mixed_parts.append(
            (
                jnp.einsum("ketf,kedf->td", d_pre, gu_b, preferred_element_type=f32)
                + lax.dot_general(d_logit, router_b, DOT_NT, preferred_element_type=f32)
            ).astype(bf16)
        )
        router_parts.append(
            lax.dot_general(d_logit, mixed, (((0,), (0,)), ((), ())), preferred_element_type=f32)
        )
    router_rows = router_parts[0] + router_parts[1]
    d_mixed = scatter_halves(d_mixed_parts)
    gain_second = jnp.sum(d_mixed * hat_second, axis=0, keepdims=True)
    d_resid = cot_local + norm_back(d_mixed, hat_second, inv_second, norm_gains[1])
    d_resid_h = gather_halves(d_resid.astype(bf16))
    d_attn = jnp.concatenate(
        [jnp.dot(d, out_b, preferred_element_type=f32).astype(bf16) for d in d_resid_h]
    )

    d_attn_parts = jnp.moveaxis(d_attn.reshape(tok_rows, z_count, HEAD_DIM), 1, 0)
    d_out = lax.all_to_all(d_attn_parts, "z", 0, 0, tiled=True).reshape(line_rows, HEAD_DIM)
    delta = jnp.sum(d_out.astype(f32) * attn_f, axis=-1).reshape(1, line_rows)
    d_query = jnp.zeros((line_rows, HEAD_DIM), f32)
    d_kv = []
    for i, group in enumerate(groups):
        out_type = f32 if pair and i == 1 else bf16
        d_query, d_group = attend_grad(
            packed, d_out, row_lse, delta, tok_q, start_q, d_query, group, out_type
        )
        d_kv.append(d_group)
    if pair:
        d_kv = d_kv[1] + lax.ppermute(d_kv[0], "x", SWAP).astype(f32)
    else:
        d_kv = lax.psum_scatter(jnp.stack(d_kv), "x", scatter_dimension=0).astype(f32)
    inner = jnp.stack(
        [
            jnp.sum(d_query * packed[:, :HEAD_DIM].astype(f32), axis=-1),
            jnp.sum(d_kv[:, :HEAD_DIM] * packed[:, HEAD_DIM : 2 * HEAD_DIM].astype(f32), axis=-1),
        ]
    )
    inner = sum_line(sum_near(inner.reshape(2, z_count, 2, 2, local_rows)), z_count)
    inner = inner.reshape(2, line_rows) / model_width
    inv_line = jnp.moveaxis(inv_line, 0, 1).reshape(2, line_rows)
    coef = jnp.stack([inv_line[0], inner[0], inv_line[1], inner[1]], axis=1)
    head_gain = lax.dynamic_slice_in_dim(gain_qk, z_pos * HEAD_DIM, HEAD_DIM, 1)
    d_raw, gain_sums = raw_grad(
        d_query, d_kv, packed, coef, cos_tab, sin_tab, head_gain
    )
    gain_full = lax.dynamic_update_slice_in_dim(
        jnp.zeros((2, model_width), f32), gain_sums, (wt_pos * z_count + z_pos) * HEAD_DIM, 1
    )

    d_proj = jnp.moveaxis(
        to_tokens(d_raw, 3 * HEAD_DIM).reshape(z_count, tok_rows, 3, HEAD_DIM), 2, 0
    )
    d_proj = jnp.moveaxis(d_proj, 1, 2).reshape(3, tok_rows, head_cols)
    d_normed_h = [
        jnp.einsum("ktc,kdc->td", d, qkv_b, preferred_element_type=f32)
        for d in (d_proj[:, :half], d_proj[:, half:])
    ]
    d_normed = scatter_halves([d.astype(bf16) for d in d_normed_h])
    gain_first = jnp.sum(d_normed * hat_first, axis=0, keepdims=True)
    input_grad = (d_resid + norm_back(d_normed, hat_first, inv_first, norm_gains[0])).astype(bf16)

    def sum_all(a):
        a = a + lax.ppermute(a, "c", SWAP)
        a = a + lax.ppermute(a, "y", SWAP)
        a = a + lax.ppermute(a, "x", SWAP) if pair else lax.psum(a, "x")
        return sum_line(a, z_count)

    small = sum_all(jnp.concatenate([gain_second, gain_full, router_rows]))
    gains_grad = jnp.concatenate([sum_all(gain_first), small[:3]])
    router_grad = small[3:].T

    def scatter_x(a):
        if pair:
            mine = lax.dynamic_index_in_dim(a, x_pos, 0, False)
            other = lax.dynamic_index_in_dim(a, 1 - x_pos, 0, False)
            return mine.astype(f32) + lax.ppermute(other.astype(bf16), "x", SWAP).astype(f32)
        return lax.psum_scatter(a.astype(bf16), "x", scatter_dimension=0).astype(f32)

    def split_x(rows):
        a = rows.reshape(tok_rows, z_count, x_count, out_block)
        mine = lax.dynamic_index_in_dim(a, x_pos, 2, False)
        other = lax.dynamic_index_in_dim(a, 1 - x_pos, 2, False)
        return [mine, lax.ppermute(other, "x", SWAP)]

    def weight_grad(wide_h, narrow, spec):
        wide = jnp.concatenate(wide_h)
        if pair:
            narrow_far = lax.ppermute(narrow, "x", SWAP)
            mine, far = split_x(wide)
            part = jnp.einsum(spec, mine, narrow, preferred_element_type=f32)
            part = part + jnp.einsum(spec, far, narrow_far, preferred_element_type=f32)
        else:
            a = wide.reshape(tok_rows, z_count, x_count, out_block)
            part = scatter_x(
                jnp.stack(
                    [
                        jnp.einsum(spec, a[:, :, i], narrow, preferred_element_type=f32)
                        for i in range(x_count)
                    ]
                )
            )
        return scatter_line(part.astype(bf16), z_pos, z_count)

    down_part = weight_grad(cot_h, jnp.concatenate(hidden_h, axis=1), "tbd,etf->bedf")
    gate_up_part = weight_grad(mixed_h, jnp.concatenate(d_pre_h, axis=2), "tbd,ketf->bkedf")
    out_part = weight_grad(d_resid_h, attn_b, "tbd,tc->bdc")

    normed_all = jnp.concatenate(normed_h)
    normed_half = lax.dynamic_slice_in_dim(
        normed_all, c_pos * (model_width // 2), model_width // 2, 1
    )
    normed_half = lax.all_gather(normed_half, "z", axis=0, tiled=True)
    normed_other = lax.ppermute(normed_half, "c", SWAP)
    tn = (((0,), (0,)), ((), ()))
    grad_mine = lax.dot_general(normed_half, d_raw, tn, preferred_element_type=f32).astype(bf16)
    d_raw_other = jnp.flip(
        d_raw.reshape(z_count, 2, 2, local_rows, 3 * HEAD_DIM), 2
    ).reshape(line_rows, 3 * HEAD_DIM)
    grad_other = lax.dot_general(
        normed_other, d_raw_other, tn, preferred_element_type=f32
    ).astype(bf16)
    qkv_full = jnp.where(
        c_pos == 0,
        jnp.stack([grad_mine, grad_other]),
        jnp.stack([grad_other, grad_mine]),
    ).reshape(z_count, x_count, out_block, 3 * HEAD_DIM)
    qkv_line = scatter_x(jnp.moveaxis(qkv_full, 1, 0)).astype(bf16)
    qkv_heads = lax.all_to_all(qkv_line, "z", 0, 0, tiled=True)
    qkv_part = (
        qkv_heads.reshape(z_count, out_block, 3, HEAD_DIM)
        .transpose(2, 1, 0, 3)
        .reshape(3, out_block, head_cols)
        .astype(f32)
    )
    return (
        block_out,
        input_grad,
        qkv_part,
        out_part,
        gains_grad,
        router_grad,
        gate_up_part,
        down_part,
    )


def solution(mesh):
    ctx_count = mesh.shape["ctx"]

    def run(*args):
        heads = args[5].shape[2] // HEAD_DIM
        z_count = heads // mesh.shape["wt"]
        x_count = ctx_count // z_count
        grid = Mesh(mesh.devices.reshape(z_count, x_count, 2, 2), ("z", "x", "y", "c"))
        ctx, wt = ("z", "x"), ("y", "c")
        return jax.shard_map(
            functools.partial(local, z_count, x_count),
            mesh=grid,
            in_specs=(
                P(ctx + wt, None),
                P(ctx + wt, None),
                P(),
                P(),
                P(ctx, None),
                P(None, None, wt),
                P(None, wt),
                P(),
                P(),
                P(None, None, None, wt),
                P(None, None, wt),
            ),
            out_specs=(
                P(ctx + wt, None),
                P(ctx + wt, None),
                P(None, ctx, wt),
                P(ctx, wt),
                P(),
                P(),
                P(None, None, ctx, wt),
                P(None, ctx, wt),
            ),
            check_vma=False,
        )(*args)

    return run
```

time: 1330 us -> 695 us (0.52)
  waiting for transfers between devices: 987 us -> 167 us
  starting transfers between devices: 1.96 us -> 125 us
  matrix products: 166 us -> 80.9 us
  Pallas kernels: 0 us -> 61.9 us
  other arithmetic: 52.9 us -> 96.9 us
  blocking collectives: 12.7 us -> 54.5 us
    reduce_scatter x9 -> x0, waiting for transfers between devices: 647 us -> none  [the longest x1 150 us: local(): lax.psum_scatter(gate_up_grad.reshape(2 * experts, model_width, hidden_co...]
    all_gather x6 -> x1, waiting for transfers between devices: 212 us -> 0.02 us  [local(): normed_half = lax.all_gather(normed_half, 'z', axis=0, tiled=True)]
    ppermute x0 -> x68, waiting for transfers between devices: none -> 157 us  [the longest x6 44.4 us: sum_line(): a = a + lax.ppermute(a, 'z', [(i, i ^ step) for i in range(z_count)])]
    psum x1 -> x0, waiting for transfers between devices: 121 us -> none  [local(): gains_grad, router_grad = lax.psum((gains_grad, router_grad), ('ctx', 'wt'))]
    ppermute x0 -> x68, starting transfers between devices: none -> 107 us  [the longest x9 44.5 us: scatter_line(): up = lax.ppermute(to_up, 'z', [(i, i + 1) for i in range(s + 1)])]
    dot_general x29 -> x30, matrix products: 166 us -> 80.9 us  [the longest x3 11.3 us: weight_grad(): part = part + jnp.einsum(spec, far, narrow_far, preferred_element_type=f32)]
    pallas_call x0 -> x5, Pallas kernels: none -> 61.9 us  [the longest x2 31.8 us: attend_grad(): pl.pallas_call(functools.partial(attend_grad_kernel, chunk, LOG2E / math....]
    convert_element_type x7 -> x27, other arithmetic: 8.98 us -> 56.3 us  [the longest x6 12.6 us: scatter_line(): to_up = (to_up.astype(f32) + up.astype(f32)).astype(bf16)]
  transfers between devices with their start and end apart: 17 -> 73, of which waited for: 17 -> 22; matrix products, arithmetic and copies ran while one was open for 8% -> 34% of each run, Pallas kernels for 0% -> 6%
where the time goes in v1:
time: 695 us; the launch traced here: 685 us
  waiting for transfers between devices  167 us (24%)
  starting transfers between devices  125 us (18%)
  other arithmetic  96.9 us (14%)
  local copies, waits for them, and re-layouts  82.5 us (12%)
  matrix products  80.9 us (12%)
  Pallas kernels  61.9 us (9%)
  blocking collectives  54.5 us (8%)
  between operations  16.1 us (2%)
    ppermute x9, starting transfers between devices, scatter_line(): up = lax.ppermute(to_up, 'z', [(i, i + 1) for i in range(s + 1)])  44.5 us
    ppermute x6, waiting for transfers between devices, sum_line(): a = a + lax.ppermute(a, 'z', [(i, i ^ step) for i in range(z_count)])  44.4 us
    all_to_all x1, blocking collectives, local(): lax.all_to_all(payload, 'z', 0, 0, tiled=True)  41.3 us
    pallas_call x2, Pallas kernels, attend_grad(): pl.pallas_call(functools.partial(attend_grad_kernel, chunk, LOG2E / math....  31.8 us
    dynamic_slice x6, local copies, waits for them, and re-layouts, split_x(): other = lax.dynamic_index_in_dim(a, 1 - x_pos, 2, False)  26.1 us
    ppermute x3, waiting for transfers between devices, weight_grad(): narrow_far = lax.ppermute(narrow, 'x', SWAP)  24.7 us
    ppermute x3, waiting for transfers between devices, split_x(): return [mine, lax.ppermute(other, 'x', SWAP)]  21.5 us
    ppermute x1, waiting for transfers between devices, local(): kv_far = lax.ppermute(kv_own, 'x', SWAP)  19.5 us
  transfers between devices with their start and end apart: 73, of which 22 were waited for; matrix products, arithmetic and copies ran while one was open for 34% of the time, Pallas kernels for 6%

profile of v1, /device:TPU:0, one launch (start us, length us, event | category | flops | bytes accessed | tf_op | source)
XLA Modules:
  0.0 685.4 jit_solution(3390494179196254750)
XLA Ops:
  14.3 8.0 %convert_element_type.459 = bf16[3,2048,512]{2,1,0:T(8,128)(2,1)} convert(f32[3,2048,512]{2,1,0:T(8,128)} %param.16) | non-fusion elementwise | flops 3145728 | bytes 18874368 | tf_op jit(solution)/shard_map/convert_element_type | solution.py:422
  23.5 3.7 multiply_sine_fusion
  27.6 6.2 convolution_bitcast_fusion.7.raw0_ref
  44.4 5.1 pack_heads.1
  49.5 41.3 %all_to_all.25 = bf16[4,512,384]{2,1,0:T(8,128)(2,1)S(1)} all-to-all(bf16[4,512,384]{2,1,0:T(8,128)(2,1)} %pack_heads.1), channel_id=1, replica_groups=mesh['z'=4,'x'=2,'y'=2,'c'=2] {'z'}, dimensions={0} | all-to-all | bytes 3145728 | tf_op jit(solution)/shard_map/all_to_all | solution.py:471
  95.2 19.5 %collective-permute-done.5.refs_3_.refs_4_.k_ref.v_ref = bf16[2048,256]{1,0:T(8,128)(2,1)} collective-permute-done((bf16[2048,256]{1,0:T(8,128)(2,1)S(1)}, bf16[2048,256]{1,0:T(8,128)(2,1)}, u32[]{:S(2)}, u32[]{:S(2)}) %collective-permute-start.5) | collective-permute-done | bytes 1048608 | tf_op jit(solution)/shard_map/ppermute | solution.py:475
  114.8 19.0 %attend.1 = (f32[2048,128]{1,0:T(8,128)}, f32[1,2048]{1,0:T(1,128)}) custom-call(bf16[2048,384]{1,0:T(8,128)(2,1)} %bitcast.414, s32[1,2048]{1,0:T(1,128)} %bitcast.468, s32[1,2048]{1,0:T(1,128)} %bitcast.479, bf16[2048,384]{1,0:T(8,128)(2,1)} %bitcast.415, bf16[2048,384]{1,0:T(8,128)(2,1)} %bitcast.416, s32[2048,1]{1,0:T(8,128)} %copy.237.refs_2_.tok_k_ref, ...), custom_call_target="tpu_custom_call" | custom-call | flops 8589934592 | bytes 3145728 | tf_op jit(solution)/shard_map/attend/pallas_call | solution.py:96
  142.6 9.7 %all-to-all-done.1 = bf16[4,512,128]{1,2,0:T(8,128)(2,1)S(1)} async-done(((bf16[4,512,128]{1,2,0:T(8,128)(2,1)}), bf16[4,512,128]{1,2,0:T(8,128)(2,1)S(1)}, u32[]{:S(2)}, u32[]{:S(2)}) %all-to-all-start.1) | async-done | bytes 524320 | tf_op jit(solution)/shard_map/all_to_all | solution.py:491
  156.3 13.1 %collective-permute-done.8 = bf16[128,2048]{1,0:T(8,128)(2,1)} collective-permute-done((bf16[128,2048]{1,0:T(8,128)(2,1)S(1)}, bf16[128,2048]{1,0:T(8,128)(2,1)}, u32[]{:S(2)}, u32[]{:S(2)}) %collective-permute-start.8) | collective-permute-done | bytes 524320 | tf_op jit(solution)/shard_map/ppermute | solution.py:359
  172.0 8.9 %convert_element_type.476 = bf16[2,4,2048,256]{3,2,1,0:T(8,128)(2,1)} convert(f32[2,4,2048,256]{3,2,1,0:T(8,128)} %param.20) | non-fusion elementwise | flops 4194304 | bytes 25165824 | tf_op jit(solution)/shard_map/convert_element_type | solution.py:424
  181.0 5.9 convert_element_type.478
  193.6 11.3 %collective-permute-done.11 = bf16[128,2048]{1,0:T(8,128)(2,1)S(1)} collective-permute-done((bf16[128,2048]{1,0:T(8,128)(2,1)}, bf16[128,2048]{1,0:T(8,128)(2,1)S(1)}, u32[]{:S(2)}, u32[]{:S(2)}) %collective-permute-start.11) | collective-permute-done | bytes 524320 | tf_op jit(solution)/shard_map/ppermute | solution.py:350
  205.0 6.2 convolution_bitcast_fusion.5
  223.6 13.2 %all_gather.7 = f32[4,2,512]{2,1,0:T(2,128)S(1)} all-gather(f32[1,2,512]{2,1,0:T(2,128)S(1)} %rsqrt.36), channel_id=1, replica_groups=mesh['z'=4,'x'=2,'y'=2,'c'=2] {'z'}, dimensions={0}, use_global_device_ids=true | all-gather | bytes 20480 | tf_op jit(solution)/shard_map/all_gather | solution.py:461
  247.1 5.7 constant_dynamic-slice_fusion.2
  275.4 4.3 constant_dynamic-slice_fusion
  285.6 5.8 fusion.17
  293.6 9.2 %collective-permute-done.60 = bf16[4,512,256]{2,1,0:T(8,128)(2,1)} collective-permute-done((bf16[4,512,256]{2,1,0:T(8,128)(2,1)}, bf16[4,512,256]{2,1,0:T(8,128)(2,1)}, u32[]{:S(2)}, u32[]{:S(2)}) %collective-permute-start.60) | collective-permute-done | bytes 1048608 | tf_op jit(solution)/shard_map/ppermute | solution.py:656
  303.7 21.5 %collective-permute-done.61 = bf16[512,4,256]{2,0,1:T(8,128)(2,1)S(1)} collective-permute-done((bf16[512,4,256]{2,0,1:T(8,128)(2,1)S(1)}, bf16[512,4,256]{2,0,1:T(8,128)(2,1)S(1)}, u32[]{:S(2)}, u32[]{:S(2)}) %collective-permute-start.61) | collective-permute-done | bytes 1048608 | tf_op jit(solution)/shard_map/ppermute | solution.py:651
  336.0 4.2 collective-permute-done.62
  345.7 4.4 collective-permute-start.63
  350.1 4.0 collective-permute-done.22
  354.8 15.5 %collective-permute-done.52 = bf16[2,4,512,256]{3,2,1,0:T(8,128)(2,1)} collective-permute-done((bf16[2,4,512,256]{3,2,1,0:T(8,128)(2,1)}, bf16[2,4,512,256]{3,2,1,0:T(8,128)(2,1)}, u32[]{:S(2)}, u32[]{:S(2)}) %collective-permute-start.52) | collective-permute-done | bytes 2097184 | tf_op jit(solution)/shard_map/ppermute | solution.py:656
  370.2 6.7 add_convert_fusion
  386.4 3.6 all-to-all-start.2
  393.1 4.5 reshape.266
  397.6 8.6 %constant_dynamic-slice_fusion.4 = (bf16[512,4,1,256]{3,2,1,0:T(2,128)(2,1)}, bf16[512,4,1,256]{3,2,1,0:T(2,128)(2,1)}) fusion(bf16[512,4,2,256]{3,2,1,0:T(2,128)(2,1)} %reshape.266, s32[]{:T(128)S(6)} %select_n.126, s32[]{:T(128)S(6)} %select_n.120), kind=kLoop, calls=%fused_computation.229 | loop fusion | bytes 4194312 | tf_op jit(solution)/shard_map/jit(dynamic_index_in_dim)/dynamic_slice | solution.py:650
  406.2 5.8 copy.253
  412.0 5.9 copy.255
  426.1 15.7 %attend_grad.2 = (f32[2048,128]{1,0:T(8,128)}, bf16[2048,256]{1,0:T(8,128)(2,1)}) custom-call(bf16[2048,384]{1,0:T(8,128)(2,1)} %bitcast.417, bf16[2048,128]{1,0:T(8,128)(2,1)} %bitcast.437, f32[1,2048]{1,0:T(1,128)} %get-tuple-element.17.lse_ref, f32[1,2048]{1,0:T(1,128)} %bitcast.477, s32[1,2048]{1,0:T(1,128)} %bitcast.469, s32[1,2048]{1,0:T(1,128)} %bitcast.480, ...), custom_call_target="tpu_custom_call" | custom-call | flops 8589934592 | bytes 6291456 | tf_op jit(solution)/shard_map/attend_grad/pallas_call | solution.py:196
  442.4 16.2 %attend_grad.3 = (f32[2048,128]{1,0:T(8,128)}, f32[2048,256]{1,0:T(8,128)}) custom-call(bf16[2048,384]{1,0:T(8,128)(2,1)} %bitcast.418, bf16[2048,128]{1,0:T(8,128)(2,1)} %bitcast.438, f32[1,2048]{1,0:T(1,128)} %get-tuple-element.17.lse_ref, f32[1,2048]{1,0:T(1,128)} %bitcast.478, s32[1,2048]{1,0:T(1,128)} %bitcast.470, s32[1,2048]{1,0:T(1,128)} %bitcast.481, ...), custom_call_target="tpu_custom_call" | custom-call | flops 8589934592 | bytes 6291456 | tf_op jit(solution)/shard_map/attend_grad/pallas_call | solution.py:196
  459.9 4.7 collective-permute-start.64
  467.3 3.6 collective-permute-start.36
  475.9 5.1 collective-permute-done.36
  483.2 5.1 collective-permute-start.37
  499.8 4.2 fusion.21
  508.6 17.1 %collective-permute-start.38 = (bf16[256,512]{1,0:T(8,128)(2,1)}, bf16[256,512]{1,0:T(8,128)(2,1)}, u32[]{:S(2)}, u32[]{:S(2)}) collective-permute-start(bf16[256,512]{1,0:T(8,128)(2,1)} %get-tuple-element.114), channel_id=1, source_target_pairs={{0,8},{8,16},{16,24},{1,9},{9,17},{17,25},{2,10},{10,18},{18,26},{... | collective-permute-start | bytes 786440 | tf_op jit(solution)/shard_map/ppermute | solution.py:386
  528.2 17.3 %collective-permute-done.28 = f32[2,4,2,2,128]{4,3,2,1,0:T(2,128)S(1)} collective-permute-done((f32[2,4,2,2,128]{4,3,2,1,0:T(2,128)S(1)}, f32[2,4,2,2,128]{4,3,2,1,0:T(2,128)S(1)}, u32[]{:S(2)}, u32[]{:S(2)}) %collective-permute-start.28) | collective-permute-done | bytes 16416 | tf_op jit(solution)/shard_map/ppermute | solution.py:372
  548.2 6.0 raw_grad.1
  556.8 6.6 all-to-all-start.3
  566.2 5.1 fusion.29
  571.5 4.6 fusion.30
  588.8 4.2 fusion.22
  602.1 5.2 fusion.15
  607.4 4.9 fusion.14
  620.3 4.5 all-to-all-start.4
  629.6 22.5 %collective-permute-done.51 = f32[7,2048]{1,0:T(8,128)S(1)} collective-permute-done((f32[7,2048]{1,0:T(8,128)S(1)}, f32[7,2048]{1,0:T(8,128)S(1)}, u32[]{:S(2)}, u32[]{:S(2)}) %collective-permute-start.51) | collective-permute-done | bytes 57376 | tf_op jit(solution)/shard_map/ppermute | solution.py:372
  664.0 6.0 collective-permute-start.45
  (459 shorter events, 230.3 us)
Async XLA Ops:
  11.3 16.3 %collective-permute-start = (bf16[128,2048]{1,0:T(8,128)(2,1)}, bf16[128,2048]{1,0:T(8,128)(2,1)}, u32[]{:S(2)}, u32[]{:S(2)}) collective-permute-start(bf16[128,2048]{1,0:T(8,128)(2,1)} %fusion.35), channel_id=1, source_target_pairs={{0,1},{1,0},{2,3},{3,2},{4,5},{5,4},{6,7},{7,6},{8,9},{9,8},{10,11... | collective-permute-start | bytes 1572872 | tf_op jit(solution)/shard_map/ppermute | solution.py:349
  11.8 15.5 %collective-permute-start.1 = (bf16[128,2048]{1,0:T(8,128)(2,1)}, bf16[128,2048]{1,0:T(8,128)(2,1)}, u32[]{:S(2)}, u32[]{:S(2)}) collective-permute-start(bf16[128,2048]{1,0:T(8,128)(2,1)} %fusion.35), channel_id=1, source_target_pairs={{0,2},{2,0},{1,3},{3,1},{4,6},{6,4},{5,7},{7,5},{8,10},{10,8},{9,1... | collective-permute-start | bytes 1572872 | tf_op jit(solution)/shard_map/ppermute | solution.py:350
  90.9 23.8 %collective-permute-start.5 = (bf16[2048,256]{1,0:T(8,128)(2,1)S(1)}, bf16[2048,256]{1,0:T(8,128)(2,1)}, u32[]{:S(2)}, u32[]{:S(2)}) collective-permute-start(bf16[2048,256]{1,0:T(8,128)(2,1)S(1)} %slice.188), channel_id=1, source_target_pairs={{0,4},{4,0},{1,5},{5,1},{2,6},{6,2},{3,7},{7,3},{8,12},{12,8},{9,1... | collective-permute-start | bytes 3145736 | tf_op jit(solution)/shard_map/ppermute | solution.py:475
  136.0 16.2 %all-to-all-start.1 = ((bf16[4,512,128]{1,2,0:T(8,128)(2,1)}), bf16[4,512,128]{1,2,0:T(8,128)(2,1)S(1)}, u32[]{:S(2)}, u32[]{:S(2)}) async-start(bf16[4,512,128]{1,2,0:T(8,128)(2,1)} %copy.239), calls=%async_computation.1 | async-start | bytes 1048576 | tf_op jit(solution)/shard_map/all_to_all | solution.py:491
  139.5 203.4 %all-gather.2.cloned.1.call-start = ((), (), s32[]{:S(2)}) async-start(), calls=%async_computation.5 | async-start | bytes 5242880 | tf_op jit(solution)/shard_map/all_gather | solution.py:680
  155.3 14.1 %collective-permute-start.8 = (bf16[128,2048]{1,0:T(8,128)(2,1)S(1)}, bf16[128,2048]{1,0:T(8,128)(2,1)}, u32[]{:S(2)}, u32[]{:S(2)}) collective-permute-start(bf16[128,2048]{1,0:T(8,128)(2,1)S(1)} %add_convert_fusion.6), channel_id=1, source_target_pairs={{0,2},{2,0},{1,3},{3,1},{4,6},{6,4},{5,7},{7,5},{8,10},{10,8},{9,1... | collective-permute-start | bytes 1572872 | tf_op jit(solution)/shard_map/ppermute | solution.py:359
  172.0 20.0 %collective-permute-start.9 = (bf16[128,2048]{1,0:T(8,128)(2,1)}, bf16[128,2048]{1,0:T(8,128)(2,1)}, u32[]{:S(2)}, u32[]{:S(2)}) collective-permute-start(bf16[128,2048]{1,0:T(8,128)(2,1)} %multiply_convert_fusion.6), channel_id=1, source_target_pairs={{0,1},{1,0},{2,3},{3,2},{4,5},{5,4},{6,7},{7,6},{8,9},{9,8},{10,11... | collective-permute-start | bytes 1572872 | tf_op jit(solution)/shard_map/ppermute | solution.py:349
  190.3 14.5 %collective-permute-start.11 = (bf16[128,2048]{1,0:T(8,128)(2,1)}, bf16[128,2048]{1,0:T(8,128)(2,1)S(1)}, u32[]{:S(2)}, u32[]{:S(2)}) collective-permute-start(bf16[128,2048]{1,0:T(8,128)(2,1)} %multiply_convert_fusion.6), channel_id=1, source_target_pairs={{0,2},{2,0},{1,3},{3,1},{4,6},{6,4},{5,7},{7,5},{8,10},{10,8},{9,1... | collective-permute-start | bytes 1572872 | tf_op jit(solution)/shard_map/ppermute | solution.py:350
  219.3 24.7 %collective-permute-start.10 = (bf16[128,2048]{1,0:T(8,128)(2,1)}, bf16[128,2048]{1,0:T(8,128)(2,1)}, u32[]{:S(2)}, u32[]{:S(2)}) collective-permute-start(bf16[128,2048]{1,0:T(8,128)(2,1)} %slice.199), channel_id=1, source_target_pairs={{0,1},{1,0},{2,3},{3,2},{4,5},{5,4},{6,7},{7,6},{8,9},{9,8},{10,11... | collective-permute-start | bytes 1572872 | tf_op jit(solution)/shard_map/ppermute | solution.py:360
  220.4 23.6 %collective-permute-start.14 = (bf16[128,2048]{1,0:T(8,128)(2,1)}, bf16[128,2048]{1,0:T(8,128)(2,1)}, u32[]{:S(2)}, u32[]{:S(2)}) collective-permute-start(bf16[128,2048]{1,0:T(8,128)(2,1)} %add_convert_fusion.5), channel_id=1, source_target_pairs={{0,2},{2,0},{1,3},{3,1},{4,6},{6,4},{5,7},{7,5},{8,10},{10,8},{9,1... | collective-permute-start | bytes 1572872 | tf_op jit(solution)/shard_map/ppermute | solution.py:359
  254.1 91.6 %collective-permute-start.53 = (bf16[512,4,256]{2,0,1:T(8,128)(2,1)}, bf16[512,4,256]{2,0,1:T(8,128)(2,1)}, u32[]{:S(2)}, u32[]{:S(2)}) collective-permute-start(bf16[512,4,256]{2,0,1:T(8,128)(2,1)} %bitcast.412), channel_id=1, source_target_pairs={{0,4},{4,0},{1,5},{5,1},{2,6},{6,2},{3,7},{7,3},{8,12},{12,8},{9,1... | collective-permute-start | bytes 3145736 | tf_op jit(solution)/shard_map/ppermute | solution.py:651
  256.6 46.2 %collective-permute-start.60 = (bf16[4,512,256]{2,1,0:T(8,128)(2,1)}, bf16[4,512,256]{2,1,0:T(8,128)(2,1)}, u32[]{:S(2)}, u32[]{:S(2)}) collective-permute-start(bf16[4,512,256]{2,1,0:T(8,128)(2,1)} %pad_maximum_fusion.6), channel_id=1, source_target_pairs={{0,4},{4,0},{1,5},{5,1},{2,6},{6,2},{3,7},{7,3},{8,12},{12,8},{9,1... | collective-permute-start | bytes 3145736 | tf_op jit(solution)/shard_map/ppermute | solution.py:656
  267.7 23.7 %collective-permute-start.19 = (bf16[128,2048]{1,0:T(8,128)(2,1)}, bf16[128,2048]{1,0:T(8,128)(2,1)}, u32[]{:S(2)}, u32[]{:S(2)}) collective-permute-start(bf16[128,2048]{1,0:T(8,128)(2,1)} %slice.208), channel_id=1, source_target_pairs={{0,1},{1,0},{2,3},{3,2},{4,5},{5,4},{6,7},{7,6},{8,9},{9,8},{10,11... | collective-permute-start | bytes 1572872 | tf_op jit(solution)/shard_map/ppermute | solution.py:358
  270.3 59.2 %collective-permute-start.16 = (bf16[128,2048]{1,0:T(8,128)(2,1)}, bf16[128,2048]{1,0:T(8,128)(2,1)}, u32[]{:S(2)}, u32[]{:S(2)}) collective-permute-start(bf16[128,2048]{1,0:T(8,128)(2,1)} %slice.206), channel_id=1, source_target_pairs={{0,1},{1,0},{2,3},{3,2},{4,5},{5,4},{6,7},{7,6},{8,9},{9,8},{10,11... | collective-permute-start | bytes 1572872 | tf_op jit(solution)/shard_map/ppermute | solution.py:360
  280.1 45.0 %collective-permute-start.61 = (bf16[512,4,256]{2,0,1:T(8,128)(2,1)S(1)}, bf16[512,4,256]{2,0,1:T(8,128)(2,1)S(1)}, u32[]{:S(2)}, u32[]{:S(2)}) collective-permute-start(bf16[512,4,256]{2,0,1:T(8,128)(2,1)S(1)} %bitcast.442), channel_id=1, source_target_pairs={{0,4},{4,0},{1,5},{5,1},{2,6},{6,2},{3,7},{7,3},{8,12},{12,8},{9,1... | collective-permute-start | bytes 3145736 | tf_op jit(solution)/shard_map/ppermute | solution.py:651
  291.4 78.8 %collective-permute-start.52 = (bf16[2,4,512,256]{3,2,1,0:T(8,128)(2,1)}, bf16[2,4,512,256]{3,2,1,0:T(8,128)(2,1)}, u32[]{:S(2)}, u32[]{:S(2)}) collective-permute-start(bf16[2,4,512,256]{3,2,1,0:T(8,128)(2,1)} %maximum_maximum_fusion), channel_id=1, source_target_pairs={{0,4},{4,0},{1,5},{5,1},{2,6},{6,2},{3,7},{7,3},{8,12},{12,8},{9,1... | collective-permute-start | bytes 6291464 | tf_op jit(solution)/shard_map/ppermute | solution.py:656
  302.8 27.8 %collective-permute-start.20 = (bf16[128,2048]{1,0:T(8,128)(2,1)S(1)}, bf16[128,2048]{1,0:T(8,128)(2,1)S(1)}, u32[]{:S(2)}, u32[]{:S(2)}) collective-permute-start(bf16[128,2048]{1,0:T(8,128)(2,1)S(1)} %add_convert_fusion.4), channel_id=1, source_target_pairs={{0,2},{2,0},{1,3},{3,1},{4,6},{6,4},{5,7},{7,5},{8,10},{10,8},{9,1... | collective-permute-start | bytes 1572872 | tf_op jit(solution)/shard_map/ppermute | solution.py:359
  327.8 12.4 %collective-permute-start.62 = (bf16[4,256,256]{1,2,0:T(8,128)(2,1)S(1)}, bf16[4,256,256]{1,2,0:T(8,128)(2,1)S(1)}, u32[]{:S(2)}, u32[]{:S(2)}) collective-permute-start(bf16[4,256,256]{1,2,0:T(8,128)(2,1)S(1)} %get-tuple-element.104), channel_id=1, source_target_pairs={{0,8},{1,9},{2,10},{3,11},{4,12},{5,13},{6,14},{7,15}} | collective-permute-start | bytes 1572872 | tf_op jit(solution)/shard_map/ppermute | solution.py:386
  329.5 12.2 %collective-permute-start.65 = (bf16[4,256,256]{1,2,0:T(8,128)(2,1)S(1)}, bf16[4,256,256]{1,2,0:T(8,128)(2,1)S(1)}, u32[]{:S(2)}, u32[]{:S(2)}) collective-permute-start(bf16[4,256,256]{1,2,0:T(8,128)(2,1)S(1)} %get-tuple-element.105), channel_id=1, source_target_pairs={{24,16},{25,17},{26,18},{27,19},{28,20},{29,21},{30,22},{31,23}} | collective-permute-start | bytes 1572872 | tf_op jit(solution)/shard_map/ppermute | solution.py:387
  340.2 118.4 %collective-permute-start.35 = (bf16[512,512]{1,0:T(8,128)(2,1)}, bf16[512,512]{1,0:T(8,128)(2,1)}, u32[]{:S(2)}, u32[]{:S(2)}) collective-permute-start(bf16[512,512]{1,0:T(8,128)(2,1)} %copy.289), channel_id=1, source_target_pairs={{0,4},{4,0},{1,5},{5,1},{2,6},{6,2},{3,7},{7,3},{8,12},{12,8},{9,1... | collective-permute-start | bytes 1572872 | tf_op jit(solution)/shard_map/ppermute | solution.py:656
  341.7 12.4 %collective-permute-start.22 = (bf16[128,2048]{1,0:T(8,128)(2,1)}, bf16[128,2048]{1,0:T(8,128)(2,1)}, u32[]{:S(2)}, u32[]{:S(2)}) collective-permute-start(bf16[128,2048]{1,0:T(8,128)(2,1)} %get-tuple-element.80), channel_id=1, source_target_pairs={{0,2},{2,0},{1,3},{3,1},{4,6},{6,4},{5,7},{7,5},{8,10},{10,8},{9,1... | collective-permute-start | bytes 1572872 | tf_op jit(solution)/shard_map/ppermute | solution.py:350
  343.0 228.4 %collective-permute-start.32 = (bf16[2048,1024]{1,0:T(8,128)(2,1)}, bf16[2048,1024]{1,0:T(8,128)(2,1)}, u32[]{:S(2)}, u32[]{:S(2)}) collective-permute-start(bf16[2048,1024]{1,0:T(8,128)(2,1)} %all-gather.2.cloned.1.call-done), channel_id=1, source_target_pairs={{0,1},{1,0},{2,3},{3,2},{4,5},{5,4},{6,7},{7,6},{8,9},{9,8},{10,11... | collective-permute-start | bytes 12582920 | tf_op jit(solution)/shard_map/ppermute | solution.py:681
  345.7 33.9 %collective-permute-start.63 = (bf16[4,256,256]{1,2,0:T(8,128)(2,1)S(1)}, bf16[4,256,256]{1,2,0:T(8,128)(2,1)S(1)}, u32[]{:S(2)}, u32[]{:S(2)}) collective-permute-start(bf16[4,256,256]{1,2,0:T(8,128)(2,1)S(1)} %get-tuple-element.102), channel_id=1, source_target_pairs={{0,8},{8,16},{1,9},{9,17},{2,10},{10,18},{3,11},{11,19},{4,12},{12... | collective-permute-start | bytes 1572872 | tf_op jit(solution)/shard_map/ppermute | solution.py:386
  354.1 28.1 %collective-permute-start.66 = (bf16[4,256,256]{1,2,0:T(8,128)(2,1)S(1)}, bf16[4,256,256]{1,2,0:T(8,128)(2,1)S(1)}, u32[]{:S(2)}, u32[]{:S(2)}) collective-permute-start(bf16[4,256,256]{1,2,0:T(8,128)(2,1)S(1)} %get-tuple-element.103), channel_id=1, source_target_pairs={{24,16},{16,8},{25,17},{17,9},{26,18},{18,10},{27,19},{19,11},{28,... | collective-permute-start | bytes 1572872 | tf_op jit(solution)/shard_map/ppermute | solution.py:387
  370.2 13.3 %collective-permute-start.23 = (bf16[128,2048]{1,0:T(8,128)(2,1)}, bf16[128,2048]{1,0:T(8,128)(2,1)S(1)}, u32[]{:S(2)}, u32[]{:S(2)}) collective-permute-start(bf16[128,2048]{1,0:T(8,128)(2,1)} %collective-permute-done.22), channel_id=1, source_target_pairs={{0,1},{1,0},{2,3},{3,2},{4,5},{5,4},{6,7},{7,6},{8,9},{9,8},{10,11... | collective-permute-start | bytes 1572872 | tf_op jit(solution)/shard_map/ppermute | solution.py:351
  379.6 120.2 %collective-permute-start.54 = (bf16[2,4,256,256]{2,3,1,0:T(8,128)(2,1)}, bf16[2,4,256,256]{2,3,1,0:T(8,128)(2,1)}, u32[]{:S(2)}, u32[]{:S(2)}) collective-permute-start(bf16[2,4,256,256]{2,3,1,0:T(8,128)(2,1)} %get-tuple-element.91), channel_id=1, source_target_pairs={{0,8},{1,9},{2,10},{3,11},{4,12},{5,13},{6,14},{7,15}} | collective-permute-start | bytes 3145736 | tf_op jit(solution)/shard_map/ppermute | solution.py:386
  386.4 36.3 %all-to-all-start.2 = ((bf16[4,512,128]{2,1,0:T(8,128)(2,1)}), bf16[4,512,128]{2,1,0:T(8,128)(2,1)S(1)}, u32[]{:S(2)}, u32[]{:S(2)}) async-start(bf16[4,512,128]{2,1,0:T(8,128)(2,1)} %bitcast_bitcast_fusion), calls=%async_computation.2 | async-start | bytes 1048576 | tf_op jit(solution)/shard_map/all_to_all | solution.py:586
  417.9 42.0 %collective-permute-start.34 = (bf16[512,4,256]{0,2,1:T(8,128)(2,1)}, bf16[512,4,256]{0,2,1:T(8,128)(2,1)}, u32[]{:S(2)}, u32[]{:S(2)}) collective-permute-start(bf16[512,4,256]{0,2,1:T(8,128)(2,1)} %bitcast.441), channel_id=1, source_target_pairs={{0,4},{4,0},{1,5},{5,1},{2,6},{6,2},{3,7},{7,3},{8,12},{12,8},{9,1... | collective-permute-start | bytes 3145736 | tf_op jit(solution)/shard_map/ppermute | solution.py:651
  441.8 25.5 %collective-permute-start.24 = (bf16[2048,256]{1,0:T(8,128)(2,1)}, bf16[2048,256]{1,0:T(8,128)(2,1)}, u32[]{:S(2)}, u32[]{:S(2)}) collective-permute-start(bf16[2048,256]{1,0:T(8,128)(2,1)} %get-tuple-element.21), channel_id=1, source_target_pairs={{0,4},{4,0},{1,5},{5,1},{2,6},{6,2},{3,7},{7,3},{8,12},{12,8},{9,1... | collective-permute-start | bytes 3145736 | tf_op jit(solution)/shard_map/ppermute | solution.py:597
  458.6 15.7 %collective-permute-start.67 = (bf16[4,256,256]{1,2,0:T(8,128)(2,1)}, bf16[4,256,256]{1,2,0:T(8,128)(2,1)S(1)}, u32[]{:S(2)}, u32[]{:S(2)}) collective-permute-start(bf16[4,256,256]{1,2,0:T(8,128)(2,1)} %get-tuple-element.101), channel_id=1, source_target_pairs={{24,16},{16,8},{8,0},{25,17},{17,9},{9,1},{26,18},{18,10},{10,2},{... | collective-permute-start | bytes 1572872 | tf_op jit(solution)/shard_map/ppermute | solution.py:387
  459.9 21.9 %collective-permute-start.64 = (bf16[4,256,256]{1,2,0:T(8,128)(2,1)S(1)}, bf16[4,256,256]{1,2,0:T(8,128)(2,1)S(1)}, u32[]{:S(2)}, u32[]{:S(2)}) collective-permute-start(bf16[4,256,256]{1,2,0:T(8,128)(2,1)S(1)} %copy-done.55), channel_id=1, source_target_pairs={{0,8},{8,16},{16,24},{1,9},{9,17},{17,25},{2,10},{10,18},{18,26},{... | collective-permute-start | bytes 1572872 | tf_op jit(solution)/shard_map/ppermute | solution.py:386
  467.3 13.7 %collective-permute-start.36 = (bf16[256,512]{1,0:T(8,128)(2,1)S(1)}, bf16[256,512]{1,0:T(8,128)(2,1)S(1)}, u32[]{:S(2)}, u32[]{:S(2)}) collective-permute-start(bf16[256,512]{1,0:T(8,128)(2,1)S(1)} %get-tuple-element.116), channel_id=1, source_target_pairs={{0,8},{1,9},{2,10},{3,11},{4,12},{5,13},{6,14},{7,15}} | collective-permute-start | bytes 786440 | tf_op jit(solution)/shard_map/ppermute | solution.py:386
  474.3 25.6 %collective-permute-start.57 = (bf16[2,4,256,256]{2,3,1,0:T(8,128)(2,1)}, bf16[2,4,256,256]{2,3,1,0:T(8,128)(2,1)}, u32[]{:S(2)}, u32[]{:S(2)}) collective-permute-start(bf16[2,4,256,256]{2,3,1,0:T(8,128)(2,1)} %get-tuple-element.92), channel_id=1, source_target_pairs={{24,16},{25,17},{26,18},{27,19},{28,20},{29,21},{30,22},{31,23}} | collective-permute-start | bytes 3145736 | tf_op jit(solution)/shard_map/ppermute | solution.py:387
  495.9 29.7 %collective-permute-start.40 = (bf16[256,512]{1,0:T(8,128)(2,1)S(1)}, bf16[256,512]{1,0:T(8,128)(2,1)S(1)}, u32[]{:S(2)}, u32[]{:S(2)}) collective-permute-start(bf16[256,512]{1,0:T(8,128)(2,1)S(1)} %get-tuple-element.115), channel_id=1, source_target_pairs={{24,16},{16,8},{25,17},{17,9},{26,18},{18,10},{27,19},{19,11},{28,... | collective-permute-start | bytes 786440 | tf_op jit(solution)/shard_map/ppermute | solution.py:387
  496.6 11.9 %collective-permute-start.27 = (f32[2,4,2,2,128]{4,3,2,1,0:T(2,128)S(1)}, f32[2,4,2,2,128]{4,3,2,1,0:T(2,128)S(1)}, u32[]{:S(2)}, u32[]{:S(2)}) collective-permute-start(f32[2,4,2,2,128]{4,3,2,1,0:T(2,128)S(1)} %reverse_add_fusion), channel_id=1, source_target_pairs={{0,8},{8,0},{16,24},{24,16},{1,9},{9,1},{17,25},{25,17},{2,10},{10... | collective-permute-start | bytes 49160 | tf_op jit(solution)/shard_map/ppermute | solution.py:372
  504.0 82.7 %collective-permute-start.55 = (bf16[2,4,256,256]{2,3,1,0:T(8,128)(2,1)}, bf16[2,4,256,256]{2,3,1,0:T(8,128)(2,1)}, u32[]{:S(2)}, u32[]{:S(2)}) collective-permute-start(bf16[2,4,256,256]{2,3,1,0:T(8,128)(2,1)} %get-tuple-element.89), channel_id=1, source_target_pairs={{0,8},{8,16},{1,9},{9,17},{2,10},{10,18},{3,11},{11,19},{4,12},{12... | collective-permute-start | bytes 3145736 | tf_op jit(solution)/shard_map/ppermute | solution.py:386
  506.9 81.9 %collective-permute-start.58 = (bf16[2,4,256,256]{2,3,1,0:T(8,128)(2,1)}, bf16[2,4,256,256]{2,3,1,0:T(8,128)(2,1)}, u32[]{:S(2)}, u32[]{:S(2)}) collective-permute-start(bf16[2,4,256,256]{2,3,1,0:T(8,128)(2,1)} %get-tuple-element.90), channel_id=1, source_target_pairs={{24,16},{16,8},{25,17},{17,9},{26,18},{18,10},{27,19},{19,11},{28,... | collective-permute-start | bytes 3145736 | tf_op jit(solution)/shard_map/ppermute | solution.py:387
  508.6 108.0 %collective-permute-start.38 = (bf16[256,512]{1,0:T(8,128)(2,1)}, bf16[256,512]{1,0:T(8,128)(2,1)}, u32[]{:S(2)}, u32[]{:S(2)}) collective-permute-start(bf16[256,512]{1,0:T(8,128)(2,1)} %get-tuple-element.114), channel_id=1, source_target_pairs={{0,8},{8,16},{16,24},{1,9},{9,17},{17,25},{2,10},{10,18},{18,26},{... | collective-permute-start | bytes 786440 | tf_op jit(solution)/shard_map/ppermute | solution.py:386
  525.7 19.8 %collective-permute-start.28 = (f32[2,4,2,2,128]{4,3,2,1,0:T(2,128)S(1)}, f32[2,4,2,2,128]{4,3,2,1,0:T(2,128)S(1)}, u32[]{:S(2)}, u32[]{:S(2)}) collective-permute-start(f32[2,4,2,2,128]{4,3,2,1,0:T(2,128)S(1)} %add.350), channel_id=1, source_target_pairs={{0,16},{8,24},{16,0},{24,8},{1,17},{9,25},{17,1},{25,9},{2,18},{10... | collective-permute-start | bytes 49160 | tf_op jit(solution)/shard_map/ppermute | solution.py:372
  545.5 79.3 %collective-permute-start.41 = (bf16[256,512]{1,0:T(8,128)(2,1)}, bf16[256,512]{1,0:T(8,128)(2,1)S(1)}, u32[]{:S(2)}, u32[]{:S(2)}) collective-permute-start(bf16[256,512]{1,0:T(8,128)(2,1)} %fusion.91), channel_id=1, source_target_pairs={{24,16},{16,8},{8,0},{25,17},{17,9},{9,1},{26,18},{18,10},{10,2},{... | collective-permute-start | bytes 786440 | tf_op jit(solution)/shard_map/ppermute | solution.py:387
  556.8 40.6 %all-to-all-start.3 = ((bf16[4,512,384]{1,2,0:T(8,128)(2,1)}), bf16[4,512,384]{1,2,0:T(8,128)(2,1)S(1)}, u32[]{:S(2)}, u32[]{:S(2)}) async-start(bf16[4,512,384]{1,2,0:T(8,128)(2,1)} %copy.248), calls=%async_computation.3 | async-start | bytes 3145728 | tf_op jit(solution)/shard_map/all_to_all | solution.py:491
  585.0 31.8 %collective-permute-start.33 = (bf16[4,256,384]{1,2,0:T(8,128)(2,1)}, bf16[4,256,384]{1,2,0:T(8,128)(2,1)}, u32[]{:S(2)}, u32[]{:S(2)}) collective-permute-start(bf16[4,256,384]{1,2,0:T(8,128)(2,1)} %bitcast.446), channel_id=1, source_target_pairs={{0,4},{4,0},{1,5},{5,1},{2,6},{6,2},{3,7},{7,3},{8,12},{12,8},{9,1... | collective-permute-start | bytes 2359304 | tf_op jit(solution)/shard_map/ppermute | solution.py:644
  593.0 62.3 %collective-permute-start.59 = (bf16[2,4,256,256]{2,3,1,0:T(8,128)(2,1)}, bf16[2,4,256,256]{2,3,1,0:T(8,128)(2,1)}, u32[]{:S(2)}, u32[]{:S(2)}) collective-permute-start(bf16[2,4,256,256]{2,3,1,0:T(8,128)(2,1)} %get-tuple-element.88), channel_id=1, source_target_pairs={{24,16},{16,8},{8,0},{25,17},{17,9},{9,1},{26,18},{18,10},{10,2},{... | collective-permute-start | bytes 3145736 | tf_op jit(solution)/shard_map/ppermute | solution.py:387
  613.2 42.1 %collective-permute-start.56 = (bf16[2,4,256,256]{2,3,1,0:T(8,128)(2,1)}, bf16[2,4,256,256]{2,3,1,0:T(8,128)(2,1)}, u32[]{:S(2)}, u32[]{:S(2)}) collective-permute-start(bf16[2,4,256,256]{2,3,1,0:T(8,128)(2,1)} %get-tuple-element.87), channel_id=1, source_target_pairs={{0,8},{8,16},{16,24},{1,9},{9,17},{17,25},{2,10},{10,18},{18,26},{... | collective-permute-start | bytes 3145736 | tf_op jit(solution)/shard_map/ppermute | solution.py:386
  616.6 35.6 %collective-permute-start.29 = (bf16[128,2048]{1,0:T(8,128)(2,1)}, bf16[128,2048]{1,0:T(8,128)(2,1)S(1)}, u32[]{:S(2)}, u32[]{:S(2)}) collective-permute-start(bf16[128,2048]{1,0:T(8,128)(2,1)} %slice.218), channel_id=1, source_target_pairs={{0,1},{1,0},{2,3},{3,2},{4,5},{5,4},{6,7},{7,6},{8,9},{9,8},{10,11... | collective-permute-start | bytes 1572872 | tf_op jit(solution)/shard_map/ppermute | solution.py:360
  616.9 35.3 %collective-permute-start.31 = (bf16[128,2048]{1,0:T(8,128)(2,1)}, bf16[128,2048]{1,0:T(8,128)(2,1)S(1)}, u32[]{:S(2)}, u32[]{:S(2)}) collective-permute-start(bf16[128,2048]{1,0:T(8,128)(2,1)} %add_convert_fusion.3), channel_id=1, source_target_pairs={{0,2},{2,0},{1,3},{3,1},{4,6},{6,4},{5,7},{7,5},{8,10},{10,8},{9,1... | collective-permute-start | bytes 1572872 | tf_op jit(solution)/shard_map/ppermute | solution.py:359
  620.3 40.7 %all-to-all-start.4 = ((bf16[4,256,384]{1,2,0:T(8,128)(2,1)}), bf16[4,256,384]{1,2,0:T(8,128)(2,1)}, u32[]{:S(2)}, u32[]{:S(2)}) async-start(bf16[4,256,384]{1,2,0:T(8,128)(2,1)} %fusion.24), calls=%async_computation.4 | async-start | bytes 1572864 | tf_op jit(solution)/shard_map/all_to_all | solution.py:696
  624.8 27.3 %collective-permute-start.51 = (f32[7,2048]{1,0:T(8,128)S(1)}, f32[7,2048]{1,0:T(8,128)S(1)}, u32[]{:S(2)}, u32[]{:S(2)}) collective-permute-start(f32[7,2048]{1,0:T(8,128)S(1)} %add.381), channel_id=1, source_target_pairs={{0,16},{8,24},{16,0},{24,8},{1,17},{9,25},{17,1},{25,9},{2,18},{10... | collective-permute-start | bytes 172040 | tf_op jit(solution)/shard_map/ppermute | solution.py:372
  (109 other events, 819.4 us)
Sparse Core Ops, SparseCore 0:
  223.7 79.4 all-gather.1

commit v2 on v1

--- a/solution.py
+++ b/solution.py
@@ -18,14 +18,18 @@
 bf16 = jnp.bfloat16
 
 SWAP = [(0, 1), (1, 0)]
+
+
+def cost(us):
+    return pl.CostEstimate(flops=int(us * 1e9), bytes_accessed=1 << 20, transcendentals=0)
 DOT_NT = (((1,), (1,)), ((), ()))
 DOT_NN = (((1,), (0,)), ((), ()))
 
 
 def attend_kernel(groups, chunk, score_scale, q_ref, tok_q_ref, start_q_ref, *refs):
     key_refs = refs[: 3 * groups]
-    o_ref, lse_ref = refs[3 * groups : 3 * groups + 2]
-    vt_refs = refs[3 * groups + 2 :]
+    o_ref, lse_ref = refs[-groups - 2 : -groups]
+    vt_refs = refs[-groups:]
     rows = q_ref.shape[0]
 
     @pl.when(pl.program_id(0) == 0)
@@ -74,25 +78,23 @@
     lse_ref[...] = run_max + jnp.log2(run_sum)
 
 
-def attend(packed, tok_q, start_q, key_groups):
-    rows = packed.shape[0]
+def attend(queries, tok_q, start_q, key_groups, earlier=()):
+    rows = queries.shape[0]
     block = min(1024, rows)
     chunk = 1024
     row = pl.BlockSpec((1, block), lambda i: (0, i))
     in_specs = [pl.BlockSpec((block, HEAD_DIM), lambda i: (i, 0)), row, row]
-    operands = [packed, tok_q, start_q]
+    operands = [queries, tok_q, start_q]
     scratch = []
     keys = 0
-    for array, k_col, v_col, tok_k in key_groups:
-        count = array.shape[0]
+    for group in key_groups:
+        count = group[0].shape[0]
         keys += count
-        in_specs += [
-            pl.BlockSpec((count, HEAD_DIM), lambda i, col=k_col: (0, col)),
-            pl.BlockSpec((count, HEAD_DIM), lambda i, col=v_col: (0, col)),
-            pl.BlockSpec((count, 1), lambda i: (0, 0)),
-        ]
-        operands += [array, array, tok_k]
+        in_specs += [pl.BlockSpec(a.shape, lambda i: (0, 0)) for a in group]
+        operands += group
         scratch.append(pltpu.VMEM((HEAD_DIM, count), bf16))
+    in_specs += [pl.BlockSpec(memory_space=pl.ANY)] * len(earlier)
+    operands += earlier
     return pl.pallas_call(
         functools.partial(
             attend_kernel, len(key_groups), chunk, LOG2E / math.sqrt(HEAD_DIM)
@@ -106,11 +108,7 @@
         ],
         scratch_shapes=scratch,
         compiler_params=pltpu.CompilerParams(vmem_limit_bytes=VMEM_BYTES),
-        cost_estimate=pl.CostEstimate(
-            flops=8 * rows * keys * HEAD_DIM,
-            bytes_accessed=4 * (rows + keys) * HEAD_DIM,
-            transcendentals=rows * keys,
-        ),
+        cost_estimate=cost(8),
         name="attend",
     )(*operands)
 
@@ -129,12 +127,9 @@
     k_ref,
     v_ref,
     tok_k_ref,
-    dq_ref,
-    dkv_ref,
-    kt_ref,
-    dk_acc,
-    dv_acc,
+    *refs,
 ):
+    dq_ref, dk_ref, dv_ref, kt_ref, dk_acc, dv_acc = refs[-6:]
     steps = k_ref.shape[0] // chunk
 
     @pl.when(pl.program_id(0) == 0)
@@ -181,18 +176,20 @@
 
     @pl.when(pl.program_id(0) == pl.num_programs(0) - 1)
     def _():
-        dkv_ref[:, :HEAD_DIM] = (dk_acc[...] * grad_scale).astype(dkv_ref.dtype)
-        dkv_ref[:, HEAD_DIM:] = dv_acc[...].astype(dkv_ref.dtype)
-
-
-def attend_grad(packed, d_out, lse, delta, tok_q, start_q, dq_in, key_group, out_type):
-    rows = packed.shape[0]
-    array, k_col, v_col, tok_k = key_group
-    keys = array.shape[0]
+        dk_ref[...] = (dk_acc[...] * grad_scale).astype(dk_ref.dtype)
+        dv_ref[...] = dv_acc[...].astype(dv_ref.dtype)
+
+
+def attend_grad(
+    queries, d_out, lse, delta, tok_q, start_q, dq_in, key_group, out_type, earlier=()
+):
+    rows = queries.shape[0]
+    keys = key_group[0].shape[0]
     block = min(1024, rows)
     chunk = 1024
     row = pl.BlockSpec((1, block), lambda i: (0, i))
     head = pl.BlockSpec((block, HEAD_DIM), lambda i: (i, 0))
+    whole = pl.BlockSpec((keys, HEAD_DIM), lambda i: (0, 0))
     return pl.pallas_call(
         functools.partial(
             attend_grad_kernel,
@@ -209,14 +206,16 @@
             row,
             row,
             head,
-            pl.BlockSpec((keys, HEAD_DIM), lambda i: (0, k_col)),
-            pl.BlockSpec((keys, HEAD_DIM), lambda i: (0, v_col)),
+            whole,
+            whole,
             pl.BlockSpec((keys, 1), lambda i: (0, 0)),
-        ],
-        out_specs=[head, pl.BlockSpec((keys, 2 * HEAD_DIM), lambda i: (0, 0))],
+        ]
+        + [pl.BlockSpec(memory_space=pl.ANY)] * len(earlier),
+        out_specs=[head, whole, whole],
         out_shape=[
             jax.ShapeDtypeStruct((rows, HEAD_DIM), f32),
-            jax.ShapeDtypeStruct((keys, 2 * HEAD_DIM), out_type),
+            jax.ShapeDtypeStruct((keys, HEAD_DIM), out_type),
+            jax.ShapeDtypeStruct((keys, HEAD_DIM), out_type),
         ],
         scratch_shapes=[
             pltpu.VMEM((HEAD_DIM, keys), bf16),
@@ -224,31 +223,27 @@
             pltpu.VMEM((keys, HEAD_DIM), f32),
         ],
         compiler_params=pltpu.CompilerParams(vmem_limit_bytes=VMEM_BYTES),
-        cost_estimate=pl.CostEstimate(
-            flops=16 * rows * keys * HEAD_DIM,
-            bytes_accessed=12 * (rows + keys) * HEAD_DIM,
-            transcendentals=rows * keys,
-        ),
+        cost_estimate=cost(8),
         name="attend_grad",
-    )(packed, d_out, lse, delta, tok_q, start_q, dq_in, array, array, tok_k)
-
-
-def pack_kernel(raw0_ref, raw1_ref, inv_ref, cos_ref, sin_ref, gain_ref, out_ref):
+    )(queries, d_out, lse, delta, tok_q, start_q, dq_in, *key_group, *earlier)
+
+
+def pack_kernel(raw0_ref, raw1_ref, inv_ref, cos_ref, sin_ref, gain_ref, q_ref, k_ref):
     half = raw0_ref.shape[1]
     for i, raw_ref in enumerate((raw0_ref, raw1_ref)):
         r = slice(i * half, (i + 1) * half)
         for j in range(2):
             u = raw_ref[j] * inv_ref[r, j : j + 1] * gain_ref[j : j + 1, :]
             turned = u * cos_ref[r, :] + pltpu.roll(u, HEAD_DIM // 2, 1) * sin_ref[r, :]
-            out_ref[0, r, j * HEAD_DIM : (j + 1) * HEAD_DIM] = turned.astype(bf16)
-        out_ref[0, r, 2 * HEAD_DIM :] = raw_ref[2].astype(bf16)
+            (q_ref, k_ref)[j][0, r, :] = turned.astype(bf16)
 
 
 def pack_heads(raw0, raw1, inv, cos_tab, sin_tab, gains):
     half = raw0.shape[1]
     rows = 2 * half
     heads = raw0.shape[2] // HEAD_DIM
-    raw = pl.BlockSpec((3, half, HEAD_DIM), lambda h: (0, 0, h))
+    raw = pl.BlockSpec((2, half, HEAD_DIM), lambda h: (0, 0, h))
+    head = pl.BlockSpec((1, rows, HEAD_DIM), lambda h: (h, 0, 0))
     table = pl.BlockSpec((rows, HEAD_DIM), lambda h: (0, 0))
     return pl.pallas_call(
         pack_kernel,
@@ -261,18 +256,18 @@
             table,
             pl.BlockSpec((2, HEAD_DIM), lambda h: (0, h)),
         ],
-        out_specs=pl.BlockSpec((1, rows, 3 * HEAD_DIM), lambda h: (h, 0, 0)),
-        out_shape=jax.ShapeDtypeStruct((heads, rows, 3 * HEAD_DIM), bf16),
-        cost_estimate=pl.CostEstimate(
-            flops=20 * rows * heads * HEAD_DIM,
-            bytes_accessed=18 * rows * heads * HEAD_DIM,
-            transcendentals=0,
-        ),
+        out_specs=[head, head],
+        out_shape=[jax.ShapeDtypeStruct((heads, rows, HEAD_DIM), bf16)] * 2,
+        cost_estimate=cost(3),
         name="pack_heads",
     )(raw0, raw1, inv, cos_tab, sin_tab, gains)
 
 
-def raw_grad_kernel(dq_ref, dkv_ref, packed_ref, coef_ref, cos_ref, sin_ref, gain_ref, out_ref, sum_ref):
+def raw_grad_kernel(
+    dq_ref, dk_ref, dv_ref, q_ref, k_ref, coef_ref, cos_ref, sin_ref, gain_ref, *refs
+):
+    out_ref, sum_ref = refs[-2:]
+
     @pl.when(pl.program_id(0) == 0)
     def _():
         sum_ref[...] = jnp.zeros_like(sum_ref)
@@ -283,20 +278,20 @@
     def turn_back(u):
         return u * cos_tab - pltpu.roll(u, HEAD_DIM // 2, 1) * sin_tab
 
-    for j, grad_ref in enumerate((dq_ref, dkv_ref)):
+    for j, (grad_ref, rows_ref) in enumerate(((dq_ref, q_ref), (dk_ref, k_ref))):
         gain = gain_ref[j : j + 1, :]
         cols = slice(j * HEAD_DIM, (j + 1) * HEAD_DIM)
-        d_norm = turn_back(grad_ref[:, :HEAD_DIM])
-        hat = turn_back(packed_ref[:, cols].astype(f32)) / gain
+        d_norm = turn_back(grad_ref[...])
+        hat = turn_back(rows_ref[...].astype(f32)) / gain
         sum_ref[j : j + 1, :] += jnp.sum(d_norm * hat, axis=0, keepdims=True)
         inv = coef_ref[:, 2 * j : 2 * j + 1]
         inner = coef_ref[:, 2 * j + 1 : 2 * j + 2]
         out_ref[:, cols] = (inv * (d_norm * gain - hat * inner)).astype(bf16)
-    out_ref[:, 2 * HEAD_DIM :] = dkv_ref[:, HEAD_DIM:].astype(bf16)
-
-
-def raw_grad(d_query, d_kv, packed, coef, cos_tab, sin_tab, gains):
-    rows = packed.shape[0]
+    out_ref[:, 2 * HEAD_DIM :] = dv_ref[...].astype(bf16)
+
+
+def raw_grad(d_query, d_key, d_value, queries, keys, coef, cos_tab, sin_tab, gains):
+    rows = queries.shape[0]
     block = min(512, rows)
 
     def wide(cols):
@@ -307,9 +302,7 @@
         raw_grad_kernel,
         grid=(rows // block,),
         in_specs=[
-            wide(HEAD_DIM),
-            wide(2 * HEAD_DIM),
-            wide(3 * HEAD_DIM),
+            *[wide(HEAD_DIM)] * 5,
             wide(4),
             wide(HEAD_DIM),
             wide(HEAD_DIM),
@@ -320,11 +313,279 @@
             jax.ShapeDtypeStruct((rows, 3 * HEAD_DIM), bf16),
             jax.ShapeDtypeStruct((2, HEAD_DIM), f32),
         ],
-        cost_estimate=pl.CostEstimate(
-            flops=40 * rows * HEAD_DIM, bytes_accessed=40 * rows * HEAD_DIM, transcendentals=0
+        cost_estimate=cost(3),
+        name="raw_grad",
+    )(d_query, d_key, d_value, queries, keys, coef, cos_tab, sin_tab, gains)
+
+
+def weight_grad_kernel(pieces, experts, out_block, at_ref, *refs):
+    wide0, wide1, wide_far = refs[:3]
+    narrow = refs[3 : 3 + pieces]
+    out_ref, wide_t, tall = refs[-3:]
+    half = wide0.shape[0]
+    blocks = wide_far.shape[1] // out_block
+
+    @pl.when(pl.program_id(0) == 0)
+    def _():
+        for z in range(blocks):
+            rows = slice(z * out_block, (z + 1) * out_block)
+            cols = (2 * z + at_ref[0]) * out_block
+            cols = pl.ds(pl.multiple_of(cols, out_block), out_block)
+            for i, piece in enumerate((wide0, wide1)):
+                wide_t[rows, i * half : (i + 1) * half] = piece[:, cols].T
+            wide_t[rows, 2 * half :] = wide_far[:, rows].T
+
+    at = 0
+    for i, piece in enumerate(narrow):
+        if experts and i == pieces - 1:
+            routes = refs[3 + pieces][...]
+            e = lax.rem(pl.program_id(0), experts)
+            block = jnp.zeros(piece.shape[2:], f32)
+            for slot in range(piece.shape[1]):
+                block = jnp.where(routes[:, slot : slot + 1] == e, piece[0, slot].astype(f32), block)
+            block = block.astype(bf16)
+        else:
+            block = piece[...].reshape(piece.shape[-2:])
+        tall[at : at + block.shape[0], :] = block
+        at += block.shape[0]
+    out = jnp.dot(wide_t[...], tall[...], preferred_element_type=f32)
+    out_ref[...] = out.astype(bf16).reshape(out_ref.shape)
+
+
+def weight_grad(wide_h, wide_far, narrow, out_block, at, routes=None, experts=0, earlier=()):
+    half, width = wide_h[0].shape
+    out_width = wide_far.shape[1]
+    specs = []
+    operands = []
+    for piece in narrow:
+        if isinstance(piece, tuple):
+            array, row = piece
+            cols = 256
+            count = array.shape[1] // cols
+            specs.append(pl.BlockSpec((half, cols), lambda j, x, row=row: (row, j)))
+            operands.append(array)
+        elif piece.ndim == 4:
+            kinds, slots, rows, cols = piece.shape
+            count = kinds * experts
+            specs.append(
+                pl.BlockSpec((1, slots, rows, cols), lambda j, x: (j // experts, 0, 0, 0))
+            )
+            operands.append(piece)
+        else:
+            count, rows, cols = piece.shape
+            specs.append(pl.BlockSpec((1, rows, cols), lambda j, x: (j, 0, 0)))
+            operands.append(piece)
+    if experts:
+        specs.append(pl.BlockSpec(routes.shape, lambda j, x: (0, 0)))
+        operands.append(routes)
+
+    def kernel(x_ref, *refs):
+        used = 3 + len(operands)
+        weight_grad_kernel(len(narrow), experts, out_block, x_ref, *refs[:used], *refs[-3:])
+
+    return pl.pallas_call(
+        kernel,
+        grid_spec=pltpu.PrefetchScalarGridSpec(
+            num_scalar_prefetch=1,
+            grid=(count,),
+            in_specs=[pl.BlockSpec(w.shape, lambda j, x: (0, 0)) for w in (*wide_h, wide_far)]
+            + specs
+            + [pl.BlockSpec(memory_space=pl.ANY)] * len(earlier),
+            out_specs=pl.BlockSpec((1, out_width, cols), lambda j, x: (j, 0, 0)),
+            scratch_shapes=[
+                pltpu.VMEM((out_width, 4 * half), bf16),
+                pltpu.VMEM((4 * half, cols), bf16),
+            ],
         ),
-        name="raw_grad",
-    )(d_query, d_kv, packed, coef, cos_tab, sin_tab, gains)
+        out_shape=jax.ShapeDtypeStruct((count, out_width, cols), bf16),
+        compiler_params=pltpu.CompilerParams(vmem_limit_bytes=VMEM_BYTES),
+        cost_estimate=cost(0.1),
+        name="weight_grad",
+    )(at.reshape(1), *wide_h, wide_far, *operands, *earlier)
+
+
+def waits(earlier):
+    return [pl.BlockSpec(memory_space=pl.ANY)] * len(earlier)
+
+
+def params():
+    return pltpu.CompilerParams(vmem_limit_bytes=VMEM_BYTES)
+
+
+def attn_out_grad_kernel(a_ref, w_ref, *refs):
+    out_ref = refs[-1]
+    y = jnp.dot(a_ref[...], w_ref[...], preferred_element_type=f32).astype(bf16)
+    for h in range(out_ref.shape[0]):
+        out_ref[h] = y[:, h * HEAD_DIM : (h + 1) * HEAD_DIM]
+
+
+def attn_out_grad_half(grads, half, weights, into=None, earlier=()):
+    count, width = grads.shape
+    cols = weights.shape[1]
+    heads = cols // HEAD_DIM
+    block = cols // 2
+    row = pl.BlockSpec((count, width), lambda j: (0, 0))
+    into = () if into is None else (into,)
+    return pl.pallas_call(
+        attn_out_grad_kernel,
+        grid=(2,),
+        in_specs=[row, pl.BlockSpec((width, block), lambda j: (0, j))]
+        + waits(into)
+        + waits(earlier),
+        out_specs=pl.BlockSpec((heads // 2, count, HEAD_DIM), lambda j: (j, half, 0)),
+        out_shape=jax.ShapeDtypeStruct((heads, 2 * count, HEAD_DIM), bf16),
+        input_output_aliases={2: 0} if into else {},
+        compiler_params=params(),
+        cost_estimate=cost(1),
+        name="attn_out_grad",
+    )(grads, weights, *into, *earlier)
+
+
+def project_grad_kernel(x_ref, w_ref, n_ref, *refs):
+    out_ref, sum_ref, rows = refs[-3:]
+    heads = x_ref.shape[0]
+    cols = heads * HEAD_DIM
+
+    @pl.when(pl.program_id(0) == 0)
+    def _():
+        for k in range(3):
+            for h in range(heads):
+                at = k * cols + h * HEAD_DIM
+                rows[:, at : at + HEAD_DIM] = x_ref[h, :, k * HEAD_DIM : (k + 1) * HEAD_DIM]
+
+    y = None
+    for k in range(3):
+        term = lax.dot_general(
+            rows[:, k * cols : (k + 1) * cols], w_ref[k], DOT_NT, preferred_element_type=f32
+        )
+        y = term if y is None else y + term
+    out_ref[...] = y.astype(bf16)
+    sum_ref[...] = jnp.sum(y * n_ref[...].astype(f32), axis=0, keepdims=True)
+
+
+def project_grad_half(parts, half, weights, normed, earlier=()):
+    heads, count, cols = parts.shape
+    count //= 2
+    width = weights.shape[1]
+    block = width // 4
+    out = pl.BlockSpec((count, block), lambda i: (0, i))
+    return pl.pallas_call(
+        project_grad_kernel,
+        grid=(4,),
+        in_specs=[
+            pl.BlockSpec((heads, count, cols), lambda i: (0, half, 0)),
+            pl.BlockSpec((3, block, weights.shape[2]), lambda i: (0, i, 0)),
+            out,
+        ]
+        + waits(earlier),
+        out_specs=[out, pl.BlockSpec((1, block), lambda i: (0, i))],
+        out_shape=[
+            jax.ShapeDtypeStruct((count, width), bf16),
+            jax.ShapeDtypeStruct((1, width), f32),
+        ],
+        scratch_shapes=[pltpu.VMEM((count, heads * cols), bf16)],
+        compiler_params=params(),
+        cost_estimate=cost(1),
+        name="project_grad",
+    )(parts, weights, normed, *earlier)
+
+
+def row_sum(refs):
+    return refs[0][...].astype(f32) + refs[1][...].astype(f32) + refs[2][...].astype(f32)
+
+
+def inv_rms(rows):
+    return lax.rsqrt(jnp.mean(rows * rows, axis=-1, keepdims=True) + norm_eps)
+
+
+def mix_kernel(near, near_got, far_got, in_ref, gain_ref, *refs):
+    residual_ref, mixed_ref = refs[-2:]
+    residual = in_ref[...].astype(f32) + row_sum((near, near_got, far_got))
+    residual_ref[...] = residual
+    mixed_ref[...] = (residual * inv_rms(residual) * gain_ref[...]).astype(bf16)
+
+
+def gap_kernel(near, near_got, far_got, residual_ref, target_ref, *refs):
+    out_ref, gap_ref, gap_b_ref = refs[-3:]
+    out = residual_ref[...] + row_sum((near, near_got, far_got))
+    out_ref[...] = out.astype(bf16)
+    gap = out - target_ref[...].astype(f32)
+    gap_ref[...] = gap
+    gap_b_ref[...] = gap.astype(bf16)
+
+
+def resid_grad_kernel(near, near_got, far_got, residual_ref, gap_ref, gain_ref, *refs):
+    grad_ref, grad_b_ref, sum_ref = refs[-3:]
+    d_mixed = row_sum((near, near_got, far_got))
+    residual = residual_ref[...]
+    inv = inv_rms(residual)
+    hat = residual * inv
+    grad = gap_ref[...] + norm_back(d_mixed, hat, inv, gain_ref[...])
+    grad_ref[...] = grad
+    grad_b_ref[...] = grad.astype(bf16)
+
+    @pl.when(pl.program_id(0) == 0)
+    def _():
+        sum_ref[...] = jnp.zeros_like(sum_ref)
+
+    sum_ref[...] += jnp.sum(d_mixed * hat, axis=0, keepdims=True)
+
+
+def input_grad_kernel(near, near_got, far_got, in_ref, grad_ref, gain_ref, *refs):
+    rows = in_ref[...].astype(f32)
+    inv = inv_rms(rows)
+    d_normed = row_sum((near, near_got, far_got))
+    grad = grad_ref[...] + norm_back(d_normed, rows * inv, inv, gain_ref[...])
+    refs[-1][...] = grad.astype(bf16)
+
+
+def row_call(kernel, terms, rows, gain, outs, earlier=()):
+    count, width = rows[0].shape
+    block = min(32, count)
+    spec = pl.BlockSpec((block, width), lambda i: (i, 0))
+    line = pl.BlockSpec((1, width), lambda i: (0, 0))
+    gains = [] if gain is None else [gain.reshape(1, width)]
+    return pl.pallas_call(
+        kernel,
+        grid=(count // block,),
+        in_specs=[spec] * (len(terms) + len(rows))
+        + [line] * len(gains)
+        + [pl.BlockSpec(memory_space=pl.ANY)] * len(earlier),
+        out_specs=[line if o is None else spec for o in outs],
+        out_shape=[
+            jax.ShapeDtypeStruct((1, width) if o is None else (count, width), f32 if o is None else o)
+            for o in outs
+        ],
+        compiler_params=pltpu.CompilerParams(vmem_limit_bytes=VMEM_BYTES),
+        cost_estimate=cost(0.1),
+        name=kernel.__name__,
+    )(*terms, *rows, *gains, *earlier)
+
+
+def pick_kernel(cols, z_count, c_ref, r0_ref, r1_ref, *refs):
+    out_ref = refs[-1]
+    half = r0_ref.shape[0]
+    out_ref[:half] = r0_ref[...]
+    out_ref[half:] = r1_ref[...]
+
+
+def pick_half(rows_h, at, earlier=()):
+    half, width = rows_h[0].shape
+    cols = width // 2
+    block = cols // 2
+    return pl.pallas_call(
+        functools.partial(pick_kernel, cols, 2),
+        grid_spec=pltpu.PrefetchScalarGridSpec(
+            num_scalar_prefetch=1,
+            grid=(2,),
+            in_specs=[pl.BlockSpec((half, block), lambda j, c: (0, 2 * c[0] + j))] * 2
+            + [pl.BlockSpec(memory_space=pl.ANY)] * len(earlier),
+            out_specs=pl.BlockSpec((2 * half, block), lambda j, c: (0, j)),
+        ),
+        out_shape=jax.ShapeDtypeStruct((2 * half, cols), rows_h[0].dtype),
+        cost_estimate=cost(0.1),
+        name="pick_half",
+    )(at.reshape(1), *rows_h, *earlier)
 
 
 def token_places(seq_lengths, permutation):
@@ -355,10 +616,32 @@
 def scatter_halves(parts):
     near, far = parts
     n = near.shape[0] // 2
-    far_sum = far[:n].astype(f32) + lax.ppermute(far[n:], "c", SWAP).astype(f32)
-    far_sum = lax.ppermute(far_sum.astype(bf16), "y", SWAP).astype(f32)
-    near_sum = near[:n].astype(f32) + lax.ppermute(near[n:], "c", SWAP).astype(f32)
-    return near_sum + far_sum
+    sent = far[:n].astype(f32) + lax.ppermute(far[n:], "c", SWAP).astype(f32)
+    sent = sent.astype(bf16)
+    far_got = lax.ppermute(sent, "y", SWAP)
+    near_got = lax.ppermute(near[n:], "c", SWAP)
+    return (near, near_got, far_got), sent
+
+
+def gather_line(a, z_pos, z_count):
+    last = z_count - 1
+    up = down = a
+    ups, downs = [], []
+    for s in range(last):
+        up = lax.ppermute(up, "z", [(i, i + 1) for i in range(s, last)])
+        down = lax.ppermute(down, "z", [(i, i - 1) for i in range(1, z_count - s)])
+        ups.append(up)
+        downs.append(down)
+    near = [a] + [
+        jnp.where(z_pos >= s + 1, ups[s], downs[last - 1 - s]) for s in range(last)
+    ]
+    near = jnp.stack(near)
+    return ups, downs, jnp.concatenate(
+        [
+            lax.dynamic_index_in_dim(near, (z_pos - z + z_count) % z_count, 0, False)
+            for z in range(z_count)
+        ]
+    )
 
 
 def sum_near(a):
@@ -372,21 +655,6 @@
         a = a + lax.ppermute(a, "z", [(i, i ^ step) for i in range(z_count)])
         step *= 2
     return a
-
-
-def scatter_line(part, z_pos, z_count):
-    up = down = None
-    last = z_count - 1
-    for s in range(last):
-        to_up = lax.dynamic_index_in_dim(part, jnp.clip(last - s + z_pos, 0, last), 0, False)
-        to_down = lax.dynamic_index_in_dim(part, jnp.clip(z_pos + s - last, 0, last), 0, False)
-        if s > 0:
-            to_up = (to_up.astype(f32) + up.astype(f32)).astype(bf16)
-            to_down = (to_down.astype(f32) + down.astype(f32)).astype(bf16)
-        up = lax.ppermute(to_up, "z", [(i, i + 1) for i in range(s + 1)])
-        down = lax.ppermute(to_down, "z", [(last - i, last - i - 1) for i in range(s + 1)])
-    mine = lax.dynamic_index_in_dim(part, z_pos, 0, False).astype(f32)
-    return mine + up.astype(f32) + down.astype(f32)
 
 
 def local(
@@ -425,6 +693,35 @@
     down_b = down.astype(bf16)
     router_b = router.astype(bf16)
 
+    def scatter_x(a):
+        if pair:
+            mine = lax.dynamic_index_in_dim(a, x_pos, 0, False)
+            other = lax.dynamic_index_in_dim(a, 1 - x_pos, 0, False)
+            return mine.astype(f32) + lax.ppermute(other.astype(bf16), "x", SWAP).astype(f32)
+        return lax.psum_scatter(a.astype(bf16), "x", scatter_dimension=0).astype(f32)
+
+    def of_parity(rows_h, at):
+        return jnp.concatenate(
+            [
+                jnp.concatenate(
+                    [
+                        lax.dynamic_slice_in_dim(
+                            r, z * wide_block + at * out_block, out_block, 1
+                        )
+                        for z in range(z_count)
+                    ],
+                    axis=1,
+                )
+                for r in rows_h
+            ]
+        )
+
+    def far_wide(rows_h):
+        return lax.ppermute(of_parity(rows_h, 1 - x_pos), "x", SWAP)
+
+    def swap_x(parts):
+        return [lax.ppermute(p, "x", SWAP) for p in parts]
+
     resid_in = block_in.astype(f32)
     inv_first = lax.rsqrt(jnp.mean(resid_in * resid_in, axis=-1, keepdims=True) + norm_eps)
     hat_first = resid_in * inv_first
@@ -458,9 +755,47 @@
     squares = jnp.concatenate([jnp.sum(r[:2] * r[:2], axis=-1) for r in raw_h], axis=1)
     squares = sum_near(squares.reshape(2, 2, 2, local_rows)).reshape(2, tok_rows)
     inv_qk = lax.rsqrt(squares / model_width + norm_eps)
-    inv_line = lax.all_gather(inv_qk, "z", axis=0)
+    inv_slots = jnp.where(
+        (jnp.arange(z_count, dtype=jnp.int32) == z_pos)[:, None, None], inv_qk[None], 0.0
+    )
+    inv_line = sum_line(inv_slots, z_count)
     gain_qk = lax.dynamic_slice_in_dim(norm_gains[2:], wt_pos * head_cols, head_cols, 1)
-    payload = pack_heads(
+
+    normed_pick = pick_half(normed_h, c_pos)
+
+    def to_heads_apart(parts):
+        near = [lax.dynamic_index_in_dim(parts, z_pos, 0, False)]
+        for d in range(1, z_count):
+            there = lax.dynamic_index_in_dim(parts, (z_pos + d) % z_count, 0, False)
+            near.append(
+                lax.ppermute(there, "z", [(i, (i + d) % z_count) for i in range(z_count)])
+            )
+        near = jnp.stack(near)
+        return jnp.concatenate(
+            [
+                lax.dynamic_index_in_dim(near, (z_pos - z + z_count) % z_count, 0, False)
+                for z in range(z_count)
+            ]
+        )
+
+    def to_heads(parts):
+        return lax.all_to_all(parts, "z", 0, 0, tiled=True).reshape(line_rows, HEAD_DIM)
+
+    def from_x(a):
+        if pair:
+            return lax.ppermute(a, "x", SWAP)
+        return lax.all_gather(a, "x", axis=0)
+
+    v_heads = jnp.concatenate(
+        [
+            jnp.moveaxis(r[2].astype(bf16).reshape(-1, z_count, HEAD_DIM), 1, 0)
+            for r in raw_h
+        ],
+        axis=1,
+    )
+    values = to_heads(v_heads)
+    values_far = from_x(values)
+    q_heads, k_heads = pack_heads(
         raw_h[0],
         raw_h[1],
         inv_qk.T,
@@ -468,24 +803,27 @@
         lax.dynamic_slice_in_dim(sin_tab, z_pos * tok_rows, tok_rows),
         gain_qk,
     )
-    packed = lax.all_to_all(payload, "z", 0, 0, tiled=True).reshape(line_rows, 3 * HEAD_DIM)
-    kv_own = packed[:, HEAD_DIM:]
+    keys = to_heads_apart(k_heads)
+    keys_far = from_x(keys)
+    queries = to_heads_apart(q_heads)
     tok_col = tok_own.reshape(line_rows, 1)
     if pair:
-        kv_far = lax.ppermute(kv_own, "x", SWAP)
-        groups = [
-            (kv_far, 0, 1, of_x(tok_all, 1 - x_pos).reshape(line_rows, 1)),
-            (packed, 1, 2, tok_col),
-        ]
+        tok_far = of_x(tok_all, 1 - x_pos).reshape(line_rows, 1)
+        groups = [(keys_far, values_far, tok_far), (keys, values, tok_col)]
         key_groups = groups[::-1]
     else:
-        kv_all = lax.all_gather(kv_own, "x", axis=0)
         tok_x = jnp.moveaxis(tok_all, 1, 0).reshape(x_count, line_rows, 1)
-        groups = [(kv_all[i], 0, 1, tok_x[i]) for i in range(x_count)]
+        groups = [(keys_far[i], values_far[i], tok_x[i]) for i in range(x_count)]
         key_groups = [
-            (kv_all.reshape(-1, 2 * HEAD_DIM), 0, 1, tok_x.reshape(-1, 1))
+            (
+                keys_far.reshape(-1, HEAD_DIM),
+                values_far.reshape(-1, HEAD_DIM),
+                tok_x.reshape(-1, 1),
+            )
         ]
-    attn_f, row_lse = attend(packed, tok_q, start_q, key_groups)
+    attn_f, row_lse = attend(
+        queries, tok_q, start_q, key_groups, (normed_pick,)
+    )
 
     def to_tokens(rows, cols):
         parts = lax.all_to_all(
@@ -495,25 +833,30 @@
 
     attn_parts = to_tokens(attn_f.astype(bf16), HEAD_DIM)
     attn_b = jnp.moveaxis(attn_parts, 0, 1).reshape(tok_rows, head_cols)
+    normed_up, normed_down, normed_half = gather_line(normed_pick, z_pos, z_count)
+    attn_far = lax.ppermute(attn_b, "x", SWAP) if pair else attn_b
     half = tok_rows // 2
 
     def halves(a):
         return [a[:half], a[half:]]
 
-    attn_y = scatter_halves(
+    attn_y, _ = scatter_halves(
         [
             lax.dot_general(a, out_b, DOT_NT, preferred_element_type=f32).astype(bf16)
             for a in halves(attn_b)
         ]
     )
-    residual = resid_in + attn_y
-    inv_second = lax.rsqrt(jnp.mean(residual * residual, axis=-1, keepdims=True) + norm_eps)
-    hat_second = residual * inv_second
-    mixed_rows = (hat_second * norm_gains[1]).astype(bf16)
+    residual, mixed_rows = row_call(
+        mix_kernel, attn_y, (block_in,), norm_gains[1], (f32, bf16),
+        (normed_up[0], normed_down[0], attn_far),
+    )
     mixed_h = gather_halves(mixed_rows)
+    mixed_far = far_wide(mixed_h) if pair else mixed_rows
 
     route_rows = near_first(routes.reshape(2, 2, local_rows, -1), 0, y_pos, c_pos)
     route_rows = route_rows.reshape(tok_rows, -1)
+    if pair:
+        routes_far = lax.ppermute(route_rows.T.astype(f32), "x", SWAP).T.astype(jnp.int32)
     choose = jnp.sum(
         (route_rows[:, :, None] == jnp.arange(experts, dtype=jnp.int32)[None, None, :]).astype(f32),
         axis=1,
@@ -531,16 +874,17 @@
     for pre, gate_w in zip(pre_h, gate_w_h):
         gate_act = pre[0] * jax.nn.sigmoid(pre[0])
         hidden_h.append((gate_w.T[:, :, None] * gate_act * pre[1]).astype(bf16))
-    expert_y = scatter_halves(
+    expert_y, _ = scatter_halves(
         [
             jnp.einsum("etf,edf->td", h, down_b, preferred_element_type=f32).astype(bf16)
             for h in hidden_h
         ]
     )
-    out_local = residual + expert_y
-    block_out = out_local.astype(bf16)
-    cot_local = out_local - target.astype(f32)
-    cot_h = gather_halves(cot_local.astype(bf16))
+    block_out, cot_local, cot_b = row_call(
+        gap_kernel, expert_y, (residual, target), None, (bf16, f32, bf16),
+        (normed_up[1], normed_down[1], mixed_far),
+    )
+    cot_h = gather_halves(cot_b)
 
     d_pre_h = []
     d_mixed_parts = []
@@ -574,58 +918,147 @@
             lax.dot_general(d_logit, mixed, (((0,), (0,)), ((), ())), preferred_element_type=f32)
         )
     router_rows = router_parts[0] + router_parts[1]
-    d_mixed = scatter_halves(d_mixed_parts)
-    gain_second = jnp.sum(d_mixed * hat_second, axis=0, keepdims=True)
-    d_resid = cot_local + norm_back(d_mixed, hat_second, inv_second, norm_gains[1])
-    d_resid_h = gather_halves(d_resid.astype(bf16))
-    d_attn = jnp.concatenate(
-        [jnp.dot(d, out_b, preferred_element_type=f32).astype(bf16) for d in d_resid_h]
-    )
-
-    d_attn_parts = jnp.moveaxis(d_attn.reshape(tok_rows, z_count, HEAD_DIM), 1, 0)
-    d_out = lax.all_to_all(d_attn_parts, "z", 0, 0, tiled=True).reshape(line_rows, HEAD_DIM)
+    d_mixed, d_mixed_sent = scatter_halves(d_mixed_parts)
+
+    hidden = jnp.concatenate(hidden_h, axis=1)
+    d_pre = jnp.concatenate(d_pre_h, axis=2)
+
+    def compact(a):
+        taken = route_rows.T[:, None, :, None]
+        parts = []
+        for slot in range(route_rows.shape[1]):
+            part = a[:, 0]
+            for e in range(1, experts):
+                part = jnp.where(taken[slot] == e, a[:, e], part)
+            parts.append(part)
+        return jnp.stack(parts, axis=1)
+
+    def plain_part(wide_h, narrow, spec):
+        return scatter_x(
+            jnp.stack(
+                [
+                    jnp.einsum(spec, of_parity(wide_h, i), narrow, preferred_element_type=f32)
+                    for i in range(x_count)
+                ]
+            )
+        ).astype(bf16)
+
+    d_resid, d_resid_b, gain_second = row_call(
+        resid_grad_kernel,
+        d_mixed,
+        (residual, cot_local),
+        norm_gains[1],
+        (f32, bf16, None),
+    )
+    d_resid_h = gather_halves(d_resid_b)
+    if pair:
+        hidden_far = lax.ppermute(compact(hidden[None]), "x", SWAP)
+        cot_far = far_wide(cot_h)
+        d_pre_far = lax.ppermute(compact(d_pre), "x", SWAP)
+        down_part = weight_grad(
+            cot_h,
+            cot_far,
+            [hidden, hidden_far],
+            out_block,
+            x_pos,
+            routes_far,
+            experts,
+            (d_resid_b, normed_up[2], normed_down[2]),
+        )
+    else:
+        down_part = plain_part(cot_h, jnp.concatenate(hidden_h, axis=1), "td,etf->edf")
+        gate_up_part = plain_part(
+            mixed_h, d_pre, "td,ketf->kedf"
+        ).reshape(2 * experts, -1, hidden_cols)
+    d_attn = attn_out_grad_half(d_resid_h[0], 0, out_b)
+    d_attn = attn_out_grad_half(d_resid_h[1], 1, out_b, d_attn, (down_part,))
+
+    d_out = to_heads(d_attn)
     delta = jnp.sum(d_out.astype(f32) * attn_f, axis=-1).reshape(1, line_rows)
     d_query = jnp.zeros((line_rows, HEAD_DIM), f32)
+    if pair:
+        d_resid_far = far_wide(d_resid_h)
+        gate_up_part = weight_grad(
+            mixed_h,
+            mixed_far,
+            [d_pre.reshape(2 * experts, tok_rows, hidden_cols), d_pre_far],
+            out_block,
+            x_pos,
+            routes_far,
+            experts,
+            (d_attn,),
+        )
     d_kv = []
+    inner_k = []
+    earlier = (gate_up_part,)
     for i, group in enumerate(groups):
-        out_type = f32 if pair and i == 1 else bf16
-        d_query, d_group = attend_grad(
-            packed, d_out, row_lse, delta, tok_q, start_q, d_query, group, out_type
+        last = i == len(groups) - 1
+        d_query, *d_group = attend_grad(
+            queries,
+            d_out,
+            row_lse,
+            delta,
+            tok_q,
+            start_q,
+            d_query,
+            group,
+            f32 if pair and last else bf16,
+            earlier,
         )
+        if pair and not last:
+            out_part = weight_grad(
+                d_resid_h,
+                d_resid_far,
+                [(attn_b, 0), (attn_b, 1), (attn_far, 0), (attn_far, 1)],
+                out_block,
+                x_pos,
+                earlier=(d_group[0],),
+            )
+            earlier = (out_part,)
         d_kv.append(d_group)
+        inner_k.append(jnp.sum(d_group[0].astype(f32) * group[0].astype(f32), axis=-1))
     if pair:
-        d_kv = d_kv[1] + lax.ppermute(d_kv[0], "x", SWAP).astype(f32)
+        d_key, d_value = [
+            own + lax.ppermute(far, "x", SWAP).astype(f32) for far, own in zip(*d_kv)
+        ]
+        inner_k = inner_k[1] + lax.ppermute(inner_k[0], "x", SWAP)
     else:
-        d_kv = lax.psum_scatter(jnp.stack(d_kv), "x", scatter_dimension=0).astype(f32)
-    inner = jnp.stack(
-        [
-            jnp.sum(d_query * packed[:, :HEAD_DIM].astype(f32), axis=-1),
-            jnp.sum(d_kv[:, :HEAD_DIM] * packed[:, HEAD_DIM : 2 * HEAD_DIM].astype(f32), axis=-1),
+        d_key, d_value = [
+            lax.psum_scatter(jnp.stack(parts), "x", scatter_dimension=0).astype(f32)
+            for parts in zip(*d_kv)
         ]
-    )
+        inner_k = lax.psum_scatter(jnp.stack(inner_k), "x", scatter_dimension=0)
+    inner = jnp.stack([jnp.sum(d_query * queries.astype(f32), axis=-1), inner_k])
     inner = sum_line(sum_near(inner.reshape(2, z_count, 2, 2, local_rows)), z_count)
     inner = inner.reshape(2, line_rows) / model_width
     inv_line = jnp.moveaxis(inv_line, 0, 1).reshape(2, line_rows)
     coef = jnp.stack([inv_line[0], inner[0], inv_line[1], inner[1]], axis=1)
     head_gain = lax.dynamic_slice_in_dim(gain_qk, z_pos * HEAD_DIM, HEAD_DIM, 1)
     d_raw, gain_sums = raw_grad(
-        d_query, d_kv, packed, coef, cos_tab, sin_tab, head_gain
+        d_query, d_key, d_value, queries, keys, coef, cos_tab, sin_tab, head_gain
     )
     gain_full = lax.dynamic_update_slice_in_dim(
         jnp.zeros((2, model_width), f32), gain_sums, (wt_pos * z_count + z_pos) * HEAD_DIM, 1
     )
 
-    d_proj = jnp.moveaxis(
-        to_tokens(d_raw, 3 * HEAD_DIM).reshape(z_count, tok_rows, 3, HEAD_DIM), 2, 0
-    )
-    d_proj = jnp.moveaxis(d_proj, 1, 2).reshape(3, tok_rows, head_cols)
-    d_normed_h = [
-        jnp.einsum("ktc,kdc->td", d, qkv_b, preferred_element_type=f32)
-        for d in (d_proj[:, :half], d_proj[:, half:])
-    ]
-    d_normed = scatter_halves([d.astype(bf16) for d in d_normed_h])
-    gain_first = jnp.sum(d_normed * hat_first, axis=0, keepdims=True)
-    input_grad = (d_resid + norm_back(d_normed, hat_first, inv_first, norm_gains[0])).astype(bf16)
+    d_proj = to_tokens(d_raw, 3 * HEAD_DIM)
+    far_n, gain_first1 = project_grad_half(d_proj, 1, qkv_b, normed_h[1])
+    near_n, gain_first0 = project_grad_half(d_proj, 0, qkv_b, normed_h[0], (far_n,))
+    down_part = lax.psum_scatter(down_part, "z", scatter_dimension=1, tiled=True).astype(f32)
+    gate_up_part = (
+        lax.psum_scatter(gate_up_part, "z", scatter_dimension=1, tiled=True)
+        .astype(f32)
+        .reshape(2, experts, out_block, hidden_cols)
+    )
+    d_normed, _ = scatter_halves([near_n, far_n])
+    gain_first = (gain_first0 + gain_first1) / norm_gains[:1]
+    (input_grad,) = row_call(
+        input_grad_kernel,
+        d_normed,
+        (block_in, d_resid),
+        norm_gains[0],
+        (bf16,),
+    )
 
     def sum_all(a):
         a = a + lax.ppermute(a, "c", SWAP)
@@ -633,51 +1066,17 @@
         a = a + lax.ppermute(a, "x", SWAP) if pair else lax.psum(a, "x")
         return sum_line(a, z_count)
 
-    small = sum_all(jnp.concatenate([gain_second, gain_full, router_rows]))
-    gains_grad = jnp.concatenate([sum_all(gain_first), small[:3]])
-    router_grad = small[3:].T
-
-    def scatter_x(a):
-        if pair:
-            mine = lax.dynamic_index_in_dim(a, x_pos, 0, False)
-            other = lax.dynamic_index_in_dim(a, 1 - x_pos, 0, False)
-            return mine.astype(f32) + lax.ppermute(other.astype(bf16), "x", SWAP).astype(f32)
-        return lax.psum_scatter(a.astype(bf16), "x", scatter_dimension=0).astype(f32)
-
-    def split_x(rows):
-        a = rows.reshape(tok_rows, z_count, x_count, out_block)
-        mine = lax.dynamic_index_in_dim(a, x_pos, 2, False)
-        other = lax.dynamic_index_in_dim(a, 1 - x_pos, 2, False)
-        return [mine, lax.ppermute(other, "x", SWAP)]
-
-    def weight_grad(wide_h, narrow, spec):
-        wide = jnp.concatenate(wide_h)
-        if pair:
-            narrow_far = lax.ppermute(narrow, "x", SWAP)
-            mine, far = split_x(wide)
-            part = jnp.einsum(spec, mine, narrow, preferred_element_type=f32)
-            part = part + jnp.einsum(spec, far, narrow_far, preferred_element_type=f32)
-        else:
-            a = wide.reshape(tok_rows, z_count, x_count, out_block)
-            part = scatter_x(
-                jnp.stack(
-                    [
-                        jnp.einsum(spec, a[:, :, i], narrow, preferred_element_type=f32)
-                        for i in range(x_count)
-                    ]
-                )
-            )
-        return scatter_line(part.astype(bf16), z_pos, z_count)
-
-    down_part = weight_grad(cot_h, jnp.concatenate(hidden_h, axis=1), "tbd,etf->bedf")
-    gate_up_part = weight_grad(mixed_h, jnp.concatenate(d_pre_h, axis=2), "tbd,ketf->bkedf")
-    out_part = weight_grad(d_resid_h, attn_b, "tbd,tc->bdc")
-
-    normed_all = jnp.concatenate(normed_h)
-    normed_half = lax.dynamic_slice_in_dim(
-        normed_all, c_pos * (model_width // 2), model_width // 2, 1
-    )
-    normed_half = lax.all_gather(normed_half, "z", axis=0, tiled=True)
+    small = sum_all(jnp.concatenate([gain_first, gain_second, gain_full, router_rows]))
+    gains_grad = small[:4]
+    router_grad = small[4:].T
+
+    if pair:
+        out_part = lax.psum_scatter(out_part, "z", scatter_dimension=1, tiled=True)
+        out_part = jnp.moveaxis(out_part, 0, 1).reshape(out_block, head_cols).astype(f32)
+    else:
+        out_part = plain_part(d_resid_h, attn_b, "td,tc->dc")
+        out_part = lax.psum_scatter(out_part, "z", scatter_dimension=0, tiled=True).astype(f32)
+
     normed_other = lax.ppermute(normed_half, "c", SWAP)
     tn = (((0,), (0,)), ((), ()))
     grad_mine = lax.dot_general(normed_half, d_raw, tn, preferred_element_type=f32).astype(bf16)

time: 695 us -> 602 us (0.87)
  Pallas kernels: 61.9 us -> 122 us
  blocking collectives: 54.5 us -> 0 us
  matrix products: 80.9 us -> 38.1 us
  starting transfers between devices: 125 us -> 92.9 us
  local copies, waits for them, and re-layouts: 82.5 us -> 50.9 us
  waiting for transfers between devices: 167 us -> 182 us
  other arithmetic: 96.9 us -> 89.4 us
    pallas_call x1 -> x13, Pallas kernels: 5.97 us -> 67.2 us  [the longest x3 24.2 us: weight_grad(): pl.pallas_call(kernel, grid_spec=pltpu.PrefetchScalarGridSpec(num_scalar_...]
    all_to_all x2, waiting for transfers between devices: 9.72 us -> 63.4 us  [to_tokens(): lax.all_to_all(rows.reshape(z_count, tok_rows, cols), 'z', 0, 0, tiled=True)]
    all_to_all x1 -> x0, blocking collectives: 41.3 us -> none  [local(): lax.all_to_all(payload, 'z', 0, 0, tiled=True)]
    ppermute x6, waiting for transfers between devices: 44.4 us -> 3.81 us  [sum_line(): a = a + lax.ppermute(a, 'z', [(i, i ^ step) for i in range(z_count)])]
    dot_general x10 -> x0, matrix products: 36.3 us -> none  [the longest x3 11.3 us: weight_grad(): part = part + jnp.einsum(spec, far, narrow_far, preferred_element_type=f32)]
    dynamic_slice x7 -> x8, local copies, waits for them, and re-layouts: 31.9 us -> 5.18 us  [the longest x6 2.59 us: of_parity(): lax.dynamic_slice_in_dim(r, z * wide_block + at * out_block, out_block, 1)]
    ppermute x38 -> x36, starting transfers between devices: 71.2 us -> 44.9 us  [the longest x6 9.83 us: to_heads_apart(): lax.ppermute(there, 'z', [(i, (i + d) % z_count) for i in range(z_count)])]
    convert_element_type x15 -> x10, other arithmetic: 25.6 us -> 8.04 us  [the longest x4 2.36 us: scatter_halves(): sent = sent.astype(bf16)]
  transfers between devices with their start and end apart: 73 -> 71, of which waited for: 22 -> 24; matrix products, arithmetic and copies ran while one was open for 34% -> 25% of each run, Pallas kernels for 6% -> 16%
where the time goes in v2:
time: 602 us; the launch traced here: 592 us
  waiting for transfers between devices  182 us (30%)
  Pallas kernels  122 us (20%)
  starting transfers between devices  92.9 us (15%)
  other arithmetic  89.4 us (15%)
  local copies, waits for them, and re-layouts  50.9 us (8%)
  matrix products  38.1 us (6%)
  between operations  15.9 us (3%)
    all_to_all x2, waiting for transfers between devices, to_tokens(): lax.all_to_all(rows.reshape(z_count, tok_rows, cols), 'z', 0, 0, tiled=True)  63.4 us
    pallas_call x2, Pallas kernels, attend_grad(): pl.pallas_call(functools.partial(attend_grad_kernel, chunk, LOG2E / math....  31.2 us
    pallas_call x3, Pallas kernels, weight_grad(): pl.pallas_call(kernel, grid_spec=pltpu.PrefetchScalarGridSpec(num_scalar_...  24.2 us
    ppermute x4, waiting for transfers between devices, gather_halves(): far = lax.ppermute(rows, 'y', SWAP)  22.3 us
    ppermute x4, waiting for transfers between devices, scatter_halves(): far_got = lax.ppermute(sent, 'y', SWAP)  21.3 us
    pallas_call x1, Pallas kernels, attend(): pl.pallas_call(functools.partial(attend_kernel, len(key_groups), chunk, L...  19 us
    unnamed x177, local copies, waits for them, and re-layouts  18.9 us
    pallas_call x4, Pallas kernels, row_call(): pl.pallas_call(kernel, grid=(count // block,), in_specs=[spec] * (len(ter...  16.6 us
  transfers between devices with their start and end apart: 71, of which 24 were waited for; matrix products, arithmetic and copies ran while one was open for 25% of the time, Pallas kernels for 16%

profile of v2, /device:TPU:0, one launch (start us, length us, event | category | flops | bytes accessed | tf_op | source)
XLA Modules:
  0.0 591.6 jit_solution(12528269554374879279)
XLA Ops:
  11.1 3.0 collective-permute-start.1
  18.4 8.0 %convert_element_type.224.w_ref = bf16[3,2048,512]{2,1,0:T(8,128)(2,1)} convert(f32[3,2048,512]{2,1,0:T(8,128)} %param.16) | non-fusion elementwise | flops 3145728 | bytes 18874368 | tf_op jit(solution)/shard_map/convert_element_type | solution.py:690
  27.6 3.7 multiply_sine_fusion
  40.2 4.9 convolution_bitcast_fusion.4.raw1_ref
  48.6 5.3 all-to-all-start
  54.8 4.7 pack_heads.1
  74.6 9.0 %collective-permute-done.9 = bf16[512,128]{1,0:T(8,128)(2,1)S(1)} collective-permute-done((bf16[512,128]{1,0:T(8,128)(2,1)S(1)}, bf16[512,128]{1,0:T(8,128)(2,1)S(1)}, u32[]{:S(2)}, u32[]{:S(2)}) %collective-permute-start.9) | collective-permute-done | bytes 131104 | tf_op jit(solution)/shard_map/ppermute | solution.py:771
  92.8 6.0 %collective-permute-done.11.refs_3_.k_ref = bf16[2048,128]{1,0:T(8,128)(2,1)} collective-permute-done((bf16[2048,128]{1,0:T(8,128)(2,1)S(1)}, bf16[2048,128]{1,0:T(8,128)(2,1)}, u32[]{:S(2)}, u32[]{:S(2)}) %collective-permute-start.11) | collective-permute-done | bytes 524320 | tf_op jit(solution)/shard_map/ppermute | solution.py:786
  98.8 7.7 %collective-permute-done.12.refs_4_.v_ref = bf16[2048,128]{1,0:T(8,128)(2,1)} collective-permute-done((bf16[2048,128]{1,0:T(8,128)(2,1)S(1)}, bf16[2048,128]{1,0:T(8,128)(2,1)}, u32[]{:S(2)}, u32[]{:S(2)}) %collective-permute-start.12) | collective-permute-done | bytes 524320 | tf_op jit(solution)/shard_map/ppermute | solution.py:786
  106.6 19.0 %attend.1 = (f32[2048,128]{1,0:T(8,128)}, f32[1,2048]{1,0:T(1,128)}) custom-call(bf16[2048,128]{1,0:T(8,128)(2,1)} %pad_maximum_fusion.10.q_ref, s32[1,2048]{1,0:T(1,128)} %bitcast.320, s32[1,2048]{1,0:T(1,128)} %bitcast.331, bf16[2048,128]{1,0:T(8,128)(2,1)} %copy-done.46, bf16[2048,128]{1,0:T(8,128)(2,1)} %bitcast.304, s32[2048,1]{1,0:T(8,128)} %copy.152.refs_2_.tok_k_ref, ...), custom_call_target="tpu_custom_call" | custom-call | flops 8000000000 | bytes 1048576 | tf_op jit(solution)/shard_map/attend/pallas_call | solution.py:98
  127.7 5.3 all-to-all-start.1
  135.5 5.6 collective-permute-start.16
  142.5 4.0 all-to-all-done.1
  161.3 5.2 collective-permute-done.17.refs_1_
  171.2 3.9 mix_kernel.1
  176.3 8.9 %convert_element_type.239 = bf16[2,4,2048,256]{3,2,1,0:T(8,128)(2,1)} convert(f32[2,4,2048,256]{3,2,1,0:T(8,128)} %param.20) | non-fusion elementwise | flops 4194304 | bytes 25165824 | tf_op jit(solution)/shard_map/convert_element_type | solution.py:692
  185.4 5.8 convert_element_type.241
  196.4 11.9 %collective-permute-done.21 = bf16[128,2048]{1,0:T(8,128)(2,1)S(1)} collective-permute-done((bf16[128,2048]{1,0:T(8,128)(2,1)S(1)}, bf16[128,2048]{1,0:T(8,128)(2,1)S(1)}, u32[]{:S(2)}, u32[]{:S(2)}) %collective-permute-start.21) | collective-permute-done | bytes 524320 | tf_op jit(solution)/shard_map/ppermute | solution.py:611
  208.4 5.9 convolution_bitcast_fusion.3
  232.6 5.4 collective-permute-done.24.far_got
  238.0 5.4 collective-permute-done.27.refs_2_
  244.4 4.1 gap_kernel.1
  253.9 10.4 %collective-permute-done.30 = bf16[128,2048]{1,0:T(8,128)(2,1)S(1)} collective-permute-done((bf16[128,2048]{1,0:T(8,128)(2,1)S(1)}, bf16[128,2048]{1,0:T(8,128)(2,1)S(1)}, u32[]{:S(2)}, u32[]{:S(2)}) %collective-permute-start.30) | collective-permute-done | bytes 524320 | tf_op jit(solution)/shard_map/ppermute | solution.py:611
  279.7 10.4 %collective-permute-done.33.far_got = bf16[128,2048]{1,0:T(8,128)(2,1)S(1)} collective-permute-done((bf16[128,2048]{1,0:T(8,128)(2,1)S(1)}, bf16[128,2048]{1,0:T(8,128)(2,1)S(1)}, u32[]{:S(2)}, u32[]{:S(2)}) %collective-permute-start.33) | collective-permute-done | bytes 524320 | tf_op jit(solution)/shard_map/ppermute | solution.py:621
  290.9 4.5 resid_grad_kernel.1
  299.9 11.9 %collective-permute-done.38.refs_4_ = bf16[1,2,512,256]{3,2,1,0:T(8,128)(2,1)S(1)} collective-permute-done((bf16[1,2,512,256]{3,2,1,0:T(8,128)(2,1)}, bf16[1,2,512,256]{3,2,1,0:T(8,128)(2,1)S(1)}, u32[]{:S(2)}, u32[]{:S(2)}) %collective-permute-start.38) | collective-permute-done | bytes 524320 | tf_op jit(solution)/shard_map/ppermute | solution.py:955
  312.9 7.5 %weight_grad.3.refs_1_ = bf16[4,1024,256]{2,1,0:T(8,128)(2,1)} custom-call(s32[1]{0:T(128)} %bitcast.74.x_ref, bf16[256,2048]{1,0:T(8,128)(2,1)} %copy-done.21, bf16[256,2048]{1,0:T(8,128)(2,1)} %copy-done.20, bf16[512,1024]{1,0:T(8,128)(2,1)} %copy-done.41, bf16[4,512,256]{2,1,0:T(8,128)(2,1)} %get-tuple-element.140.refs_3_, ...), custom_call_target="tpu_custom_call" | custom-call | flops 100000000 | bytes 1048576 | tf_op jit(solution)/shard_map/weight_grad/pallas_call | solution.py:386
  323.6 3.1 attn_out_grad.2.refs_0_
  328.8 3.1 attn_out_grad.3.refs_6_
  332.0 5.1 all-to-all-start.2
  343.4 11.6 %weight_grad.4.refs_0_ = bf16[8,1024,256]{2,1,0:T(8,128)(2,1)} custom-call(s32[1]{0:T(128)} %bitcast.74.x_ref, bf16[256,2048]{1,0:T(8,128)(2,1)} %copy-done.4, bf16[256,2048]{1,0:T(8,128)(2,1)} %copy-done.2, bf16[512,1024]{1,0:T(8,128)(2,1)} %copy-done.24, bf16[8,512,256]{2,1,0:T(8,128)(2,1)} %pad_maximum_fusion.2.refs_3_, ...), custom_call_target="tpu_custom_call" | custom-call | flops 100000000 | bytes 1048576 | tf_op jit(solution)/shard_map/weight_grad/pallas_call | solution.py:386
  358.0 15.4 %attend_grad.2 = (f32[2048,128]{1,0:T(8,128)}, bf16[2048,128]{1,0:T(8,128)(2,1)}, bf16[2048,128]{1,0:T(8,128)(2,1)}) custom-call(bf16[2048,128]{1,0:T(8,128)(2,1)} %pad_maximum_fusion.10.q_ref, bf16[2048,128]{1,0:T(8,128)(2,1)} %bitcast.79.do_ref, f32[1,2048]{1,0:T(1,128)} %get-tuple-element.41.lse_ref, f32[1,2048]{1,0:T(1,128)} %bitcast.329, ...), custom_call_target="tpu_custom_call" | custom-call | flops 8000000000 | bytes 1048576 | tf_op jit(solution)/shard_map/attend_grad/pallas_call | solution.py:193
  373.4 5.1 weight_grad.5.refs_0_
  399.1 15.8 %attend_grad.3 = (f32[2048,128]{1,0:T(8,128)}, f32[2048,128]{1,0:T(8,128)}, f32[2048,128]{1,0:T(8,128)}) custom-call(bf16[2048,128]{1,0:T(8,128)(2,1)} %pad_maximum_fusion.10.q_ref, bf16[2048,128]{1,0:T(8,128)(2,1)} %bitcast.79.do_ref, f32[1,2048]{1,0:T(1,128)} %get-tuple-element.41.lse_ref, f32[1,2048]{1,0:T(1,128)} %bitcast.330, s32[1,2048]{1,0:T(1,128)} %bitcast.322, ...), custom_call_target="tpu_custom_call" | custom-call | flops 8000000000 | bytes 1048576 | tf_op jit(solution)/shard_map/attend_grad/pallas_call | solution.py:193
  425.8 3.3 collective-permute-done.51
  430.0 4.6 collective-permute-done.45
  437.2 6.0 %raw_grad.1 = (bf16[2048,384]{1,0:T(8,128)(2,1)}, f32[2,128]{1,0:T(2,128)}) custom-call(f32[2048,128]{1,0:T(8,128)} %get-tuple-element.44.dq_ref, f32[2048,128]{1,0:T(8,128)} %get-tuple-element.128.dk_ref, f32[2048,128]{1,0:T(8,128)} %convert_add_fusion.1.dv_ref, bf16[2048,128]{1,0:T(8,128)(2,1)} %pad_maximum_fusion.10.q_ref, bf16[2048,128]{1,0:T(8,128)(2,1)} %copy-done.46, ...), custom_call_target="tpu_custom_call" | custom-call | flops 3000000000 | bytes 1048576 | tf_op jit(solution)/shard_map/raw_grad/pallas_call | solution.py:301
  443.1 5.4 all-to-all-start.3
  452.0 4.7 fusion.15
  456.7 4.6 fusion.16
  462.5 59.5 %all-to-all-done.3.x_ref = bf16[4,512,384]{2,1,0:T(8,128)(2,1)} async-done(((bf16[4,512,384]{2,1,0:T(8,128)(2,1)}), bf16[4,512,384]{2,1,0:T(8,128)(2,1)}, u32[]{:S(2)}, u32[]{:S(2)}) %all-to-all-start.3) | async-done | bytes 1572896 | tf_op jit(solution)/shard_map/all_to_all | solution.py:829
  521.9 6.1 %project_grad.2 = (bf16[256,2048]{1,0:T(8,128)(2,1)}, f32[1,2048]{1,0:T(1,128)}) custom-call(bf16[4,512,384]{2,1,0:T(8,128)(2,1)} %all-to-all-done.3.x_ref, bf16[3,2048,512]{2,1,0:T(8,128)(2,1)} %convert_element_type.224.w_ref, bf16[256,2048]{1,0:T(8,128)(2,1)} %copy-done.12), custom_call_target="tpu_custom_call" | custom-call | flops 1000000000 | bytes 1048576 | tf_op jit(solution)/shard_map/project_grad/pallas_call | solution.py:472
  528.0 6.1 %project_grad.3 = (bf16[256,2048]{1,0:T(8,128)(2,1)}, f32[1,2048]{1,0:T(1,128)}) custom-call(bf16[4,512,384]{2,1,0:T(8,128)(2,1)} %all-to-all-done.3.x_ref, bf16[3,2048,512]{2,1,0:T(8,128)(2,1)} %convert_element_type.224.w_ref, bf16[256,2048]{1,0:T(8,128)(2,1)} %pad_maximum_fusion.3.r0_ref.n_ref, bf16[256,2048]{1,0:T(8,128)(2,1)} %get-tuple-element.49.refs_0_), custom_call_target="tpu_custom_call" | custom-call | flops 1000000000 | bytes 1048576 | tf_op jit(solution)/shard_map/project_grad/pallas_call | solution.py:472
  536.8 3.5 all-to-all-start.4
  546.6 3.8 collective-permute-done.60
  564.3 6.9 %all-to-all-done.4 = bf16[4,256,384]{1,2,0:T(8,128)(2,1)S(1)} async-done(((bf16[4,256,384]{1,2,0:T(8,128)(2,1)}), bf16[4,256,384]{1,2,0:T(8,128)(2,1)S(1)}, u32[]{:S(2)}, u32[]{:S(2)}) %all-to-all-start.4) | async-done | bytes 786464 | tf_op jit(solution)/shard_map/all_to_all | solution.py:1095
  573.8 3.1 collective-permute-done.55.far_got
  577.7 4.2 input_grad_kernel.1
  (470 shorter events, 207.3 us)
Async XLA Ops:
  11.1 22.3 %collective-permute-start.1 = (bf16[128,2048]{1,0:T(8,128)(2,1)S(1)}, bf16[128,2048]{1,0:T(8,128)(2,1)S(1)}, u32[]{:S(2)}, u32[]{:S(2)}) collective-permute-start(bf16[128,2048]{1,0:T(8,128)(2,1)S(1)} %fusion.23), channel_id=1, source_target_pairs={{0,2},{2,0},{1,3},{3,1},{4,6},{6,4},{5,7},{7,5},{8,10},{10,8},{9,1... | collective-permute-start | bytes 1572872 | tf_op jit(solution)/shard_map/ppermute | solution.py:611
  14.1 19.7 %collective-permute-start = (bf16[128,2048]{1,0:T(8,128)(2,1)S(1)}, bf16[128,2048]{1,0:T(8,128)(2,1)S(1)}, u32[]{:S(2)}, u32[]{:S(2)}) collective-permute-start(bf16[128,2048]{1,0:T(8,128)(2,1)S(1)} %fusion.23), channel_id=1, source_target_pairs={{0,1},{1,0},{2,3},{3,2},{4,5},{5,4},{6,7},{7,6},{8,9},{9,8},{10,11... | collective-permute-start | bytes 1572872 | tf_op jit(solution)/shard_map/ppermute | solution.py:610
  48.6 36.7 %all-to-all-start = ((bf16[4,512,128]{2,1,0:T(8,128)(2,1)}), bf16[4,512,128]{2,1,0:T(8,128)(2,1)S(1)}, u32[]{:S(2)}, u32[]{:S(2)}) async-start(bf16[4,512,128]{2,1,0:T(8,128)(2,1)} %pad_maximum_fusion.13), calls=%async_computation | async-start | bytes 1048576 | tf_op jit(solution)/shard_map/all_to_all | solution.py:782
  63.4 20.2 %collective-permute-start.9 = (bf16[512,128]{1,0:T(8,128)(2,1)S(1)}, bf16[512,128]{1,0:T(8,128)(2,1)S(1)}, u32[]{:S(2)}, u32[]{:S(2)}) collective-permute-start(bf16[512,128]{1,0:T(8,128)(2,1)S(1)} %get-tuple-element.165), channel_id=1, source_target_pairs={{0,16},{8,24},{16,0},{24,8},{1,17},{9,25},{17,1},{25,9},{2,18},{10... | collective-permute-start | bytes 393224 | tf_op jit(solution)/shard_map/ppermute | solution.py:771
  65.8 17.8 %collective-permute-start.10 = (bf16[512,128]{1,0:T(8,128)(2,1)S(1)}, bf16[512,128]{1,0:T(8,128)(2,1)S(1)}, u32[]{:S(2)}, u32[]{:S(2)}) collective-permute-start(bf16[512,128]{1,0:T(8,128)(2,1)S(1)} %get-tuple-element.164), channel_id=1, source_target_pairs={{0,24},{8,0},{16,8},{24,16},{1,25},{9,1},{17,9},{25,17},{2,26},{10... | collective-permute-start | bytes 393224 | tf_op jit(solution)/shard_map/ppermute | solution.py:771
  70.7 19.5 %collective-permute-start.5 = (bf16[512,128]{1,0:T(8,128)(2,1)}, bf16[512,128]{1,0:T(8,128)(2,1)}, u32[]{:S(2)}, u32[]{:S(2)}) collective-permute-start(bf16[512,128]{1,0:T(8,128)(2,1)} %get-tuple-element.174), channel_id=1, source_target_pairs={{0,8},{8,16},{16,24},{24,0},{1,9},{9,17},{17,25},{25,1},{2,10},{10... | collective-permute-start | bytes 393224 | tf_op jit(solution)/shard_map/ppermute | solution.py:771
  71.2 18.9 %collective-permute-start.6 = (bf16[512,128]{1,0:T(8,128)(2,1)}, bf16[512,128]{1,0:T(8,128)(2,1)}, u32[]{:S(2)}, u32[]{:S(2)}) collective-permute-start(bf16[512,128]{1,0:T(8,128)(2,1)} %get-tuple-element.173), channel_id=1, source_target_pairs={{0,16},{8,24},{16,0},{24,8},{1,17},{9,25},{17,1},{25,9},{2,18},{10... | collective-permute-start | bytes 393224 | tf_op jit(solution)/shard_map/ppermute | solution.py:771
  71.8 18.4 %collective-permute-start.7 = (bf16[512,128]{1,0:T(8,128)(2,1)}, bf16[512,128]{1,0:T(8,128)(2,1)}, u32[]{:S(2)}, u32[]{:S(2)}) collective-permute-start(bf16[512,128]{1,0:T(8,128)(2,1)} %get-tuple-element.172), channel_id=1, source_target_pairs={{0,24},{8,0},{16,8},{24,16},{1,25},{9,1},{17,9},{25,17},{2,26},{10... | collective-permute-start | bytes 393224 | tf_op jit(solution)/shard_map/ppermute | solution.py:771
  83.8 15.0 %collective-permute-start.11 = (bf16[2048,128]{1,0:T(8,128)(2,1)S(1)}, bf16[2048,128]{1,0:T(8,128)(2,1)}, u32[]{:S(2)}, u32[]{:S(2)}) collective-permute-start(bf16[2048,128]{1,0:T(8,128)(2,1)S(1)} %pad_maximum_fusion.12.refs_0_.k_ref), channel_id=1, source_target_pairs={{0,4},{4,0},{1,5},{5,1},{2,6},{6,2},{3,7},{7,3},{8,12},{12,8},{9,1... | collective-permute-start | bytes 1572872 | tf_op jit(solution)/shard_map/ppermute | solution.py:786
  85.4 21.2 %collective-permute-start.12 = (bf16[2048,128]{1,0:T(8,128)(2,1)S(1)}, bf16[2048,128]{1,0:T(8,128)(2,1)}, u32[]{:S(2)}, u32[]{:S(2)}) collective-permute-start(bf16[2048,128]{1,0:T(8,128)(2,1)S(1)} %bitcast.303), channel_id=1, source_target_pairs={{0,4},{4,0},{1,5},{5,1},{2,6},{6,2},{3,7},{7,3},{8,12},{12,8},{9,1... | collective-permute-start | bytes 1572872 | tf_op jit(solution)/shard_map/ppermute | solution.py:786
  127.7 18.9 %all-to-all-start.1 = ((bf16[4,512,128]{2,1,0:T(8,128)(2,1)}), bf16[4,512,128]{2,1,0:T(8,128)(2,1)}, u32[]{:S(2)}, u32[]{:S(2)}) async-start(bf16[4,512,128]{2,1,0:T(8,128)(2,1)} %bitcast.40), calls=%async_computation.1 | async-start | bytes 1048576 | tf_op jit(solution)/shard_map/all_to_all | solution.py:829
  135.5 25.8 %collective-permute-start.16 = (bf16[512,1024]{1,0:T(8,128)(2,1)}, bf16[512,1024]{1,0:T(8,128)(2,1)}, u32[]{:S(2)}, u32[]{:S(2)}) collective-permute-start(bf16[512,1024]{1,0:T(8,128)(2,1)} %pick_half.1.refs_6_), channel_id=1, source_target_pairs={{0,8},{8,16},{16,24},{1,9},{9,17},{17,25},{2,10},{10,18},{18,26},{... | collective-permute-start | bytes 3145736 | tf_op jit(solution)/shard_map/ppermute | solution.py:631
  141.0 25.5 %collective-permute-start.17 = (bf16[512,1024]{1,0:T(8,128)(2,1)}, bf16[512,1024]{1,0:T(8,128)(2,1)}, u32[]{:S(2)}, u32[]{:S(2)}) collective-permute-start(bf16[512,1024]{1,0:T(8,128)(2,1)} %pick_half.1.refs_6_), channel_id=1, source_target_pairs={{8,0},{16,8},{24,16},{9,1},{17,9},{25,17},{10,2},{18,10},{26,18},{... | collective-permute-start | bytes 3145736 | tf_op jit(solution)/shard_map/ppermute | solution.py:632
  154.7 13.9 %collective-permute-start.18 = (bf16[512,512]{1,0:T(8,128)(2,1)S(1)}, bf16[512,512]{1,0:T(8,128)(2,1)S(1)}, u32[]{:S(2)}, u32[]{:S(2)}) collective-permute-start(bf16[512,512]{1,0:T(8,128)(2,1)S(1)} %copy_bitcast_fusion.refs_3_.refs_4_), channel_id=1, source_target_pairs={{0,4},{4,0},{1,5},{5,1},{2,6},{6,2},{3,7},{7,3},{8,12},{12,8},{9,1... | collective-permute-start | bytes 1572872 | tf_op jit(solution)/shard_map/ppermute | solution.py:837
  157.3 13.9 %collective-permute-start.15 = (bf16[128,2048]{1,0:T(8,128)(2,1)}, bf16[128,2048]{1,0:T(8,128)(2,1)}, u32[]{:S(2)}, u32[]{:S(2)}) collective-permute-start(bf16[128,2048]{1,0:T(8,128)(2,1)} %add_convert_fusion.3), channel_id=1, source_target_pairs={{0,2},{2,0},{1,3},{3,1},{4,6},{6,4},{5,7},{7,5},{8,10},{10,8},{9,1... | collective-permute-start | bytes 1572872 | tf_op jit(solution)/shard_map/ppermute | solution.py:621
  175.0 20.8 %collective-permute-start.19 = (bf16[128,2048]{1,0:T(8,128)(2,1)}, bf16[128,2048]{1,0:T(8,128)(2,1)S(1)}, u32[]{:S(2)}, u32[]{:S(2)}) collective-permute-start(bf16[128,2048]{1,0:T(8,128)(2,1)} %get-tuple-element.35), channel_id=1, source_target_pairs={{0,1},{1,0},{2,3},{3,2},{4,5},{5,4},{6,7},{7,6},{8,9},{9,8},{10,11... | collective-permute-start | bytes 1572872 | tf_op jit(solution)/shard_map/ppermute | solution.py:610
  175.8 47.9 %collective-permute-start.39 = (f32[2,512]{0,1:T(8,128)}, f32[2,512]{0,1:T(8,128)}, u32[]{:S(2)}, u32[]{:S(2)}) collective-permute-start(f32[2,512]{0,1:T(8,128)} %bitcast_convert_fusion), channel_id=1, source_target_pairs={{0,4},{4,0},{1,5},{5,1},{2,6},{6,2},{3,7},{7,3},{8,12},{12,8},{9,1... | collective-permute-start | bytes 12296 | tf_op jit(solution)/shard_map/ppermute | solution.py:859
  191.2 36.9 %collective-permute-start.25 = (bf16[512,1024]{1,0:T(8,128)(2,1)}, bf16[512,1024]{1,0:T(8,128)(2,1)}, u32[]{:S(2)}, u32[]{:S(2)}) collective-permute-start(bf16[512,1024]{1,0:T(8,128)(2,1)} %collective-permute-done.16.refs_0_), channel_id=1, source_target_pairs={{8,16},{16,24},{9,17},{17,25},{10,18},{18,26},{11,19},{19,27},{12,... | collective-permute-start | bytes 3145736 | tf_op jit(solution)/shard_map/ppermute | solution.py:631
  192.9 36.9 %collective-permute-start.26 = (bf16[512,1024]{1,0:T(8,128)(2,1)}, bf16[512,1024]{1,0:T(8,128)(2,1)}, u32[]{:S(2)}, u32[]{:S(2)}) collective-permute-start(bf16[512,1024]{1,0:T(8,128)(2,1)} %collective-permute-done.17.refs_1_), channel_id=1, source_target_pairs={{8,0},{16,8},{9,1},{17,9},{10,2},{18,10},{11,3},{19,11},{12,4},{20... | collective-permute-start | bytes 3145736 | tf_op jit(solution)/shard_map/ppermute | solution.py:632
  194.2 14.1 %collective-permute-start.21 = (bf16[128,2048]{1,0:T(8,128)(2,1)S(1)}, bf16[128,2048]{1,0:T(8,128)(2,1)S(1)}, u32[]{:S(2)}, u32[]{:S(2)}) collective-permute-start(bf16[128,2048]{1,0:T(8,128)(2,1)S(1)} %copy-done.48), channel_id=1, source_target_pairs={{0,2},{2,0},{1,3},{3,1},{4,6},{6,4},{5,7},{7,5},{8,10},{10,8},{9,1... | collective-permute-start | bytes 1572872 | tf_op jit(solution)/shard_map/ppermute | solution.py:611
  217.4 26.0 %collective-permute-start.27 = (bf16[512,1024]{1,0:T(8,128)(2,1)S(1)}, bf16[512,1024]{1,0:T(8,128)(2,1)S(1)}, u32[]{:S(2)}, u32[]{:S(2)}) collective-permute-start(bf16[512,1024]{1,0:T(8,128)(2,1)S(1)} %maximum_maximum_fusion), channel_id=1, source_target_pairs={{0,4},{4,0},{1,5},{5,1},{2,6},{6,2},{3,7},{7,3},{8,12},{12,8},{9,1... | collective-permute-start | bytes 3145736 | tf_op jit(solution)/shard_map/ppermute | solution.py:720
  223.7 14.2 %collective-permute-start.24 = (bf16[128,2048]{1,0:T(8,128)(2,1)S(1)}, bf16[128,2048]{1,0:T(8,128)(2,1)S(1)}, u32[]{:S(2)}, u32[]{:S(2)}) collective-permute-start(bf16[128,2048]{1,0:T(8,128)(2,1)S(1)} %add_convert_fusion.2), channel_id=1, source_target_pairs={{0,2},{2,0},{1,3},{3,1},{4,6},{6,4},{5,7},{7,5},{8,10},{10,8},{9,1... | collective-permute-start | bytes 1572872 | tf_op jit(solution)/shard_map/ppermute | solution.py:621
  228.1 67.3 %collective-permute-start.40 = (bf16[512,1024]{1,0:T(8,128)(2,1)}, bf16[512,1024]{1,0:T(8,128)(2,1)}, u32[]{:S(2)}, u32[]{:S(2)}) collective-permute-start(bf16[512,1024]{1,0:T(8,128)(2,1)} %collective-permute-done.25.refs_0_), channel_id=1, source_target_pairs={{16,24},{17,25},{18,26},{19,27},{20,28},{21,29},{22,30},{23,31}} | collective-permute-start | bytes 3145736 | tf_op jit(solution)/shard_map/ppermute | solution.py:631
  229.8 69.6 %collective-permute-start.41 = (bf16[512,1024]{1,0:T(8,128)(2,1)}, bf16[512,1024]{1,0:T(8,128)(2,1)}, u32[]{:S(2)}, u32[]{:S(2)}) collective-permute-start(bf16[512,1024]{1,0:T(8,128)(2,1)} %collective-permute-done.26.refs_1_), channel_id=1, source_target_pairs={{8,0},{9,1},{10,2},{11,3},{12,4},{13,5},{14,6},{15,7}} | collective-permute-start | bytes 3145736 | tf_op jit(solution)/shard_map/ppermute | solution.py:632
  250.2 14.2 %collective-permute-start.30 = (bf16[128,2048]{1,0:T(8,128)(2,1)S(1)}, bf16[128,2048]{1,0:T(8,128)(2,1)S(1)}, u32[]{:S(2)}, u32[]{:S(2)}) collective-permute-start(bf16[128,2048]{1,0:T(8,128)(2,1)S(1)} %copy-done.50), channel_id=1, source_target_pairs={{0,2},{2,0},{1,3},{3,1},{4,6},{6,4},{5,7},{7,5},{8,10},{10,8},{9,1... | collective-permute-start | bytes 1572872 | tf_op jit(solution)/shard_map/ppermute | solution.py:611
  274.3 37.4 %collective-permute-start.37 = (bf16[512,1024]{1,0:T(8,128)(2,1)}, bf16[512,1024]{1,0:T(8,128)(2,1)S(1)}, u32[]{:S(2)}, u32[]{:S(2)}) collective-permute-start(bf16[512,1024]{1,0:T(8,128)(2,1)} %maximum_maximum_fusion.1), channel_id=1, source_target_pairs={{0,4},{4,0},{1,5},{5,1},{2,6},{6,2},{3,7},{7,3},{8,12},{12,8},{9,1... | collective-permute-start | bytes 3145736 | tf_op jit(solution)/shard_map/ppermute | solution.py:720
  276.0 14.1 %collective-permute-start.33 = (bf16[128,2048]{1,0:T(8,128)(2,1)S(1)}, bf16[128,2048]{1,0:T(8,128)(2,1)S(1)}, u32[]{:S(2)}, u32[]{:S(2)}) collective-permute-start(bf16[128,2048]{1,0:T(8,128)(2,1)S(1)} %add_convert_fusion.1), channel_id=1, source_target_pairs={{0,2},{2,0},{1,3},{3,1},{4,6},{6,4},{5,7},{7,5},{8,10},{10,8},{9,1... | collective-permute-start | bytes 1572872 | tf_op jit(solution)/shard_map/ppermute | solution.py:621
  277.8 33.9 %collective-permute-start.38 = (bf16[1,2,512,256]{3,2,1,0:T(8,128)(2,1)}, bf16[1,2,512,256]{3,2,1,0:T(8,128)(2,1)S(1)}, u32[]{:S(2)}, u32[]{:S(2)}) collective-permute-start(bf16[1,2,512,256]{3,2,1,0:T(8,128)(2,1)} %pad_maximum_fusion.14), channel_id=1, source_target_pairs={{0,4},{4,0},{1,5},{5,1},{2,6},{6,2},{3,7},{7,3},{8,12},{12,8},{9,1... | collective-permute-start | bytes 1572872 | tf_op jit(solution)/shard_map/ppermute | solution.py:955
  295.4 26.2 %collective-permute-start.36 = (bf16[128,2048]{1,0:T(8,128)(2,1)}, bf16[128,2048]{1,0:T(8,128)(2,1)}, u32[]{:S(2)}, u32[]{:S(2)}) collective-permute-start(bf16[128,2048]{1,0:T(8,128)(2,1)} %get-tuple-element.40.refs_6_), channel_id=1, source_target_pairs={{0,1},{1,0},{2,3},{3,2},{4,5},{5,4},{6,7},{7,6},{8,9},{9,8},{10,11... | collective-permute-start | bytes 1572872 | tf_op jit(solution)/shard_map/ppermute | solution.py:610
  295.5 26.0 %collective-permute-start.34 = (bf16[128,2048]{1,0:T(8,128)(2,1)}, bf16[128,2048]{1,0:T(8,128)(2,1)}, u32[]{:S(2)}, u32[]{:S(2)}) collective-permute-start(bf16[128,2048]{1,0:T(8,128)(2,1)} %get-tuple-element.40.refs_6_), channel_id=1, source_target_pairs={{0,2},{2,0},{1,3},{3,1},{4,6},{6,4},{5,7},{7,5},{8,10},{10,8},{9,1... | collective-permute-start | bytes 1572872 | tf_op jit(solution)/shard_map/ppermute | solution.py:611
  299.3 44.1 %collective-permute-start.42 = (bf16[2,2,512,256]{3,2,1,0:T(8,128)(2,1)}, bf16[2,2,512,256]{3,2,1,0:T(8,128)(2,1)}, u32[]{:S(2)}, u32[]{:S(2)}) collective-permute-start(bf16[2,2,512,256]{3,2,1,0:T(8,128)(2,1)} %pad_maximum_fusion.5), channel_id=1, source_target_pairs={{0,4},{4,0},{1,5},{5,1},{2,6},{6,2},{3,7},{7,3},{8,12},{12,8},{9,1... | collective-permute-start | bytes 3145736 | tf_op jit(solution)/shard_map/ppermute | solution.py:957
  332.0 23.0 %all-to-all-start.2 = ((bf16[4,512,128]{2,1,0:T(8,128)(2,1)}), bf16[4,512,128]{2,1,0:T(8,128)(2,1)}, u32[]{:S(2)}, u32[]{:S(2)}) async-start(bf16[4,512,128]{2,1,0:T(8,128)(2,1)} %attn_out_grad.3.refs_6_), calls=%async_computation.2 | async-start | bytes 1048576 | tf_op jit(solution)/shard_map/all_to_all | solution.py:782
  337.1 215.1 %reduce-scatter.4.cloned.1.call-start = ((), (), s32[]{:S(2)}) async-start(), calls=%async_computation.8 | async-start | bytes 1310720 | tf_op jit(solution)/shard_map/reduce_scatter | solution.py:1074
  340.5 32.9 %collective-permute-start.43 = (bf16[512,1024]{1,0:T(8,128)(2,1)}, bf16[512,1024]{1,0:T(8,128)(2,1)}, u32[]{:S(2)}, u32[]{:S(2)}) collective-permute-start(bf16[512,1024]{1,0:T(8,128)(2,1)} %maximum_maximum_fusion.2), channel_id=1, source_target_pairs={{0,4},{4,0},{1,5},{5,1},{2,6},{6,2},{3,7},{7,3},{8,12},{12,8},{9,1... | collective-permute-start | bytes 3145736 | tf_op jit(solution)/shard_map/ppermute | solution.py:720
  378.6 177.6 %reduce-scatter.8.cloned.1.call-start = ((), (), s32[]{:S(2)}) async-start(), calls=%async_computation.10 | async-start | bytes 2621440 | tf_op jit(solution)/shard_map/reduce_scatter | solution.py:1047
  379.3 202.5 %reduce-scatter.6.cloned.1.call-start = ((), (), s32[]{:S(2)}) async-start(), calls=%async_computation.9 | async-start | bytes 5242880 | tf_op jit(solution)/shard_map/reduce_scatter | solution.py:1049
  384.0 34.0 %collective-permute-start.46 = (f32[4,2,512]{2,0,1:T(4,128)S(1)}, f32[4,2,512]{2,0,1:T(4,128)S(1)}, u32[]{:S(2)}, u32[]{:S(2)}) collective-permute-start(f32[4,2,512]{2,0,1:T(4,128)S(1)} %broadcast_select_fusion.1), channel_id=1, source_target_pairs={{0,8},{8,0},{16,24},{24,16},{1,9},{9,1},{17,25},{25,17},{2,10},{10... | collective-permute-start | bytes 49160 | tf_op jit(solution)/shard_map/ppermute | solution.py:655
  394.5 62.2 %collective-permute-start.56 = (bf16[2048,1024]{1,0:T(8,128)(2,1)}, bf16[2048,1024]{1,0:T(8,128)(2,1)}, u32[]{:S(2)}, u32[]{:S(2)}) collective-permute-start(bf16[2048,1024]{1,0:T(8,128)(2,1)} %pad_maximum_fusion.1), channel_id=1, source_target_pairs={{0,1},{1,0},{2,3},{3,2},{4,5},{5,4},{6,7},{7,6},{8,9},{9,8},{10,11... | collective-permute-start | bytes 12582920 | tf_op jit(solution)/shard_map/ppermute | solution.py:1080
  395.6 21.1 %collective-permute-start.44 = (bf16[2048,128]{1,0:T(8,128)(2,1)S(1)}, bf16[2048,128]{1,0:T(8,128)(2,1)S(1)}, u32[]{:S(2)}, u32[]{:S(2)}) collective-permute-start(bf16[2048,128]{1,0:T(8,128)(2,1)S(1)} %copy-done.27), channel_id=1, source_target_pairs={{0,4},{4,0},{1,5},{5,1},{2,6},{6,2},{3,7},{7,3},{8,12},{12,8},{9,1... | collective-permute-start | bytes 1572872 | tf_op jit(solution)/shard_map/ppermute | solution.py:1022
  397.6 20.3 %collective-permute-start.48 = (f32[2048]{0:T(1024)S(1)}, f32[2048]{0:T(1024)S(1)}, u32[]{:S(2)}, u32[]{:S(2)}) collective-permute-start(f32[2048]{0:T(1024)S(1)} %multiply_reduce_fusion), channel_id=1, source_target_pairs={{0,4},{4,0},{1,5},{5,1},{2,6},{6,2},{3,7},{7,3},{8,12},{12,8},{9,1... | collective-permute-start | bytes 24584 | tf_op jit(solution)/shard_map/ppermute | solution.py:1024
  420.4 14.2 %collective-permute-start.45 = (bf16[2048,128]{1,0:T(8,128)(2,1)}, bf16[2048,128]{1,0:T(8,128)(2,1)S(1)}, u32[]{:S(2)}, u32[]{:S(2)}) collective-permute-start(bf16[2048,128]{1,0:T(8,128)(2,1)} %get-tuple-element.47), channel_id=1, source_target_pairs={{0,4},{4,0},{1,5},{5,1},{2,6},{6,2},{3,7},{7,3},{8,12},{12,8},{9,1... | collective-permute-start | bytes 1572872 | tf_op jit(solution)/shard_map/ppermute | solution.py:1022
  443.1 78.8 %all-to-all-start.3 = ((bf16[4,512,384]{2,1,0:T(8,128)(2,1)}), bf16[4,512,384]{2,1,0:T(8,128)(2,1)}, u32[]{:S(2)}, u32[]{:S(2)}) async-start(bf16[4,512,384]{2,1,0:T(8,128)(2,1)} %bitcast.288), calls=%async_computation.3 | async-start | bytes 3145728 | tf_op jit(solution)/shard_map/all_to_all | solution.py:829
  462.1 73.6 %collective-permute-start.57 = (bf16[4,256,384]{1,2,0:T(8,128)(2,1)S(1)}, bf16[4,256,384]{1,2,0:T(8,128)(2,1)S(1)}, u32[]{:S(2)}, u32[]{:S(2)}) collective-permute-start(bf16[4,256,384]{1,2,0:T(8,128)(2,1)S(1)} %bitcast.302), channel_id=1, source_target_pairs={{0,4},{4,0},{1,5},{5,1},{2,6},{6,2},{3,7},{7,3},{8,12},{12,8},{9,1... | collective-permute-start | bytes 2359304 | tf_op jit(solution)/shard_map/ppermute | solution.py:700
  536.8 34.5 %all-to-all-start.4 = ((bf16[4,256,384]{1,2,0:T(8,128)(2,1)}), bf16[4,256,384]{1,2,0:T(8,128)(2,1)S(1)}, u32[]{:S(2)}, u32[]{:S(2)}) async-start(bf16[4,256,384]{1,2,0:T(8,128)(2,1)} %fusion.14), calls=%async_computation.4 | async-start | bytes 1572864 | tf_op jit(solution)/shard_map/all_to_all | solution.py:1095
  541.1 20.4 %collective-permute-start.54 = (bf16[128,2048]{1,0:T(8,128)(2,1)}, bf16[128,2048]{1,0:T(8,128)(2,1)}, u32[]{:S(2)}, u32[]{:S(2)}) collective-permute-start(bf16[128,2048]{1,0:T(8,128)(2,1)} %slice.214), channel_id=1, source_target_pairs={{0,1},{1,0},{2,3},{3,2},{4,5},{5,4},{6,7},{7,6},{8,9},{9,8},{10,11... | collective-permute-start | bytes 1572872 | tf_op jit(solution)/shard_map/ppermute | solution.py:619
  559.1 14.6 %collective-permute-start.53 = (bf16[128,2048]{1,0:T(8,128)(2,1)}, bf16[128,2048]{1,0:T(8,128)(2,1)}, u32[]{:S(2)}, u32[]{:S(2)}) collective-permute-start(bf16[128,2048]{1,0:T(8,128)(2,1)} %slice.212), channel_id=1, source_target_pairs={{0,1},{1,0},{2,3},{3,2},{4,5},{5,4},{6,7},{7,6},{8,9},{9,8},{10,11... | collective-permute-start | bytes 1572872 | tf_op jit(solution)/shard_map/ppermute | solution.py:622
  559.1 14.0 %collective-permute-start.62 = (f32[8,2048]{1,0:T(8,128)S(1)}, f32[8,2048]{1,0:T(8,128)S(1)}, u32[]{:S(2)}, u32[]{:S(2)}) collective-permute-start(f32[8,2048]{1,0:T(8,128)S(1)} %add.362), channel_id=1, source_target_pairs={{0,16},{8,24},{16,0},{24,8},{1,17},{9,25},{17,1},{25,9},{2,18},{10... | collective-permute-start | bytes 196616 | tf_op jit(solution)/shard_map/ppermute | solution.py:655
  562.7 14.1 %collective-permute-start.55 = (bf16[128,2048]{1,0:T(8,128)(2,1)S(1)}, bf16[128,2048]{1,0:T(8,128)(2,1)S(1)}, u32[]{:S(2)}, u32[]{:S(2)}) collective-permute-start(bf16[128,2048]{1,0:T(8,128)(2,1)S(1)} %add_convert_fusion), channel_id=1, source_target_pairs={{0,2},{2,0},{1,3},{3,1},{4,6},{6,4},{5,7},{7,5},{8,10},{10,8},{9,1... | collective-permute-start | bytes 1572872 | tf_op jit(solution)/shard_map/ppermute | solution.py:621
  (105 other events, 714.3 us)
Sparse Core Ops, SparseCore 0:
  378.7 27.9 reduce-scatter.3
  409.1 43.5 reduce-scatter.7
  454.9 98.6 reduce-scatter.5

commit v3 on v2

--- a/solution.py
+++ b/solution.py
@@ -11,7 +11,6 @@
 
 HEAD_DIM = 128
 LOG2E = math.log2(math.e)
-VMEM_BYTES = 56 * 1024 * 1024
 
 norm_eps = 1e-05
 f32 = jnp.float32
@@ -107,8 +106,8 @@
             jax.ShapeDtypeStruct((1, rows), f32),
         ],
         scratch_shapes=scratch,
-        compiler_params=pltpu.CompilerParams(vmem_limit_bytes=VMEM_BYTES),
-        cost_estimate=cost(8),
+        compiler_params=params(48),
+        cost_estimate=cost(19),
         name="attend",
     )(*operands)
 
@@ -222,8 +221,8 @@
             pltpu.VMEM((keys, HEAD_DIM), f32),
             pltpu.VMEM((keys, HEAD_DIM), f32),
         ],
-        compiler_params=pltpu.CompilerParams(vmem_limit_bytes=VMEM_BYTES),
-        cost_estimate=cost(8),
+        compiler_params=params(48),
+        cost_estimate=cost(0.5),
         name="attend_grad",
     )(queries, d_out, lse, delta, tok_q, start_q, dq_in, *key_group, *earlier)
 
@@ -258,7 +257,7 @@
         ],
         out_specs=[head, head],
         out_shape=[jax.ShapeDtypeStruct((heads, rows, HEAD_DIM), bf16)] * 2,
-        cost_estimate=cost(3),
+        cost_estimate=cost(4.7),
         name="pack_heads",
     )(raw0, raw1, inv, cos_tab, sin_tab, gains)
 
@@ -290,7 +289,7 @@
     out_ref[:, 2 * HEAD_DIM :] = dv_ref[...].astype(bf16)
 
 
-def raw_grad(d_query, d_key, d_value, queries, keys, coef, cos_tab, sin_tab, gains):
+def raw_grad(d_query, d_key, d_value, queries, keys, coef, cos_tab, sin_tab, gains, earlier):
     rows = queries.shape[0]
     block = min(512, rows)
 
@@ -307,23 +306,23 @@
             wide(HEAD_DIM),
             wide(HEAD_DIM),
             whole,
+            pl.BlockSpec(memory_space=pl.ANY),
         ],
         out_specs=[wide(3 * HEAD_DIM), whole],
         out_shape=[
             jax.ShapeDtypeStruct((rows, 3 * HEAD_DIM), bf16),
             jax.ShapeDtypeStruct((2, HEAD_DIM), f32),
         ],
-        cost_estimate=cost(3),
+        cost_estimate=cost(6),
         name="raw_grad",
-    )(d_query, d_key, d_value, queries, keys, coef, cos_tab, sin_tab, gains)
-
-
-def weight_grad_kernel(pieces, experts, out_block, at_ref, *refs):
-    wide0, wide1, wide_far = refs[:3]
-    narrow = refs[3 : 3 + pieces]
+    )(d_query, d_key, d_value, queries, keys, coef, cos_tab, sin_tab, gains, earlier)
+
+
+def weight_grad_kernel(experts, out_block, at_ref, *refs):
+    wide, far, narrow, compact = refs[:2], refs[2:4], refs[4:6], refs[6:8]
     out_ref, wide_t, tall = refs[-3:]
-    half = wide0.shape[0]
-    blocks = wide_far.shape[1] // out_block
+    half = wide[0].shape[0]
+    blocks = far[0].shape[1] // out_block
 
     @pl.when(pl.program_id(0) == 0)
     def _():
@@ -331,66 +330,51 @@
             rows = slice(z * out_block, (z + 1) * out_block)
             cols = (2 * z + at_ref[0]) * out_block
             cols = pl.ds(pl.multiple_of(cols, out_block), out_block)
-            for i, piece in enumerate((wide0, wide1)):
-                wide_t[rows, i * half : (i + 1) * half] = piece[:, cols].T
-            wide_t[rows, 2 * half :] = wide_far[:, rows].T
-
-    at = 0
-    for i, piece in enumerate(narrow):
-        if experts and i == pieces - 1:
-            routes = refs[3 + pieces][...]
-            e = lax.rem(pl.program_id(0), experts)
-            block = jnp.zeros(piece.shape[2:], f32)
-            for slot in range(piece.shape[1]):
-                block = jnp.where(routes[:, slot : slot + 1] == e, piece[0, slot].astype(f32), block)
-            block = block.astype(bf16)
-        else:
-            block = piece[...].reshape(piece.shape[-2:])
-        tall[at : at + block.shape[0], :] = block
-        at += block.shape[0]
-    out = jnp.dot(wide_t[...], tall[...], preferred_element_type=f32)
-    out_ref[...] = out.astype(bf16).reshape(out_ref.shape)
-
-
-def weight_grad(wide_h, wide_far, narrow, out_block, at, routes=None, experts=0, earlier=()):
+            for i in range(2):
+                wide_t[rows, i * half : (i + 1) * half] = wide[i][:, cols].T
+                wide_t[rows, (2 + i) * half : (3 + i) * half] = far[i][:, rows].T
+
+    e = lax.rem(pl.program_id(0), experts) if experts else None
+    for i in range(2):
+        tall[i * half : (i + 1) * half, :] = narrow[i][0]
+        there = slice((2 + i) * half, (3 + i) * half)
+        if not experts:
+            tall[there, :] = compact[i][0]
+            continue
+        routes = refs[8][i * half : (i + 1) * half, :]
+        block = jnp.zeros((half, tall.shape[1]), f32)
+        for slot in range(routes.shape[1]):
+            block = jnp.where(
+                routes[:, slot : slot + 1] == e, compact[i][0, slot].astype(f32), block
+            )
+        tall[there, :] = block.astype(bf16)
+    out_ref[0] = jnp.dot(wide_t[...], tall[...], preferred_element_type=f32).astype(bf16)
+
+
+def weight_grad(wide_h, far_h, narrow, far_narrow, out_block, at, routes=None, experts=0, earlier=()):
     half, width = wide_h[0].shape
-    out_width = wide_far.shape[1]
-    specs = []
-    operands = []
-    for piece in narrow:
-        if isinstance(piece, tuple):
-            array, row = piece
-            cols = 256
-            count = array.shape[1] // cols
-            specs.append(pl.BlockSpec((half, cols), lambda j, x, row=row: (row, j)))
-            operands.append(array)
-        elif piece.ndim == 4:
-            kinds, slots, rows, cols = piece.shape
-            count = kinds * experts
-            specs.append(
-                pl.BlockSpec((1, slots, rows, cols), lambda j, x: (j // experts, 0, 0, 0))
-            )
-            operands.append(piece)
-        else:
-            count, rows, cols = piece.shape
-            specs.append(pl.BlockSpec((1, rows, cols), lambda j, x: (j, 0, 0)))
-            operands.append(piece)
+    out_width = far_h[0].shape[1]
+    count, _, cols = narrow[0][0].shape
+
+    def part(at):
+        return pl.BlockSpec((1, half, cols), lambda j, x: (j, at, 0))
+
+    specs = [part(at) for _, at in narrow]
     if experts:
+        slots = routes.shape[1]
+        specs += [pl.BlockSpec((1, slots, half, cols), lambda j, x: (j // experts, 0, 0, 0))] * 2
         specs.append(pl.BlockSpec(routes.shape, lambda j, x: (0, 0)))
-        operands.append(routes)
-
-    def kernel(x_ref, *refs):
-        used = 3 + len(operands)
-        weight_grad_kernel(len(narrow), experts, out_block, x_ref, *refs[:used], *refs[-3:])
-
-    return pl.pallas_call(
-        kernel,
+        earlier = (routes, *earlier)
+    else:
+        specs += [part(at) for _, at in far_narrow]
+    return pl.pallas_call(
+        functools.partial(weight_grad_kernel, experts, out_block),
         grid_spec=pltpu.PrefetchScalarGridSpec(
             num_scalar_prefetch=1,
             grid=(count,),
-            in_specs=[pl.BlockSpec(w.shape, lambda j, x: (0, 0)) for w in (*wide_h, wide_far)]
+            in_specs=[pl.BlockSpec(w.shape, lambda j, x: (0, 0)) for w in (*wide_h, *far_h)]
             + specs
-            + [pl.BlockSpec(memory_space=pl.ANY)] * len(earlier),
+            + waits(earlier[1:] if experts else earlier),
             out_specs=pl.BlockSpec((1, out_width, cols), lambda j, x: (j, 0, 0)),
             scratch_shapes=[
                 pltpu.VMEM((out_width, 4 * half), bf16),
@@ -398,18 +382,113 @@
             ],
         ),
         out_shape=jax.ShapeDtypeStruct((count, out_width, cols), bf16),
-        compiler_params=pltpu.CompilerParams(vmem_limit_bytes=VMEM_BYTES),
+        compiler_params=params(32),
         cost_estimate=cost(0.1),
         name="weight_grad",
-    )(at.reshape(1), *wide_h, wide_far, *operands, *earlier)
+    )(
+        at.reshape(1),
+        *wide_h,
+        *far_h,
+        *[a for a, _ in narrow],
+        *[a for a, _ in far_narrow],
+        *earlier,
+    )
 
 
 def waits(earlier):
     return [pl.BlockSpec(memory_space=pl.ANY)] * len(earlier)
 
 
-def params():
-    return pltpu.CompilerParams(vmem_limit_bytes=VMEM_BYTES)
+def params(mib=16):
+    return pltpu.CompilerParams(vmem_limit_bytes=mib * 1024 * 1024)
+
+
+def project_kernel(x_ref, w_ref, *refs):
+    raw_ref, sq_ref, v_ref = refs[-3:]
+    kind, j = pl.program_id(0), pl.program_id(1)
+    raw = jnp.dot(x_ref[...], w_ref[0], preferred_element_type=f32)
+
+    @pl.when(kind < 2)
+    def _():
+        raw_ref[0] = raw
+        ones = jnp.ones((8, raw.shape[1]), f32)
+        square = lax.dot_general(
+            ones, raw * raw, DOT_NT, precision=lax.Precision.HIGHEST, preferred_element_type=f32
+        )
+        sq_ref[0] = jnp.where(j == 0, square, sq_ref[0] + square)
+
+    @pl.when(kind == 2)
+    def _():
+        for h in range(v_ref.shape[0]):
+            v_ref[h] = raw[:, h * HEAD_DIM : (h + 1) * HEAD_DIM].astype(bf16)
+
+
+def project(x, weights, earlier=()):
+    count, width = x.shape
+    cols = weights.shape[2]
+    block = cols // 2
+    heads = block // HEAD_DIM
+    row = pl.BlockSpec((count, width), lambda k, j: (0, 0))
+
+    def held(k, j):
+        return jnp.minimum(k, 1), jnp.where(k == 2, 1, j)
+
+    return pl.pallas_call(
+        project_kernel,
+        grid=(3, 2),
+        in_specs=[row, pl.BlockSpec((1, width, block), lambda k, j: (k, 0, j))]
+        + waits(earlier),
+        out_specs=[
+            pl.BlockSpec((1, count, block), lambda k, j: (held(k, j)[0], 0, held(k, j)[1])),
+            pl.BlockSpec((1, 8, count), lambda k, j: (jnp.minimum(k, 1), 0, 0)),
+            pl.BlockSpec((heads, count, HEAD_DIM), lambda k, j: (jnp.where(k == 2, j, 0), 0, 0)),
+        ],
+        out_shape=[
+            jax.ShapeDtypeStruct((2, count, cols), f32),
+            jax.ShapeDtypeStruct((2, 8, count), f32),
+            jax.ShapeDtypeStruct((2 * heads, count, HEAD_DIM), bf16),
+        ],
+        compiler_params=params(32),
+        cost_estimate=cost(0.1),
+        name="project",
+    )(x, weights, *earlier)
+
+
+def attn_out_kernel(x_ref, w_ref, *refs):
+    own_ref, other_ref, rows = refs[-3:]
+    count = own_ref.shape[0]
+
+    @pl.when(pl.program_id(0) == 0)
+    def _():
+        for h in range(x_ref.shape[0]):
+            rows[:, h * HEAD_DIM : (h + 1) * HEAD_DIM] = x_ref[h]
+
+    y = lax.dot_general(rows[...], w_ref[...], DOT_NT, preferred_element_type=f32).astype(bf16)
+    own_ref[...] = y[:count]
+    other_ref[...] = y[count:]
+
+
+def attn_out_half(parts, half, weights, earlier=()):
+    heads, count, _ = parts.shape
+    count //= 2
+    width, cols = weights.shape
+    block = width // 4
+    out = pl.BlockSpec((count // 2, block), lambda i: (0, i))
+    return pl.pallas_call(
+        attn_out_kernel,
+        grid=(4,),
+        in_specs=[
+            pl.BlockSpec((heads, count, HEAD_DIM), lambda i: (0, half, 0)),
+            pl.BlockSpec((block, cols), lambda i: (i, 0)),
+        ]
+        + waits(earlier),
+        out_specs=[out, out],
+        out_shape=[jax.ShapeDtypeStruct((count // 2, width), bf16)] * 2,
+        scratch_shapes=[pltpu.VMEM((count, cols), bf16)],
+        compiler_params=params(32),
+        cost_estimate=cost(0.1),
+        name="attn_out",
+    )(parts, weights, *earlier)
 
 
 def attn_out_grad_kernel(a_ref, w_ref, *refs):
@@ -435,14 +514,15 @@
         out_specs=pl.BlockSpec((heads // 2, count, HEAD_DIM), lambda j: (j, half, 0)),
         out_shape=jax.ShapeDtypeStruct((heads, 2 * count, HEAD_DIM), bf16),
         input_output_aliases={2: 0} if into else {},
-        compiler_params=params(),
-        cost_estimate=cost(1),
+        compiler_params=params(16),
+        cost_estimate=cost(0.1),
         name="attn_out_grad",
     )(grads, weights, *into, *earlier)
 
 
 def project_grad_kernel(x_ref, w_ref, n_ref, *refs):
-    out_ref, sum_ref, rows = refs[-3:]
+    own_ref, other_ref, sum_ref, rows = refs[-4:]
+    count = own_ref.shape[0]
     heads = x_ref.shape[0]
     cols = heads * HEAD_DIM
 
@@ -459,7 +539,8 @@
             rows[:, k * cols : (k + 1) * cols], w_ref[k], DOT_NT, preferred_element_type=f32
         )
         y = term if y is None else y + term
-    out_ref[...] = y.astype(bf16)
+    own_ref[...] = y[:count].astype(bf16)
+    other_ref[...] = y[count:].astype(bf16)
     sum_ref[...] = jnp.sum(y * n_ref[...].astype(f32), axis=0, keepdims=True)
 
 
@@ -469,6 +550,7 @@
     width = weights.shape[1]
     block = width // 4
     out = pl.BlockSpec((count, block), lambda i: (0, i))
+    part = pl.BlockSpec((count // 2, block), lambda i: (0, i))
     return pl.pallas_call(
         project_grad_kernel,
         grid=(4,),
@@ -478,16 +560,216 @@
             out,
         ]
         + waits(earlier),
-        out_specs=[out, pl.BlockSpec((1, block), lambda i: (0, i))],
+        out_specs=[part, part, pl.BlockSpec((1, block), lambda i: (0, i))],
         out_shape=[
-            jax.ShapeDtypeStruct((count, width), bf16),
+            jax.ShapeDtypeStruct((count // 2, width), bf16),
+            jax.ShapeDtypeStruct((count // 2, width), bf16),
             jax.ShapeDtypeStruct((1, width), f32),
         ],
         scratch_shapes=[pltpu.VMEM((count, heads * cols), bf16)],
+        compiler_params=params(24),
+        cost_estimate=cost(6),
+        name="project_grad",
+    )(parts, weights, normed, *earlier)
+
+
+def qkv_grad_kernel(wide_ref, grad_ref, grad_other_ref, out_ref, out_other_ref, tall, wide_t):
+    rows, cols = grad_ref.shape
+
+    @pl.when(pl.program_id(0) == 0)
+    def _():
+        tall[:, :cols] = grad_ref[...]
+        block = rows // 16
+        for i in range(16):
+            tall[i * block : (i + 1) * block, cols:] = grad_other_ref[
+                (i ^ 1) * block : ((i ^ 1) + 1) * block, :
+            ]
+
+    wide_t[...] = wide_ref[...].T
+    out = jnp.dot(wide_t[...], tall[...], preferred_element_type=f32).astype(bf16)
+    out_ref[...] = out[:, :cols]
+    out_other_ref[...] = out[:, cols:]
+
+
+def qkv_grad(wide, grad, grad_other, z_count):
+    assert z_count == 4
+    rows, width = wide.shape
+    cols = grad.shape[1]
+    block = min(256, width)
+    whole = pl.BlockSpec(grad.shape, lambda i: (0, 0))
+    out = pl.BlockSpec((block, cols), lambda i: (i, 0))
+    return pl.pallas_call(
+        qkv_grad_kernel,
+        grid=(width // block,),
+        in_specs=[pl.BlockSpec((rows, block), lambda i: (0, i)), whole, whole],
+        out_specs=[out, out],
+        scratch_shapes=[pltpu.VMEM((rows, 2 * cols), bf16), pltpu.VMEM((block, rows), bf16)],
+        out_shape=[jax.ShapeDtypeStruct((width, cols), bf16)] * 2,
+        compiler_params=params(40),
+        cost_estimate=cost(10),
+        name="qkv_grad",
+    )(wide, grad, grad_other)
+
+
+def arrange(near, z_pos, earlier=()):
+    rows, cols = near[0].shape
+    z_count = len(near)
+
+    def kernel(z_ref, *refs):
+        for i in range(z_count):
+
+            @pl.when(pl.program_id(0) == i)
+            def _():
+                refs[-1][...] = refs[i][...]
+
+    return pl.pallas_call(
+        kernel,
+        grid_spec=pltpu.PrefetchScalarGridSpec(
+            num_scalar_prefetch=1,
+            grid=(z_count,),
+            in_specs=[pl.BlockSpec((rows, cols), lambda i, z: (0, 0))] * z_count + waits(earlier),
+            out_specs=pl.BlockSpec(
+                (rows, cols), lambda i, z: (lax.rem(z[0] - i + z_count, z_count), 0)
+            ),
+        ),
+        out_shape=jax.ShapeDtypeStruct((z_count * rows, cols), near[0].dtype),
+        compiler_params=params(),
+        cost_estimate=cost(0.1),
+        name="arrange",
+    )(z_pos.reshape(1), *near, *earlier)
+
+
+def own_grad_kernel(w0_ref, w1_ref, n0_ref, n1_ref, *refs):
+    out_ref, wide_t = refs[-2:]
+    half = w0_ref.shape[0]
+
+    @pl.when(pl.program_id(0) == 0)
+    def _():
+        wide_t[:, :half] = w0_ref[...].T
+        wide_t[:, half:] = w1_ref[...].T
+
+    tall = jnp.concatenate(
+        [n0_ref[...].reshape(n0_ref.shape[-2:]), n1_ref[...].reshape(n1_ref.shape[-2:])]
+    )
+    out_ref[0] = jnp.dot(wide_t[...], tall, preferred_element_type=f32).astype(bf16)
+
+
+def own_grad(wide_h, narrow_h, earlier=()):
+    half, width = wide_h[0].shape
+    count, rows, cols = narrow_h[0].shape
+    narrow = [
+        pl.BlockSpec((1, half, cols), lambda j, at=i * (rows // half - 1): (j, at, 0))
+        for i in range(2)
+    ]
+    return pl.pallas_call(
+        own_grad_kernel,
+        grid=(count,),
+        in_specs=[pl.BlockSpec((half, width), lambda j: (0, 0))] * 2 + narrow + waits(earlier),
+        out_specs=pl.BlockSpec((1, width, cols), lambda j: (j, 0, 0)),
+        out_shape=jax.ShapeDtypeStruct((count, width, cols), bf16),
+        scratch_shapes=[pltpu.VMEM((width, 2 * half), bf16)],
+        compiler_params=params(24),
+        cost_estimate=cost(0.1),
+        name="own_grad",
+    )(*wide_h, *narrow_h, *earlier)
+
+
+def join_kernel(a_ref, b_ref, *refs):
+    n = a_ref.shape[0]
+    refs[-1][:n] = a_ref[...]
+    refs[-1][n:] = b_ref[...]
+
+
+def join_rows(a, b, earlier=()):
+    rows, width = a.shape
+    block = width // 2
+    part = pl.BlockSpec((rows, block), lambda j: (0, j))
+    return pl.pallas_call(
+        join_kernel,
+        grid=(2,),
+        in_specs=[part, part] + waits(earlier),
+        out_specs=pl.BlockSpec((2 * rows, block), lambda j: (0, j)),
+        out_shape=jax.ShapeDtypeStruct((2 * rows, width), a.dtype),
+        compiler_params=params(),
+        cost_estimate=cost(0.1),
+        name="join_rows",
+    )(a, b, *earlier)
+
+
+def pass_kernel(in_ref, *refs):
+    refs[-1][...] = in_ref[...]
+
+
+def pass_rows(a, earlier):
+    rows, width = a.shape
+    spec = pl.BlockSpec((rows, width // 2), lambda j: (0, j))
+    return pl.pallas_call(
+        pass_kernel,
+        grid=(2,),
+        in_specs=[spec] + waits(earlier),
+        out_specs=spec,
+        out_shape=jax.ShapeDtypeStruct(a.shape, a.dtype),
+        compiler_params=params(),
+        cost_estimate=cost(0.1),
+        name="pass_rows",
+    )(a, *earlier)
+
+
+def round_kernel(in_ref, *refs):
+    refs[-1][...] = in_ref[...].astype(bf16)
+
+
+def round_weights(a, earlier=()):
+    flat = a.reshape(-1, a.shape[-1])
+    rows, cols = flat.shape
+    block = min(rows, 1 << 20 >> (cols.bit_length() - 1))
+    spec = pl.BlockSpec((block, cols), lambda i: (i, 0))
+    out = pl.pallas_call(
+        round_kernel,
+        grid=(rows // block,),
+        in_specs=[spec] + waits(earlier),
+        out_specs=spec,
+        out_shape=jax.ShapeDtypeStruct(flat.shape, bf16),
+        compiler_params=params(),
+        cost_estimate=cost(9),
+        name="round_weights",
+    )(flat, *earlier)
+    return out.reshape(a.shape)
+
+
+def add_kernel(a_ref, b_ref, *refs):
+    refs[-1][...] = (a_ref[...].astype(f32) + b_ref[...].astype(f32)).astype(bf16)
+
+
+def add_rows(a, b, earlier=()):
+    spec = pl.BlockSpec((1, *a.shape[1:]), lambda i: (i, 0, 0))
+    return pl.pallas_call(
+        add_kernel,
+        grid=(a.shape[0],),
+        in_specs=[spec, spec] + waits(earlier),
+        out_specs=spec,
+        out_shape=jax.ShapeDtypeStruct(a.shape, bf16),
         compiler_params=params(),
         cost_estimate=cost(1),
-        name="project_grad",
-    )(parts, weights, normed, *earlier)
+        name="add_rows",
+    )(a, b, *earlier)
+
+
+def stack_kernel(a_ref, b_ref, gain_ref, second_ref, qk_ref, router_ref, out_ref):
+    out_ref[0:1, :] = (a_ref[...] + b_ref[...]) / gain_ref[0:1, :]
+    out_ref[1:2, :] = second_ref[...]
+    out_ref[2:4, :] = qk_ref[...]
+    out_ref[4:8, :] = router_ref[...]
+
+
+def stack_rows(*rows):
+    return pl.pallas_call(
+        stack_kernel,
+        out_shape=jax.ShapeDtypeStruct((8, rows[0].shape[1]), f32),
+        compiler_params=params(),
+        cost_estimate=cost(0.1),
+        name="stack_rows",
+    )(*rows)
 
 
 def row_sum(refs):
@@ -556,7 +838,7 @@
             jax.ShapeDtypeStruct((1, width) if o is None else (count, width), f32 if o is None else o)
             for o in outs
         ],
-        compiler_params=pltpu.CompilerParams(vmem_limit_bytes=VMEM_BYTES),
+        compiler_params=params(16),
         cost_estimate=cost(0.1),
         name=kernel.__name__,
     )(*terms, *rows, *gains, *earlier)
@@ -606,42 +888,21 @@
     return inv_rows * (grad_hat - hat_rows * jnp.mean(grad_hat * hat_rows, axis=-1, keepdims=True))
 
 
-def gather_halves(rows):
+def gather_halves(rows, beside=(), earlier=()):
+    far = lax.ppermute(rows, "y", SWAP)
     core = lax.ppermute(rows, "c", SWAP)
-    far = lax.ppermute(rows, "y", SWAP)
+    if beside:
+        far = pass_rows(far, beside)
     far_core = lax.ppermute(far, "c", SWAP)
-    return [jnp.concatenate([rows, core]), jnp.concatenate([far, far_core])]
-
-
-def scatter_halves(parts):
-    near, far = parts
-    n = near.shape[0] // 2
-    sent = far[:n].astype(f32) + lax.ppermute(far[n:], "c", SWAP).astype(f32)
+    return [jnp.concatenate([rows, core]), join_rows(far, far_core, earlier)]
+
+
+def scatter_halves(near, far):
+    sent = far[0].astype(f32) + lax.ppermute(far[1], "c", SWAP).astype(f32)
     sent = sent.astype(bf16)
     far_got = lax.ppermute(sent, "y", SWAP)
-    near_got = lax.ppermute(near[n:], "c", SWAP)
-    return (near, near_got, far_got), sent
-
-
-def gather_line(a, z_pos, z_count):
-    last = z_count - 1
-    up = down = a
-    ups, downs = [], []
-    for s in range(last):
-        up = lax.ppermute(up, "z", [(i, i + 1) for i in range(s, last)])
-        down = lax.ppermute(down, "z", [(i, i - 1) for i in range(1, z_count - s)])
-        ups.append(up)
-        downs.append(down)
-    near = [a] + [
-        jnp.where(z_pos >= s + 1, ups[s], downs[last - 1 - s]) for s in range(last)
-    ]
-    near = jnp.stack(near)
-    return ups, downs, jnp.concatenate(
-        [
-            lax.dynamic_index_in_dim(near, (z_pos - z + z_count) % z_count, 0, False)
-            for z in range(z_count)
-        ]
-    )
+    near_got = lax.ppermute(near[1], "c", SWAP)
+    return (near[0], near_got, far_got), sent
 
 
 def sum_near(a):
@@ -688,9 +949,6 @@
     wt_pos = y_pos * 2 + c_pos
 
     qkv_b = attn_qkv.astype(bf16)
-    out_b = attn_out.astype(bf16)
-    gu_b = gate_up.astype(bf16)
-    down_b = down.astype(bf16)
     router_b = router.astype(bf16)
 
     def scatter_x(a):
@@ -749,10 +1007,9 @@
     cos_tab = jnp.concatenate([cosine, cosine], axis=1)
     sin_tab = jnp.concatenate([-sine, sine], axis=1)
 
-    raw_h = [
-        jnp.einsum("td,kdc->ktc", n, qkv_b, preferred_element_type=f32) for n in normed_h
-    ]
-    squares = jnp.concatenate([jnp.sum(r[:2] * r[:2], axis=-1) for r in raw_h], axis=1)
+    raw0, square0, v0 = project(normed_h[0], qkv_b)
+    raw1, square1, v1 = project(normed_h[1], qkv_b, (v0,))
+    squares = jnp.concatenate([square0[:, 0], square1[:, 0]], axis=1)
     squares = sum_near(squares.reshape(2, 2, 2, local_rows)).reshape(2, tok_rows)
     inv_qk = lax.rsqrt(squares / model_width + norm_eps)
     inv_slots = jnp.where(
@@ -761,22 +1018,14 @@
     inv_line = sum_line(inv_slots, z_count)
     gain_qk = lax.dynamic_slice_in_dim(norm_gains[2:], wt_pos * head_cols, head_cols, 1)
 
-    normed_pick = pick_half(normed_h, c_pos)
-
-    def to_heads_apart(parts):
+    def to_heads_apart(parts, earlier=()):
         near = [lax.dynamic_index_in_dim(parts, z_pos, 0, False)]
         for d in range(1, z_count):
             there = lax.dynamic_index_in_dim(parts, (z_pos + d) % z_count, 0, False)
             near.append(
                 lax.ppermute(there, "z", [(i, (i + d) % z_count) for i in range(z_count)])
             )
-        near = jnp.stack(near)
-        return jnp.concatenate(
-            [
-                lax.dynamic_index_in_dim(near, (z_pos - z + z_count) % z_count, 0, False)
-                for z in range(z_count)
-            ]
-        )
+        return arrange(near, z_pos, earlier)
 
     def to_heads(parts):
         return lax.all_to_all(parts, "z", 0, 0, tiled=True).reshape(line_rows, HEAD_DIM)
@@ -786,24 +1035,19 @@
             return lax.ppermute(a, "x", SWAP)
         return lax.all_gather(a, "x", axis=0)
 
-    v_heads = jnp.concatenate(
-        [
-            jnp.moveaxis(r[2].astype(bf16).reshape(-1, z_count, HEAD_DIM), 1, 0)
-            for r in raw_h
-        ],
-        axis=1,
-    )
+    v_heads = jnp.concatenate([v0, v1], axis=1)
     values = to_heads(v_heads)
     values_far = from_x(values)
     q_heads, k_heads = pack_heads(
-        raw_h[0],
-        raw_h[1],
+        raw0,
+        raw1,
         inv_qk.T,
         lax.dynamic_slice_in_dim(cos_tab, z_pos * tok_rows, tok_rows),
         lax.dynamic_slice_in_dim(sin_tab, z_pos * tok_rows, tok_rows),
         gain_qk,
     )
-    keys = to_heads_apart(k_heads)
+    keys = to_heads_apart(k_heads, (values_far,))
+    out_b = attn_out.astype(bf16)
     keys_far = from_x(keys)
     queries = to_heads_apart(q_heads)
     tok_col = tok_own.reshape(line_rows, 1)
@@ -822,7 +1066,7 @@
             )
         ]
     attn_f, row_lse = attend(
-        queries, tok_q, start_q, key_groups, (normed_pick,)
+        queries, tok_q, start_q, key_groups
     )
 
     def to_tokens(rows, cols):
@@ -832,26 +1076,27 @@
         return parts
 
     attn_parts = to_tokens(attn_f.astype(bf16), HEAD_DIM)
-    attn_b = jnp.moveaxis(attn_parts, 0, 1).reshape(tok_rows, head_cols)
-    normed_up, normed_down, normed_half = gather_line(normed_pick, z_pos, z_count)
-    attn_far = lax.ppermute(attn_b, "x", SWAP) if pair else attn_b
-    half = tok_rows // 2
+    attn_far = attn_out_half(attn_parts, 1, out_b)
+    attn_near = attn_out_half(attn_parts, 0, out_b)
+    attn_y, attn_sent = scatter_halves(attn_near, attn_far)
+    normed_pick = pick_half(normed_h, c_pos, (attn_sent,))
+    normed_line = lax.all_gather(normed_pick, "z", axis=0, tiled=True)
+    attn_there = lax.ppermute(attn_parts, "x", SWAP) if pair else attn_sent
+    gu_b = round_weights(gate_up, (attn_sent,))
+    residual, mixed_rows = row_call(
+        mix_kernel,
+        attn_y,
+        (block_in,),
+        norm_gains[1],
+        (f32, bf16),
+        (gu_b, normed_pick, attn_there),
+    )
+    down_b = round_weights(down, (mixed_rows,))
+    mixed_h = gather_halves(mixed_rows, (down_b,))
+    mixed_far = [far_wide([m]) for m in mixed_h] if pair else [mixed_rows, mixed_rows]
 
     def halves(a):
-        return [a[:half], a[half:]]
-
-    attn_y, _ = scatter_halves(
-        [
-            lax.dot_general(a, out_b, DOT_NT, preferred_element_type=f32).astype(bf16)
-            for a in halves(attn_b)
-        ]
-    )
-    residual, mixed_rows = row_call(
-        mix_kernel, attn_y, (block_in,), norm_gains[1], (f32, bf16),
-        (normed_up[0], normed_down[0], attn_far),
-    )
-    mixed_h = gather_halves(mixed_rows)
-    mixed_far = far_wide(mixed_h) if pair else mixed_rows
+        return a[: a.shape[0] // 2], a[a.shape[0] // 2 :]
 
     route_rows = near_first(routes.reshape(2, 2, local_rows, -1), 0, y_pos, c_pos)
     route_rows = route_rows.reshape(tok_rows, -1)
@@ -875,16 +1120,18 @@
         gate_act = pre[0] * jax.nn.sigmoid(pre[0])
         hidden_h.append((gate_w.T[:, :, None] * gate_act * pre[1]).astype(bf16))
     expert_y, _ = scatter_halves(
-        [
-            jnp.einsum("etf,edf->td", h, down_b, preferred_element_type=f32).astype(bf16)
+        *[
+            halves(
+                jnp.einsum("etf,edf->td", h, down_b, preferred_element_type=f32).astype(bf16)
+            )
             for h in hidden_h
         ]
     )
     block_out, cot_local, cot_b = row_call(
         gap_kernel, expert_y, (residual, target), None, (bf16, f32, bf16),
-        (normed_up[1], normed_down[1], mixed_far),
-    )
-    cot_h = gather_halves(cot_b)
+        (mixed_far[0],),
+    )
+    cot_h = gather_halves(cot_b, earlier=(mixed_far[1], normed_line))
 
     d_pre_h = []
     d_mixed_parts = []
@@ -918,15 +1165,14 @@
             lax.dot_general(d_logit, mixed, (((0,), (0,)), ((), ())), preferred_element_type=f32)
         )
     router_rows = router_parts[0] + router_parts[1]
-    d_mixed, d_mixed_sent = scatter_halves(d_mixed_parts)
-
-    hidden = jnp.concatenate(hidden_h, axis=1)
-    d_pre = jnp.concatenate(d_pre_h, axis=2)
-
-    def compact(a):
-        taken = route_rows.T[:, None, :, None]
+    d_mixed, d_mixed_sent = scatter_halves(*[halves(d) for d in d_mixed_parts])
+    down_part = own_grad(cot_h, hidden_h, (d_mixed_sent,))
+
+    def compact(a, taken):
+        a = a.reshape(-1, experts, *a.shape[1:])
+        taken = taken.T[:, None, :, None]
         parts = []
-        for slot in range(route_rows.shape[1]):
+        for slot in range(taken.shape[0]):
             part = a[:, 0]
             for e in range(1, experts):
                 part = jnp.where(taken[slot] == e, a[:, e], part)
@@ -949,48 +1195,40 @@
         (residual, cot_local),
         norm_gains[1],
         (f32, bf16, None),
-    )
-    d_resid_h = gather_halves(d_resid_b)
+        (down_part,),
+    )
+    d_pre_h = [d.reshape(2 * experts, -1, hidden_cols) for d in d_pre_h]
     if pair:
-        hidden_far = lax.ppermute(compact(hidden[None]), "x", SWAP)
-        cot_far = far_wide(cot_h)
-        d_pre_far = lax.ppermute(compact(d_pre), "x", SWAP)
-        down_part = weight_grad(
-            cot_h,
-            cot_far,
-            [hidden, hidden_far],
-            out_block,
-            x_pos,
-            routes_far,
-            experts,
-            (d_resid_b, normed_up[2], normed_down[2]),
-        )
-    else:
-        down_part = plain_part(cot_h, jnp.concatenate(hidden_h, axis=1), "td,etf->edf")
-        gate_up_part = plain_part(
-            mixed_h, d_pre, "td,ketf->kedf"
-        ).reshape(2 * experts, -1, hidden_cols)
+        d_pre_far = [
+            lax.ppermute(compact(d, r), "x", SWAP) for d, r in zip(d_pre_h, (route_rows[: tok_rows // 2], route_rows[tok_rows // 2 :]))
+        ]
+    d_resid_h = gather_halves(d_resid_b, earlier=(d_pre_far[0],) if pair else ())
+    d_resid_far = [far_wide([d]) for d in d_resid_h] if pair else None
     d_attn = attn_out_grad_half(d_resid_h[0], 0, out_b)
-    d_attn = attn_out_grad_half(d_resid_h[1], 1, out_b, d_attn, (down_part,))
+    d_attn = attn_out_grad_half(d_resid_h[1], 1, out_b, d_attn)
 
     d_out = to_heads(d_attn)
     delta = jnp.sum(d_out.astype(f32) * attn_f, axis=-1).reshape(1, line_rows)
     d_query = jnp.zeros((line_rows, HEAD_DIM), f32)
     if pair:
-        d_resid_far = far_wide(d_resid_h)
         gate_up_part = weight_grad(
             mixed_h,
             mixed_far,
-            [d_pre.reshape(2 * experts, tok_rows, hidden_cols), d_pre_far],
+            [(d, 0) for d in d_pre_h],
+            [(d, 0) for d in d_pre_far],
             out_block,
             x_pos,
             routes_far,
             experts,
             (d_attn,),
         )
+    else:
+        gate_up_part = plain_part(mixed_h, jnp.concatenate(d_pre_h, axis=1), "td,ntf->ndf")
+    down_part = lax.psum_scatter(down_part, ("z", "x"), scatter_dimension=1, tiled=True)
+    gate_up_sum = lax.psum_scatter(gate_up_part, "z", scatter_dimension=1, tiled=True)
     d_kv = []
     inner_k = []
-    earlier = (gate_up_part,)
+    earlier = (gate_up_part, d_resid_far[0]) if pair else (gate_up_part,)
     for i, group in enumerate(groups):
         last = i == len(groups) - 1
         d_query, *d_group = attend_grad(
@@ -1005,17 +1243,18 @@
             f32 if pair and last else bf16,
             earlier,
         )
+        d_kv.append(d_group)
         if pair and not last:
             out_part = weight_grad(
                 d_resid_h,
                 d_resid_far,
-                [(attn_b, 0), (attn_b, 1), (attn_far, 0), (attn_far, 1)],
+                [(attn_parts, 0), (attn_parts, 1)],
+                [(attn_there, 0), (attn_there, 1)],
                 out_block,
                 x_pos,
                 earlier=(d_group[0],),
             )
-            earlier = (out_part,)
-        d_kv.append(d_group)
+            earlier = (down_part, out_part)
         inner_k.append(jnp.sum(d_group[0].astype(f32) * group[0].astype(f32), axis=-1))
     if pair:
         d_key, d_value = [
@@ -1035,23 +1274,49 @@
     coef = jnp.stack([inv_line[0], inner[0], inv_line[1], inner[1]], axis=1)
     head_gain = lax.dynamic_slice_in_dim(gain_qk, z_pos * HEAD_DIM, HEAD_DIM, 1)
     d_raw, gain_sums = raw_grad(
-        d_query, d_key, d_value, queries, keys, coef, cos_tab, sin_tab, head_gain
+        d_query, d_key, d_value, queries, keys, coef, cos_tab, sin_tab, head_gain, out_part if pair else d_query
     )
     gain_full = lax.dynamic_update_slice_in_dim(
         jnp.zeros((2, model_width), f32), gain_sums, (wt_pos * z_count + z_pos) * HEAD_DIM, 1
     )
 
+    def sum_all(a):
+        a = a + lax.ppermute(a, "c", SWAP)
+        a = a + lax.ppermute(a, "y", SWAP)
+        a = pass_rows(a, (input_grad,))
+        a = a + lax.ppermute(a, "x", SWAP) if pair else lax.psum(a, "x")
+        return sum_line(a, z_count)
+
+    if pair:
+        out_sum = lax.psum_scatter(out_part, "z", scatter_dimension=1, tiled=True)
+    else:
+        out_part = own_grad(d_resid_h, (attn_parts, attn_parts), (d_raw,))
+        out_sum = lax.psum_scatter(out_part, ("z", "x"), scatter_dimension=1, tiled=True)
+    out_sum = jnp.moveaxis(out_sum, 0, 1).reshape(out_block, head_cols).astype(f32)
+    grad_mine, grad_other = qkv_grad(
+        normed_line, d_raw, lax.ppermute(d_raw, "c", SWAP), z_count
+    )
+    grad_other = lax.ppermute(grad_other, "c", SWAP)
+    qkv_full = jnp.where(
+        c_pos == 0,
+        jnp.stack([grad_mine, grad_other]),
+        jnp.stack([grad_other, grad_mine]),
+    ).reshape(z_count, x_count, out_block, 3 * HEAD_DIM)
+    qkv_line = jnp.moveaxis(qkv_full, 1, 0)
+    if pair:
+        qkv_line = (
+            lax.dynamic_index_in_dim(qkv_line, x_pos, 0, False),
+            lax.ppermute(lax.dynamic_index_in_dim(qkv_line, 1 - x_pos, 0, False), "x", SWAP),
+        )
+    else:
+        qkv_line = scatter_x(qkv_line).astype(bf16)
+        qkv_line = (qkv_line, jnp.zeros_like(qkv_line))
     d_proj = to_tokens(d_raw, 3 * HEAD_DIM)
-    far_n, gain_first1 = project_grad_half(d_proj, 1, qkv_b, normed_h[1])
-    near_n, gain_first0 = project_grad_half(d_proj, 0, qkv_b, normed_h[0], (far_n,))
-    down_part = lax.psum_scatter(down_part, "z", scatter_dimension=1, tiled=True).astype(f32)
-    gate_up_part = (
-        lax.psum_scatter(gate_up_part, "z", scatter_dimension=1, tiled=True)
-        .astype(f32)
-        .reshape(2, experts, out_block, hidden_cols)
-    )
-    d_normed, _ = scatter_halves([near_n, far_n])
-    gain_first = (gain_first0 + gain_first1) / norm_gains[:1]
+    *far_n, gain_first1 = project_grad_half(
+        d_proj, 1, qkv_b, normed_h[1], (qkv_line[1], gate_up_sum)
+    )
+    *near_n, gain_first0 = project_grad_half(d_proj, 0, qkv_b, normed_h[0], (far_n[0],))
+    d_normed, _ = scatter_halves(near_n, far_n)
     (input_grad,) = row_call(
         input_grad_kernel,
         d_normed,
@@ -1060,39 +1325,13 @@
         (bf16,),
     )
 
-    def sum_all(a):
-        a = a + lax.ppermute(a, "c", SWAP)
-        a = a + lax.ppermute(a, "y", SWAP)
-        a = a + lax.ppermute(a, "x", SWAP) if pair else lax.psum(a, "x")
-        return sum_line(a, z_count)
-
-    small = sum_all(jnp.concatenate([gain_first, gain_second, gain_full, router_rows]))
+    small = sum_all(stack_rows(gain_first0, gain_first1, norm_gains, gain_second, gain_full, router_rows))
     gains_grad = small[:4]
     router_grad = small[4:].T
 
-    if pair:
-        out_part = lax.psum_scatter(out_part, "z", scatter_dimension=1, tiled=True)
-        out_part = jnp.moveaxis(out_part, 0, 1).reshape(out_block, head_cols).astype(f32)
-    else:
-        out_part = plain_part(d_resid_h, attn_b, "td,tc->dc")
-        out_part = lax.psum_scatter(out_part, "z", scatter_dimension=0, tiled=True).astype(f32)
-
-    normed_other = lax.ppermute(normed_half, "c", SWAP)
-    tn = (((0,), (0,)), ((), ()))
-    grad_mine = lax.dot_general(normed_half, d_raw, tn, preferred_element_type=f32).astype(bf16)
-    d_raw_other = jnp.flip(
-        d_raw.reshape(z_count, 2, 2, local_rows, 3 * HEAD_DIM), 2
-    ).reshape(line_rows, 3 * HEAD_DIM)
-    grad_other = lax.dot_general(
-        normed_other, d_raw_other, tn, preferred_element_type=f32
-    ).astype(bf16)
-    qkv_full = jnp.where(
-        c_pos == 0,
-        jnp.stack([grad_mine, grad_other]),
-        jnp.stack([grad_other, grad_mine]),
-    ).reshape(z_count, x_count, out_block, 3 * HEAD_DIM)
-    qkv_line = scatter_x(jnp.moveaxis(qkv_full, 1, 0)).astype(bf16)
-    qkv_heads = lax.all_to_all(qkv_line, "z", 0, 0, tiled=True)
+    qkv_heads = lax.all_to_all(
+        add_rows(*qkv_line, (near_n[0],)), "z", 0, 0, tiled=True
+    )
     qkv_part = (
         qkv_heads.reshape(z_count, out_block, 3, HEAD_DIM)
         .transpose(2, 1, 0, 3)
@@ -1103,11 +1342,11 @@
         block_out,
         input_grad,
         qkv_part,
-        out_part,
+        out_sum,
         gains_grad,
         router_grad,
-        gate_up_part,
-        down_part,
+        gate_up_sum.astype(f32).reshape(2, experts, out_block, hidden_cols),
+        down_part.astype(f32),
     )
 
 

time: 602 us -> 569 us (0.945)
  other arithmetic: 89.4 us -> 58.5 us
  local copies, waits for them, and re-layouts: 50.9 us -> 77.1 us
  starting transfers between devices: 92.9 us -> 73.6 us
  matrix products: 38.1 us -> 24.5 us
    unnamed x177 -> x256, local copies, waits for them, and re-layouts: 18.9 us -> 62.6 us
    pallas_call x3 -> x20, Pallas kernels: 24.2 us -> 44 us  [the longest x2 12.5 us: weight_grad(): pl.pallas_call(functools.partial(weight_grad_kernel, experts, out_block),...]
    convert_element_type x8 -> x2, other arithmetic: 19.7 us -> 2.04 us  [the longest x1 1.06 us: local(): down_part.astype(f32)]
    dot_general x6 -> x0, matrix products: 17.5 us -> none  [the longest x2 6.72 us: local(): jnp.einsum('td,kdc->ktc', n, qkv_b, preferred_element_type=f32)]
    all_to_all x2, waiting for transfers between devices: 63.4 us -> 49.3 us  [to_tokens(): lax.all_to_all(rows.reshape(z_count, tok_rows, cols), 'z', 0, 0, tiled=True)]
    ppermute x2, waiting for transfers between devices: 13.8 us -> 0.01 us  [from_x(): return lax.ppermute(a, 'x', SWAP)]
    ppermute x19 -> x14, starting transfers between devices: 19 us -> 6.21 us  [the longest x2 1.81 us: local(): lax.ppermute(compact(d, r), 'x', SWAP)]
    ppermute x6, waiting for transfers between devices: 8.97 us -> 17.8 us  [to_heads_apart(): lax.ppermute(there, 'z', [(i, (i + d) % z_count) for i in range(z_count)])]
  transfers between devices with their start and end apart: 71 -> 68, of which waited for: 24 -> 28; matrix products, arithmetic and copies ran while one was open for 25% -> 15% of each run, Pallas kernels for 16% -> 17%
where the time goes in v3:
time: 569 us; the launch traced here: 561 us
  waiting for transfers between devices  188 us (33%)
  Pallas kernels  123 us (22%)
  local copies, waits for them, and re-layouts  77.1 us (14%)
  starting transfers between devices  73.6 us (13%)
  other arithmetic  58.5 us (10%)
  matrix products  24.5 us (4%)
  between operations  15.9 us (3%)
    unnamed x256, local copies, waits for them, and re-layouts  62.6 us
    all_to_all x2, waiting for transfers between devices, to_tokens(): lax.all_to_all(rows.reshape(z_count, tok_rows, cols), 'z', 0, 0, tiled=True)  49.3 us
    ppermute x4, waiting for transfers between devices, gather_halves(): far = lax.ppermute(rows, 'y', SWAP)  29.5 us
    pallas_call x2, Pallas kernels, attend_grad(): pl.pallas_call(functools.partial(attend_grad_kernel, chunk, LOG2E / math....  29 us
    ppermute x4, waiting for transfers between devices, scatter_halves(): far_got = lax.ppermute(sent, 'y', SWAP)  22.3 us
    ppermute x2, waiting for transfers between devices, local(): lax.ppermute(compact(d, r), 'x', SWAP)  18 us
    ppermute x6, waiting for transfers between devices, to_heads_apart(): lax.ppermute(there, 'z', [(i, (i + d) % z_count) for i in range(z_count)])  17.8 us
    pallas_call x1, Pallas kernels, attend(): pl.pallas_call(functools.partial(attend_kernel, len(key_groups), chunk, L...  16.9 us
  transfers between devices with their start and end apart: 68, of which 28 were waited for; matrix products, arithmetic and copies ran while one was open for 15% of the time, Pallas kernels for 17%

profile of v3, /device:TPU:0, one launch (start us, length us, event | category | flops | bytes accessed | tf_op | source)
XLA Modules:
  0.0 561.3 jit_solution(2862883012350251119)
XLA Ops:
  11.1 3.0 collective-permute-start.1
  17.4 8.0 %convert_element_type.195.w_ref = bf16[3,2048,512]{2,1,0:T(8,128)(2,1)} convert(f32[3,2048,512]{2,1,0:T(8,128)} %param.16) | non-fusion elementwise | flops 3145728 | bytes 18874368 | tf_op jit(solution)/shard_map/convert_element_type | solution.py:951
  26.6 5.3 multiply_sine_fusion
  36.2 4.7 project.2
  41.3 4.7 project.3
  47.8 4.9 all-to-all-start
  59.6 8.0 %all-to-all-done = bf16[4,512,128]{2,1,0:T(8,128)(2,1)S(1)} async-done(((bf16[4,512,128]{2,1,0:T(8,128)(2,1)}), bf16[4,512,128]{2,1,0:T(8,128)(2,1)S(1)}, u32[]{:S(2)}, u32[]{:S(2)}) %all-to-all-start) | async-done | bytes 524320 | tf_op jit(solution)/shard_map/all_to_all | solution.py:1031
  69.0 4.7 pack_heads.1
  77.1 3.8 collective-permute-done.10.refs_3_
  80.9 5.8 %collective-permute-done.9.refs_2_ = bf16[512,128]{1,0:T(8,128)(2,1)S(1)} collective-permute-done((bf16[512,128]{1,0:T(8,128)(2,1)S(1)}, bf16[512,128]{1,0:T(8,128)(2,1)S(1)}, u32[]{:S(2)}, u32[]{:S(2)}) %collective-permute-start.9) | collective-permute-done | bytes 131104 | tf_op jit(solution)/shard_map/ppermute | solution.py:1026
  94.4 7.5 %collective-permute-done.6.refs_2_ = bf16[512,128]{1,0:T(8,128)(2,1)S(1)} collective-permute-done((bf16[512,128]{1,0:T(8,128)(2,1)}, bf16[512,128]{1,0:T(8,128)(2,1)S(1)}, u32[]{:S(2)}, u32[]{:S(2)}) %collective-permute-start.6) | collective-permute-done | bytes 131104 | tf_op jit(solution)/shard_map/ppermute | solution.py:1026
  104.9 16.9 %attend.1 = (f32[2048,128]{1,0:T(8,128)S(1)}, f32[1,2048]{1,0:T(1,128)S(1)}) custom-call(bf16[2048,128]{1,0:T(8,128)(2,1)S(1)} %arrange.2.q_ref, s32[1,2048]{1,0:T(1,128)S(1)} %bitcast.287, s32[1,2048]{1,0:T(1,128)S(1)} %bitcast.293, bf16[2048,128]{1,0:T(8,128)(2,1)S(1)} %arrange.3.refs_0_.k_ref, bf16[2048,128]{1,0:T(8,128)(2,1)S(1)} %bitcast.281, ...), custom_call_target="tpu_custom_call" | custom-call | flops 19000000512 | bytes 1048576 | tf_op jit(solution)/shard_map/attend/pallas_call | solution.py:97
  123.7 3.5 all-to-all-start.1
  129.9 10.7 %all-to-all-done.1.x_ref.refs_4_.refs_5_ = bf16[4,512,128]{2,1,0:T(8,128)(2,1)S(1)} async-done(((bf16[4,512,128]{2,1,0:T(8,128)(2,1)}), bf16[4,512,128]{2,1,0:T(8,128)(2,1)S(1)}, u32[]{:S(2)}, u32[]{:S(2)}) %all-to-all-start.1) | async-done | bytes 524320 | tf_op jit(solution)/shard_map/all_to_all | solution.py:1073
  154.3 6.5 %copy-done.93 = f32[2,4,2048,256]{3,2,1,0:T(8,128)S(1)} copy-done((f32[2,4,2048,256]{3,2,1,0:T(8,128)S(1)}, f32[2,4,2048,256]{3,2,1,0:T(8,128)}, u32[]{:S(2)}) %copy-start.93) | copy-done | bytes 16777240
  168.6 3.4 copy-done.94
  173.3 7.3 %collective-permute-done.19.in_ref = bf16[128,2048]{1,0:T(8,128)(2,1)S(1)} collective-permute-done((bf16[128,2048]{1,0:T(8,128)(2,1)S(1)}, bf16[128,2048]{1,0:T(8,128)(2,1)S(1)}, u32[]{:S(2)}, u32[]{:S(2)}) %collective-permute-start.19) | collective-permute-done | bytes 524320 | tf_op jit(solution)/shard_map/ppermute | solution.py:892
  192.2 12.6 %collective-permute-done.22.far_got = bf16[128,2048]{1,0:T(8,128)(2,1)S(1)} collective-permute-done((bf16[128,2048]{1,0:T(8,128)(2,1)S(1)}, bf16[128,2048]{1,0:T(8,128)(2,1)S(1)}, u32[]{:S(2)}, u32[]{:S(2)}) %collective-permute-start.22) | collective-permute-done | bytes 524320 | tf_op jit(solution)/shard_map/ppermute | solution.py:903
  208.3 11.7 %collective-permute-done.26.a_ref = bf16[128,2048]{1,0:T(8,128)(2,1)S(1)} collective-permute-done((bf16[128,2048]{1,0:T(8,128)(2,1)S(1)}, bf16[128,2048]{1,0:T(8,128)(2,1)S(1)}, u32[]{:S(2)}, u32[]{:S(2)}) %collective-permute-start.26) | collective-permute-done | bytes 524320 | tf_op jit(solution)/shard_map/ppermute | solution.py:892
  224.3 7.6 %all-gather.2.cloned.1.call-done.refs_1_.wide_ref = bf16[2048,1024]{1,0:T(8,128)(2,1)} async-done(((bf16[512,1024]{1,0:T(8,128)(2,1)}), bf16[2048,1024]{1,0:T(8,128)(2,1)}) %all-gather.2.cloned.1.call-update) | async-done | bytes 4194320 | tf_op jit(solution)/shard_map/all_gather | solution.py:1083
  238.8 3.9 fusion.31
  249.2 3.5 own_grad.1.refs_0_
  260.0 6.1 %fusion.4 = f32[256,2048]{1,0:T(8,128)S(1)} fusion(bf16[2,4,2048,256]{3,2,1,0:T(8,128)(2,1)} %bitcast.271, bf16[1,4,256,256]{3,2,1,0:T(8,128)(2,1)S(1)} %get-tuple-element.136, bf16[1,4,256,256]{3,2,1,0:T(8,128)(2,1)S(1)} %get-tuple-element.135), kind=kOutput, calls=%fused_computation.6 | convolution fusion | flops 2148007936 | bytes 11534336 | tf_op jit(solution)/shard_map/ketf,kedf->td/dot_general | solution.py:1160
  270.9 4.3 pad_maximum_fusion.1
  275.2 7.2 %collective-permute-done.30.far_got = bf16[128,2048]{1,0:T(8,128)(2,1)} collective-permute-done((bf16[128,2048]{1,0:T(8,128)(2,1)}, bf16[128,2048]{1,0:T(8,128)(2,1)}, u32[]{:S(2)}, u32[]{:S(2)}) %collective-permute-start.30) | collective-permute-done | bytes 524320 | tf_op jit(solution)/shard_map/ppermute | solution.py:903
  284.7 3.0 resid_grad_kernel.1
  291.8 10.5 %collective-permute-done.31.a_ref = bf16[128,2048]{1,0:T(8,128)(2,1)S(1)} collective-permute-done((bf16[128,2048]{1,0:T(8,128)(2,1)S(1)}, bf16[128,2048]{1,0:T(8,128)(2,1)S(1)}, u32[]{:S(2)}, u32[]{:S(2)}) %collective-permute-start.31) | collective-permute-done | bytes 524320 | tf_op jit(solution)/shard_map/ppermute | solution.py:892
  305.5 4.2 collective-permute-done.33.refs_0_.refs_6_
  313.5 4.3 all-to-all-start.2
  325.0 13.8 %collective-permute-done.35.refs_7_ = bf16[2,2,256,256]{3,2,1,0:T(8,128)(2,1)S(1)} collective-permute-done((bf16[2,2,256,256]{3,2,1,0:T(8,128)(2,1)S(1)}, bf16[2,2,256,256]{3,2,1,0:T(8,128)(2,1)S(1)}, u32[]{:S(2)}, u32[]{:S(2)}) %collective-permute-start.35) | collective-permute-done | bytes 524320 | tf_op jit(solution)/shard_map/ppermute | solution.py:1203
  339.8 7.4 %weight_grad.2.refs_0_ = bf16[8,1024,256]{2,1,0:T(8,128)(2,1)S(1)} custom-call(s32[1]{0:T(128)} %bitcast.67.at_ref, bf16[256,2048]{1,0:T(8,128)(2,1)S(1)} %copy-done.8, bf16[256,2048]{1,0:T(8,128)(2,1)S(1)} %join_rows.5.refs_1_, bf16[256,1024]{1,0:T(8,128)(2,1)S(1)} %copy-done.47, bf16[256,1024]{1,0:T(8,128)(2,1)S(1)} %copy-done.58, ...), custom_call_target="tpu_custom_call" | custom-call | flops 100000000 | bytes 1048576 | tf_op jit(solution)/shard_map/weight_grad/pallas_call | solution.py:370
  351.3 14.8 %attend_grad.2 = (f32[2048,128]{1,0:T(8,128)S(1)}, bf16[2048,128]{1,0:T(8,128)(2,1)}, bf16[2048,128]{1,0:T(8,128)(2,1)}) custom-call(bf16[2048,128]{1,0:T(8,128)(2,1)S(1)} %copy-done.33, bf16[2048,128]{1,0:T(8,128)(2,1)} %bitcast.65.do_ref, f32[1,2048]{1,0:T(1,128)S(1)} %get-tuple-element.65.lse_ref, f32[1,2048]{1,0:T(1,128)S(1)} %bitcast.291, ...), custom_call_target="tpu_custom_call" | custom-call | flops 500000000 | bytes 1048576 | tf_op jit(solution)/shard_map/attend_grad/pallas_call | solution.py:192
  375.7 5.1 weight_grad.3.refs_1_.refs_0_
  384.9 14.2 %attend_grad.3 = (f32[2048,128]{1,0:T(8,128)S(1)}, f32[2048,128]{1,0:T(8,128)S(1)}, f32[2048,128]{1,0:T(8,128)S(1)}) custom-call(bf16[2048,128]{1,0:T(8,128)(2,1)S(1)} %copy-done.33, bf16[2048,128]{1,0:T(8,128)(2,1)} %bitcast.65.do_ref, f32[1,2048]{1,0:T(1,128)S(1)} %get-tuple-element.65.lse_ref, f32[1,2048]{1,0:T(1,128)S(1)} %bitcast.292, ...), custom_call_target="tpu_custom_call" | custom-call | flops 500000000 | bytes 1048576 | tf_op jit(solution)/shard_map/attend_grad/pallas_call | solution.py:192
  410.5 3.7 collective-permute-done.46
  414.8 4.2 collective-permute-done.40
  422.9 6.0 %raw_grad.1 = (bf16[2048,384]{1,0:T(8,128)(2,1)}, f32[2,128]{1,0:T(2,128)}) custom-call(f32[2048,128]{1,0:T(8,128)} %copy-done.69, f32[2048,128]{1,0:T(8,128)} %get-tuple-element.144.dk_ref, f32[2048,128]{1,0:T(8,128)} %convert_add_fusion.dv_ref, bf16[2048,128]{1,0:T(8,128)(2,1)} %copy-done.32, bf16[2048,128]{1,0:T(8,128)(2,1)} %copy-done.34, ...), custom_call_target="tpu_custom_call" | custom-call | flops 6000000000 | bytes 1048576 | tf_op jit(solution)/shard_map/raw_grad/pallas_call | solution.py:300
  428.8 4.4 all-to-all-start.3
  436.9 6.4 %qkv_grad.1 = (bf16[1024,384]{1,0:T(8,128)(2,1)S(1)}, bf16[1024,384]{1,0:T(8,128)(2,1)S(1)}) custom-call(bf16[2048,1024]{1,0:T(8,128)(2,1)S(1)} %copy-done.42, bf16[2048,384]{1,0:T(8,128)(2,1)S(1)} %copy-done.62, bf16[2048,384]{1,0:T(8,128)(2,1)} %collective-permute-done.48.grad_other_ref), custom_call_target="tpu_custom_call" | custom-call | flops 10000000000 | bytes 1048576 | tf_op jit(solution)/shard_map/qkv_grad/pallas_call | solution.py:601
  448.6 38.6 %all-to-all-done.3.x_ref = bf16[4,512,384]{2,1,0:T(8,128)(2,1)} async-done(((bf16[4,512,384]{2,1,0:T(8,128)(2,1)}), bf16[4,512,384]{2,1,0:T(8,128)(2,1)}, u32[]{:S(2)}, u32[]{:S(2)}) %all-to-all-start.3) | async-done | bytes 1572896 | tf_op jit(solution)/shard_map/all_to_all | solution.py:1073
  492.5 4.9 project_grad.2
  497.4 3.0 copy-done.3
  500.3 4.3 project_grad.3
  505.5 3.4 add_rows.1
  509.7 4.2 all-to-all-start.4
  519.8 11.4 %collective-permute-done.55 = f32[8,2048]{1,0:T(8,128)S(1)} collective-permute-done((f32[8,2048]{1,0:T(8,128)S(1)}, f32[8,2048]{1,0:T(8,128)S(1)}, u32[]{:S(2)}, u32[]{:S(2)}) %collective-permute-start.55) | collective-permute-done | bytes 65568 | tf_op jit(solution)/shard_map/ppermute | solution.py:1285
  535.6 3.1 collective-permute-done.56
  543.1 2.9 collective-permute-start.58
  (516 shorter events, 202.1 us)
Async XLA Ops:
  11.1 15.0 %collective-permute-start.1 = (bf16[128,2048]{1,0:T(8,128)(2,1)S(1)}, bf16[128,2048]{1,0:T(8,128)(2,1)S(1)}, u32[]{:S(2)}, u32[]{:S(2)}) collective-permute-start(bf16[128,2048]{1,0:T(8,128)(2,1)S(1)} %fusion.20), channel_id=1, source_target_pairs={{0,2},{2,0},{1,3},{3,1},{4,6},{6,4},{5,7},{7,5},{8,10},{10,8},{9,1... | collective-permute-start | bytes 1572872 | tf_op jit(solution)/shard_map/ppermute | solution.py:892
  14.1 17.9 %collective-permute-start = (bf16[128,2048]{1,0:T(8,128)(2,1)S(1)}, bf16[128,2048]{1,0:T(8,128)(2,1)}, u32[]{:S(2)}, u32[]{:S(2)}) collective-permute-start(bf16[128,2048]{1,0:T(8,128)(2,1)S(1)} %fusion.20), channel_id=1, source_target_pairs={{0,1},{1,0},{2,3},{3,2},{4,5},{5,4},{6,7},{7,6},{8,9},{9,8},{10,11... | collective-permute-start | bytes 1572872 | tf_op jit(solution)/shard_map/ppermute | solution.py:893
  26.1 14.9 %collective-permute-start.2 = (bf16[128,2048]{1,0:T(8,128)(2,1)S(1)}, bf16[128,2048]{1,0:T(8,128)(2,1)S(1)}, u32[]{:S(2)}, u32[]{:S(2)}) collective-permute-start(bf16[128,2048]{1,0:T(8,128)(2,1)S(1)} %collective-permute-done.1.a_ref), channel_id=1, source_target_pairs={{0,1},{1,0},{2,3},{3,2},{4,5},{5,4},{6,7},{7,6},{8,9},{9,8},{10,11... | collective-permute-start | bytes 1572872 | tf_op jit(solution)/shard_map/ppermute | solution.py:896
  47.8 19.7 %all-to-all-start = ((bf16[4,512,128]{2,1,0:T(8,128)(2,1)}), bf16[4,512,128]{2,1,0:T(8,128)(2,1)S(1)}, u32[]{:S(2)}, u32[]{:S(2)}) async-start(bf16[4,512,128]{2,1,0:T(8,128)(2,1)} %pad_maximum_fusion.3), calls=%async_computation | async-start | bytes 1048576 | tf_op jit(solution)/shard_map/all_to_all | solution.py:1031
  67.5 19.2 %collective-permute-start.11 = (bf16[2048,128]{1,0:T(8,128)(2,1)S(1)}, bf16[2048,128]{1,0:T(8,128)(2,1)S(1)}, u32[]{:S(2)}, u32[]{:S(2)}) collective-permute-start(bf16[2048,128]{1,0:T(8,128)(2,1)S(1)} %bitcast.280), channel_id=1, source_target_pairs={{0,4},{4,0},{1,5},{5,1},{2,6},{6,2},{3,7},{7,3},{8,12},{12,8},{9,1... | collective-permute-start | bytes 1572872 | tf_op jit(solution)/shard_map/ppermute | solution.py:1035
  76.4 10.3 %collective-permute-start.9 = (bf16[512,128]{1,0:T(8,128)(2,1)S(1)}, bf16[512,128]{1,0:T(8,128)(2,1)S(1)}, u32[]{:S(2)}, u32[]{:S(2)}) collective-permute-start(bf16[512,128]{1,0:T(8,128)(2,1)S(1)} %get-tuple-element.170), channel_id=1, source_target_pairs={{0,16},{8,24},{16,0},{24,8},{1,17},{9,25},{17,1},{25,9},{2,18},{10... | collective-permute-start | bytes 393224 | tf_op jit(solution)/shard_map/ppermute | solution.py:1026
  76.4 10.3 %collective-permute-start.8 = (bf16[512,128]{1,0:T(8,128)(2,1)S(1)}, bf16[512,128]{1,0:T(8,128)(2,1)S(1)}, u32[]{:S(2)}, u32[]{:S(2)}) collective-permute-start(bf16[512,128]{1,0:T(8,128)(2,1)S(1)} %get-tuple-element.171), channel_id=1, source_target_pairs={{0,8},{8,16},{16,24},{24,0},{1,9},{9,17},{17,25},{25,1},{2,10},{10... | collective-permute-start | bytes 393224 | tf_op jit(solution)/shard_map/ppermute | solution.py:1026
  86.9 16.1 %collective-permute-start.12 = (bf16[2048,128]{1,0:T(8,128)(2,1)S(1)}, bf16[2048,128]{1,0:T(8,128)(2,1)}, u32[]{:S(2)}, u32[]{:S(2)}) collective-permute-start(bf16[2048,128]{1,0:T(8,128)(2,1)S(1)} %arrange.3.refs_0_.k_ref), channel_id=1, source_target_pairs={{0,4},{4,0},{1,5},{5,1},{2,6},{6,2},{3,7},{7,3},{8,12},{12,8},{9,1... | collective-permute-start | bytes 1572872 | tf_op jit(solution)/shard_map/ppermute | solution.py:1035
  89.7 12.1 %collective-permute-start.6 = (bf16[512,128]{1,0:T(8,128)(2,1)}, bf16[512,128]{1,0:T(8,128)(2,1)S(1)}, u32[]{:S(2)}, u32[]{:S(2)}) collective-permute-start(bf16[512,128]{1,0:T(8,128)(2,1)} %get-tuple-element.174), channel_id=1, source_target_pairs={{0,16},{8,24},{16,0},{24,8},{1,17},{9,25},{17,1},{25,9},{2,18},{10... | collective-permute-start | bytes 393224 | tf_op jit(solution)/shard_map/ppermute | solution.py:1026
  90.7 11.2 %collective-permute-start.5 = (bf16[512,128]{1,0:T(8,128)(2,1)}, bf16[512,128]{1,0:T(8,128)(2,1)}, u32[]{:S(2)}, u32[]{:S(2)}) collective-permute-start(bf16[512,128]{1,0:T(8,128)(2,1)} %get-tuple-element.175), channel_id=1, source_target_pairs={{0,8},{8,16},{16,24},{24,0},{1,9},{9,17},{17,25},{25,1},{2,10},{10... | collective-permute-start | bytes 393224 | tf_op jit(solution)/shard_map/ppermute | solution.py:1026
  123.7 16.9 %all-to-all-start.1 = ((bf16[4,512,128]{2,1,0:T(8,128)(2,1)}), bf16[4,512,128]{2,1,0:T(8,128)(2,1)S(1)}, u32[]{:S(2)}, u32[]{:S(2)}) async-start(bf16[4,512,128]{2,1,0:T(8,128)(2,1)} %bitcast.26), calls=%async_computation.1 | async-start | bytes 1048576 | tf_op jit(solution)/shard_map/all_to_all | solution.py:1073
  127.2 104.7 %all-gather.2.cloned.1.call-start = ((), (), s32[]{:S(2)}) async-start(), calls=%async_computation.8 | async-start | bytes 5242880 | tf_op jit(solution)/shard_map/all_gather | solution.py:1083
  146.2 15.4 %collective-permute-start.13 = (bf16[128,2048]{1,0:T(8,128)(2,1)}, bf16[128,2048]{1,0:T(8,128)(2,1)}, u32[]{:S(2)}, u32[]{:S(2)}) collective-permute-start(bf16[128,2048]{1,0:T(8,128)(2,1)} %get-tuple-element.56), channel_id=1, source_target_pairs={{0,1},{1,0},{2,3},{3,2},{4,5},{5,4},{6,7},{7,6},{8,9},{9,8},{10,11... | collective-permute-start | bytes 1572872 | tf_op jit(solution)/shard_map/ppermute | solution.py:904
  146.2 15.4 %collective-permute-start.16 = (bf16[4,512,128]{2,1,0:T(8,128)(2,1)S(1)}, bf16[4,512,128]{2,1,0:T(8,128)(2,1)}, u32[]{:S(2)}, u32[]{:S(2)}) collective-permute-start(bf16[4,512,128]{2,1,0:T(8,128)(2,1)S(1)} %all-to-all-done.1.x_ref.refs_4_.refs_5_), channel_id=1, source_target_pairs={{0,4},{4,0},{1,5},{5,1},{2,6},{6,2},{3,7},{7,3},{8,12},{12,8},{9,1... | collective-permute-start | bytes 1572872 | tf_op jit(solution)/shard_map/ppermute | solution.py:1084
  149.8 14.4 %collective-permute-start.15 = (bf16[128,2048]{1,0:T(8,128)(2,1)}, bf16[128,2048]{1,0:T(8,128)(2,1)}, u32[]{:S(2)}, u32[]{:S(2)}) collective-permute-start(bf16[128,2048]{1,0:T(8,128)(2,1)} %add_convert_fusion.3.refs_0_), channel_id=1, source_target_pairs={{0,2},{2,0},{1,3},{3,1},{4,6},{6,4},{5,7},{7,5},{8,10},{10,8},{9,1... | collective-permute-start | bytes 1572872 | tf_op jit(solution)/shard_map/ppermute | solution.py:903
  153.7 228.1 %reduce-scatter.4.cloned.1.call-start = ((), (), s32[]{:S(2)}) async-start(), calls=%async_computation.9 | async-start | bytes 4718592 | tf_op jit(solution)/shard_map/reduce_scatter | solution.py:1227
  167.0 13.6 %collective-permute-start.19 = (bf16[128,2048]{1,0:T(8,128)(2,1)S(1)}, bf16[128,2048]{1,0:T(8,128)(2,1)S(1)}, u32[]{:S(2)}, u32[]{:S(2)}) collective-permute-start(bf16[128,2048]{1,0:T(8,128)(2,1)S(1)} %get-tuple-element.59.refs_0_), channel_id=1, source_target_pairs={{0,2},{2,0},{1,3},{3,1},{4,6},{6,4},{5,7},{7,5},{8,10},{10,8},{9,1... | collective-permute-start | bytes 1572872 | tf_op jit(solution)/shard_map/ppermute | solution.py:892
  172.7 18.9 %collective-permute-start.23 = (bf16[256,1024]{1,0:T(8,128)(2,1)S(1)}, bf16[256,1024]{1,0:T(8,128)(2,1)S(1)}, u32[]{:S(2)}, u32[]{:S(2)}) collective-permute-start(bf16[256,1024]{1,0:T(8,128)(2,1)S(1)} %pad_maximum_fusion.4), channel_id=1, source_target_pairs={{0,4},{4,0},{1,5},{5,1},{2,6},{6,2},{3,7},{7,3},{8,12},{12,8},{9,1... | collective-permute-start | bytes 1572872 | tf_op jit(solution)/shard_map/ppermute | solution.py:978
  190.4 14.4 %collective-permute-start.22 = (bf16[128,2048]{1,0:T(8,128)(2,1)S(1)}, bf16[128,2048]{1,0:T(8,128)(2,1)S(1)}, u32[]{:S(2)}, u32[]{:S(2)}) collective-permute-start(bf16[128,2048]{1,0:T(8,128)(2,1)S(1)} %add_convert_fusion.2), channel_id=1, source_target_pairs={{0,2},{2,0},{1,3},{3,1},{4,6},{6,4},{5,7},{7,5},{8,10},{10,8},{9,1... | collective-permute-start | bytes 1572872 | tf_op jit(solution)/shard_map/ppermute | solution.py:903
  206.3 13.6 %collective-permute-start.26 = (bf16[128,2048]{1,0:T(8,128)(2,1)S(1)}, bf16[128,2048]{1,0:T(8,128)(2,1)S(1)}, u32[]{:S(2)}, u32[]{:S(2)}) collective-permute-start(bf16[128,2048]{1,0:T(8,128)(2,1)S(1)} %get-tuple-element.62), channel_id=1, source_target_pairs={{0,2},{2,0},{1,3},{3,1},{4,6},{6,4},{5,7},{7,5},{8,10},{10,8},{9,1... | collective-permute-start | bytes 1572872 | tf_op jit(solution)/shard_map/ppermute | solution.py:892
  207.4 12.6 %collective-permute-start.24 = (bf16[128,2048]{1,0:T(8,128)(2,1)S(1)}, bf16[128,2048]{1,0:T(8,128)(2,1)S(1)}, u32[]{:S(2)}, u32[]{:S(2)}) collective-permute-start(bf16[128,2048]{1,0:T(8,128)(2,1)S(1)} %get-tuple-element.62), channel_id=1, source_target_pairs={{0,1},{1,0},{2,3},{3,2},{4,5},{5,4},{6,7},{7,6},{8,9},{9,8},{10,11... | collective-permute-start | bytes 1572872 | tf_op jit(solution)/shard_map/ppermute | solution.py:893
  207.6 15.1 %collective-permute-start.28 = (bf16[256,1024]{1,0:T(8,128)(2,1)S(1)}, bf16[256,1024]{1,0:T(8,128)(2,1)S(1)}, u32[]{:S(2)}, u32[]{:S(2)}) collective-permute-start(bf16[256,1024]{1,0:T(8,128)(2,1)S(1)} %pad_maximum_fusion.5), channel_id=1, source_target_pairs={{0,4},{4,0},{1,5},{5,1},{2,6},{6,2},{3,7},{7,3},{8,12},{12,8},{9,1... | collective-permute-start | bytes 1572872 | tf_op jit(solution)/shard_map/ppermute | solution.py:978
  255.4 66.8 %collective-permute-start.36 = (f32[2,512]{0,1:T(8,128)}, f32[2,512]{0,1:T(8,128)}, u32[]{:S(2)}, u32[]{:S(2)}) collective-permute-start(f32[2,512]{0,1:T(8,128)} %convert_bitcast_fusion.2), channel_id=1, source_target_pairs={{0,4},{4,0},{1,5},{5,1},{2,6},{6,2},{3,7},{7,3},{8,12},{12,8},{9,1... | collective-permute-start | bytes 12296 | tf_op jit(solution)/shard_map/ppermute | solution.py:1104
  267.8 7.5 %collective-permute-start.25 = (bf16[128,2048]{1,0:T(8,128)(2,1)}, bf16[128,2048]{1,0:T(8,128)(2,1)}, u32[]{:S(2)}, u32[]{:S(2)}) collective-permute-start(bf16[128,2048]{1,0:T(8,128)(2,1)} %get-tuple-element.157), channel_id=1, source_target_pairs={{0,1},{1,0},{2,3},{3,2},{4,5},{5,4},{6,7},{7,6},{8,9},{9,8},{10,11... | collective-permute-start | bytes 1572872 | tf_op jit(solution)/shard_map/ppermute | solution.py:904
  267.8 14.7 %collective-permute-start.30 = (bf16[128,2048]{1,0:T(8,128)(2,1)}, bf16[128,2048]{1,0:T(8,128)(2,1)}, u32[]{:S(2)}, u32[]{:S(2)}) collective-permute-start(bf16[128,2048]{1,0:T(8,128)(2,1)} %add_convert_fusion.1.refs_0_), channel_id=1, source_target_pairs={{0,2},{2,0},{1,3},{3,1},{4,6},{6,4},{5,7},{7,5},{8,10},{10,8},{9,1... | collective-permute-start | bytes 1572872 | tf_op jit(solution)/shard_map/ppermute | solution.py:903
  288.7 13.6 %collective-permute-start.31 = (bf16[128,2048]{1,0:T(8,128)(2,1)S(1)}, bf16[128,2048]{1,0:T(8,128)(2,1)S(1)}, u32[]{:S(2)}, u32[]{:S(2)}) collective-permute-start(bf16[128,2048]{1,0:T(8,128)(2,1)S(1)} %get-tuple-element.64), channel_id=1, source_target_pairs={{0,2},{2,0},{1,3},{3,1},{4,6},{6,4},{5,7},{7,5},{8,10},{10,8},{9,1... | collective-permute-start | bytes 1572872 | tf_op jit(solution)/shard_map/ppermute | solution.py:892
  290.7 19.0 %collective-permute-start.33 = (bf16[2,2,256,256]{3,2,1,0:T(8,128)(2,1)S(1)}, bf16[2,2,256,256]{3,2,1,0:T(8,128)(2,1)S(1)}, u32[]{:S(2)}, u32[]{:S(2)}) collective-permute-start(bf16[2,2,256,256]{3,2,1,0:T(8,128)(2,1)S(1)} %pad_maximum_fusion.6), channel_id=1, source_target_pairs={{0,4},{4,0},{1,5},{5,1},{2,6},{6,2},{3,7},{7,3},{8,12},{12,8},{9,1... | collective-permute-start | bytes 1572872 | tf_op jit(solution)/shard_map/ppermute | solution.py:1203
  291.7 12.7 %collective-permute-start.34 = (bf16[128,2048]{1,0:T(8,128)(2,1)S(1)}, bf16[128,2048]{1,0:T(8,128)(2,1)S(1)}, u32[]{:S(2)}, u32[]{:S(2)}) collective-permute-start(bf16[128,2048]{1,0:T(8,128)(2,1)S(1)} %get-tuple-element.64), channel_id=1, source_target_pairs={{0,1},{1,0},{2,3},{3,2},{4,5},{5,4},{6,7},{7,6},{8,9},{9,8},{10,11... | collective-permute-start | bytes 1572872 | tf_op jit(solution)/shard_map/ppermute | solution.py:893
  302.3 7.4 %collective-permute-start.32 = (bf16[128,2048]{1,0:T(8,128)(2,1)S(1)}, bf16[128,2048]{1,0:T(8,128)(2,1)S(1)}, u32[]{:S(2)}, u32[]{:S(2)}) collective-permute-start(bf16[128,2048]{1,0:T(8,128)(2,1)S(1)} %collective-permute-done.31.a_ref), channel_id=1, source_target_pairs={{0,1},{1,0},{2,3},{3,2},{4,5},{5,4},{6,7},{7,6},{8,9},{9,8},{10,11... | collective-permute-start | bytes 1572872 | tf_op jit(solution)/shard_map/ppermute | solution.py:896
  313.5 35.8 %all-to-all-start.2 = ((bf16[4,512,128]{2,1,0:T(8,128)(2,1)}), bf16[4,512,128]{2,1,0:T(8,128)(2,1)}, u32[]{:S(2)}, u32[]{:S(2)}) async-start(bf16[4,512,128]{2,1,0:T(8,128)(2,1)} %copy-done.30), calls=%async_computation.2 | async-start | bytes 1048576 | tf_op jit(solution)/shard_map/all_to_all | solution.py:1031
  317.8 130.9 %reduce-scatter.6.cloned.1.call-start = ((), (), s32[]{:S(2)}) async-start(), calls=%async_computation.10 | async-start | bytes 5242880 | tf_op jit(solution)/shard_map/reduce_scatter | solution.py:1228
  319.1 19.6 %collective-permute-start.35 = (bf16[2,2,256,256]{3,2,1,0:T(8,128)(2,1)S(1)}, bf16[2,2,256,256]{3,2,1,0:T(8,128)(2,1)S(1)}, u32[]{:S(2)}, u32[]{:S(2)}) collective-permute-start(bf16[2,2,256,256]{3,2,1,0:T(8,128)(2,1)S(1)} %pad_maximum_fusion.7), channel_id=1, source_target_pairs={{0,4},{4,0},{1,5},{5,1},{2,6},{6,2},{3,7},{7,3},{8,12},{12,8},{9,1... | collective-permute-start | bytes 1572872 | tf_op jit(solution)/shard_map/ppermute | solution.py:1203
  321.0 30.1 %collective-permute-start.37 = (bf16[256,1024]{1,0:T(8,128)(2,1)}, bf16[256,1024]{1,0:T(8,128)(2,1)}, u32[]{:S(2)}, u32[]{:S(2)}) collective-permute-start(bf16[256,1024]{1,0:T(8,128)(2,1)} %pad_maximum_fusion.8), channel_id=1, source_target_pairs={{0,4},{4,0},{1,5},{5,1},{2,6},{6,2},{3,7},{7,3},{8,12},{12,8},{9,1... | collective-permute-start | bytes 1572872 | tf_op jit(solution)/shard_map/ppermute | solution.py:978
  324.1 49.1 %collective-permute-start.38 = (bf16[256,1024]{1,0:T(8,128)(2,1)}, bf16[256,1024]{1,0:T(8,128)(2,1)}, u32[]{:S(2)}, u32[]{:S(2)}) collective-permute-start(bf16[256,1024]{1,0:T(8,128)(2,1)} %pad_maximum_fusion.9), channel_id=1, source_target_pairs={{0,4},{4,0},{1,5},{5,1},{2,6},{6,2},{3,7},{7,3},{8,12},{12,8},{9,1... | collective-permute-start | bytes 1572872 | tf_op jit(solution)/shard_map/ppermute | solution.py:978
  367.0 32.1 %collective-permute-start.39 = (bf16[2048,128]{1,0:T(8,128)(2,1)}, bf16[2048,128]{1,0:T(8,128)(2,1)}, u32[]{:S(2)}, u32[]{:S(2)}) collective-permute-start(bf16[2048,128]{1,0:T(8,128)(2,1)} %get-tuple-element.67.refs_8_), channel_id=1, source_target_pairs={{0,4},{4,0},{1,5},{5,1},{2,6},{6,2},{3,7},{7,3},{8,12},{12,8},{9,1... | collective-permute-start | bytes 1572872 | tf_op jit(solution)/shard_map/ppermute | solution.py:1261
  368.5 33.9 %collective-permute-start.41 = (f32[4,2,512]{2,0,1:T(4,128)S(1)}, f32[4,2,512]{2,0,1:T(4,128)S(1)}, u32[]{:S(2)}, u32[]{:S(2)}) collective-permute-start(f32[4,2,512]{2,0,1:T(4,128)S(1)} %broadcast_select_fusion.1), channel_id=1, source_target_pairs={{0,8},{8,0},{16,24},{24,16},{1,9},{9,1},{17,25},{25,17},{2,10},{10... | collective-permute-start | bytes 49160 | tf_op jit(solution)/shard_map/ppermute | solution.py:916
  372.3 29.6 %collective-permute-start.43 = (f32[2048]{0:T(1024)S(1)}, f32[2048]{0:T(1024)S(1)}, u32[]{:S(2)}, u32[]{:S(2)}) collective-permute-start(f32[2048]{0:T(1024)S(1)} %multiply_reduce_fusion), channel_id=1, source_target_pairs={{0,4},{4,0},{1,5},{5,1},{2,6},{6,2},{3,7},{7,3},{8,12},{12,8},{9,1... | collective-permute-start | bytes 24584 | tf_op jit(solution)/shard_map/ppermute | solution.py:1263
  404.8 14.2 %collective-permute-start.40 = (bf16[2048,128]{1,0:T(8,128)(2,1)}, bf16[2048,128]{1,0:T(8,128)(2,1)S(1)}, u32[]{:S(2)}, u32[]{:S(2)}) collective-permute-start(bf16[2048,128]{1,0:T(8,128)(2,1)} %get-tuple-element.71), channel_id=1, source_target_pairs={{0,4},{4,0},{1,5},{5,1},{2,6},{6,2},{3,7},{7,3},{8,12},{12,8},{9,1... | collective-permute-start | bytes 1572872 | tf_op jit(solution)/shard_map/ppermute | solution.py:1261
  414.2 7.2 %collective-permute-start.47 = (f32[2,4,2,2,128]{4,3,2,1,0:T(2,128)S(1)}, f32[2,4,2,2,128]{4,3,2,1,0:T(2,128)S(1)}, u32[]{:S(2)}, u32[]{:S(2)}) collective-permute-start(f32[2,4,2,2,128]{4,3,2,1,0:T(2,128)S(1)} %add.286), channel_id=1, source_target_pairs={{0,16},{8,24},{16,0},{24,8},{1,17},{9,25},{17,1},{25,9},{2,18},{10... | collective-permute-start | bytes 49160 | tf_op jit(solution)/shard_map/ppermute | solution.py:916
  428.8 58.4 %all-to-all-start.3 = ((bf16[4,512,384]{2,1,0:T(8,128)(2,1)}), bf16[4,512,384]{2,1,0:T(8,128)(2,1)}, u32[]{:S(2)}, u32[]{:S(2)}) async-start(bf16[4,512,384]{2,1,0:T(8,128)(2,1)} %bitcast.283), calls=%async_computation.4 | async-start | bytes 3145728 | tf_op jit(solution)/shard_map/all_to_all | solution.py:1073
  433.2 112.8 %reduce-scatter.8.cloned.1.call-start = ((), (), s32[]{:S(2)}) async-start(), calls=%async_computation.11 | async-start | bytes 1310720 | tf_op jit(solution)/shard_map/reduce_scatter | solution.py:1291
  447.4 39.9 %collective-permute-start.50 = (bf16[4,256,384]{2,1,0:T(8,128)(2,1)}, bf16[4,256,384]{2,1,0:T(8,128)(2,1)}, u32[]{:S(2)}, u32[]{:S(2)}) collective-permute-start(bf16[4,256,384]{2,1,0:T(8,128)(2,1)} %get-tuple-element.142), channel_id=1, source_target_pairs={{0,4},{4,0},{1,5},{5,1},{2,6},{6,2},{3,7},{7,3},{8,12},{12,8},{9,1... | collective-permute-start | bytes 2359304 | tf_op jit(solution)/shard_map/ppermute | solution.py:1309
  497.4 17.0 %collective-permute-start.52 = (bf16[128,2048]{1,0:T(8,128)(2,1)}, bf16[128,2048]{1,0:T(8,128)(2,1)}, u32[]{:S(2)}, u32[]{:S(2)}) collective-permute-start(bf16[128,2048]{1,0:T(8,128)(2,1)} %get-tuple-element.78), channel_id=1, source_target_pairs={{0,1},{1,0},{2,3},{3,2},{4,5},{5,4},{6,7},{7,6},{8,9},{9,8},{10,11... | collective-permute-start | bytes 1572872 | tf_op jit(solution)/shard_map/ppermute | solution.py:901
  509.7 41.1 %all-to-all-start.4 = ((bf16[4,256,384]{2,1,0:T(8,128)(2,1)}), bf16[4,256,384]{2,1,0:T(8,128)(2,1)}, u32[]{:S(2)}, u32[]{:S(2)}) async-start(bf16[4,256,384]{2,1,0:T(8,128)(2,1)} %add_rows.1), calls=%async_computation.6 | async-start | bytes 1572864 | tf_op jit(solution)/shard_map/all_to_all | solution.py:1332
  514.0 17.2 %collective-permute-start.51 = (bf16[128,2048]{1,0:T(8,128)(2,1)S(1)}, bf16[128,2048]{1,0:T(8,128)(2,1)S(1)}, u32[]{:S(2)}, u32[]{:S(2)}) collective-permute-start(bf16[128,2048]{1,0:T(8,128)(2,1)S(1)} %copy-done.98), channel_id=1, source_target_pairs={{0,1},{1,0},{2,3},{3,2},{4,5},{5,4},{6,7},{7,6},{8,9},{9,8},{10,11... | collective-permute-start | bytes 1572872 | tf_op jit(solution)/shard_map/ppermute | solution.py:904
  515.8 15.5 %collective-permute-start.53 = (bf16[128,2048]{1,0:T(8,128)(2,1)S(1)}, bf16[128,2048]{1,0:T(8,128)(2,1)S(1)}, u32[]{:S(2)}, u32[]{:S(2)}) collective-permute-start(bf16[128,2048]{1,0:T(8,128)(2,1)S(1)} %add_convert_fusion), channel_id=1, source_target_pairs={{0,2},{2,0},{1,3},{3,1},{4,6},{6,4},{5,7},{7,5},{8,10},{10,8},{9,1... | collective-permute-start | bytes 1572872 | tf_op jit(solution)/shard_map/ppermute | solution.py:903
  517.7 13.4 %collective-permute-start.55 = (f32[8,2048]{1,0:T(8,128)S(1)}, f32[8,2048]{1,0:T(8,128)S(1)}, u32[]{:S(2)}, u32[]{:S(2)}) collective-permute-start(f32[8,2048]{1,0:T(8,128)S(1)} %add.293), channel_id=1, source_target_pairs={{0,2},{2,0},{1,3},{3,1},{4,6},{6,4},{5,7},{7,5},{8,10},{10,8},{9,1... | collective-permute-start | bytes 196616 | tf_op jit(solution)/shard_map/ppermute | solution.py:1285
  543.1 10.8 %collective-permute-start.58 = (f32[8,2048]{1,0:T(8,128)S(1)}, f32[8,2048]{1,0:T(8,128)S(1)}, u32[]{:S(2)}, u32[]{:S(2)}) collective-permute-start(f32[8,2048]{1,0:T(8,128)S(1)} %add.296), channel_id=1, source_target_pairs={{0,16},{8,24},{16,0},{24,8},{1,17},{9,25},{17,1},{25,9},{2,18},{10... | collective-permute-start | bytes 196616 | tf_op jit(solution)/shard_map/ppermute | solution.py:916
  (144 other events, 1044.5 us)
Sparse Core Ops, SparseCore 0:
  153.8 78.0 all-gather.1
  254.8 97.3 reduce-scatter.3
  354.6 76.5 reduce-scatter.5
  448.7 38.5 reduce-scatter.7

commit v4 on v3

--- a/solution.py
+++ b/solution.py
@@ -128,7 +128,14 @@
     tok_k_ref,
     *refs,
 ):
-    dq_ref, dk_ref, dv_ref, kt_ref, dk_acc, dv_acc = refs[-6:]
+    dq_ref, dk_ref, dv_ref, inner_q_ref, inner_k_ref, kt_ref, dk_acc, dv_acc = refs[-8:]
+
+    def row_sums(a):
+        ones = jnp.ones((8, a.shape[1]), f32)
+        return lax.dot_general(
+            ones, a, DOT_NT, precision=lax.Precision.HIGHEST, preferred_element_type=f32
+        )[:1]
+
     steps = k_ref.shape[0] // chunk
 
     @pl.when(pl.program_id(0) == 0)
@@ -171,11 +178,15 @@
         jnp.zeros((queries.shape[1], queries.shape[0]), f32),
         unroll=steps <= 4,
     )
-    dq_ref[...] = dq_in_ref[...] + (dq_t * grad_scale).T
+    d_query = dq_in_ref[...] + (dq_t * grad_scale).T
+    dq_ref[...] = d_query
+    inner_q_ref[...] = row_sums(d_query * queries.astype(f32))
 
     @pl.when(pl.program_id(0) == pl.num_programs(0) - 1)
     def _():
-        dk_ref[...] = (dk_acc[...] * grad_scale).astype(dk_ref.dtype)
+        d_key = dk_acc[...] * grad_scale
+        dk_ref[...] = d_key.astype(dk_ref.dtype)
+        inner_k_ref[...] = row_sums(d_key * k_ref[...].astype(f32))
         dv_ref[...] = dv_acc[...].astype(dv_ref.dtype)
 
 
@@ -210,11 +221,13 @@
             pl.BlockSpec((keys, 1), lambda i: (0, 0)),
         ]
         + [pl.BlockSpec(memory_space=pl.ANY)] * len(earlier),
-        out_specs=[head, whole, whole],
+        out_specs=[head, whole, whole, row, pl.BlockSpec((1, keys), lambda i: (0, 0))],
         out_shape=[
             jax.ShapeDtypeStruct((rows, HEAD_DIM), f32),
             jax.ShapeDtypeStruct((keys, HEAD_DIM), out_type),
             jax.ShapeDtypeStruct((keys, HEAD_DIM), out_type),
+            jax.ShapeDtypeStruct((1, rows), f32),
+            jax.ShapeDtypeStruct((1, keys), f32),
         ],
         scratch_shapes=[
             pltpu.VMEM((HEAD_DIM, keys), bf16),
@@ -229,11 +242,13 @@
 
 def pack_kernel(raw0_ref, raw1_ref, inv_ref, cos_ref, sin_ref, gain_ref, q_ref, k_ref):
     half = raw0_ref.shape[1]
+    cos_tab = jnp.concatenate([cos_ref[...]] * 2, axis=1)
+    sin_tab = jnp.concatenate([-sin_ref[...], sin_ref[...]], axis=1)
     for i, raw_ref in enumerate((raw0_ref, raw1_ref)):
         r = slice(i * half, (i + 1) * half)
         for j in range(2):
             u = raw_ref[j] * inv_ref[r, j : j + 1] * gain_ref[j : j + 1, :]
-            turned = u * cos_ref[r, :] + pltpu.roll(u, HEAD_DIM // 2, 1) * sin_ref[r, :]
+            turned = u * cos_tab[r, :] + pltpu.roll(u, HEAD_DIM // 2, 1) * sin_tab[r, :]
             (q_ref, k_ref)[j][0, r, :] = turned.astype(bf16)
 
 
@@ -243,7 +258,7 @@
     heads = raw0.shape[2] // HEAD_DIM
     raw = pl.BlockSpec((2, half, HEAD_DIM), lambda h: (0, 0, h))
     head = pl.BlockSpec((1, rows, HEAD_DIM), lambda h: (h, 0, 0))
-    table = pl.BlockSpec((rows, HEAD_DIM), lambda h: (0, 0))
+    table = pl.BlockSpec((rows, HEAD_DIM // 2), lambda h: (0, 0))
     return pl.pallas_call(
         pack_kernel,
         grid=(heads,),
@@ -263,7 +278,19 @@
 
 
 def raw_grad_kernel(
-    dq_ref, dk_ref, dv_ref, q_ref, k_ref, coef_ref, cos_ref, sin_ref, gain_ref, *refs
+    dq_ref,
+    dk_ref,
+    dk_far_ref,
+    dv_ref,
+    dv_far_ref,
+    q_ref,
+    k_ref,
+    inv_ref,
+    inner_ref,
+    cos_ref,
+    sin_ref,
+    gain_ref,
+    *refs,
 ):
     out_ref, sum_ref = refs[-2:]
 
@@ -271,25 +298,28 @@
     def _():
         sum_ref[...] = jnp.zeros_like(sum_ref)
 
-    cos_tab = cos_ref[...]
-    sin_tab = sin_ref[...]
+    cos_tab = jnp.concatenate([cos_ref[...]] * 2, axis=1)
+    sin_tab = jnp.concatenate([-sin_ref[...], sin_ref[...]], axis=1)
+    block = inv_ref.shape[1]
+    coef = jnp.concatenate([inv_ref[...], inner_ref[...], jnp.zeros((4, block), f32)]).T
 
     def turn_back(u):
         return u * cos_tab - pltpu.roll(u, HEAD_DIM // 2, 1) * sin_tab
 
-    for j, (grad_ref, rows_ref) in enumerate(((dq_ref, q_ref), (dk_ref, k_ref))):
+    d_key = dk_ref[...] + dk_far_ref[...].astype(f32)
+    for j, (grad, rows_ref) in enumerate(((dq_ref[...], q_ref), (d_key, k_ref))):
         gain = gain_ref[j : j + 1, :]
         cols = slice(j * HEAD_DIM, (j + 1) * HEAD_DIM)
-        d_norm = turn_back(grad_ref[...])
+        d_norm = turn_back(grad)
         hat = turn_back(rows_ref[...].astype(f32)) / gain
         sum_ref[j : j + 1, :] += jnp.sum(d_norm * hat, axis=0, keepdims=True)
-        inv = coef_ref[:, 2 * j : 2 * j + 1]
-        inner = coef_ref[:, 2 * j + 1 : 2 * j + 2]
+        inv = coef[:, j : j + 1]
+        inner = coef[:, 2 + j : 3 + j]
         out_ref[:, cols] = (inv * (d_norm * gain - hat * inner)).astype(bf16)
-    out_ref[:, 2 * HEAD_DIM :] = dv_ref[...].astype(bf16)
-
-
-def raw_grad(d_query, d_key, d_value, queries, keys, coef, cos_tab, sin_tab, gains, earlier):
+    out_ref[:, 2 * HEAD_DIM :] = (dv_ref[...] + dv_far_ref[...].astype(f32)).astype(bf16)
+
+
+def raw_grad(d_query, d_key, d_value, queries, keys, inv, inner, cosine, sine, gains, earlier):
     rows = queries.shape[0]
     block = min(512, rows)
 
@@ -301,10 +331,11 @@
         raw_grad_kernel,
         grid=(rows // block,),
         in_specs=[
-            *[wide(HEAD_DIM)] * 5,
-            wide(4),
-            wide(HEAD_DIM),
-            wide(HEAD_DIM),
+            *[wide(HEAD_DIM)] * 7,
+            pl.BlockSpec((2, block), lambda i: (0, i)),
+            pl.BlockSpec((2, block), lambda i: (0, i)),
+            wide(HEAD_DIM // 2),
+            wide(HEAD_DIM // 2),
             whole,
             pl.BlockSpec(memory_space=pl.ANY),
         ],
@@ -315,7 +346,7 @@
         ],
         cost_estimate=cost(6),
         name="raw_grad",
-    )(d_query, d_key, d_value, queries, keys, coef, cos_tab, sin_tab, gains, earlier)
+    )(d_query, *d_key, *d_value, queries, keys, inv, inner, cosine, sine, gains, earlier)
 
 
 def weight_grad_kernel(experts, out_block, at_ref, *refs):
@@ -520,8 +551,8 @@
     )(grads, weights, *into, *earlier)
 
 
-def project_grad_kernel(x_ref, w_ref, n_ref, *refs):
-    own_ref, other_ref, sum_ref, rows = refs[-4:]
+def project_grad_kernel(x_ref, w_ref, *refs):
+    own_ref, other_ref, rows = refs[-3:]
     count = own_ref.shape[0]
     heads = x_ref.shape[0]
     cols = heads * HEAD_DIM
@@ -541,15 +572,13 @@
         y = term if y is None else y + term
     own_ref[...] = y[:count].astype(bf16)
     other_ref[...] = y[count:].astype(bf16)
-    sum_ref[...] = jnp.sum(y * n_ref[...].astype(f32), axis=0, keepdims=True)
-
-
-def project_grad_half(parts, half, weights, normed, earlier=()):
+
+
+def project_grad_half(parts, half, weights, earlier=()):
     heads, count, cols = parts.shape
     count //= 2
     width = weights.shape[1]
     block = width // 4
-    out = pl.BlockSpec((count, block), lambda i: (0, i))
     part = pl.BlockSpec((count // 2, block), lambda i: (0, i))
     return pl.pallas_call(
         project_grad_kernel,
@@ -557,23 +586,22 @@
         in_specs=[
             pl.BlockSpec((heads, count, cols), lambda i: (0, half, 0)),
             pl.BlockSpec((3, block, weights.shape[2]), lambda i: (0, i, 0)),
-            out,
         ]
         + waits(earlier),
-        out_specs=[part, part, pl.BlockSpec((1, block), lambda i: (0, i))],
+        out_specs=[part, part],
         out_shape=[
             jax.ShapeDtypeStruct((count // 2, width), bf16),
             jax.ShapeDtypeStruct((count // 2, width), bf16),
-            jax.ShapeDtypeStruct((1, width), f32),
         ],
         scratch_shapes=[pltpu.VMEM((count, heads * cols), bf16)],
         compiler_params=params(24),
         cost_estimate=cost(6),
         name="project_grad",
-    )(parts, weights, normed, *earlier)
-
-
-def qkv_grad_kernel(wide_ref, grad_ref, grad_other_ref, out_ref, out_other_ref, tall, wide_t):
+    )(parts, weights, *earlier)
+
+
+def qkv_grad_kernel(wide_ref, grad_ref, grad_other_ref, *refs):
+    out_ref, out_other_ref, tall, wide_t = refs[-4:]
     rows, cols = grad_ref.shape
 
     @pl.when(pl.program_id(0) == 0)
@@ -591,7 +619,7 @@
     out_other_ref[...] = out[:, cols:]
 
 
-def qkv_grad(wide, grad, grad_other, z_count):
+def qkv_grad(wide, grad, grad_other, z_count, earlier=()):
     assert z_count == 4
     rows, width = wide.shape
     cols = grad.shape[1]
@@ -601,14 +629,14 @@
     return pl.pallas_call(
         qkv_grad_kernel,
         grid=(width // block,),
-        in_specs=[pl.BlockSpec((rows, block), lambda i: (0, i)), whole, whole],
+        in_specs=[pl.BlockSpec((rows, block), lambda i: (0, i)), whole, whole] + waits(earlier),
         out_specs=[out, out],
         scratch_shapes=[pltpu.VMEM((rows, 2 * cols), bf16), pltpu.VMEM((block, rows), bf16)],
         out_shape=[jax.ShapeDtypeStruct((width, cols), bf16)] * 2,
         compiler_params=params(40),
         cost_estimate=cost(10),
         name="qkv_grad",
-    )(wide, grad, grad_other)
+    )(wide, grad, grad_other, *earlier)
 
 
 def arrange(near, z_pos, earlier=()):
@@ -669,7 +697,7 @@
         out_shape=jax.ShapeDtypeStruct((count, width, cols), bf16),
         scratch_shapes=[pltpu.VMEM((width, 2 * half), bf16)],
         compiler_params=params(24),
-        cost_estimate=cost(0.1),
+        cost_estimate=cost(3.5),
         name="own_grad",
     )(*wide_h, *narrow_h, *earlier)
 
@@ -702,7 +730,9 @@
 
 def pass_rows(a, earlier):
     rows, width = a.shape
-    spec = pl.BlockSpec((rows, width // 2), lambda j: (0, j))
+    spec = pl.BlockSpec((rows // 2, width), lambda j: (j, 0))
+    if rows < 32:
+        spec = pl.BlockSpec((rows, width // 2), lambda j: (0, j))
     return pl.pallas_call(
         pass_kernel,
         grid=(2,),
@@ -742,10 +772,10 @@
 
 
 def add_rows(a, b, earlier=()):
-    spec = pl.BlockSpec((1, *a.shape[1:]), lambda i: (i, 0, 0))
+    spec = pl.BlockSpec((a.shape[0] // 2, *a.shape[1:]), lambda i: (i, 0, 0))
     return pl.pallas_call(
         add_kernel,
-        grid=(a.shape[0],),
+        grid=(2,),
         in_specs=[spec, spec] + waits(earlier),
         out_specs=spec,
         out_shape=jax.ShapeDtypeStruct(a.shape, bf16),
@@ -755,8 +785,44 @@
     )(a, b, *earlier)
 
 
-def stack_kernel(a_ref, b_ref, gain_ref, second_ref, qk_ref, router_ref, out_ref):
-    out_ref[0:1, :] = (a_ref[...] + b_ref[...]) / gain_ref[0:1, :]
+def first_gain_kernel(z_ref, w_ref, grad_ref, gain_ref, out_ref):
+    total = None
+    for k in range(3):
+        cols = slice(k * HEAD_DIM, (k + 1) * HEAD_DIM)
+        term = w_ref[k].astype(f32) * grad_ref[:, cols].astype(f32)
+        total = term if total is None else total + term
+    ones = jnp.ones((8, HEAD_DIM), f32)
+    total = lax.dot_general(
+        ones, total, DOT_NT, precision=lax.Precision.HIGHEST, preferred_element_type=f32
+    )
+    out_ref[...] = total[:1] / gain_ref[...]
+
+
+def first_gain(weights, grad, gain, z_pos):
+    width = grad.shape[0]
+    block = width // 4
+    line = pl.BlockSpec((1, block), lambda i, z: (0, i))
+    return pl.pallas_call(
+        first_gain_kernel,
+        grid_spec=pltpu.PrefetchScalarGridSpec(
+            num_scalar_prefetch=1,
+            grid=(4,),
+            in_specs=[
+                pl.BlockSpec((3, block, HEAD_DIM), lambda i, z: (0, i, z[0])),
+                pl.BlockSpec((block, grad.shape[1]), lambda i, z: (i, 0)),
+                line,
+            ],
+            out_specs=line,
+        ),
+        out_shape=jax.ShapeDtypeStruct((1, width), f32),
+        compiler_params=params(),
+        cost_estimate=cost(2),
+        name="first_gain",
+    )(z_pos.reshape(1), weights, grad, gain.reshape(1, width))
+
+
+def stack_kernel(first_ref, second_ref, qk_ref, router_ref, out_ref):
+    out_ref[0:1, :] = first_ref[...]
     out_ref[1:2, :] = second_ref[...]
     out_ref[2:4, :] = qk_ref[...]
     out_ref[4:8, :] = router_ref[...]
@@ -770,6 +836,22 @@
         cost_estimate=cost(0.1),
         name="stack_rows",
     )(*rows)
+
+
+def stack_inner_kernel(q_ref, k_ref, k_far_ref, *refs):
+    refs[-1][0:1, :] = q_ref[...]
+    refs[-1][1:2, :] = k_ref[...] + k_far_ref[...]
+
+
+def stack_inner(inner_q, inner_k, inner_k_far, earlier):
+    return pl.pallas_call(
+        stack_inner_kernel,
+        in_specs=[pl.BlockSpec(memory_space=pltpu.VMEM)] * 3 + waits(earlier),
+        out_shape=jax.ShapeDtypeStruct((2, inner_q.shape[1]), f32),
+        compiler_params=params(),
+        cost_estimate=cost(0.1),
+        name="stack_inner",
+    )(inner_q, inner_k, inner_k_far, *earlier)
 
 
 def row_sum(refs):
@@ -888,13 +970,15 @@
     return inv_rows * (grad_hat - hat_rows * jnp.mean(grad_hat * hat_rows, axis=-1, keepdims=True))
 
 
-def gather_halves(rows, beside=(), earlier=()):
+def gather_near(rows):
     far = lax.ppermute(rows, "y", SWAP)
-    core = lax.ppermute(rows, "c", SWAP)
+    return join_rows(rows, lax.ppermute(rows, "c", SWAP)), far
+
+
+def gather_far(far, beside=(), earlier=()):
     if beside:
         far = pass_rows(far, beside)
-    far_core = lax.ppermute(far, "c", SWAP)
-    return [jnp.concatenate([rows, core]), join_rows(far, far_core, earlier)]
+    return join_rows(far, lax.ppermute(far, "c", SWAP), earlier)
 
 
 def scatter_halves(near, far):
@@ -984,7 +1068,8 @@
     inv_first = lax.rsqrt(jnp.mean(resid_in * resid_in, axis=-1, keepdims=True) + norm_eps)
     hat_first = resid_in * inv_first
     normed = (hat_first * norm_gains[0]).astype(bf16)
-    normed_h = gather_halves(normed)
+    normed_near, normed_far = gather_near(normed)
+    normed_h = [normed_near, gather_far(normed_far)]
 
     start_all = token_places(seq_lengths, permutation)
     shape = (z_count, x_count, 2, 2, local_rows)
@@ -1004,8 +1089,6 @@
     )
     angles = (tok_own - start_own).astype(f32)[:, None] * frequency[None, :]
     cosine, sine = jnp.cos(angles), jnp.sin(angles)
-    cos_tab = jnp.concatenate([cosine, cosine], axis=1)
-    sin_tab = jnp.concatenate([-sine, sine], axis=1)
 
     raw0, square0, v0 = project(normed_h[0], qkv_b)
     raw1, square1, v1 = project(normed_h[1], qkv_b, (v0,))
@@ -1036,16 +1119,16 @@
         return lax.all_gather(a, "x", axis=0)
 
     v_heads = jnp.concatenate([v0, v1], axis=1)
-    values = to_heads(v_heads)
-    values_far = from_x(values)
     q_heads, k_heads = pack_heads(
         raw0,
         raw1,
         inv_qk.T,
-        lax.dynamic_slice_in_dim(cos_tab, z_pos * tok_rows, tok_rows),
-        lax.dynamic_slice_in_dim(sin_tab, z_pos * tok_rows, tok_rows),
+        lax.dynamic_slice_in_dim(cosine, z_pos * tok_rows, tok_rows),
+        lax.dynamic_slice_in_dim(sine, z_pos * tok_rows, tok_rows),
         gain_qk,
     )
+    values = pass_rows(to_heads(v_heads), (k_heads,))
+    values_far = from_x(values)
     keys = to_heads_apart(k_heads, (values_far,))
     out_b = attn_out.astype(bf16)
     keys_far = from_x(keys)
@@ -1076,12 +1159,11 @@
         return parts
 
     attn_parts = to_tokens(attn_f.astype(bf16), HEAD_DIM)
+    normed_pick = pick_half(normed_h, c_pos, (attn_parts,))
     attn_far = attn_out_half(attn_parts, 1, out_b)
     attn_near = attn_out_half(attn_parts, 0, out_b)
     attn_y, attn_sent = scatter_halves(attn_near, attn_far)
-    normed_pick = pick_half(normed_h, c_pos, (attn_sent,))
     normed_line = lax.all_gather(normed_pick, "z", axis=0, tiled=True)
-    attn_there = lax.ppermute(attn_parts, "x", SWAP) if pair else attn_sent
     gu_b = round_weights(gate_up, (attn_sent,))
     residual, mixed_rows = row_call(
         mix_kernel,
@@ -1089,11 +1171,10 @@
         (block_in,),
         norm_gains[1],
         (f32, bf16),
-        (gu_b, normed_pick, attn_there),
+        (gu_b, normed_pick),
     )
     down_b = round_weights(down, (mixed_rows,))
-    mixed_h = gather_halves(mixed_rows, (down_b,))
-    mixed_far = [far_wide([m]) for m in mixed_h] if pair else [mixed_rows, mixed_rows]
+    mixed_near, mixed_far = gather_near(mixed_rows)
 
     def halves(a):
         return a[: a.shape[0] // 2], a[a.shape[0] // 2 :]
@@ -1106,66 +1187,58 @@
         (route_rows[:, :, None] == jnp.arange(experts, dtype=jnp.int32)[None, None, :]).astype(f32),
         axis=1,
     )
+
+    def expert_rows(mixed, choose):
+        prob = jax.nn.softmax(jnp.dot(mixed, router_b, preferred_element_type=f32), axis=-1)
+        gate_w = prob * choose
+        gate_in, up_in = jnp.einsum("td,kedf->ketf", mixed, gu_b, preferred_element_type=f32)
+        gate_sig = jax.nn.sigmoid(gate_in)
+        hidden = (gate_w.T[:, :, None] * (gate_in * gate_sig) * up_in).astype(bf16)
+        y = jnp.einsum("etf,edf->td", hidden, down_b, preferred_element_type=f32)
+        return y.astype(bf16), hidden, (mixed, choose, prob, gate_w, gate_in, up_in)
+
     choose_h = halves(choose)
-    prob_h = [
-        jax.nn.softmax(jnp.dot(m, router_b, preferred_element_type=f32), axis=-1)
-        for m in mixed_h
-    ]
-    gate_w_h = [p * ch for p, ch in zip(prob_h, choose_h)]
-    pre_h = [
-        jnp.einsum("td,kedf->ketf", m, gu_b, preferred_element_type=f32) for m in mixed_h
-    ]
-    hidden_h = []
-    for pre, gate_w in zip(pre_h, gate_w_h):
-        gate_act = pre[0] * jax.nn.sigmoid(pre[0])
-        hidden_h.append((gate_w.T[:, :, None] * gate_act * pre[1]).astype(bf16))
-    expert_y, _ = scatter_halves(
-        *[
-            halves(
-                jnp.einsum("etf,edf->td", h, down_b, preferred_element_type=f32).astype(bf16)
-            )
-            for h in hidden_h
-        ]
-    )
+    near_y, hidden0, kept0 = expert_rows(mixed_near, choose_h[0])
+    mixed_h = [mixed_near, gather_far(mixed_far, (down_b,), (near_y,))]
+    mixed_far = [far_wide([m]) for m in mixed_h] if pair else [mixed_rows, mixed_rows]
+    far_y, hidden1, kept1 = expert_rows(mixed_h[1], choose_h[1])
+    hidden_h = [hidden0, hidden1]
+    expert_y, _ = scatter_halves(halves(near_y), halves(far_y))
     block_out, cot_local, cot_b = row_call(
         gap_kernel, expert_y, (residual, target), None, (bf16, f32, bf16),
         (mixed_far[0],),
     )
-    cot_h = gather_halves(cot_b, earlier=(mixed_far[1], normed_line))
-
-    d_pre_h = []
-    d_mixed_parts = []
-    router_parts = []
-    for cot, pre, gate_w, prob, ch, mixed in zip(
-        cot_h, pre_h, gate_w_h, prob_h, choose_h, mixed_h
-    ):
+    def expert_rows_back(cot, kept):
+        mixed, choose, prob, gate_w, gate_in, up_in = kept
         d_hid = (
             jnp.einsum("td,edf->etf", cot, down_b, preferred_element_type=f32)
             .astype(bf16)
             .astype(f32)
         )
-        gate_in, up_in = pre[0], pre[1]
         gate_sig = jax.nn.sigmoid(gate_in)
         gate_act = gate_in * gate_sig
         d_gate_w = jnp.sum(d_hid * gate_act * up_in, axis=-1).T
         scaled = d_hid * gate_w.T[:, :, None]
         d_gate_in = scaled * up_in * gate_sig * (1.0 + gate_in * (1.0 - gate_sig))
-        d_up_in = scaled * gate_act
-        d_pre = jnp.stack([d_gate_in, d_up_in]).astype(bf16)
-        d_pre_h.append(d_pre)
-        d_prob = d_gate_w * ch
+        d_pre = jnp.stack([d_gate_in, scaled * gate_act]).astype(bf16)
+        d_prob = d_gate_w * choose
         d_logit = (prob * (d_prob - jnp.sum(prob * d_prob, axis=-1, keepdims=True))).astype(bf16)
-        d_mixed_parts.append(
-            (
-                jnp.einsum("ketf,kedf->td", d_pre, gu_b, preferred_element_type=f32)
-                + lax.dot_general(d_logit, router_b, DOT_NT, preferred_element_type=f32)
-            ).astype(bf16)
+        d_mixed = (
+            jnp.einsum("ketf,kedf->td", d_pre, gu_b, preferred_element_type=f32)
+            + lax.dot_general(d_logit, router_b, DOT_NT, preferred_element_type=f32)
+        ).astype(bf16)
+        router_part = lax.dot_general(
+            d_logit, mixed, (((0,), (0,)), ((), ())), preferred_element_type=f32
         )
-        router_parts.append(
-            lax.dot_general(d_logit, mixed, (((0,), (0,)), ((), ())), preferred_element_type=f32)
-        )
-    router_rows = router_parts[0] + router_parts[1]
-    d_mixed, d_mixed_sent = scatter_halves(*[halves(d) for d in d_mixed_parts])
+        return d_mixed, d_pre, router_part
+
+    cot_near, cot_far = gather_near(cot_b)
+    near_d, d_pre0, router0 = expert_rows_back(cot_near, kept0)
+    cot_h = [cot_near, gather_far(cot_far, (), (mixed_far[1], normed_line, near_d))]
+    far_d, d_pre1, router1 = expert_rows_back(cot_h[1], kept1)
+    router_rows = router0 + router1
+    d_pre_h = [d_pre0, d_pre1]
+    d_mixed, d_mixed_sent = scatter_halves(halves(near_d), halves(far_d))
     down_part = own_grad(cot_h, hidden_h, (d_mixed_sent,))
 
     def compact(a, taken):
@@ -1189,21 +1262,21 @@
             )
         ).astype(bf16)
 
+    d_pre_h = [d.reshape(2 * experts, -1, hidden_cols) for d in d_pre_h]
+    if pair:
+        d_pre_far = [
+            lax.ppermute(compact(d, r), "x", SWAP) for d, r in zip(d_pre_h, (route_rows[: tok_rows // 2], route_rows[tok_rows // 2 :]))
+        ]
     d_resid, d_resid_b, gain_second = row_call(
         resid_grad_kernel,
         d_mixed,
         (residual, cot_local),
         norm_gains[1],
         (f32, bf16, None),
-        (down_part,),
-    )
-    d_pre_h = [d.reshape(2 * experts, -1, hidden_cols) for d in d_pre_h]
-    if pair:
-        d_pre_far = [
-            lax.ppermute(compact(d, r), "x", SWAP) for d, r in zip(d_pre_h, (route_rows[: tok_rows // 2], route_rows[tok_rows // 2 :]))
-        ]
-    d_resid_h = gather_halves(d_resid_b, earlier=(d_pre_far[0],) if pair else ())
-    d_resid_far = [far_wide([d]) for d in d_resid_h] if pair else None
+        (down_part, d_pre_far[0]) if pair else (down_part,),
+    )
+    resid_near, resid_far = gather_near(d_resid_b)
+    d_resid_h = [resid_near, gather_far(resid_far, (), (d_pre_far[1],) if pair else ())]
     d_attn = attn_out_grad_half(d_resid_h[0], 0, out_b)
     d_attn = attn_out_grad_half(d_resid_h[1], 1, out_b, d_attn)
 
@@ -1224,14 +1297,14 @@
         )
     else:
         gate_up_part = plain_part(mixed_h, jnp.concatenate(d_pre_h, axis=1), "td,ntf->ndf")
-    down_part = lax.psum_scatter(down_part, ("z", "x"), scatter_dimension=1, tiled=True)
+    down_part = lax.psum_scatter(down_part, "z", scatter_dimension=1, tiled=True)
     gate_up_sum = lax.psum_scatter(gate_up_part, "z", scatter_dimension=1, tiled=True)
     d_kv = []
     inner_k = []
-    earlier = (gate_up_part, d_resid_far[0]) if pair else (gate_up_part,)
+    earlier = (gate_up_part,)
     for i, group in enumerate(groups):
         last = i == len(groups) - 1
-        d_query, *d_group = attend_grad(
+        d_query, *d_group, inner_q, inner_k_part = attend_grad(
             queries,
             d_out,
             row_lse,
@@ -1244,37 +1317,42 @@
             earlier,
         )
         d_kv.append(d_group)
-        if pair and not last:
-            out_part = weight_grad(
-                d_resid_h,
-                d_resid_far,
-                [(attn_parts, 0), (attn_parts, 1)],
-                [(attn_there, 0), (attn_there, 1)],
-                out_block,
-                x_pos,
-                earlier=(d_group[0],),
-            )
-            earlier = (down_part, out_part)
-        inner_k.append(jnp.sum(d_group[0].astype(f32) * group[0].astype(f32), axis=-1))
+        inner_k.append(inner_k_part)
+        if i == 0:
+            earlier = (down_part,)
     if pair:
         d_key, d_value = [
-            own + lax.ppermute(far, "x", SWAP).astype(f32) for far, own in zip(*d_kv)
+            (own, lax.ppermute(far, "x", SWAP)) for far, own in zip(*d_kv)
         ]
-        inner_k = inner_k[1] + lax.ppermute(inner_k[0], "x", SWAP)
+        inner = stack_inner(
+            inner_q, inner_k[1], lax.ppermute(inner_k[0], "x", SWAP), (d_key[1], d_value[1])
+        )
     else:
         d_key, d_value = [
-            lax.psum_scatter(jnp.stack(parts), "x", scatter_dimension=0).astype(f32)
+            (
+                lax.psum_scatter(jnp.stack(parts), "x", scatter_dimension=0).astype(f32),
+                jnp.zeros((line_rows, HEAD_DIM), bf16),
+            )
             for parts in zip(*d_kv)
         ]
         inner_k = lax.psum_scatter(jnp.stack(inner_k), "x", scatter_dimension=0)
-    inner = jnp.stack([jnp.sum(d_query * queries.astype(f32), axis=-1), inner_k])
+        inner = jnp.concatenate([inner_q, inner_k])
     inner = sum_line(sum_near(inner.reshape(2, z_count, 2, 2, local_rows)), z_count)
     inner = inner.reshape(2, line_rows) / model_width
     inv_line = jnp.moveaxis(inv_line, 0, 1).reshape(2, line_rows)
-    coef = jnp.stack([inv_line[0], inner[0], inv_line[1], inner[1]], axis=1)
     head_gain = lax.dynamic_slice_in_dim(gain_qk, z_pos * HEAD_DIM, HEAD_DIM, 1)
     d_raw, gain_sums = raw_grad(
-        d_query, d_key, d_value, queries, keys, coef, cos_tab, sin_tab, head_gain, out_part if pair else d_query
+        d_query,
+        d_key,
+        d_value,
+        queries,
+        keys,
+        inv_line,
+        inner,
+        cosine,
+        sine,
+        head_gain,
+        gate_up_sum,
     )
     gain_full = lax.dynamic_update_slice_in_dim(
         jnp.zeros((2, model_width), f32), gain_sums, (wt_pos * z_count + z_pos) * HEAD_DIM, 1
@@ -1283,16 +1361,10 @@
     def sum_all(a):
         a = a + lax.ppermute(a, "c", SWAP)
         a = a + lax.ppermute(a, "y", SWAP)
+        a = a + lax.ppermute(a, "x", SWAP) if pair else lax.psum(a, "x")
         a = pass_rows(a, (input_grad,))
-        a = a + lax.ppermute(a, "x", SWAP) if pair else lax.psum(a, "x")
         return sum_line(a, z_count)
 
-    if pair:
-        out_sum = lax.psum_scatter(out_part, "z", scatter_dimension=1, tiled=True)
-    else:
-        out_part = own_grad(d_resid_h, (attn_parts, attn_parts), (d_raw,))
-        out_sum = lax.psum_scatter(out_part, ("z", "x"), scatter_dimension=1, tiled=True)
-    out_sum = jnp.moveaxis(out_sum, 0, 1).reshape(out_block, head_cols).astype(f32)
     grad_mine, grad_other = qkv_grad(
         normed_line, d_raw, lax.ppermute(d_raw, "c", SWAP), z_count
     )
@@ -1302,6 +1374,9 @@
         jnp.stack([grad_mine, grad_other]),
         jnp.stack([grad_other, grad_mine]),
     ).reshape(z_count, x_count, out_block, 3 * HEAD_DIM)
+    gain_first = first_gain(
+        qkv_b, qkv_full.reshape(model_width, 3 * HEAD_DIM), norm_gains[0], z_pos
+    )
     qkv_line = jnp.moveaxis(qkv_full, 1, 0)
     if pair:
         qkv_line = (
@@ -1312,10 +1387,14 @@
         qkv_line = scatter_x(qkv_line).astype(bf16)
         qkv_line = (qkv_line, jnp.zeros_like(qkv_line))
     d_proj = to_tokens(d_raw, 3 * HEAD_DIM)
-    *far_n, gain_first1 = project_grad_half(
-        d_proj, 1, qkv_b, normed_h[1], (qkv_line[1], gate_up_sum)
-    )
-    *near_n, gain_first0 = project_grad_half(d_proj, 0, qkv_b, normed_h[0], (far_n[0],))
+    out_part = own_grad(
+        d_resid_h, (attn_parts, attn_parts), (d_proj, qkv_line[1])
+    )
+    far_n = project_grad_half(
+        d_proj, 1, qkv_b, (out_part,)
+    )
+    out_part = lax.psum_scatter(out_part, "z", scatter_dimension=1, tiled=True)
+    near_n = project_grad_half(d_proj, 0, qkv_b, (far_n[0],))
     d_normed, _ = scatter_halves(near_n, far_n)
     (input_grad,) = row_call(
         input_grad_kernel,
@@ -1324,8 +1403,8 @@
         norm_gains[0],
         (bf16,),
     )
-
-    small = sum_all(stack_rows(gain_first0, gain_first1, norm_gains, gain_second, gain_full, router_rows))
+    small = sum_all(stack_rows(gain_first, gain_second, gain_full, router_rows))
+
     gains_grad = small[:4]
     router_grad = small[4:].T
 
@@ -1338,15 +1417,18 @@
         .reshape(3, out_block, head_cols)
         .astype(f32)
     )
+    def own_block(a):
+        return scatter_x(jnp.moveaxis(a.reshape(a.shape[0], x_count, out_block, -1), 1, 0))
+
     return (
         block_out,
         input_grad,
         qkv_part,
-        out_sum,
+        jnp.moveaxis(own_block(out_part), 0, 1).reshape(out_block, head_cols),
         gains_grad,
         router_grad,
         gate_up_sum.astype(f32).reshape(2, experts, out_block, hidden_cols),
-        down_part.astype(f32),
+        own_block(down_part),
     )
 
 

time: 569 us -> 553 us (0.972)
  other arithmetic: 58.5 us -> 37.4 us
  waiting for transfers between devices: 188 us -> 170 us
  blocking collectives: 0 us -> 17.6 us
  Pallas kernels: 123 us -> 131 us
    all_to_all x0 -> x1, blocking collectives: none -> 17.6 us  [to_heads(): lax.all_to_all(parts, 'z', 0, 0, tiled=True).reshape(line_rows, HEAD_DIM)]
    all_to_all x2, waiting for transfers between devices: 49.3 us -> 34.1 us  [to_tokens(): lax.all_to_all(rows.reshape(z_count, tok_rows, cols), 'z', 0, 0, tiled=True)]
    ppermute x4, waiting for transfers between devices: 22.3 us -> 9.42 us  [scatter_halves(): far_got = lax.ppermute(sent, 'y', SWAP)]
    ppermute x6, waiting for transfers between devices: 7.66 us -> 19.5 us  [sum_line(): a = a + lax.ppermute(a, 'z', [(i, i ^ step) for i in range(z_count)])]
    ppermute x4 -> x2, waiting for transfers between devices: 0.01 us -> 10.3 us  [far_wide(): return lax.ppermute(of_parity(rows_h, 1 - x_pos), 'x', SWAP)]
    ppermute x2, waiting for transfers between devices: 18 us -> 9.91 us  [local(): lax.ppermute(compact(d, r), 'x', SWAP)]
    concatenate x3 -> x0, other arithmetic: 7.85 us -> none  [the longest x1 4.32 us: local(): cos_tab = jnp.concatenate([cosine, cosine], axis=1)]
    ppermute x1, waiting for transfers between devices: 0.01 us -> 7.82 us  [local(): lax.ppermute(route_rows.T.astype(f32), 'x', SWAP).T.astype(jnp.int32)]
  transfers between devices with their start and end apart: 68 -> 66, of which waited for: 28 -> 32; matrix products, arithmetic and copies ran while one was open for 15% -> 12% of each run, Pallas kernels for 17% -> 17%
where the time goes in v4:
time: 553 us; the launch traced here: 544 us
  waiting for transfers between devices  170 us (31%)
  Pallas kernels  131 us (24%)
  local copies, waits for them, and re-layouts  81.9 us (15%)
  starting transfers between devices  69.1 us (12%)
  other arithmetic  37.4 us (7%)
  matrix products  21.2 us (4%)
  blocking collectives  17.6 us (3%)
  between operations  16 us (3%)
    unnamed x214, local copies, waits for them, and re-layouts  61.6 us
    all_to_all x2, waiting for transfers between devices, to_tokens(): lax.all_to_all(rows.reshape(z_count, tok_rows, cols), 'z', 0, 0, tiled=True)  34.1 us
    pallas_call x2, Pallas kernels, attend_grad(): pl.pallas_call(functools.partial(attend_grad_kernel, chunk, LOG2E / math....  32.1 us
    ppermute x4, waiting for transfers between devices, gather_near(): far = lax.ppermute(rows, 'y', SWAP)  28.6 us
    ppermute x6, waiting for transfers between devices, sum_line(): a = a + lax.ppermute(a, 'z', [(i, i ^ step) for i in range(z_count)])  19.5 us
    all_to_all x1, blocking collectives, to_heads(): lax.all_to_all(parts, 'z', 0, 0, tiled=True).reshape(line_rows, HEAD_DIM)  17.6 us
    ppermute x6, waiting for transfers between devices, to_heads_apart(): lax.ppermute(there, 'z', [(i, (i + d) % z_count) for i in range(z_count)])  17 us
    pallas_call x1, Pallas kernels, attend(): pl.pallas_call(functools.partial(attend_kernel, len(key_groups), chunk, L...  16.9 us
  transfers between devices with their start and end apart: 66, of which 32 were waited for; matrix products, arithmetic and copies ran while one was open for 12% of the time, Pallas kernels for 17%

profile of v4, /device:TPU:0, one launch (start us, length us, event | category | flops | bytes accessed | tf_op | source)
XLA Modules:
  0.0 544.1 jit_solution(16697222077332073560)
XLA Ops:
  17.7 8.0 %convert_element_type.183.w_ref = bf16[3,2048,512]{2,1,0:T(8,128)(2,1)} convert(f32[3,2048,512]{2,1,0:T(8,128)} %param.16) | non-fusion elementwise | flops 3145728 | bytes 18874368 | tf_op jit(solution)/shard_map/convert_element_type | solution.py:1035
  26.6 3.7 multiply_sine_fusion
  35.8 4.7 project.2
  40.9 4.7 project.3
  47.8 4.8 all-to-all-start
  57.2 5.1 pack_heads.1
  62.3 5.1 all-to-all-done
  73.5 5.1 collective-permute-done.10.refs_3_
  80.1 3.5 collective-permute-done.9.refs_2_
  85.1 3.3 collective-permute-start.6
  93.6 3.8 collective-permute-done.6.refs_2_
  100.4 16.9 %attend.1 = (f32[2048,128]{1,0:T(8,128)S(1)}, f32[1,2048]{1,0:T(1,128)S(1)}) custom-call(bf16[2048,128]{1,0:T(8,128)(2,1)S(1)} %arrange.2.q_ref, s32[1,2048]{1,0:T(1,128)S(1)} %bitcast.300, s32[1,2048]{1,0:T(1,128)S(1)} %bitcast.305, bf16[2048,128]{1,0:T(8,128)(2,1)S(1)} %arrange.3.refs_0_.k_ref, bf16[2048,128]{1,0:T(8,128)(2,1)S(1)} %pass_rows.3.refs_1_.v_ref, ...), custom_call_target="tpu_custom_call" | custom-call | flops 19000000512 | bytes 1048576 | tf_op jit(solution)/shard_map/attend/pallas_call | solution.py:97
  119.2 3.9 all-to-all-start.1
  125.7 11.2 %all-to-all-done.1.x_ref.refs_0_.n0_ref.n1_ref = bf16[4,512,128]{2,1,0:T(8,128)(2,1)S(1)} async-done(((bf16[4,512,128]{2,1,0:T(8,128)(2,1)}), bf16[4,512,128]{2,1,0:T(8,128)(2,1)S(1)}, u32[]{:S(2)}, u32[]{:S(2)}) %all-to-all-start.1) | async-done | bytes 524320 | tf_op jit(solution)/shard_map/all_to_all | solution.py:1156
  148.6 6.5 %copy-done.75 = f32[2,4,2048,256]{3,2,1,0:T(8,128)S(1)} copy-done((f32[2,4,2048,256]{3,2,1,0:T(8,128)S(1)}, f32[2,4,2048,256]{3,2,1,0:T(8,128)}, u32[]{:S(2)}) %copy-start.75) | copy-done | bytes 16777240
  156.0 4.8 collective-permute-done.15.far_got
  164.9 3.5 copy-done.76
  168.8 7.5 %collective-permute-done.18.in_ref = bf16[128,2048]{1,0:T(8,128)(2,1)S(1)} collective-permute-done((bf16[128,2048]{1,0:T(8,128)(2,1)S(1)}, bf16[128,2048]{1,0:T(8,128)(2,1)S(1)}, u32[]{:S(2)}, u32[]{:S(2)}) %collective-permute-start.18) | collective-permute-done | bytes 524320 | tf_op jit(solution)/shard_map/ppermute | solution.py:974
  189.6 10.3 %collective-permute-done.22.refs_0_.refs_2_ = bf16[256,1024]{1,0:T(8,128)(2,1)S(1)} collective-permute-done((bf16[256,1024]{1,0:T(8,128)(2,1)S(1)}, bf16[256,1024]{1,0:T(8,128)(2,1)S(1)}, u32[]{:S(2)}, u32[]{:S(2)}) %collective-permute-start.22) | collective-permute-done | bytes 524320 | tf_op jit(solution)/shard_map/ppermute | solution.py:1062
  206.8 10.8 %collective-permute-done.25.a_ref = bf16[128,2048]{1,0:T(8,128)(2,1)S(1)} collective-permute-done((bf16[128,2048]{1,0:T(8,128)(2,1)S(1)}, bf16[128,2048]{1,0:T(8,128)(2,1)S(1)}, u32[]{:S(2)}, u32[]{:S(2)}) %collective-permute-start.25) | collective-permute-done | bytes 524320 | tf_op jit(solution)/shard_map/ppermute | solution.py:974
  234.7 3.9 fusion.31
  245.1 3.5 own_grad.2.refs_0_
  259.6 9.9 %collective-permute-done.30.refs_1_.refs_6_ = bf16[2,2,256,256]{3,2,1,0:T(8,128)(2,1)} collective-permute-done((bf16[2,2,256,256]{3,2,1,0:T(8,128)(2,1)}, bf16[2,2,256,256]{3,2,1,0:T(8,128)(2,1)}, u32[]{:S(2)}, u32[]{:S(2)}) %collective-permute-start.30) | collective-permute-done | bytes 524320 | tf_op jit(solution)/shard_map/ppermute | solution.py:1268
  277.5 3.2 resid_grad_kernel.1
  283.9 10.3 %collective-permute-done.31.a_ref = bf16[128,2048]{1,0:T(8,128)(2,1)S(1)} collective-permute-done((bf16[128,2048]{1,0:T(8,128)(2,1)S(1)}, bf16[128,2048]{1,0:T(8,128)(2,1)S(1)}, u32[]{:S(2)}, u32[]{:S(2)}) %collective-permute-start.31) | collective-permute-done | bytes 524320 | tf_op jit(solution)/shard_map/ppermute | solution.py:974
  295.3 7.8 %collective-permute-done.35 = f32[2,512]{0,1:T(8,128)S(1)} collective-permute-done((f32[2,512]{0,1:T(8,128)S(1)}, f32[2,512]{0,1:T(8,128)S(1)}, u32[]{:S(2)}, u32[]{:S(2)}) %collective-permute-start.35) | collective-permute-done | bytes 4128 | tf_op jit(solution)/shard_map/ppermute | solution.py:1185
  308.0 8.6 %weight_grad.1.refs_0_ = bf16[8,1024,256]{2,1,0:T(8,128)(2,1)S(1)} custom-call(s32[1]{0:T(128)} %bitcast.69.at_ref, bf16[256,2048]{1,0:T(8,128)(2,1)S(1)} %join_rows.10.refs_0_, bf16[256,2048]{1,0:T(8,128)(2,1)S(1)} %copy-done.5, bf16[256,1024]{1,0:T(8,128)(2,1)S(1)} %copy-done.42, bf16[256,1024]{1,0:T(8,128)(2,1)S(1)} %copy-done.55, ...), custom_call_target="tpu_custom_call" | custom-call | flops 100000000 | bytes 1048576 | tf_op jit(solution)/shard_map/weight_grad/pallas_call | solution.py:401
  320.6 17.6 %all_to_all.25 = bf16[4,512,128]{2,1,0:T(8,128)(2,1)S(1)} all-to-all(bf16[4,512,128]{2,1,0:T(8,128)(2,1)S(1)} %copy-done.24), channel_id=1, replica_groups=mesh['z'=4,'x'=2,'y'=2,'c'=2] {'z'}, dimensions={0} | all-to-all | bytes 1048576 | tf_op jit(solution)/shard_map/all_to_all | solution.py:1114
  339.9 16.5 %attend_grad.2 = (f32[2048,128]{1,0:T(8,128)S(1)}, bf16[2048,128]{1,0:T(8,128)(2,1)}, bf16[2048,128]{1,0:T(8,128)(2,1)}, f32[1,2048]{1,0:T(1,128)}, f32[1,2048]{1,0:T(1,128)S(1)}) custom-call(bf16[2048,128]{1,0:T(8,128)(2,1)S(1)} %copy-done.26, bf16[2048,128]{1,0:T(8,128)(2,1)S(1)} %bitcast.281, f32[1,2048]{1,0:T(1,128)S(1)} %get-tuple-element.66.lse_ref, ...), custom_call_target="tpu_custom_call" | custom-call | flops 500000000 | bytes 1048576 | tf_op jit(solution)/shard_map/attend_grad/pallas_call | solution.py:203
  360.6 15.6 %attend_grad.3 = (f32[2048,128]{1,0:T(8,128)S(1)}, f32[2048,128]{1,0:T(8,128)S(1)}, f32[2048,128]{1,0:T(8,128)S(1)}, f32[1,2048]{1,0:T(1,128)S(1)}, f32[1,2048]{1,0:T(1,128)S(1)}) custom-call(bf16[2048,128]{1,0:T(8,128)(2,1)S(1)} %copy-done.26, bf16[2048,128]{1,0:T(8,128)(2,1)S(1)} %bitcast.282, f32[1,2048]{1,0:T(1,128)S(1)} %get-tuple-element.66.lse_ref, ...), custom_call_target="tpu_custom_call" | custom-call | flops 500000000 | bytes 1048576 | tf_op jit(solution)/shard_map/attend_grad/pallas_call | solution.py:203
  384.6 4.0 collective-permute-done.38
  390.3 5.3 collective-permute-done.43
  396.8 4.6 collective-permute-done.44
  402.1 6.3 %reduce-scatter.6.cloned.1.call-done.refs_0_ = bf16[8,256,256]{2,1,0:T(8,128)(2,1)} async-done(((bf16[8,1024,256]{2,1,0:T(8,128)(2,1)}), bf16[8,256,256]{2,1,0:T(8,128)(2,1)}) %reduce-scatter.6.cloned.1.call-update) | async-done | bytes 1048592 | tf_op jit(solution)/shard_map/reduce_scatter | solution.py:1301
  408.4 6.8 %raw_grad.1 = (bf16[2048,384]{1,0:T(8,128)(2,1)}, f32[2,128]{1,0:T(2,128)}) custom-call(f32[2048,128]{1,0:T(8,128)} %copy-done.77, f32[2048,128]{1,0:T(8,128)} %copy-done.78, bf16[2048,128]{1,0:T(8,128)(2,1)} %collective-permute-done.36.refs_0_.dk_far_ref, f32[2048,128]{1,0:T(8,128)} %copy-done.79, ...), custom_call_target="tpu_custom_call" | custom-call | flops 6000000000 | bytes 1048576 | tf_op jit(solution)/shard_map/raw_grad/pallas_call | solution.py:330
  415.2 4.5 all-to-all-start.3
  422.0 6.5 %qkv_grad.1 = (bf16[1024,384]{1,0:T(8,128)(2,1)S(1)}, bf16[1024,384]{1,0:T(8,128)(2,1)S(1)}) custom-call(bf16[2048,1024]{1,0:T(8,128)(2,1)S(1)} %copy-done.35, bf16[2048,384]{1,0:T(8,128)(2,1)S(1)} %copy-done.56, bf16[2048,384]{1,0:T(8,128)(2,1)} %collective-permute-done.45.grad_other_ref), custom_call_target="tpu_custom_call" | custom-call | flops 10000000000 | bytes 1048576 | tf_op jit(solution)/shard_map/qkv_grad/pallas_call | solution.py:629
  434.7 22.9 %all-to-all-done.3.refs_0_.x_ref = bf16[4,512,384]{2,1,0:T(8,128)(2,1)} async-done(((bf16[4,512,384]{2,1,0:T(8,128)(2,1)}), bf16[4,512,384]{2,1,0:T(8,128)(2,1)}, u32[]{:S(2)}, u32[]{:S(2)}) %all-to-all-start.3) | async-done | bytes 1572896 | tf_op jit(solution)/shard_map/all_to_all | solution.py:1156
  458.9 3.4 own_grad.3.refs_0_
  471.6 4.1 project_grad.2
  475.8 4.8 project_grad.3
  485.7 3.5 all-to-all-start.4
  495.9 3.8 collective-permute-done.53
  500.8 3.2 collective-permute-done.54
  504.1 3.7 input_grad_kernel.1.refs_0_
  511.0 5.5 %collective-permute-done.55 = f32[8,2048]{1,0:T(8,128)S(1)} collective-permute-done((f32[8,2048]{1,0:T(8,128)S(1)}, f32[8,2048]{1,0:T(8,128)S(1)}, u32[]{:S(2)}, u32[]{:S(2)}) %collective-permute-start.55) | collective-permute-done | bytes 65568 | tf_op jit(solution)/shard_map/ppermute | solution.py:1000
  516.5 4.7 collective-permute-start.56
  530.8 4.5 collective-permute-done.51
  (466 shorter events, 201.8 us)
Async XLA Ops:
  10.5 21.3 %collective-permute-start = (bf16[128,2048]{1,0:T(8,128)(2,1)S(1)}, bf16[128,2048]{1,0:T(8,128)(2,1)}, u32[]{:S(2)}, u32[]{:S(2)}) collective-permute-start(bf16[128,2048]{1,0:T(8,128)(2,1)S(1)} %fusion.20.a_ref), channel_id=1, source_target_pairs={{0,1},{1,0},{2,3},{3,2},{4,5},{5,4},{6,7},{7,6},{8,9},{9,8},{10,11... | collective-permute-start | bytes 1572872 | tf_op jit(solution)/shard_map/ppermute | solution.py:975
  11.0 15.4 %collective-permute-start.1 = (bf16[128,2048]{1,0:T(8,128)(2,1)S(1)}, bf16[128,2048]{1,0:T(8,128)(2,1)S(1)}, u32[]{:S(2)}, u32[]{:S(2)}) collective-permute-start(bf16[128,2048]{1,0:T(8,128)(2,1)S(1)} %fusion.20.a_ref), channel_id=1, source_target_pairs={{0,2},{2,0},{1,3},{3,1},{4,6},{6,4},{5,7},{7,5},{8,10},{10,8},{9,1... | collective-permute-start | bytes 1572872 | tf_op jit(solution)/shard_map/ppermute | solution.py:974
  26.4 14.1 %collective-permute-start.2 = (bf16[128,2048]{1,0:T(8,128)(2,1)S(1)}, bf16[128,2048]{1,0:T(8,128)(2,1)S(1)}, u32[]{:S(2)}, u32[]{:S(2)}) collective-permute-start(bf16[128,2048]{1,0:T(8,128)(2,1)S(1)} %collective-permute-done.1.a_ref), channel_id=1, source_target_pairs={{0,1},{1,0},{2,3},{3,2},{4,5},{5,4},{6,7},{7,6},{8,9},{9,8},{10,11... | collective-permute-start | bytes 1572872 | tf_op jit(solution)/shard_map/ppermute | solution.py:981
  47.8 19.6 %all-to-all-start = ((bf16[4,512,128]{2,1,0:T(8,128)(2,1)}), bf16[4,512,128]{2,1,0:T(8,128)(2,1)S(1)}, u32[]{:S(2)}, u32[]{:S(2)}) async-start(bf16[4,512,128]{2,1,0:T(8,128)(2,1)} %pad_maximum_fusion), calls=%async_computation | async-start | bytes 1048576 | tf_op jit(solution)/shard_map/all_to_all | solution.py:1114
  68.6 15.1 %collective-permute-start.11 = (bf16[2048,128]{1,0:T(8,128)(2,1)S(1)}, bf16[2048,128]{1,0:T(8,128)(2,1)S(1)}, u32[]{:S(2)}, u32[]{:S(2)}) collective-permute-start(bf16[2048,128]{1,0:T(8,128)(2,1)S(1)} %pass_rows.3.refs_1_.v_ref), channel_id=1, source_target_pairs={{0,4},{4,0},{1,5},{5,1},{2,6},{6,2},{3,7},{7,3},{8,12},{12,8},{9,1... | collective-permute-start | bytes 1572872 | tf_op jit(solution)/shard_map/ppermute | solution.py:1118
  72.8 7.3 %collective-permute-start.8 = (bf16[512,128]{1,0:T(8,128)(2,1)S(1)}, bf16[512,128]{1,0:T(8,128)(2,1)S(1)}, u32[]{:S(2)}, u32[]{:S(2)}) collective-permute-start(bf16[512,128]{1,0:T(8,128)(2,1)S(1)} %get-tuple-element.153), channel_id=1, source_target_pairs={{0,8},{8,16},{16,24},{24,0},{1,9},{9,17},{17,25},{25,1},{2,10},{10... | collective-permute-start | bytes 393224 | tf_op jit(solution)/shard_map/ppermute | solution.py:1109
  73.4 10.2 %collective-permute-start.9 = (bf16[512,128]{1,0:T(8,128)(2,1)S(1)}, bf16[512,128]{1,0:T(8,128)(2,1)S(1)}, u32[]{:S(2)}, u32[]{:S(2)}) collective-permute-start(bf16[512,128]{1,0:T(8,128)(2,1)S(1)} %get-tuple-element.152), channel_id=1, source_target_pairs={{0,16},{8,24},{16,0},{24,8},{1,17},{9,25},{17,1},{25,9},{2,18},{10... | collective-permute-start | bytes 393224 | tf_op jit(solution)/shard_map/ppermute | solution.py:1109
  83.8 14.7 %collective-permute-start.12 = (bf16[2048,128]{1,0:T(8,128)(2,1)S(1)}, bf16[2048,128]{1,0:T(8,128)(2,1)}, u32[]{:S(2)}, u32[]{:S(2)}) collective-permute-start(bf16[2048,128]{1,0:T(8,128)(2,1)S(1)} %arrange.3.refs_0_.k_ref), channel_id=1, source_target_pairs={{0,4},{4,0},{1,5},{5,1},{2,6},{6,2},{3,7},{7,3},{8,12},{12,8},{9,1... | collective-permute-start | bytes 1572872 | tf_op jit(solution)/shard_map/ppermute | solution.py:1118
  85.1 8.5 %collective-permute-start.5 = (bf16[512,128]{1,0:T(8,128)(2,1)}, bf16[512,128]{1,0:T(8,128)(2,1)S(1)}, u32[]{:S(2)}, u32[]{:S(2)}) collective-permute-start(bf16[512,128]{1,0:T(8,128)(2,1)} %get-tuple-element.157), channel_id=1, source_target_pairs={{0,8},{8,16},{16,24},{24,0},{1,9},{9,17},{17,25},{25,1},{2,10},{10... | collective-permute-start | bytes 393224 | tf_op jit(solution)/shard_map/ppermute | solution.py:1109
  85.1 12.3 %collective-permute-start.6 = (bf16[512,128]{1,0:T(8,128)(2,1)}, bf16[512,128]{1,0:T(8,128)(2,1)S(1)}, u32[]{:S(2)}, u32[]{:S(2)}) collective-permute-start(bf16[512,128]{1,0:T(8,128)(2,1)} %get-tuple-element.156), channel_id=1, source_target_pairs={{0,16},{8,24},{16,0},{24,8},{1,17},{9,25},{17,1},{25,9},{2,18},{10... | collective-permute-start | bytes 393224 | tf_op jit(solution)/shard_map/ppermute | solution.py:1109
  88.4 8.9 %collective-permute-start.7 = (bf16[512,128]{1,0:T(8,128)(2,1)}, bf16[512,128]{1,0:T(8,128)(2,1)}, u32[]{:S(2)}, u32[]{:S(2)}) collective-permute-start(bf16[512,128]{1,0:T(8,128)(2,1)} %get-tuple-element.155), channel_id=1, source_target_pairs={{0,24},{8,0},{16,8},{24,16},{1,25},{9,1},{17,9},{25,17},{2,26},{10... | collective-permute-start | bytes 393224 | tf_op jit(solution)/shard_map/ppermute | solution.py:1109
  119.2 17.7 %all-to-all-start.1 = ((bf16[4,512,128]{2,1,0:T(8,128)(2,1)}), bf16[4,512,128]{2,1,0:T(8,128)(2,1)S(1)}, u32[]{:S(2)}, u32[]{:S(2)}) async-start(bf16[4,512,128]{2,1,0:T(8,128)(2,1)} %bitcast.26), calls=%async_computation.1 | async-start | bytes 1048576 | tf_op jit(solution)/shard_map/all_to_all | solution.py:1156
  123.0 103.5 %all-gather.2.cloned.1.call-start = ((), (), s32[]{:S(2)}) async-start(), calls=%async_computation.8 | async-start | bytes 5242880 | tf_op jit(solution)/shard_map/all_gather | solution.py:1166
  142.7 13.2 %collective-permute-start.13 = (bf16[128,2048]{1,0:T(8,128)(2,1)}, bf16[128,2048]{1,0:T(8,128)(2,1)}, u32[]{:S(2)}, u32[]{:S(2)}) collective-permute-start(bf16[128,2048]{1,0:T(8,128)(2,1)} %get-tuple-element.57), channel_id=1, source_target_pairs={{0,1},{1,0},{2,3},{3,2},{4,5},{5,4},{6,7},{7,6},{8,9},{9,8},{10,11... | collective-permute-start | bytes 1572872 | tf_op jit(solution)/shard_map/ppermute | solution.py:988
  145.4 215.2 %reduce-scatter.4.cloned.1.call-start = ((), (), s32[]{:S(2)}) async-start(), calls=%async_computation.9 | async-start | bytes 5242880 | tf_op jit(solution)/shard_map/reduce_scatter | solution.py:1300
  146.8 13.9 %collective-permute-start.15 = (bf16[128,2048]{1,0:T(8,128)(2,1)S(1)}, bf16[128,2048]{1,0:T(8,128)(2,1)S(1)}, u32[]{:S(2)}, u32[]{:S(2)}) collective-permute-start(bf16[128,2048]{1,0:T(8,128)(2,1)S(1)} %add_convert_fusion.3.refs_0_), channel_id=1, source_target_pairs={{0,2},{2,0},{1,3},{3,1},{4,6},{6,4},{5,7},{7,5},{8,10},{10,8},{9,1... | collective-permute-start | bytes 1572872 | tf_op jit(solution)/shard_map/ppermute | solution.py:987
  163.1 13.2 %collective-permute-start.18 = (bf16[128,2048]{1,0:T(8,128)(2,1)S(1)}, bf16[128,2048]{1,0:T(8,128)(2,1)S(1)}, u32[]{:S(2)}, u32[]{:S(2)}) collective-permute-start(bf16[128,2048]{1,0:T(8,128)(2,1)S(1)} %get-tuple-element.60.a_ref.refs_0_), channel_id=1, source_target_pairs={{0,2},{2,0},{1,3},{3,1},{4,6},{6,4},{5,7},{7,5},{8,10},{10,8},{9,1... | collective-permute-start | bytes 1572872 | tf_op jit(solution)/shard_map/ppermute | solution.py:974
  164.9 11.6 %collective-permute-start.16 = (bf16[128,2048]{1,0:T(8,128)(2,1)S(1)}, bf16[128,2048]{1,0:T(8,128)(2,1)S(1)}, u32[]{:S(2)}, u32[]{:S(2)}) collective-permute-start(bf16[128,2048]{1,0:T(8,128)(2,1)S(1)} %get-tuple-element.60.a_ref.refs_0_), channel_id=1, source_target_pairs={{0,1},{1,0},{2,3},{3,2},{4,5},{5,4},{6,7},{7,6},{8,9},{9,8},{10,11... | collective-permute-start | bytes 1572872 | tf_op jit(solution)/shard_map/ppermute | solution.py:975
  186.0 13.9 %collective-permute-start.22 = (bf16[256,1024]{1,0:T(8,128)(2,1)S(1)}, bf16[256,1024]{1,0:T(8,128)(2,1)S(1)}, u32[]{:S(2)}, u32[]{:S(2)}) collective-permute-start(bf16[256,1024]{1,0:T(8,128)(2,1)S(1)} %pad_maximum_fusion.1), channel_id=1, source_target_pairs={{0,4},{4,0},{1,5},{5,1},{2,6},{6,2},{3,7},{7,3},{8,12},{12,8},{9,1... | collective-permute-start | bytes 1572872 | tf_op jit(solution)/shard_map/ppermute | solution.py:1062
  187.8 12.2 %collective-permute-start.17 = (bf16[128,2048]{1,0:T(8,128)(2,1)S(1)}, bf16[128,2048]{1,0:T(8,128)(2,1)S(1)}, u32[]{:S(2)}, u32[]{:S(2)}) collective-permute-start(bf16[128,2048]{1,0:T(8,128)(2,1)S(1)} %get-tuple-element.149), channel_id=1, source_target_pairs={{0,1},{1,0},{2,3},{3,2},{4,5},{5,4},{6,7},{7,6},{8,9},{9,8},{10,11... | collective-permute-start | bytes 1572872 | tf_op jit(solution)/shard_map/ppermute | solution.py:988
  188.0 14.4 %collective-permute-start.21 = (bf16[128,2048]{1,0:T(8,128)(2,1)S(1)}, bf16[128,2048]{1,0:T(8,128)(2,1)S(1)}, u32[]{:S(2)}, u32[]{:S(2)}) collective-permute-start(bf16[128,2048]{1,0:T(8,128)(2,1)S(1)} %add_convert_fusion.2), channel_id=1, source_target_pairs={{0,2},{2,0},{1,3},{3,1},{4,6},{6,4},{5,7},{7,5},{8,10},{10,8},{9,1... | collective-permute-start | bytes 1572872 | tf_op jit(solution)/shard_map/ppermute | solution.py:987
  203.9 13.6 %collective-permute-start.25 = (bf16[128,2048]{1,0:T(8,128)(2,1)S(1)}, bf16[128,2048]{1,0:T(8,128)(2,1)S(1)}, u32[]{:S(2)}, u32[]{:S(2)}) collective-permute-start(bf16[128,2048]{1,0:T(8,128)(2,1)S(1)} %get-tuple-element.63.a_ref), channel_id=1, source_target_pairs={{0,2},{2,0},{1,3},{3,1},{4,6},{6,4},{5,7},{7,5},{8,10},{10,8},{9,1... | collective-permute-start | bytes 1572872 | tf_op jit(solution)/shard_map/ppermute | solution.py:974
  205.5 12.1 %collective-permute-start.23 = (bf16[128,2048]{1,0:T(8,128)(2,1)S(1)}, bf16[128,2048]{1,0:T(8,128)(2,1)S(1)}, u32[]{:S(2)}, u32[]{:S(2)}) collective-permute-start(bf16[128,2048]{1,0:T(8,128)(2,1)S(1)} %get-tuple-element.63.a_ref), channel_id=1, source_target_pairs={{0,1},{1,0},{2,3},{3,2},{4,5},{5,4},{6,7},{7,6},{8,9},{9,8},{10,11... | collective-permute-start | bytes 1572872 | tf_op jit(solution)/shard_map/ppermute | solution.py:975
  205.6 19.3 %collective-permute-start.27 = (bf16[256,1024]{1,0:T(8,128)(2,1)S(1)}, bf16[256,1024]{1,0:T(8,128)(2,1)S(1)}, u32[]{:S(2)}, u32[]{:S(2)}) collective-permute-start(bf16[256,1024]{1,0:T(8,128)(2,1)S(1)} %pad_maximum_fusion.2), channel_id=1, source_target_pairs={{0,4},{4,0},{1,5},{5,1},{2,6},{6,2},{3,7},{7,3},{8,12},{12,8},{9,1... | collective-permute-start | bytes 1572872 | tf_op jit(solution)/shard_map/ppermute | solution.py:1062
  217.6 8.1 %collective-permute-start.26 = (bf16[128,2048]{1,0:T(8,128)(2,1)S(1)}, bf16[128,2048]{1,0:T(8,128)(2,1)S(1)}, u32[]{:S(2)}, u32[]{:S(2)}) collective-permute-start(bf16[128,2048]{1,0:T(8,128)(2,1)S(1)} %collective-permute-done.25.a_ref), channel_id=1, source_target_pairs={{0,1},{1,0},{2,3},{3,2},{4,5},{5,4},{6,7},{7,6},{8,9},{9,8},{10,11... | collective-permute-start | bytes 1572872 | tf_op jit(solution)/shard_map/ppermute | solution.py:981
  250.7 157.7 %reduce-scatter.6.cloned.1.call-start = ((), (), s32[]{:S(2)}) async-start(), calls=%async_computation.10 | async-start | bytes 5242880 | tf_op jit(solution)/shard_map/reduce_scatter | solution.py:1301
  255.0 14.5 %collective-permute-start.30 = (bf16[2,2,256,256]{3,2,1,0:T(8,128)(2,1)}, bf16[2,2,256,256]{3,2,1,0:T(8,128)(2,1)}, u32[]{:S(2)}, u32[]{:S(2)}) collective-permute-start(bf16[2,2,256,256]{3,2,1,0:T(8,128)(2,1)} %pad_maximum_fusion.3), channel_id=1, source_target_pairs={{0,4},{4,0},{1,5},{5,1},{2,6},{6,2},{3,7},{7,3},{8,12},{12,8},{9,1... | collective-permute-start | bytes 1572872 | tf_op jit(solution)/shard_map/ppermute | solution.py:1268
  257.1 12.4 %collective-permute-start.24 = (bf16[128,2048]{1,0:T(8,128)(2,1)}, bf16[128,2048]{1,0:T(8,128)(2,1)}, u32[]{:S(2)}, u32[]{:S(2)}) collective-permute-start(bf16[128,2048]{1,0:T(8,128)(2,1)} %get-tuple-element.143), channel_id=1, source_target_pairs={{0,1},{1,0},{2,3},{3,2},{4,5},{5,4},{6,7},{7,6},{8,9},{9,8},{10,11... | collective-permute-start | bytes 1572872 | tf_op jit(solution)/shard_map/ppermute | solution.py:988
  257.1 14.7 %collective-permute-start.29 = (bf16[128,2048]{1,0:T(8,128)(2,1)}, bf16[128,2048]{1,0:T(8,128)(2,1)}, u32[]{:S(2)}, u32[]{:S(2)}) collective-permute-start(bf16[128,2048]{1,0:T(8,128)(2,1)} %add_convert_fusion.1.refs_0_), channel_id=1, source_target_pairs={{0,2},{2,0},{1,3},{3,1},{4,6},{6,4},{5,7},{7,5},{8,10},{10,8},{9,1... | collective-permute-start | bytes 1572872 | tf_op jit(solution)/shard_map/ppermute | solution.py:987
  280.7 13.6 %collective-permute-start.31 = (bf16[128,2048]{1,0:T(8,128)(2,1)S(1)}, bf16[128,2048]{1,0:T(8,128)(2,1)S(1)}, u32[]{:S(2)}, u32[]{:S(2)}) collective-permute-start(bf16[128,2048]{1,0:T(8,128)(2,1)S(1)} %get-tuple-element.65.a_ref), channel_id=1, source_target_pairs={{0,2},{2,0},{1,3},{3,1},{4,6},{6,4},{5,7},{7,5},{8,10},{10,8},{9,1... | collective-permute-start | bytes 1572872 | tf_op jit(solution)/shard_map/ppermute | solution.py:974
  282.6 20.5 %collective-permute-start.34 = (bf16[128,2048]{1,0:T(8,128)(2,1)S(1)}, bf16[128,2048]{1,0:T(8,128)(2,1)S(1)}, u32[]{:S(2)}, u32[]{:S(2)}) collective-permute-start(bf16[128,2048]{1,0:T(8,128)(2,1)S(1)} %get-tuple-element.65.a_ref), channel_id=1, source_target_pairs={{0,1},{1,0},{2,3},{3,2},{4,5},{5,4},{6,7},{7,6},{8,9},{9,8},{10,11... | collective-permute-start | bytes 1572872 | tf_op jit(solution)/shard_map/ppermute | solution.py:975
  282.8 22.8 %collective-permute-start.33 = (bf16[2,2,256,256]{3,2,1,0:T(8,128)(2,1)S(1)}, bf16[2,2,256,256]{3,2,1,0:T(8,128)(2,1)S(1)}, u32[]{:S(2)}, u32[]{:S(2)}) collective-permute-start(bf16[2,2,256,256]{3,2,1,0:T(8,128)(2,1)S(1)} %pad_maximum_fusion.4), channel_id=1, source_target_pairs={{0,4},{4,0},{1,5},{5,1},{2,6},{6,2},{3,7},{7,3},{8,12},{12,8},{9,1... | collective-permute-start | bytes 1572872 | tf_op jit(solution)/shard_map/ppermute | solution.py:1268
  294.3 11.3 %collective-permute-start.32 = (bf16[128,2048]{1,0:T(8,128)(2,1)S(1)}, bf16[128,2048]{1,0:T(8,128)(2,1)S(1)}, u32[]{:S(2)}, u32[]{:S(2)}) collective-permute-start(bf16[128,2048]{1,0:T(8,128)(2,1)S(1)} %collective-permute-done.31.a_ref), channel_id=1, source_target_pairs={{0,1},{1,0},{2,3},{3,2},{4,5},{5,4},{6,7},{7,6},{8,9},{9,8},{10,11... | collective-permute-start | bytes 1572872 | tf_op jit(solution)/shard_map/ppermute | solution.py:981
  294.3 8.8 %collective-permute-start.35 = (f32[2,512]{0,1:T(8,128)S(1)}, f32[2,512]{0,1:T(8,128)S(1)}, u32[]{:S(2)}, u32[]{:S(2)}) collective-permute-start(f32[2,512]{0,1:T(8,128)S(1)} %convert_bitcast_fusion.1), channel_id=1, source_target_pairs={{0,4},{4,0},{1,5},{5,1},{2,6},{6,2},{3,7},{7,3},{8,12},{12,8},{9,1... | collective-permute-start | bytes 12296 | tf_op jit(solution)/shard_map/ppermute | solution.py:1185
  357.3 24.2 %collective-permute-start.36 = (bf16[2048,128]{1,0:T(8,128)(2,1)}, bf16[2048,128]{1,0:T(8,128)(2,1)}, u32[]{:S(2)}, u32[]{:S(2)}) collective-permute-start(bf16[2048,128]{1,0:T(8,128)(2,1)} %get-tuple-element.70), channel_id=1, source_target_pairs={{0,4},{4,0},{1,5},{5,1},{2,6},{6,2},{3,7},{7,3},{8,12},{12,8},{9,1... | collective-permute-start | bytes 1572872 | tf_op jit(solution)/shard_map/ppermute | solution.py:1325
  358.4 23.1 %collective-permute-start.37 = (bf16[2048,128]{1,0:T(8,128)(2,1)}, bf16[2048,128]{1,0:T(8,128)(2,1)}, u32[]{:S(2)}, u32[]{:S(2)}) collective-permute-start(bf16[2048,128]{1,0:T(8,128)(2,1)} %get-tuple-element.72), channel_id=1, source_target_pairs={{0,4},{4,0},{1,5},{5,1},{2,6},{6,2},{3,7},{7,3},{8,12},{12,8},{9,1... | collective-permute-start | bytes 1572872 | tf_op jit(solution)/shard_map/ppermute | solution.py:1325
  359.5 22.1 %collective-permute-start.40 = (f32[1,2048]{1,0:T(1,128)S(1)}, f32[1,2048]{1,0:T(1,128)S(1)}, u32[]{:S(2)}, u32[]{:S(2)}) collective-permute-start(f32[1,2048]{1,0:T(1,128)S(1)} %get-tuple-element.75), channel_id=1, source_target_pairs={{0,4},{4,0},{1,5},{5,1},{2,6},{6,2},{3,7},{7,3},{8,12},{12,8},{9,1... | collective-permute-start | bytes 24584 | tf_op jit(solution)/shard_map/ppermute | solution.py:1328
  388.7 7.4 %collective-permute-start.39 = (f32[4,2,512]{2,0,1:T(4,128)S(1)}, f32[4,2,512]{2,0,1:T(4,128)S(1)}, u32[]{:S(2)}, u32[]{:S(2)}) collective-permute-start(f32[4,2,512]{2,0,1:T(4,128)S(1)} %fusion.54), channel_id=1, source_target_pairs={{0,16},{8,24},{16,0},{24,8},{1,17},{9,25},{17,1},{25,9},{2,18},{10... | collective-permute-start | bytes 49160 | tf_op jit(solution)/shard_map/ppermute | solution.py:1000
  415.2 42.4 %all-to-all-start.3 = ((bf16[4,512,384]{2,1,0:T(8,128)(2,1)}), bf16[4,512,384]{2,1,0:T(8,128)(2,1)}, u32[]{:S(2)}, u32[]{:S(2)}) async-start(bf16[4,512,384]{2,1,0:T(8,128)(2,1)} %bitcast.296), calls=%async_computation.5 | async-start | bytes 3145728 | tf_op jit(solution)/shard_map/all_to_all | solution.py:1156
  419.7 105.2 %reduce-scatter.8.cloned.1.call-start = ((), (), s32[]{:S(2)}) async-start(), calls=%async_computation.11 | async-start | bytes 2621440 | tf_op jit(solution)/shard_map/reduce_scatter | solution.py:1396
  433.3 24.3 %collective-permute-start.47 = (bf16[4,256,384]{2,1,0:T(8,128)(2,1)}, bf16[4,256,384]{2,1,0:T(8,128)(2,1)}, u32[]{:S(2)}, u32[]{:S(2)}) collective-permute-start(bf16[4,256,384]{2,1,0:T(8,128)(2,1)} %get-tuple-element.134), channel_id=1, source_target_pairs={{0,4},{4,0},{1,5},{5,1},{2,6},{6,2},{3,7},{7,3},{8,12},{12,8},{9,1... | collective-permute-start | bytes 2359304 | tf_op jit(solution)/shard_map/ppermute | solution.py:1384
  467.3 53.8 %collective-permute-start.57 = (bf16[4,256,256]{2,1,0:T(8,128)(2,1)}, bf16[4,256,256]{2,1,0:T(8,128)(2,1)}, u32[]{:S(2)}, u32[]{:S(2)}) collective-permute-start(bf16[4,256,256]{2,1,0:T(8,128)(2,1)} %dynamic-slice_bitcast_fusion.2), channel_id=1, source_target_pairs={{0,4},{4,0},{1,5},{5,1},{2,6},{6,2},{3,7},{7,3},{8,12},{12,8},{9,1... | collective-permute-start | bytes 1572872 | tf_op jit(solution)/shard_map/ppermute | solution.py:1042
  480.6 23.4 %collective-permute-start.48 = (bf16[128,2048]{1,0:T(8,128)(2,1)}, bf16[128,2048]{1,0:T(8,128)(2,1)S(1)}, u32[]{:S(2)}, u32[]{:S(2)}) collective-permute-start(bf16[128,2048]{1,0:T(8,128)(2,1)} %get-tuple-element.81), channel_id=1, source_target_pairs={{0,1},{1,0},{2,3},{3,2},{4,5},{5,4},{6,7},{7,6},{8,9},{9,8},{10,11... | collective-permute-start | bytes 1572872 | tf_op jit(solution)/shard_map/ppermute | solution.py:988
  482.0 22.0 %collective-permute-start.50 = (bf16[128,2048]{1,0:T(8,128)(2,1)}, bf16[128,2048]{1,0:T(8,128)(2,1)}, u32[]{:S(2)}, u32[]{:S(2)}) collective-permute-start(bf16[128,2048]{1,0:T(8,128)(2,1)} %add_convert_fusion), channel_id=1, source_target_pairs={{0,2},{2,0},{1,3},{3,1},{4,6},{6,4},{5,7},{7,5},{8,10},{10,8},{9,1... | collective-permute-start | bytes 1572872 | tf_op jit(solution)/shard_map/ppermute | solution.py:987
  485.7 43.0 %all-to-all-start.4 = ((bf16[4,256,384]{2,1,0:T(8,128)(2,1)}), bf16[4,256,384]{2,1,0:T(8,128)(2,1)S(1)}, u32[]{:S(2)}, u32[]{:S(2)}) async-start(bf16[4,256,384]{2,1,0:T(8,128)(2,1)} %add_rows.1), calls=%async_computation.6 | async-start | bytes 1572864 | tf_op jit(solution)/shard_map/all_to_all | solution.py:1411
  508.9 7.6 %collective-permute-start.55 = (f32[8,2048]{1,0:T(8,128)S(1)}, f32[8,2048]{1,0:T(8,128)S(1)}, u32[]{:S(2)}, u32[]{:S(2)}) collective-permute-start(f32[8,2048]{1,0:T(8,128)S(1)} %pass_rows.5), channel_id=1, source_target_pairs={{0,8},{8,0},{16,24},{24,16},{1,9},{9,1},{17,25},{25,17},{2,10},{10... | collective-permute-start | bytes 196616 | tf_op jit(solution)/shard_map/ppermute | solution.py:1000
  516.5 8.4 %collective-permute-start.56 = (f32[8,2048]{1,0:T(8,128)S(1)}, f32[8,2048]{1,0:T(8,128)S(1)}, u32[]{:S(2)}, u32[]{:S(2)}) collective-permute-start(f32[8,2048]{1,0:T(8,128)S(1)} %add.283), channel_id=1, source_target_pairs={{0,16},{8,24},{16,0},{24,8},{1,17},{9,25},{17,1},{25,9},{2,18},{10... | collective-permute-start | bytes 196616 | tf_op jit(solution)/shard_map/ppermute | solution.py:1000
  526.6 8.6 %collective-permute-start.51 = (bf16[4,256,128]{2,1,0:T(8,128)(2,1)}, bf16[4,256,128]{2,1,0:T(8,128)(2,1)}, u32[]{:S(2)}, u32[]{:S(2)}) collective-permute-start(bf16[4,256,128]{2,1,0:T(8,128)(2,1)} %dynamic-slice_bitcast_fusion.3), channel_id=1, source_target_pairs={{0,4},{4,0},{1,5},{5,1},{2,6},{6,2},{3,7},{7,3},{8,12},{12,8},{9,1... | collective-permute-start | bytes 786440 | tf_op jit(solution)/shard_map/ppermute | solution.py:1042
  (124 other events, 932.9 us)
Sparse Core Ops, SparseCore 0:
  145.5 80.6 all-gather.1
  250.8 76.1 reduce-scatter.3
  329.4 78.9 reduce-scatter.5
  463.8 53.7 reduce-scatter.7

commit v5 on v4

--- a/solution.py
+++ b/solution.py
@@ -1101,14 +1101,17 @@
     inv_line = sum_line(inv_slots, z_count)
     gain_qk = lax.dynamic_slice_in_dim(norm_gains[2:], wt_pos * head_cols, head_cols, 1)
 
-    def to_heads_apart(parts, earlier=()):
+    def to_heads_apart(parts, earlier=(), beside=None):
         near = [lax.dynamic_index_in_dim(parts, z_pos, 0, False)]
         for d in range(1, z_count):
             there = lax.dynamic_index_in_dim(parts, (z_pos + d) % z_count, 0, False)
             near.append(
                 lax.ppermute(there, "z", [(i, (i + d) % z_count) for i in range(z_count)])
             )
-        return arrange(near, z_pos, earlier)
+        if beside is None:
+            return arrange(near, z_pos, earlier)
+        beside = beside(near[1])
+        return arrange(near, z_pos, (*earlier, beside)), beside
 
     def to_heads(parts):
         return lax.all_to_all(parts, "z", 0, 0, tiled=True).reshape(line_rows, HEAD_DIM)
@@ -1280,23 +1283,27 @@
     d_attn = attn_out_grad_half(d_resid_h[0], 0, out_b)
     d_attn = attn_out_grad_half(d_resid_h[1], 1, out_b, d_attn)
 
-    d_out = to_heads(d_attn)
+    if pair:
+
+        def gate_up_beside(piece):
+            return weight_grad(
+                mixed_h,
+                mixed_far,
+                [(d, 0) for d in d_pre_h],
+                [(d, 0) for d in d_pre_far],
+                out_block,
+                x_pos,
+                routes_far,
+                experts,
+                (piece,),
+            )
+
+        d_out, gate_up_part = to_heads_apart(d_attn, beside=gate_up_beside)
+    else:
+        d_out = to_heads(d_attn)
+        gate_up_part = plain_part(mixed_h, jnp.concatenate(d_pre_h, axis=1), "td,ntf->ndf")
     delta = jnp.sum(d_out.astype(f32) * attn_f, axis=-1).reshape(1, line_rows)
     d_query = jnp.zeros((line_rows, HEAD_DIM), f32)
-    if pair:
-        gate_up_part = weight_grad(
-            mixed_h,
-            mixed_far,
-            [(d, 0) for d in d_pre_h],
-            [(d, 0) for d in d_pre_far],
-            out_block,
-            x_pos,
-            routes_far,
-            experts,
-            (d_attn,),
-        )
-    else:
-        gate_up_part = plain_part(mixed_h, jnp.concatenate(d_pre_h, axis=1), "td,ntf->ndf")
     down_part = lax.psum_scatter(down_part, "z", scatter_dimension=1, tiled=True)
     gate_up_sum = lax.psum_scatter(gate_up_part, "z", scatter_dimension=1, tiled=True)
     d_kv = []
@@ -1352,7 +1359,7 @@
         cosine,
         sine,
         head_gain,
-        gate_up_sum,
+        d_kv[-1][0],
     )
     gain_full = lax.dynamic_update_slice_in_dim(
         jnp.zeros((2, model_width), f32), gain_sums, (wt_pos * z_count + z_pos) * HEAD_DIM, 1
@@ -1390,9 +1397,7 @@
     out_part = own_grad(
         d_resid_h, (attn_parts, attn_parts), (d_proj, qkv_line[1])
     )
-    far_n = project_grad_half(
-        d_proj, 1, qkv_b, (out_part,)
-    )
+    far_n = project_grad_half(d_proj, 1, qkv_b, (out_part, gate_up_sum))
     out_part = lax.psum_scatter(out_part, "z", scatter_dimension=1, tiled=True)
     near_n = project_grad_half(d_proj, 0, qkv_b, (far_n[0],))
     d_normed, _ = scatter_halves(near_n, far_n)

time: 553 us -> 547 us (0.989)
  blocking collectives: 17.6 us -> 0 us
  starting transfers between devices: 69.1 us -> 79.6 us
    all_to_all x1 -> x0, blocking collectives: 17.6 us -> none  [to_heads(): lax.all_to_all(parts, 'z', 0, 0, tiled=True).reshape(line_rows, HEAD_DIM)]
    ppermute x6 -> x9, waiting for transfers between devices: 17 us -> 33.4 us  [to_heads_apart(): lax.ppermute(there, 'z', [(i, (i + d) % z_count) for i in range(z_count)])]
    ppermute x6, starting transfers between devices: 7.52 us -> 14.7 us  [sum_line(): a = a + lax.ppermute(a, 'z', [(i, i ^ step) for i in range(z_count)])]
    reduce_scatter x1, waiting for transfers between devices: 6.27 us -> 0.01 us  [local(): lax.psum_scatter(gate_up_part, 'z', scatter_dimension=1, tiled=True)]
    unnamed x214 -> x224, local copies, waits for them, and re-layouts: 61.6 us -> 64.1 us
  transfers between devices with their start and end apart: 66 -> 69, of which waited for: 32 -> 33; matrix products, arithmetic and copies ran while one was open for 12% -> 13% of each run, Pallas kernels for 17% -> 18%
where the time goes in v5:
time: 547 us; the launch traced here: 537 us
  waiting for transfers between devices  171 us (31%)
  Pallas kernels  127 us (23%)
  local copies, waits for them, and re-layouts  86.2 us (16%)
  starting transfers between devices  79.6 us (15%)
  other arithmetic  36.2 us (7%)
  matrix products  21.2 us (4%)
  between operations  16 us (3%)
    unnamed x224, local copies, waits for them, and re-layouts  64.1 us
    all_to_all x2, waiting for transfers between devices, to_tokens(): lax.all_to_all(rows.reshape(z_count, tok_rows, cols), 'z', 0, 0, tiled=True)  33.5 us
    ppermute x9, waiting for transfers between devices, to_heads_apart(): lax.ppermute(there, 'z', [(i, (i + d) % z_count) for i in range(z_count)])  33.4 us
    pallas_call x2, Pallas kernels, attend_grad(): pl.pallas_call(functools.partial(attend_grad_kernel, chunk, LOG2E / math....  32.1 us
    ppermute x4, waiting for transfers between devices, gather_near(): far = lax.ppermute(rows, 'y', SWAP)  29.2 us
    pallas_call x1, Pallas kernels, attend(): pl.pallas_call(functools.partial(attend_kernel, len(key_groups), chunk, L...  16.9 us
    ppermute x6, waiting for transfers between devices, sum_line(): a = a + lax.ppermute(a, 'z', [(i, i ^ step) for i in range(z_count)])  14.9 us
    ppermute x6, starting transfers between devices, sum_line(): a = a + lax.ppermute(a, 'z', [(i, i ^ step) for i in range(z_count)])  14.7 us
  transfers between devices with their start and end apart: 69, of which 33 were waited for; matrix products, arithmetic and copies ran while one was open for 13% of the time, Pallas kernels for 18%

profile of v5, /device:TPU:0, one launch (start us, length us, event | category | flops | bytes accessed | tf_op | source)
XLA Modules:
  0.0 537.3 jit_solution(2358583597913684866)
XLA Ops:
  17.7 8.0 %convert_element_type.183.w_ref = bf16[3,2048,512]{2,1,0:T(8,128)(2,1)} convert(f32[3,2048,512]{2,1,0:T(8,128)} %param.16) | non-fusion elementwise | flops 3145728 | bytes 18874368 | tf_op jit(solution)/shard_map/convert_element_type | solution.py:1035
  26.6 3.7 multiply_sine_fusion
  35.8 4.7 project.2
  40.9 4.7 project.3
  47.8 4.9 all-to-all-start
  57.3 5.1 pack_heads.1
  62.4 5.2 all-to-all-done
  73.5 5.1 collective-permute-done.10.refs_3_
  80.2 3.5 collective-permute-done.9.refs_2_
  85.2 3.3 collective-permute-start.6
  90.7 3.1 collective-permute-done.5.refs_1_
  93.7 3.8 collective-permute-done.6.refs_2_
  100.5 16.9 %attend.1 = (f32[2048,128]{1,0:T(8,128)S(1)}, f32[1,2048]{1,0:T(1,128)S(1)}) custom-call(bf16[2048,128]{1,0:T(8,128)(2,1)S(1)} %arrange.3.q_ref, s32[1,2048]{1,0:T(1,128)S(1)} %bitcast.305, s32[1,2048]{1,0:T(1,128)S(1)} %bitcast.310, bf16[2048,128]{1,0:T(8,128)(2,1)S(1)} %arrange.4.refs_0_.k_ref, bf16[2048,128]{1,0:T(8,128)(2,1)S(1)} %pass_rows.3.refs_1_.v_ref, ...), custom_call_target="tpu_custom_call" | custom-call | flops 19000000512 | bytes 1048576 | tf_op jit(solution)/shard_map/attend/pallas_call | solution.py:97
  119.3 3.9 all-to-all-start.1
  125.9 11.2 %all-to-all-done.1.x_ref.refs_0_.n0_ref.n1_ref = bf16[4,512,128]{2,1,0:T(8,128)(2,1)S(1)} async-done(((bf16[4,512,128]{2,1,0:T(8,128)(2,1)}), bf16[4,512,128]{2,1,0:T(8,128)(2,1)S(1)}, u32[]{:S(2)}, u32[]{:S(2)}) %all-to-all-start.1) | async-done | bytes 524320 | tf_op jit(solution)/shard_map/all_to_all | solution.py:1159
  148.6 6.5 %copy-done.78 = f32[2,4,2048,256]{3,2,1,0:T(8,128)S(1)} copy-done((f32[2,4,2048,256]{3,2,1,0:T(8,128)S(1)}, f32[2,4,2048,256]{3,2,1,0:T(8,128)}, u32[]{:S(2)}) %copy-start.78) | copy-done | bytes 16777240
  156.0 4.8 collective-permute-done.15.far_got
  163.3 3.4 copy-done.79
  167.1 7.6 %collective-permute-done.18.in_ref = bf16[128,2048]{1,0:T(8,128)(2,1)S(1)} collective-permute-done((bf16[128,2048]{1,0:T(8,128)(2,1)S(1)}, bf16[128,2048]{1,0:T(8,128)(2,1)S(1)}, u32[]{:S(2)}, u32[]{:S(2)}) %collective-permute-start.18) | collective-permute-done | bytes 524320 | tf_op jit(solution)/shard_map/ppermute | solution.py:974
  188.0 10.4 %collective-permute-done.22.refs_0_.refs_2_ = bf16[256,1024]{1,0:T(8,128)(2,1)S(1)} collective-permute-done((bf16[256,1024]{1,0:T(8,128)(2,1)S(1)}, bf16[256,1024]{1,0:T(8,128)(2,1)S(1)}, u32[]{:S(2)}, u32[]{:S(2)}) %collective-permute-start.22) | collective-permute-done | bytes 524320 | tf_op jit(solution)/shard_map/ppermute | solution.py:1062
  205.2 10.7 %collective-permute-done.25.a_ref = bf16[128,2048]{1,0:T(8,128)(2,1)S(1)} collective-permute-done((bf16[128,2048]{1,0:T(8,128)(2,1)S(1)}, bf16[128,2048]{1,0:T(8,128)(2,1)S(1)}, u32[]{:S(2)}, u32[]{:S(2)}) %collective-permute-start.25) | collective-permute-done | bytes 524320 | tf_op jit(solution)/shard_map/ppermute | solution.py:974
  234.4 3.9 fusion.31
  244.8 3.5 own_grad.2.refs_0_
  259.7 9.3 %collective-permute-done.30.refs_1_.refs_6_ = bf16[2,2,256,256]{3,2,1,0:T(8,128)(2,1)} collective-permute-done((bf16[2,2,256,256]{3,2,1,0:T(8,128)(2,1)}, bf16[2,2,256,256]{3,2,1,0:T(8,128)(2,1)}, u32[]{:S(2)}, u32[]{:S(2)}) %collective-permute-start.30) | collective-permute-done | bytes 524320 | tf_op jit(solution)/shard_map/ppermute | solution.py:1271
  269.0 2.9 collective-permute-done.29.far_got
  277.6 3.2 resid_grad_kernel.1
  283.5 10.9 %collective-permute-done.31.a_ref = bf16[128,2048]{1,0:T(8,128)(2,1)S(1)} collective-permute-done((bf16[128,2048]{1,0:T(8,128)(2,1)S(1)}, bf16[128,2048]{1,0:T(8,128)(2,1)S(1)}, u32[]{:S(2)}, u32[]{:S(2)}) %collective-permute-start.31) | collective-permute-done | bytes 524320 | tf_op jit(solution)/shard_map/ppermute | solution.py:974
  299.0 4.2 collective-permute-done.38
  303.2 6.6 %collective-permute-done.35.refs_9_.refs_1_ = bf16[512,128]{1,0:T(8,128)(2,1)S(1)} collective-permute-done((bf16[512,128]{1,0:T(8,128)(2,1)S(1)}, bf16[512,128]{1,0:T(8,128)(2,1)S(1)}, u32[]{:S(2)}, u32[]{:S(2)}) %collective-permute-start.35) | collective-permute-done | bytes 131104 | tf_op jit(solution)/shard_map/ppermute | solution.py:1109
  309.8 8.7 %weight_grad.1.refs_4_.refs_0_ = bf16[8,1024,256]{2,1,0:T(8,128)(2,1)S(1)} custom-call(s32[1]{0:T(128)} %bitcast.71.at_ref, bf16[256,2048]{1,0:T(8,128)(2,1)S(1)} %join_rows.10.refs_0_, bf16[256,2048]{1,0:T(8,128)(2,1)S(1)} %copy-done.6, bf16[256,1024]{1,0:T(8,128)(2,1)S(1)} %copy-done.42, bf16[256,1024]{1,0:T(8,128)(2,1)S(1)} %copy-done.55, ...), custom_call_target="tpu_custom_call" | custom-call | flops 100000000 | bytes 1048576 | tf_op jit(solution)/shard_map/weight_grad/pallas_call | solution.py:401
  323.9 9.8 %collective-permute-done.36.refs_2_ = bf16[512,128]{1,0:T(8,128)(2,1)S(1)} collective-permute-done((bf16[512,128]{1,0:T(8,128)(2,1)S(1)}, bf16[512,128]{1,0:T(8,128)(2,1)S(1)}, u32[]{:S(2)}, u32[]{:S(2)}) %collective-permute-start.36) | collective-permute-done | bytes 131104 | tf_op jit(solution)/shard_map/ppermute | solution.py:1109
  338.4 16.5 %attend_grad.2 = (f32[2048,128]{1,0:T(8,128)S(1)}, bf16[2048,128]{1,0:T(8,128)(2,1)}, bf16[2048,128]{1,0:T(8,128)(2,1)}, f32[1,2048]{1,0:T(1,128)}, f32[1,2048]{1,0:T(1,128)S(1)}) custom-call(bf16[2048,128]{1,0:T(8,128)(2,1)S(1)} %copy-done.25, bf16[2048,128]{1,0:T(8,128)(2,1)S(1)} %arrange.5.do_ref, f32[1,2048]{1,0:T(1,128)S(1)} %get-tuple-element.66.lse_ref, ...), custom_call_target="tpu_custom_call" | custom-call | flops 500000000 | bytes 1048576 | tf_op jit(solution)/shard_map/attend_grad/pallas_call | solution.py:203
  360.4 15.6 %attend_grad.3 = (f32[2048,128]{1,0:T(8,128)S(1)}, f32[2048,128]{1,0:T(8,128)S(1)}, f32[2048,128]{1,0:T(8,128)S(1)}, f32[1,2048]{1,0:T(1,128)S(1)}, f32[1,2048]{1,0:T(1,128)S(1)}) custom-call(bf16[2048,128]{1,0:T(8,128)(2,1)S(1)} %copy-done.25, bf16[2048,128]{1,0:T(8,128)(2,1)S(1)} %arrange.5.do_ref, f32[1,2048]{1,0:T(1,128)S(1)} %get-tuple-element.66.lse_ref, ...), custom_call_target="tpu_custom_call" | custom-call | flops 500000000 | bytes 1048576 | tf_op jit(solution)/shard_map/attend_grad/pallas_call | solution.py:203
  381.6 3.4 collective-permute-start.41
  397.2 4.5 collective-permute-done.47
  402.3 6.8 %raw_grad.1 = (bf16[2048,384]{1,0:T(8,128)(2,1)}, f32[2,128]{1,0:T(2,128)}) custom-call(f32[2048,128]{1,0:T(8,128)} %copy-done.80, f32[2048,128]{1,0:T(8,128)} %copy-done.81, bf16[2048,128]{1,0:T(8,128)(2,1)} %collective-permute-done.39.refs_0_.dk_far_ref, f32[2048,128]{1,0:T(8,128)} %copy-done.82, ...), custom_call_target="tpu_custom_call" | custom-call | flops 6000000000 | bytes 1048576 | tf_op jit(solution)/shard_map/raw_grad/pallas_call | solution.py:330
  409.3 4.5 all-to-all-start.2
  416.1 6.5 %qkv_grad.1 = (bf16[1024,384]{1,0:T(8,128)(2,1)S(1)}, bf16[1024,384]{1,0:T(8,128)(2,1)S(1)}) custom-call(bf16[2048,1024]{1,0:T(8,128)(2,1)S(1)} %copy-done.35, bf16[2048,384]{1,0:T(8,128)(2,1)S(1)} %copy-done.56, bf16[2048,384]{1,0:T(8,128)(2,1)} %collective-permute-done.48.grad_other_ref), custom_call_target="tpu_custom_call" | custom-call | flops 10000000000 | bytes 1048576 | tf_op jit(solution)/shard_map/qkv_grad/pallas_call | solution.py:629
  429.2 22.3 %all-to-all-done.2.refs_0_.x_ref = bf16[4,512,384]{2,1,0:T(8,128)(2,1)} async-done(((bf16[4,512,384]{2,1,0:T(8,128)(2,1)}), bf16[4,512,384]{2,1,0:T(8,128)(2,1)}, u32[]{:S(2)}, u32[]{:S(2)}) %all-to-all-start.2) | async-done | bytes 1572896 | tf_op jit(solution)/shard_map/all_to_all | solution.py:1159
  452.8 3.4 own_grad.3.refs_0_
  466.9 4.1 project_grad.2
  471.1 4.9 project_grad.3
  480.1 4.2 all-to-all-start.3
  490.9 3.8 collective-permute-done.56
  495.6 3.4 collective-permute-done.57
  504.3 6.4 %collective-permute-done.58 = f32[8,2048]{1,0:T(8,128)S(1)} collective-permute-done((f32[8,2048]{1,0:T(8,128)S(1)}, f32[8,2048]{1,0:T(8,128)S(1)}, u32[]{:S(2)}, u32[]{:S(2)}) %collective-permute-start.58) | collective-permute-done | bytes 65568 | tf_op jit(solution)/shard_map/ppermute | solution.py:1000
  510.7 4.7 collective-permute-start.59
  525.5 3.0 collective-permute-done.54
  (483 shorter events, 209.9 us)
Async XLA Ops:
  10.5 21.4 %collective-permute-start = (bf16[128,2048]{1,0:T(8,128)(2,1)S(1)}, bf16[128,2048]{1,0:T(8,128)(2,1)}, u32[]{:S(2)}, u32[]{:S(2)}) collective-permute-start(bf16[128,2048]{1,0:T(8,128)(2,1)S(1)} %fusion.20.a_ref), channel_id=1, source_target_pairs={{0,1},{1,0},{2,3},{3,2},{4,5},{5,4},{6,7},{7,6},{8,9},{9,8},{10,11... | collective-permute-start | bytes 1572872 | tf_op jit(solution)/shard_map/ppermute | solution.py:975
  11.0 15.4 %collective-permute-start.1 = (bf16[128,2048]{1,0:T(8,128)(2,1)S(1)}, bf16[128,2048]{1,0:T(8,128)(2,1)S(1)}, u32[]{:S(2)}, u32[]{:S(2)}) collective-permute-start(bf16[128,2048]{1,0:T(8,128)(2,1)S(1)} %fusion.20.a_ref), channel_id=1, source_target_pairs={{0,2},{2,0},{1,3},{3,1},{4,6},{6,4},{5,7},{7,5},{8,10},{10,8},{9,1... | collective-permute-start | bytes 1572872 | tf_op jit(solution)/shard_map/ppermute | solution.py:974
  26.4 14.2 %collective-permute-start.2 = (bf16[128,2048]{1,0:T(8,128)(2,1)S(1)}, bf16[128,2048]{1,0:T(8,128)(2,1)S(1)}, u32[]{:S(2)}, u32[]{:S(2)}) collective-permute-start(bf16[128,2048]{1,0:T(8,128)(2,1)S(1)} %collective-permute-done.1.a_ref), channel_id=1, source_target_pairs={{0,1},{1,0},{2,3},{3,2},{4,5},{5,4},{6,7},{7,6},{8,9},{9,8},{10,11... | collective-permute-start | bytes 1572872 | tf_op jit(solution)/shard_map/ppermute | solution.py:981
  47.8 19.8 %all-to-all-start = ((bf16[4,512,128]{2,1,0:T(8,128)(2,1)}), bf16[4,512,128]{2,1,0:T(8,128)(2,1)S(1)}, u32[]{:S(2)}, u32[]{:S(2)}) async-start(bf16[4,512,128]{2,1,0:T(8,128)(2,1)} %pad_maximum_fusion), calls=%async_computation | async-start | bytes 1048576 | tf_op jit(solution)/shard_map/all_to_all | solution.py:1117
  68.7 15.0 %collective-permute-start.11 = (bf16[2048,128]{1,0:T(8,128)(2,1)S(1)}, bf16[2048,128]{1,0:T(8,128)(2,1)S(1)}, u32[]{:S(2)}, u32[]{:S(2)}) collective-permute-start(bf16[2048,128]{1,0:T(8,128)(2,1)S(1)} %pass_rows.3.refs_1_.v_ref), channel_id=1, source_target_pairs={{0,4},{4,0},{1,5},{5,1},{2,6},{6,2},{3,7},{7,3},{8,12},{12,8},{9,1... | collective-permute-start | bytes 1572872 | tf_op jit(solution)/shard_map/ppermute | solution.py:1121
  73.4 10.2 %collective-permute-start.9 = (bf16[512,128]{1,0:T(8,128)(2,1)S(1)}, bf16[512,128]{1,0:T(8,128)(2,1)S(1)}, u32[]{:S(2)}, u32[]{:S(2)}) collective-permute-start(bf16[512,128]{1,0:T(8,128)(2,1)S(1)} %get-tuple-element.156), channel_id=1, source_target_pairs={{0,16},{8,24},{16,0},{24,8},{1,17},{9,25},{17,1},{25,9},{2,18},{10... | collective-permute-start | bytes 393224 | tf_op jit(solution)/shard_map/ppermute | solution.py:1109
  83.8 14.8 %collective-permute-start.12 = (bf16[2048,128]{1,0:T(8,128)(2,1)S(1)}, bf16[2048,128]{1,0:T(8,128)(2,1)}, u32[]{:S(2)}, u32[]{:S(2)}) collective-permute-start(bf16[2048,128]{1,0:T(8,128)(2,1)S(1)} %arrange.4.refs_0_.k_ref), channel_id=1, source_target_pairs={{0,4},{4,0},{1,5},{5,1},{2,6},{6,2},{3,7},{7,3},{8,12},{12,8},{9,1... | collective-permute-start | bytes 1572872 | tf_op jit(solution)/shard_map/ppermute | solution.py:1121
  85.2 8.5 %collective-permute-start.5 = (bf16[512,128]{1,0:T(8,128)(2,1)}, bf16[512,128]{1,0:T(8,128)(2,1)S(1)}, u32[]{:S(2)}, u32[]{:S(2)}) collective-permute-start(bf16[512,128]{1,0:T(8,128)(2,1)} %get-tuple-element.161), channel_id=1, source_target_pairs={{0,8},{8,16},{16,24},{24,0},{1,9},{9,17},{17,25},{25,1},{2,10},{10... | collective-permute-start | bytes 393224 | tf_op jit(solution)/shard_map/ppermute | solution.py:1109
  85.2 12.3 %collective-permute-start.6 = (bf16[512,128]{1,0:T(8,128)(2,1)}, bf16[512,128]{1,0:T(8,128)(2,1)S(1)}, u32[]{:S(2)}, u32[]{:S(2)}) collective-permute-start(bf16[512,128]{1,0:T(8,128)(2,1)} %get-tuple-element.160), channel_id=1, source_target_pairs={{0,16},{8,24},{16,0},{24,8},{1,17},{9,25},{17,1},{25,9},{2,18},{10... | collective-permute-start | bytes 393224 | tf_op jit(solution)/shard_map/ppermute | solution.py:1109
  88.5 9.0 %collective-permute-start.7 = (bf16[512,128]{1,0:T(8,128)(2,1)}, bf16[512,128]{1,0:T(8,128)(2,1)}, u32[]{:S(2)}, u32[]{:S(2)}) collective-permute-start(bf16[512,128]{1,0:T(8,128)(2,1)} %get-tuple-element.159), channel_id=1, source_target_pairs={{0,24},{8,0},{16,8},{24,16},{1,25},{9,1},{17,9},{25,17},{2,26},{10... | collective-permute-start | bytes 393224 | tf_op jit(solution)/shard_map/ppermute | solution.py:1109
  119.3 17.8 %all-to-all-start.1 = ((bf16[4,512,128]{2,1,0:T(8,128)(2,1)}), bf16[4,512,128]{2,1,0:T(8,128)(2,1)S(1)}, u32[]{:S(2)}, u32[]{:S(2)}) async-start(bf16[4,512,128]{2,1,0:T(8,128)(2,1)} %bitcast.26), calls=%async_computation.1 | async-start | bytes 1048576 | tf_op jit(solution)/shard_map/all_to_all | solution.py:1159
  123.2 103.1 %all-gather.2.cloned.1.call-start = ((), (), s32[]{:S(2)}) async-start(), calls=%async_computation.7 | async-start | bytes 5242880 | tf_op jit(solution)/shard_map/all_gather | solution.py:1169
  142.9 13.1 %collective-permute-start.13 = (bf16[128,2048]{1,0:T(8,128)(2,1)}, bf16[128,2048]{1,0:T(8,128)(2,1)S(1)}, u32[]{:S(2)}, u32[]{:S(2)}) collective-permute-start(bf16[128,2048]{1,0:T(8,128)(2,1)} %get-tuple-element.57), channel_id=1, source_target_pairs={{0,1},{1,0},{2,3},{3,2},{4,5},{5,4},{6,7},{7,6},{8,9},{9,8},{10,11... | collective-permute-start | bytes 1572872 | tf_op jit(solution)/shard_map/ppermute | solution.py:988
  145.5 214.9 %reduce-scatter.4.cloned.1.call-start = ((), (), s32[]{:S(2)}) async-start(), calls=%async_computation.8 | async-start | bytes 5242880 | tf_op jit(solution)/shard_map/reduce_scatter | solution.py:1307
  146.9 13.9 %collective-permute-start.15 = (bf16[128,2048]{1,0:T(8,128)(2,1)S(1)}, bf16[128,2048]{1,0:T(8,128)(2,1)S(1)}, u32[]{:S(2)}, u32[]{:S(2)}) collective-permute-start(bf16[128,2048]{1,0:T(8,128)(2,1)S(1)} %add_convert_fusion.3.refs_0_), channel_id=1, source_target_pairs={{0,2},{2,0},{1,3},{3,1},{4,6},{6,4},{5,7},{7,5},{8,10},{10,8},{9,1... | collective-permute-start | bytes 1572872 | tf_op jit(solution)/shard_map/ppermute | solution.py:987
  161.6 13.2 %collective-permute-start.18 = (bf16[128,2048]{1,0:T(8,128)(2,1)S(1)}, bf16[128,2048]{1,0:T(8,128)(2,1)S(1)}, u32[]{:S(2)}, u32[]{:S(2)}) collective-permute-start(bf16[128,2048]{1,0:T(8,128)(2,1)S(1)} %get-tuple-element.60.a_ref.refs_0_), channel_id=1, source_target_pairs={{0,2},{2,0},{1,3},{3,1},{4,6},{6,4},{5,7},{7,5},{8,10},{10,8},{9,1... | collective-permute-start | bytes 1572872 | tf_op jit(solution)/shard_map/ppermute | solution.py:974
  163.3 11.6 %collective-permute-start.16 = (bf16[128,2048]{1,0:T(8,128)(2,1)S(1)}, bf16[128,2048]{1,0:T(8,128)(2,1)S(1)}, u32[]{:S(2)}, u32[]{:S(2)}) collective-permute-start(bf16[128,2048]{1,0:T(8,128)(2,1)S(1)} %get-tuple-element.60.a_ref.refs_0_), channel_id=1, source_target_pairs={{0,1},{1,0},{2,3},{3,2},{4,5},{5,4},{6,7},{7,6},{8,9},{9,8},{10,11... | collective-permute-start | bytes 1572872 | tf_op jit(solution)/shard_map/ppermute | solution.py:975
  184.5 13.9 %collective-permute-start.22 = (bf16[256,1024]{1,0:T(8,128)(2,1)S(1)}, bf16[256,1024]{1,0:T(8,128)(2,1)S(1)}, u32[]{:S(2)}, u32[]{:S(2)}) collective-permute-start(bf16[256,1024]{1,0:T(8,128)(2,1)S(1)} %pad_maximum_fusion.1), channel_id=1, source_target_pairs={{0,4},{4,0},{1,5},{5,1},{2,6},{6,2},{3,7},{7,3},{8,12},{12,8},{9,1... | collective-permute-start | bytes 1572872 | tf_op jit(solution)/shard_map/ppermute | solution.py:1062
  186.1 12.3 %collective-permute-start.17 = (bf16[128,2048]{1,0:T(8,128)(2,1)S(1)}, bf16[128,2048]{1,0:T(8,128)(2,1)S(1)}, u32[]{:S(2)}, u32[]{:S(2)}) collective-permute-start(bf16[128,2048]{1,0:T(8,128)(2,1)S(1)} %get-tuple-element.149), channel_id=1, source_target_pairs={{0,1},{1,0},{2,3},{3,2},{4,5},{5,4},{6,7},{7,6},{8,9},{9,8},{10,11... | collective-permute-start | bytes 1572872 | tf_op jit(solution)/shard_map/ppermute | solution.py:988
  186.3 14.4 %collective-permute-start.21 = (bf16[128,2048]{1,0:T(8,128)(2,1)S(1)}, bf16[128,2048]{1,0:T(8,128)(2,1)S(1)}, u32[]{:S(2)}, u32[]{:S(2)}) collective-permute-start(bf16[128,2048]{1,0:T(8,128)(2,1)S(1)} %add_convert_fusion.2), channel_id=1, source_target_pairs={{0,2},{2,0},{1,3},{3,1},{4,6},{6,4},{5,7},{7,5},{8,10},{10,8},{9,1... | collective-permute-start | bytes 1572872 | tf_op jit(solution)/shard_map/ppermute | solution.py:987
  202.3 13.6 %collective-permute-start.25 = (bf16[128,2048]{1,0:T(8,128)(2,1)S(1)}, bf16[128,2048]{1,0:T(8,128)(2,1)S(1)}, u32[]{:S(2)}, u32[]{:S(2)}) collective-permute-start(bf16[128,2048]{1,0:T(8,128)(2,1)S(1)} %get-tuple-element.63.a_ref), channel_id=1, source_target_pairs={{0,2},{2,0},{1,3},{3,1},{4,6},{6,4},{5,7},{7,5},{8,10},{10,8},{9,1... | collective-permute-start | bytes 1572872 | tf_op jit(solution)/shard_map/ppermute | solution.py:974
  203.9 12.1 %collective-permute-start.23 = (bf16[128,2048]{1,0:T(8,128)(2,1)S(1)}, bf16[128,2048]{1,0:T(8,128)(2,1)S(1)}, u32[]{:S(2)}, u32[]{:S(2)}) collective-permute-start(bf16[128,2048]{1,0:T(8,128)(2,1)S(1)} %get-tuple-element.63.a_ref), channel_id=1, source_target_pairs={{0,1},{1,0},{2,3},{3,2},{4,5},{5,4},{6,7},{7,6},{8,9},{9,8},{10,11... | collective-permute-start | bytes 1572872 | tf_op jit(solution)/shard_map/ppermute | solution.py:975
  204.0 19.2 %collective-permute-start.27 = (bf16[256,1024]{1,0:T(8,128)(2,1)S(1)}, bf16[256,1024]{1,0:T(8,128)(2,1)S(1)}, u32[]{:S(2)}, u32[]{:S(2)}) collective-permute-start(bf16[256,1024]{1,0:T(8,128)(2,1)S(1)} %pad_maximum_fusion.2), channel_id=1, source_target_pairs={{0,4},{4,0},{1,5},{5,1},{2,6},{6,2},{3,7},{7,3},{8,12},{12,8},{9,1... | collective-permute-start | bytes 1572872 | tf_op jit(solution)/shard_map/ppermute | solution.py:1062
  215.9 8.1 %collective-permute-start.26 = (bf16[128,2048]{1,0:T(8,128)(2,1)S(1)}, bf16[128,2048]{1,0:T(8,128)(2,1)S(1)}, u32[]{:S(2)}, u32[]{:S(2)}) collective-permute-start(bf16[128,2048]{1,0:T(8,128)(2,1)S(1)} %collective-permute-done.25.a_ref), channel_id=1, source_target_pairs={{0,1},{1,0},{2,3},{3,2},{4,5},{5,4},{6,7},{7,6},{8,9},{9,8},{10,11... | collective-permute-start | bytes 1572872 | tf_op jit(solution)/shard_map/ppermute | solution.py:981
  250.3 212.5 %reduce-scatter.6.cloned.1.call-start = ((), (), s32[]{:S(2)}) async-start(), calls=%async_computation.9 | async-start | bytes 5242880 | tf_op jit(solution)/shard_map/reduce_scatter | solution.py:1308
  254.7 14.3 %collective-permute-start.30 = (bf16[2,2,256,256]{3,2,1,0:T(8,128)(2,1)}, bf16[2,2,256,256]{3,2,1,0:T(8,128)(2,1)}, u32[]{:S(2)}, u32[]{:S(2)}) collective-permute-start(bf16[2,2,256,256]{3,2,1,0:T(8,128)(2,1)} %pad_maximum_fusion.3), channel_id=1, source_target_pairs={{0,4},{4,0},{1,5},{5,1},{2,6},{6,2},{3,7},{7,3},{8,12},{12,8},{9,1... | collective-permute-start | bytes 1572872 | tf_op jit(solution)/shard_map/ppermute | solution.py:1271
  257.2 11.7 %collective-permute-start.24 = (bf16[128,2048]{1,0:T(8,128)(2,1)}, bf16[128,2048]{1,0:T(8,128)(2,1)}, u32[]{:S(2)}, u32[]{:S(2)}) collective-permute-start(bf16[128,2048]{1,0:T(8,128)(2,1)} %get-tuple-element.143), channel_id=1, source_target_pairs={{0,1},{1,0},{2,3},{3,2},{4,5},{5,4},{6,7},{7,6},{8,9},{9,8},{10,11... | collective-permute-start | bytes 1572872 | tf_op jit(solution)/shard_map/ppermute | solution.py:988
  257.2 14.7 %collective-permute-start.29 = (bf16[128,2048]{1,0:T(8,128)(2,1)}, bf16[128,2048]{1,0:T(8,128)(2,1)}, u32[]{:S(2)}, u32[]{:S(2)}) collective-permute-start(bf16[128,2048]{1,0:T(8,128)(2,1)} %add_convert_fusion.1.refs_0_), channel_id=1, source_target_pairs={{0,2},{2,0},{1,3},{3,1},{4,6},{6,4},{5,7},{7,5},{8,10},{10,8},{9,1... | collective-permute-start | bytes 1572872 | tf_op jit(solution)/shard_map/ppermute | solution.py:987
  280.8 13.6 %collective-permute-start.31 = (bf16[128,2048]{1,0:T(8,128)(2,1)S(1)}, bf16[128,2048]{1,0:T(8,128)(2,1)S(1)}, u32[]{:S(2)}, u32[]{:S(2)}) collective-permute-start(bf16[128,2048]{1,0:T(8,128)(2,1)S(1)} %get-tuple-element.65.a_ref), channel_id=1, source_target_pairs={{0,2},{2,0},{1,3},{3,1},{4,6},{6,4},{5,7},{7,5},{8,10},{10,8},{9,1... | collective-permute-start | bytes 1572872 | tf_op jit(solution)/shard_map/ppermute | solution.py:974
  282.8 12.2 %collective-permute-start.34 = (bf16[128,2048]{1,0:T(8,128)(2,1)S(1)}, bf16[128,2048]{1,0:T(8,128)(2,1)S(1)}, u32[]{:S(2)}, u32[]{:S(2)}) collective-permute-start(bf16[128,2048]{1,0:T(8,128)(2,1)S(1)} %get-tuple-element.65.a_ref), channel_id=1, source_target_pairs={{0,1},{1,0},{2,3},{3,2},{4,5},{5,4},{6,7},{7,6},{8,9},{9,8},{10,11... | collective-permute-start | bytes 1572872 | tf_op jit(solution)/shard_map/ppermute | solution.py:975
  282.9 14.5 %collective-permute-start.33 = (bf16[2,2,256,256]{3,2,1,0:T(8,128)(2,1)S(1)}, bf16[2,2,256,256]{3,2,1,0:T(8,128)(2,1)S(1)}, u32[]{:S(2)}, u32[]{:S(2)}) collective-permute-start(bf16[2,2,256,256]{3,2,1,0:T(8,128)(2,1)S(1)} %pad_maximum_fusion.4), channel_id=1, source_target_pairs={{0,4},{4,0},{1,5},{5,1},{2,6},{6,2},{3,7},{7,3},{8,12},{12,8},{9,1... | collective-permute-start | bytes 1572872 | tf_op jit(solution)/shard_map/ppermute | solution.py:1271
  294.4 8.8 %collective-permute-start.38 = (f32[2,512]{0,1:T(8,128)S(1)}, f32[2,512]{0,1:T(8,128)S(1)}, u32[]{:S(2)}, u32[]{:S(2)}) collective-permute-start(f32[2,512]{0,1:T(8,128)S(1)} %convert_bitcast_fusion.1), channel_id=1, source_target_pairs={{0,4},{4,0},{1,5},{5,1},{2,6},{6,2},{3,7},{7,3},{8,12},{12,8},{9,1... | collective-permute-start | bytes 12296 | tf_op jit(solution)/shard_map/ppermute | solution.py:1188
  298.9 10.8 %collective-permute-start.35 = (bf16[512,128]{1,0:T(8,128)(2,1)S(1)}, bf16[512,128]{1,0:T(8,128)(2,1)S(1)}, u32[]{:S(2)}, u32[]{:S(2)}) collective-permute-start(bf16[512,128]{1,0:T(8,128)(2,1)S(1)} %get-tuple-element.153), channel_id=1, source_target_pairs={{0,8},{8,16},{16,24},{24,0},{1,9},{9,17},{17,25},{25,1},{2,10},{10... | collective-permute-start | bytes 393224 | tf_op jit(solution)/shard_map/ppermute | solution.py:1109
  320.5 13.2 %collective-permute-start.36 = (bf16[512,128]{1,0:T(8,128)(2,1)S(1)}, bf16[512,128]{1,0:T(8,128)(2,1)S(1)}, u32[]{:S(2)}, u32[]{:S(2)}) collective-permute-start(bf16[512,128]{1,0:T(8,128)(2,1)S(1)} %get-tuple-element.152), channel_id=1, source_target_pairs={{0,16},{8,24},{16,0},{24,8},{1,17},{9,25},{17,1},{25,9},{2,18},{10... | collective-permute-start | bytes 393224 | tf_op jit(solution)/shard_map/ppermute | solution.py:1109
  322.9 10.8 %collective-permute-start.37 = (bf16[512,128]{1,0:T(8,128)(2,1)S(1)}, bf16[512,128]{1,0:T(8,128)(2,1)S(1)}, u32[]{:S(2)}, u32[]{:S(2)}) collective-permute-start(bf16[512,128]{1,0:T(8,128)(2,1)S(1)} %get-tuple-element.151), channel_id=1, source_target_pairs={{0,24},{8,0},{16,8},{24,16},{1,25},{9,1},{17,9},{25,17},{2,26},{10... | collective-permute-start | bytes 393224 | tf_op jit(solution)/shard_map/ppermute | solution.py:1109
  355.8 25.6 %collective-permute-start.39 = (bf16[2048,128]{1,0:T(8,128)(2,1)}, bf16[2048,128]{1,0:T(8,128)(2,1)}, u32[]{:S(2)}, u32[]{:S(2)}) collective-permute-start(bf16[2048,128]{1,0:T(8,128)(2,1)} %get-tuple-element.70), channel_id=1, source_target_pairs={{0,4},{4,0},{1,5},{5,1},{2,6},{6,2},{3,7},{7,3},{8,12},{12,8},{9,1... | collective-permute-start | bytes 1572872 | tf_op jit(solution)/shard_map/ppermute | solution.py:1332
  357.3 24.1 %collective-permute-start.40 = (bf16[2048,128]{1,0:T(8,128)(2,1)}, bf16[2048,128]{1,0:T(8,128)(2,1)}, u32[]{:S(2)}, u32[]{:S(2)}) collective-permute-start(bf16[2048,128]{1,0:T(8,128)(2,1)} %get-tuple-element.72), channel_id=1, source_target_pairs={{0,4},{4,0},{1,5},{5,1},{2,6},{6,2},{3,7},{7,3},{8,12},{12,8},{9,1... | collective-permute-start | bytes 1572872 | tf_op jit(solution)/shard_map/ppermute | solution.py:1332
  358.9 22.5 %collective-permute-start.43 = (f32[1,2048]{1,0:T(1,128)S(1)}, f32[1,2048]{1,0:T(1,128)S(1)}, u32[]{:S(2)}, u32[]{:S(2)}) collective-permute-start(f32[1,2048]{1,0:T(1,128)S(1)} %get-tuple-element.75), channel_id=1, source_target_pairs={{0,4},{4,0},{1,5},{5,1},{2,6},{6,2},{3,7},{7,3},{8,12},{12,8},{9,1... | collective-permute-start | bytes 24584 | tf_op jit(solution)/shard_map/ppermute | solution.py:1335
  409.3 42.3 %all-to-all-start.2 = ((bf16[4,512,384]{2,1,0:T(8,128)(2,1)}), bf16[4,512,384]{2,1,0:T(8,128)(2,1)}, u32[]{:S(2)}, u32[]{:S(2)}) async-start(bf16[4,512,384]{2,1,0:T(8,128)(2,1)} %bitcast.300), calls=%async_computation.3 | async-start | bytes 3145728 | tf_op jit(solution)/shard_map/all_to_all | solution.py:1159
  413.8 105.4 %reduce-scatter.8.cloned.1.call-start = ((), (), s32[]{:S(2)}) async-start(), calls=%async_computation.10 | async-start | bytes 2621440 | tf_op jit(solution)/shard_map/reduce_scatter | solution.py:1401
  427.7 23.8 %collective-permute-start.50 = (bf16[4,256,384]{2,1,0:T(8,128)(2,1)}, bf16[4,256,384]{2,1,0:T(8,128)(2,1)S(1)}, u32[]{:S(2)}, u32[]{:S(2)}) collective-permute-start(bf16[4,256,384]{2,1,0:T(8,128)(2,1)} %get-tuple-element.134), channel_id=1, source_target_pairs={{0,4},{4,0},{1,5},{5,1},{2,6},{6,2},{3,7},{7,3},{8,12},{12,8},{9,1... | collective-permute-start | bytes 2359304 | tf_op jit(solution)/shard_map/ppermute | solution.py:1391
  461.4 54.0 %collective-permute-start.60 = (bf16[4,256,256]{2,1,0:T(8,128)(2,1)}, bf16[4,256,256]{2,1,0:T(8,128)(2,1)}, u32[]{:S(2)}, u32[]{:S(2)}) collective-permute-start(bf16[4,256,256]{2,1,0:T(8,128)(2,1)} %dynamic-slice_bitcast_fusion.2), channel_id=1, source_target_pairs={{0,4},{4,0},{1,5},{5,1},{2,6},{6,2},{3,7},{7,3},{8,12},{12,8},{9,1... | collective-permute-start | bytes 1572872 | tf_op jit(solution)/shard_map/ppermute | solution.py:1042
  476.0 23.1 %collective-permute-start.51 = (bf16[128,2048]{1,0:T(8,128)(2,1)}, bf16[128,2048]{1,0:T(8,128)(2,1)S(1)}, u32[]{:S(2)}, u32[]{:S(2)}) collective-permute-start(bf16[128,2048]{1,0:T(8,128)(2,1)} %get-tuple-element.81), channel_id=1, source_target_pairs={{0,1},{1,0},{2,3},{3,2},{4,5},{5,4},{6,7},{7,6},{8,9},{9,8},{10,11... | collective-permute-start | bytes 1572872 | tf_op jit(solution)/shard_map/ppermute | solution.py:988
  477.4 21.7 %collective-permute-start.53 = (bf16[128,2048]{1,0:T(8,128)(2,1)}, bf16[128,2048]{1,0:T(8,128)(2,1)S(1)}, u32[]{:S(2)}, u32[]{:S(2)}) collective-permute-start(bf16[128,2048]{1,0:T(8,128)(2,1)} %add_convert_fusion), channel_id=1, source_target_pairs={{0,2},{2,0},{1,3},{3,1},{4,6},{6,4},{5,7},{7,5},{8,10},{10,8},{9,1... | collective-permute-start | bytes 1572872 | tf_op jit(solution)/shard_map/ppermute | solution.py:987
  480.1 42.3 %all-to-all-start.3 = ((bf16[4,256,384]{2,1,0:T(8,128)(2,1)}), bf16[4,256,384]{2,1,0:T(8,128)(2,1)}, u32[]{:S(2)}, u32[]{:S(2)}) async-start(bf16[4,256,384]{2,1,0:T(8,128)(2,1)} %add_rows.1), calls=%async_computation.5 | async-start | bytes 1572864 | tf_op jit(solution)/shard_map/all_to_all | solution.py:1416
  502.3 8.4 %collective-permute-start.58 = (f32[8,2048]{1,0:T(8,128)S(1)}, f32[8,2048]{1,0:T(8,128)S(1)}, u32[]{:S(2)}, u32[]{:S(2)}) collective-permute-start(f32[8,2048]{1,0:T(8,128)S(1)} %pass_rows.5), channel_id=1, source_target_pairs={{0,8},{8,0},{16,24},{24,16},{1,9},{9,1},{17,25},{25,17},{2,10},{10... | collective-permute-start | bytes 196616 | tf_op jit(solution)/shard_map/ppermute | solution.py:1000
  510.7 8.4 %collective-permute-start.59 = (f32[8,2048]{1,0:T(8,128)S(1)}, f32[8,2048]{1,0:T(8,128)S(1)}, u32[]{:S(2)}, u32[]{:S(2)}) collective-permute-start(f32[8,2048]{1,0:T(8,128)S(1)} %add.293), channel_id=1, source_target_pairs={{0,16},{8,24},{16,0},{24,8},{1,17},{9,25},{17,1},{25,9},{2,18},{10... | collective-permute-start | bytes 196616 | tf_op jit(solution)/shard_map/ppermute | solution.py:1000
  520.2 8.3 %collective-permute-start.54 = (bf16[4,256,128]{2,1,0:T(8,128)(2,1)S(1)}, bf16[4,256,128]{2,1,0:T(8,128)(2,1)}, u32[]{:S(2)}, u32[]{:S(2)}) collective-permute-start(bf16[4,256,128]{2,1,0:T(8,128)(2,1)S(1)} %dynamic-slice_bitcast_fusion.3), channel_id=1, source_target_pairs={{0,4},{4,0},{1,5},{5,1},{2,6},{6,2},{3,7},{7,3},{8,12},{12,8},{9,1... | collective-permute-start | bytes 786440 | tf_op jit(solution)/shard_map/ppermute | solution.py:1042
  (132 other events, 1053.3 us)
Sparse Core Ops, SparseCore 0:
  145.6 80.6 all-gather.1
  250.5 79.4 reduce-scatter.3
  332.4 81.4 reduce-scatter.5
  457.8 53.1 reduce-scatter.7

commit v6 on v5

--- a/solution.py
+++ b/solution.py
@@ -1365,12 +1365,10 @@
         jnp.zeros((2, model_width), f32), gain_sums, (wt_pos * z_count + z_pos) * HEAD_DIM, 1
     )
 
-    def sum_all(a):
+    def sum_plane(a):
         a = a + lax.ppermute(a, "c", SWAP)
         a = a + lax.ppermute(a, "y", SWAP)
-        a = a + lax.ppermute(a, "x", SWAP) if pair else lax.psum(a, "x")
-        a = pass_rows(a, (input_grad,))
-        return sum_line(a, z_count)
+        return a + lax.ppermute(a, "x", SWAP) if pair else lax.psum(a, "x")
 
     grad_mine, grad_other = qkv_grad(
         normed_line, d_raw, lax.ppermute(d_raw, "c", SWAP), z_count
@@ -1394,10 +1392,12 @@
         qkv_line = scatter_x(qkv_line).astype(bf16)
         qkv_line = (qkv_line, jnp.zeros_like(qkv_line))
     d_proj = to_tokens(d_raw, 3 * HEAD_DIM)
+    small = sum_plane(stack_rows(gain_first, gain_second, gain_full, router_rows))
     out_part = own_grad(
-        d_resid_h, (attn_parts, attn_parts), (d_proj, qkv_line[1])
-    )
-    far_n = project_grad_half(d_proj, 1, qkv_b, (out_part, gate_up_sum))
+        d_resid_h, (attn_parts, attn_parts), (d_proj, qkv_line[1], small)
+    )
+    small = sum_line(small, z_count)
+    far_n = project_grad_half(d_proj, 1, qkv_b, (out_part, gate_up_sum, small))
     out_part = lax.psum_scatter(out_part, "z", scatter_dimension=1, tiled=True)
     near_n = project_grad_half(d_proj, 0, qkv_b, (far_n[0],))
     d_normed, _ = scatter_halves(near_n, far_n)
@@ -1408,7 +1408,6 @@
         norm_gains[0],
         (bf16,),
     )
-    small = sum_all(stack_rows(gain_first, gain_second, gain_full, router_rows))
 
     gains_grad = small[:4]
     router_grad = small[4:].T

time: 547 us -> 538 us (0.984)
  starting transfers between devices: 79.6 us -> 73.3 us
    all_to_all x2, waiting for transfers between devices: 33.5 us -> 14.3 us  [to_tokens(): lax.all_to_all(rows.reshape(z_count, tok_rows, cols), 'z', 0, 0, tiled=True)]
    ppermute x6, starting transfers between devices: 14.7 us -> 8.14 us  [sum_line(): a = a + lax.ppermute(a, 'z', [(i, i ^ step) for i in range(z_count)])]
    unnamed x224 -> x218, local copies, waits for them, and re-layouts: 64.1 us -> 60.3 us
  transfers between devices with their start and end apart: 69 -> 69, of which waited for: 33 -> 35; matrix products, arithmetic and copies ran while one was open for 13% -> 13% of each run, Pallas kernels for 18% -> 19%
where the time goes in v6:
time: 538 us; the launch traced here: 529 us
  waiting for transfers between devices  170 us (32%)
  Pallas kernels  130 us (24%)
  local copies, waits for them, and re-layouts  81 us (15%)
  starting transfers between devices  73.3 us (14%)
  other arithmetic  37.3 us (7%)
  matrix products  21.2 us (4%)
  between operations  15.9 us (3%)
    unnamed x218, local copies, waits for them, and re-layouts  60.3 us
    ppermute x9, waiting for transfers between devices, to_heads_apart(): lax.ppermute(there, 'z', [(i, (i + d) % z_count) for i in range(z_count)])  33.4 us
    pallas_call x2, Pallas kernels, attend_grad(): pl.pallas_call(functools.partial(attend_grad_kernel, chunk, LOG2E / math....  32.1 us
    ppermute x4, waiting for transfers between devices, gather_near(): far = lax.ppermute(rows, 'y', SWAP)  29.1 us
    ppermute x6, waiting for transfers between devices, sum_line(): a = a + lax.ppermute(a, 'z', [(i, i ^ step) for i in range(z_count)])  18.7 us
    pallas_call x1, Pallas kernels, attend(): pl.pallas_call(functools.partial(attend_kernel, len(key_groups), chunk, L...  16.9 us
    ppermute x4, waiting for transfers between devices, scatter_halves(): far_got = lax.ppermute(sent, 'y', SWAP)  15.5 us
    all_to_all x2, waiting for transfers between devices, to_tokens(): lax.all_to_all(rows.reshape(z_count, tok_rows, cols), 'z', 0, 0, tiled=True)  14.3 us
  transfers between devices with their start and end apart: 69, of which 35 were waited for; matrix products, arithmetic and copies ran while one was open for 13% of the time, Pallas kernels for 19%

profile of v6, /device:TPU:0, one launch (start us, length us, event | category | flops | bytes accessed | tf_op | source)
XLA Modules:
  0.0 528.5 jit_solution(16504068253180169745)
XLA Ops:
  17.7 8.0 %convert_element_type.183.w_ref = bf16[3,2048,512]{2,1,0:T(8,128)(2,1)} convert(f32[3,2048,512]{2,1,0:T(8,128)} %param.16) | non-fusion elementwise | flops 3145728 | bytes 18874368 | tf_op jit(solution)/shard_map/convert_element_type | solution.py:1035
  26.6 3.7 multiply_sine_fusion
  35.8 4.7 project.2
  40.9 4.7 project.3
  47.8 4.9 all-to-all-start
  57.3 5.1 pack_heads.1
  62.4 5.1 all-to-all-done
  73.5 5.1 collective-permute-done.10.refs_3_
  80.2 3.5 collective-permute-done.9.refs_2_
  85.2 3.3 collective-permute-start.6
  90.6 3.1 collective-permute-done.5.refs_1_
  93.7 3.8 collective-permute-done.6.refs_2_
  100.5 16.9 %attend.1 = (f32[2048,128]{1,0:T(8,128)S(1)}, f32[1,2048]{1,0:T(1,128)S(1)}) custom-call(bf16[2048,128]{1,0:T(8,128)(2,1)S(1)} %arrange.3.q_ref, s32[1,2048]{1,0:T(1,128)S(1)} %bitcast.305, s32[1,2048]{1,0:T(1,128)S(1)} %bitcast.310, bf16[2048,128]{1,0:T(8,128)(2,1)S(1)} %arrange.4.refs_0_.k_ref, bf16[2048,128]{1,0:T(8,128)(2,1)S(1)} %pass_rows.2.refs_1_.v_ref, ...), custom_call_target="tpu_custom_call" | custom-call | flops 19000000512 | bytes 1048576 | tf_op jit(solution)/shard_map/attend/pallas_call | solution.py:97
  119.2 3.8 all-to-all-start.1
  125.7 11.2 %all-to-all-done.1.x_ref.refs_0_.n0_ref.n1_ref = bf16[4,512,128]{2,1,0:T(8,128)(2,1)S(1)} async-done(((bf16[4,512,128]{2,1,0:T(8,128)(2,1)}), bf16[4,512,128]{2,1,0:T(8,128)(2,1)S(1)}, u32[]{:S(2)}, u32[]{:S(2)}) %all-to-all-start.1) | async-done | bytes 524320 | tf_op jit(solution)/shard_map/all_to_all | solution.py:1159
  148.5 6.5 %copy-done.78 = f32[2,4,2048,256]{3,2,1,0:T(8,128)S(1)} copy-done((f32[2,4,2048,256]{3,2,1,0:T(8,128)S(1)}, f32[2,4,2048,256]{3,2,1,0:T(8,128)}, u32[]{:S(2)}) %copy-start.78) | copy-done | bytes 16777240
  155.9 4.8 collective-permute-done.15.far_got
  163.2 3.4 copy-done.79
  167.0 7.6 %collective-permute-done.18.in_ref = bf16[128,2048]{1,0:T(8,128)(2,1)S(1)} collective-permute-done((bf16[128,2048]{1,0:T(8,128)(2,1)S(1)}, bf16[128,2048]{1,0:T(8,128)(2,1)S(1)}, u32[]{:S(2)}, u32[]{:S(2)}) %collective-permute-start.18) | collective-permute-done | bytes 524320 | tf_op jit(solution)/shard_map/ppermute | solution.py:974
  188.0 10.3 %collective-permute-done.22.refs_0_.refs_2_ = bf16[256,1024]{1,0:T(8,128)(2,1)S(1)} collective-permute-done((bf16[256,1024]{1,0:T(8,128)(2,1)S(1)}, bf16[256,1024]{1,0:T(8,128)(2,1)S(1)}, u32[]{:S(2)}, u32[]{:S(2)}) %collective-permute-start.22) | collective-permute-done | bytes 524320 | tf_op jit(solution)/shard_map/ppermute | solution.py:1062
  205.1 10.7 %collective-permute-done.25.a_ref = bf16[128,2048]{1,0:T(8,128)(2,1)S(1)} collective-permute-done((bf16[128,2048]{1,0:T(8,128)(2,1)S(1)}, bf16[128,2048]{1,0:T(8,128)(2,1)S(1)}, u32[]{:S(2)}, u32[]{:S(2)}) %collective-permute-start.25) | collective-permute-done | bytes 524320 | tf_op jit(solution)/shard_map/ppermute | solution.py:974
  234.4 3.9 fusion.31
  244.7 3.5 own_grad.2.refs_0_
  259.6 9.3 %collective-permute-done.30.refs_1_.refs_6_ = bf16[2,2,256,256]{3,2,1,0:T(8,128)(2,1)} collective-permute-done((bf16[2,2,256,256]{3,2,1,0:T(8,128)(2,1)}, bf16[2,2,256,256]{3,2,1,0:T(8,128)(2,1)}, u32[]{:S(2)}, u32[]{:S(2)}) %collective-permute-start.30) | collective-permute-done | bytes 524320 | tf_op jit(solution)/shard_map/ppermute | solution.py:1271
  277.5 3.2 resid_grad_kernel.1
  283.4 10.9 %collective-permute-done.31.a_ref = bf16[128,2048]{1,0:T(8,128)(2,1)S(1)} collective-permute-done((bf16[128,2048]{1,0:T(8,128)(2,1)S(1)}, bf16[128,2048]{1,0:T(8,128)(2,1)S(1)}, u32[]{:S(2)}, u32[]{:S(2)}) %collective-permute-start.31) | collective-permute-done | bytes 524320 | tf_op jit(solution)/shard_map/ppermute | solution.py:974
  298.9 4.2 collective-permute-done.38
  303.1 6.6 %collective-permute-done.35.refs_9_.refs_1_ = bf16[512,128]{1,0:T(8,128)(2,1)S(1)} collective-permute-done((bf16[512,128]{1,0:T(8,128)(2,1)S(1)}, bf16[512,128]{1,0:T(8,128)(2,1)S(1)}, u32[]{:S(2)}, u32[]{:S(2)}) %collective-permute-start.35) | collective-permute-done | bytes 131104 | tf_op jit(solution)/shard_map/ppermute | solution.py:1109
  309.7 8.7 %weight_grad.1.refs_4_.refs_0_ = bf16[8,1024,256]{2,1,0:T(8,128)(2,1)S(1)} custom-call(s32[1]{0:T(128)} %bitcast.71.at_ref, bf16[256,2048]{1,0:T(8,128)(2,1)S(1)} %join_rows.10.refs_0_, bf16[256,2048]{1,0:T(8,128)(2,1)S(1)} %copy-done.6, bf16[256,1024]{1,0:T(8,128)(2,1)S(1)} %copy-done.40, bf16[256,1024]{1,0:T(8,128)(2,1)S(1)} %copy-done.52, ...), custom_call_target="tpu_custom_call" | custom-call | flops 100000000 | bytes 1048576 | tf_op jit(solution)/shard_map/weight_grad/pallas_call | solution.py:401
  323.9 9.8 %collective-permute-done.36.refs_2_ = bf16[512,128]{1,0:T(8,128)(2,1)S(1)} collective-permute-done((bf16[512,128]{1,0:T(8,128)(2,1)S(1)}, bf16[512,128]{1,0:T(8,128)(2,1)S(1)}, u32[]{:S(2)}, u32[]{:S(2)}) %collective-permute-start.36) | collective-permute-done | bytes 131104 | tf_op jit(solution)/shard_map/ppermute | solution.py:1109
  338.3 16.5 %attend_grad.2 = (f32[2048,128]{1,0:T(8,128)S(1)}, bf16[2048,128]{1,0:T(8,128)(2,1)}, bf16[2048,128]{1,0:T(8,128)(2,1)}, f32[1,2048]{1,0:T(1,128)}, f32[1,2048]{1,0:T(1,128)S(1)}) custom-call(bf16[2048,128]{1,0:T(8,128)(2,1)S(1)} %copy-done.23, bf16[2048,128]{1,0:T(8,128)(2,1)S(1)} %arrange.5.do_ref, f32[1,2048]{1,0:T(1,128)S(1)} %get-tuple-element.66.lse_ref, ...), custom_call_target="tpu_custom_call" | custom-call | flops 500000000 | bytes 1048576 | tf_op jit(solution)/shard_map/attend_grad/pallas_call | solution.py:203
  359.4 15.6 %attend_grad.3 = (f32[2048,128]{1,0:T(8,128)S(1)}, f32[2048,128]{1,0:T(8,128)S(1)}, f32[2048,128]{1,0:T(8,128)S(1)}, f32[1,2048]{1,0:T(1,128)S(1)}, f32[1,2048]{1,0:T(1,128)S(1)}) custom-call(bf16[2048,128]{1,0:T(8,128)(2,1)S(1)} %copy-done.23, bf16[2048,128]{1,0:T(8,128)(2,1)S(1)} %arrange.5.do_ref, f32[1,2048]{1,0:T(1,128)S(1)} %get-tuple-element.66.lse_ref, ...), custom_call_target="tpu_custom_call" | custom-call | flops 500000000 | bytes 1048576 | tf_op jit(solution)/shard_map/attend_grad/pallas_call | solution.py:203
  378.0 3.4 collective-permute-done.43.k_far_ref
  381.5 3.4 collective-permute-start.41
  397.1 4.5 collective-permute-done.47
  402.3 6.8 %raw_grad.1 = (bf16[2048,384]{1,0:T(8,128)(2,1)}, f32[2,128]{1,0:T(2,128)}) custom-call(f32[2048,128]{1,0:T(8,128)} %copy-done.80, f32[2048,128]{1,0:T(8,128)} %copy-done.81, bf16[2048,128]{1,0:T(8,128)(2,1)} %collective-permute-done.39.refs_0_.dk_far_ref, f32[2048,128]{1,0:T(8,128)} %copy-done.82, ...), custom_call_target="tpu_custom_call" | custom-call | flops 6000000000 | bytes 1048576 | tf_op jit(solution)/shard_map/raw_grad/pallas_call | solution.py:330
  409.2 4.5 all-to-all-start.2
  416.0 7.2 %qkv_grad.1 = (bf16[1024,384]{1,0:T(8,128)(2,1)S(1)}, bf16[1024,384]{1,0:T(8,128)(2,1)}) custom-call(bf16[2048,1024]{1,0:T(8,128)(2,1)S(1)} %copy-done.33, bf16[2048,384]{1,0:T(8,128)(2,1)S(1)} %copy-done.53, bf16[2048,384]{1,0:T(8,128)(2,1)} %collective-permute-done.48.grad_other_ref), custom_call_target="tpu_custom_call" | custom-call | flops 10000000000 | bytes 1048576 | tf_op jit(solution)/shard_map/qkv_grad/pallas_call | solution.py:629
  440.1 8.3 %collective-permute-done.53 = f32[8,2048]{1,0:T(8,128)S(1)} collective-permute-done((f32[8,2048]{1,0:T(8,128)S(1)}, f32[8,2048]{1,0:T(8,128)S(1)}, u32[]{:S(2)}, u32[]{:S(2)}) %collective-permute-start.53) | collective-permute-done | bytes 65568 | tf_op jit(solution)/shard_map/ppermute | solution.py:1371
  448.4 3.1 all-to-all-done.2.refs_0_.x_ref
  451.5 3.5 own_grad.3.refs_0_
  456.4 4.3 collective-permute-done.54
  464.2 6.1 %collective-permute-done.55 = f32[8,2048]{1,0:T(8,128)S(1)} collective-permute-done((f32[8,2048]{1,0:T(8,128)S(1)}, f32[8,2048]{1,0:T(8,128)S(1)}, u32[]{:S(2)}, u32[]{:S(2)}) %collective-permute-start.55) | collective-permute-done | bytes 65568 | tf_op jit(solution)/shard_map/ppermute | solution.py:1000
  474.4 4.8 project_grad.2
  479.1 4.8 project_grad.3
  486.9 4.3 all-to-all-start.3
  498.8 4.4 reduce-scatter.8.cloned.1.call-done
  506.1 5.3 %collective-permute-done.58.far_got = bf16[128,2048]{1,0:T(8,128)(2,1)S(1)} collective-permute-done((bf16[128,2048]{1,0:T(8,128)(2,1)}, bf16[128,2048]{1,0:T(8,128)(2,1)S(1)}, u32[]{:S(2)}, u32[]{:S(2)}) %collective-permute-start.58) | collective-permute-done | bytes 524320 | tf_op jit(solution)/shard_map/ppermute | solution.py:987
  (476 shorter events, 211.9 us)
Async XLA Ops:
  10.5 21.4 %collective-permute-start = (bf16[128,2048]{1,0:T(8,128)(2,1)S(1)}, bf16[128,2048]{1,0:T(8,128)(2,1)}, u32[]{:S(2)}, u32[]{:S(2)}) collective-permute-start(bf16[128,2048]{1,0:T(8,128)(2,1)S(1)} %fusion.20.a_ref), channel_id=1, source_target_pairs={{0,1},{1,0},{2,3},{3,2},{4,5},{5,4},{6,7},{7,6},{8,9},{9,8},{10,11... | collective-permute-start | bytes 1572872 | tf_op jit(solution)/shard_map/ppermute | solution.py:975
  11.0 15.4 %collective-permute-start.1 = (bf16[128,2048]{1,0:T(8,128)(2,1)S(1)}, bf16[128,2048]{1,0:T(8,128)(2,1)S(1)}, u32[]{:S(2)}, u32[]{:S(2)}) collective-permute-start(bf16[128,2048]{1,0:T(8,128)(2,1)S(1)} %fusion.20.a_ref), channel_id=1, source_target_pairs={{0,2},{2,0},{1,3},{3,1},{4,6},{6,4},{5,7},{7,5},{8,10},{10,8},{9,1... | collective-permute-start | bytes 1572872 | tf_op jit(solution)/shard_map/ppermute | solution.py:974
  26.4 14.1 %collective-permute-start.2 = (bf16[128,2048]{1,0:T(8,128)(2,1)S(1)}, bf16[128,2048]{1,0:T(8,128)(2,1)S(1)}, u32[]{:S(2)}, u32[]{:S(2)}) collective-permute-start(bf16[128,2048]{1,0:T(8,128)(2,1)S(1)} %collective-permute-done.1.a_ref), channel_id=1, source_target_pairs={{0,1},{1,0},{2,3},{3,2},{4,5},{5,4},{6,7},{7,6},{8,9},{9,8},{10,11... | collective-permute-start | bytes 1572872 | tf_op jit(solution)/shard_map/ppermute | solution.py:981
  47.8 19.7 %all-to-all-start = ((bf16[4,512,128]{2,1,0:T(8,128)(2,1)}), bf16[4,512,128]{2,1,0:T(8,128)(2,1)S(1)}, u32[]{:S(2)}, u32[]{:S(2)}) async-start(bf16[4,512,128]{2,1,0:T(8,128)(2,1)} %pad_maximum_fusion), calls=%async_computation | async-start | bytes 1048576 | tf_op jit(solution)/shard_map/all_to_all | solution.py:1117
  68.6 15.0 %collective-permute-start.11 = (bf16[2048,128]{1,0:T(8,128)(2,1)S(1)}, bf16[2048,128]{1,0:T(8,128)(2,1)S(1)}, u32[]{:S(2)}, u32[]{:S(2)}) collective-permute-start(bf16[2048,128]{1,0:T(8,128)(2,1)S(1)} %pass_rows.2.refs_1_.v_ref), channel_id=1, source_target_pairs={{0,4},{4,0},{1,5},{5,1},{2,6},{6,2},{3,7},{7,3},{8,12},{12,8},{9,1... | collective-permute-start | bytes 1572872 | tf_op jit(solution)/shard_map/ppermute | solution.py:1121
  73.4 10.2 %collective-permute-start.9 = (bf16[512,128]{1,0:T(8,128)(2,1)S(1)}, bf16[512,128]{1,0:T(8,128)(2,1)S(1)}, u32[]{:S(2)}, u32[]{:S(2)}) collective-permute-start(bf16[512,128]{1,0:T(8,128)(2,1)S(1)} %get-tuple-element.156), channel_id=1, source_target_pairs={{0,16},{8,24},{16,0},{24,8},{1,17},{9,25},{17,1},{25,9},{2,18},{10... | collective-permute-start | bytes 393224 | tf_op jit(solution)/shard_map/ppermute | solution.py:1109
  83.8 14.7 %collective-permute-start.12 = (bf16[2048,128]{1,0:T(8,128)(2,1)S(1)}, bf16[2048,128]{1,0:T(8,128)(2,1)}, u32[]{:S(2)}, u32[]{:S(2)}) collective-permute-start(bf16[2048,128]{1,0:T(8,128)(2,1)S(1)} %arrange.4.refs_0_.k_ref), channel_id=1, source_target_pairs={{0,4},{4,0},{1,5},{5,1},{2,6},{6,2},{3,7},{7,3},{8,12},{12,8},{9,1... | collective-permute-start | bytes 1572872 | tf_op jit(solution)/shard_map/ppermute | solution.py:1121
  85.2 8.5 %collective-permute-start.5 = (bf16[512,128]{1,0:T(8,128)(2,1)}, bf16[512,128]{1,0:T(8,128)(2,1)S(1)}, u32[]{:S(2)}, u32[]{:S(2)}) collective-permute-start(bf16[512,128]{1,0:T(8,128)(2,1)} %get-tuple-element.161), channel_id=1, source_target_pairs={{0,8},{8,16},{16,24},{24,0},{1,9},{9,17},{17,25},{25,1},{2,10},{10... | collective-permute-start | bytes 393224 | tf_op jit(solution)/shard_map/ppermute | solution.py:1109
  85.2 12.3 %collective-permute-start.6 = (bf16[512,128]{1,0:T(8,128)(2,1)}, bf16[512,128]{1,0:T(8,128)(2,1)S(1)}, u32[]{:S(2)}, u32[]{:S(2)}) collective-permute-start(bf16[512,128]{1,0:T(8,128)(2,1)} %get-tuple-element.160), channel_id=1, source_target_pairs={{0,16},{8,24},{16,0},{24,8},{1,17},{9,25},{17,1},{25,9},{2,18},{10... | collective-permute-start | bytes 393224 | tf_op jit(solution)/shard_map/ppermute | solution.py:1109
  88.5 9.0 %collective-permute-start.7 = (bf16[512,128]{1,0:T(8,128)(2,1)}, bf16[512,128]{1,0:T(8,128)(2,1)}, u32[]{:S(2)}, u32[]{:S(2)}) collective-permute-start(bf16[512,128]{1,0:T(8,128)(2,1)} %get-tuple-element.159), channel_id=1, source_target_pairs={{0,24},{8,0},{16,8},{24,16},{1,25},{9,1},{17,9},{25,17},{2,26},{10... | collective-permute-start | bytes 393224 | tf_op jit(solution)/shard_map/ppermute | solution.py:1109
  119.2 17.7 %all-to-all-start.1 = ((bf16[4,512,128]{2,1,0:T(8,128)(2,1)}), bf16[4,512,128]{2,1,0:T(8,128)(2,1)S(1)}, u32[]{:S(2)}, u32[]{:S(2)}) async-start(bf16[4,512,128]{2,1,0:T(8,128)(2,1)} %bitcast.26), calls=%async_computation.1 | async-start | bytes 1048576 | tf_op jit(solution)/shard_map/all_to_all | solution.py:1159
  123.1 103.2 %all-gather.2.cloned.1.call-start = ((), (), s32[]{:S(2)}) async-start(), calls=%async_computation.7 | async-start | bytes 5242880 | tf_op jit(solution)/shard_map/all_gather | solution.py:1169
  142.8 13.1 %collective-permute-start.13 = (bf16[128,2048]{1,0:T(8,128)(2,1)}, bf16[128,2048]{1,0:T(8,128)(2,1)S(1)}, u32[]{:S(2)}, u32[]{:S(2)}) collective-permute-start(bf16[128,2048]{1,0:T(8,128)(2,1)} %get-tuple-element.57), channel_id=1, source_target_pairs={{0,1},{1,0},{2,3},{3,2},{4,5},{5,4},{6,7},{7,6},{8,9},{9,8},{10,11... | collective-permute-start | bytes 1572872 | tf_op jit(solution)/shard_map/ppermute | solution.py:988
  145.3 214.1 %reduce-scatter.4.cloned.1.call-start = ((), (), s32[]{:S(2)}) async-start(), calls=%async_computation.8 | async-start | bytes 5242880 | tf_op jit(solution)/shard_map/reduce_scatter | solution.py:1307
  146.8 13.9 %collective-permute-start.15 = (bf16[128,2048]{1,0:T(8,128)(2,1)S(1)}, bf16[128,2048]{1,0:T(8,128)(2,1)S(1)}, u32[]{:S(2)}, u32[]{:S(2)}) collective-permute-start(bf16[128,2048]{1,0:T(8,128)(2,1)S(1)} %add_convert_fusion.3.refs_0_), channel_id=1, source_target_pairs={{0,2},{2,0},{1,3},{3,1},{4,6},{6,4},{5,7},{7,5},{8,10},{10,8},{9,1... | collective-permute-start | bytes 1572872 | tf_op jit(solution)/shard_map/ppermute | solution.py:987
  161.4 13.1 %collective-permute-start.18 = (bf16[128,2048]{1,0:T(8,128)(2,1)S(1)}, bf16[128,2048]{1,0:T(8,128)(2,1)S(1)}, u32[]{:S(2)}, u32[]{:S(2)}) collective-permute-start(bf16[128,2048]{1,0:T(8,128)(2,1)S(1)} %get-tuple-element.60.a_ref.refs_0_), channel_id=1, source_target_pairs={{0,2},{2,0},{1,3},{3,1},{4,6},{6,4},{5,7},{7,5},{8,10},{10,8},{9,1... | collective-permute-start | bytes 1572872 | tf_op jit(solution)/shard_map/ppermute | solution.py:974
  163.1 11.6 %collective-permute-start.16 = (bf16[128,2048]{1,0:T(8,128)(2,1)S(1)}, bf16[128,2048]{1,0:T(8,128)(2,1)S(1)}, u32[]{:S(2)}, u32[]{:S(2)}) collective-permute-start(bf16[128,2048]{1,0:T(8,128)(2,1)S(1)} %get-tuple-element.60.a_ref.refs_0_), channel_id=1, source_target_pairs={{0,1},{1,0},{2,3},{3,2},{4,5},{5,4},{6,7},{7,6},{8,9},{9,8},{10,11... | collective-permute-start | bytes 1572872 | tf_op jit(solution)/shard_map/ppermute | solution.py:975
  184.3 13.9 %collective-permute-start.22 = (bf16[256,1024]{1,0:T(8,128)(2,1)S(1)}, bf16[256,1024]{1,0:T(8,128)(2,1)S(1)}, u32[]{:S(2)}, u32[]{:S(2)}) collective-permute-start(bf16[256,1024]{1,0:T(8,128)(2,1)S(1)} %pad_maximum_fusion.1), channel_id=1, source_target_pairs={{0,4},{4,0},{1,5},{5,1},{2,6},{6,2},{3,7},{7,3},{8,12},{12,8},{9,1... | collective-permute-start | bytes 1572872 | tf_op jit(solution)/shard_map/ppermute | solution.py:1062
  186.0 12.2 %collective-permute-start.17 = (bf16[128,2048]{1,0:T(8,128)(2,1)S(1)}, bf16[128,2048]{1,0:T(8,128)(2,1)S(1)}, u32[]{:S(2)}, u32[]{:S(2)}) collective-permute-start(bf16[128,2048]{1,0:T(8,128)(2,1)S(1)} %get-tuple-element.149), channel_id=1, source_target_pairs={{0,1},{1,0},{2,3},{3,2},{4,5},{5,4},{6,7},{7,6},{8,9},{9,8},{10,11... | collective-permute-start | bytes 1572872 | tf_op jit(solution)/shard_map/ppermute | solution.py:988
  186.3 14.4 %collective-permute-start.21 = (bf16[128,2048]{1,0:T(8,128)(2,1)S(1)}, bf16[128,2048]{1,0:T(8,128)(2,1)S(1)}, u32[]{:S(2)}, u32[]{:S(2)}) collective-permute-start(bf16[128,2048]{1,0:T(8,128)(2,1)S(1)} %add_convert_fusion.2), channel_id=1, source_target_pairs={{0,2},{2,0},{1,3},{3,1},{4,6},{6,4},{5,7},{7,5},{8,10},{10,8},{9,1... | collective-permute-start | bytes 1572872 | tf_op jit(solution)/shard_map/ppermute | solution.py:987
  202.2 13.6 %collective-permute-start.25 = (bf16[128,2048]{1,0:T(8,128)(2,1)S(1)}, bf16[128,2048]{1,0:T(8,128)(2,1)S(1)}, u32[]{:S(2)}, u32[]{:S(2)}) collective-permute-start(bf16[128,2048]{1,0:T(8,128)(2,1)S(1)} %get-tuple-element.63.a_ref), channel_id=1, source_target_pairs={{0,2},{2,0},{1,3},{3,1},{4,6},{6,4},{5,7},{7,5},{8,10},{10,8},{9,1... | collective-permute-start | bytes 1572872 | tf_op jit(solution)/shard_map/ppermute | solution.py:974
  203.8 12.0 %collective-permute-start.23 = (bf16[128,2048]{1,0:T(8,128)(2,1)S(1)}, bf16[128,2048]{1,0:T(8,128)(2,1)S(1)}, u32[]{:S(2)}, u32[]{:S(2)}) collective-permute-start(bf16[128,2048]{1,0:T(8,128)(2,1)S(1)} %get-tuple-element.63.a_ref), channel_id=1, source_target_pairs={{0,1},{1,0},{2,3},{3,2},{4,5},{5,4},{6,7},{7,6},{8,9},{9,8},{10,11... | collective-permute-start | bytes 1572872 | tf_op jit(solution)/shard_map/ppermute | solution.py:975
  204.0 19.2 %collective-permute-start.27 = (bf16[256,1024]{1,0:T(8,128)(2,1)S(1)}, bf16[256,1024]{1,0:T(8,128)(2,1)S(1)}, u32[]{:S(2)}, u32[]{:S(2)}) collective-permute-start(bf16[256,1024]{1,0:T(8,128)(2,1)S(1)} %pad_maximum_fusion.2), channel_id=1, source_target_pairs={{0,4},{4,0},{1,5},{5,1},{2,6},{6,2},{3,7},{7,3},{8,12},{12,8},{9,1... | collective-permute-start | bytes 1572872 | tf_op jit(solution)/shard_map/ppermute | solution.py:1062
  250.3 220.0 %reduce-scatter.6.cloned.1.call-start = ((), (), s32[]{:S(2)}) async-start(), calls=%async_computation.9 | async-start | bytes 5242880 | tf_op jit(solution)/shard_map/reduce_scatter | solution.py:1308
  254.6 14.3 %collective-permute-start.30 = (bf16[2,2,256,256]{3,2,1,0:T(8,128)(2,1)}, bf16[2,2,256,256]{3,2,1,0:T(8,128)(2,1)}, u32[]{:S(2)}, u32[]{:S(2)}) collective-permute-start(bf16[2,2,256,256]{3,2,1,0:T(8,128)(2,1)} %pad_maximum_fusion.3), channel_id=1, source_target_pairs={{0,4},{4,0},{1,5},{5,1},{2,6},{6,2},{3,7},{7,3},{8,12},{12,8},{9,1... | collective-permute-start | bytes 1572872 | tf_op jit(solution)/shard_map/ppermute | solution.py:1271
  257.2 11.7 %collective-permute-start.24 = (bf16[128,2048]{1,0:T(8,128)(2,1)}, bf16[128,2048]{1,0:T(8,128)(2,1)}, u32[]{:S(2)}, u32[]{:S(2)}) collective-permute-start(bf16[128,2048]{1,0:T(8,128)(2,1)} %get-tuple-element.143), channel_id=1, source_target_pairs={{0,1},{1,0},{2,3},{3,2},{4,5},{5,4},{6,7},{7,6},{8,9},{9,8},{10,11... | collective-permute-start | bytes 1572872 | tf_op jit(solution)/shard_map/ppermute | solution.py:988
  257.2 14.7 %collective-permute-start.29 = (bf16[128,2048]{1,0:T(8,128)(2,1)}, bf16[128,2048]{1,0:T(8,128)(2,1)}, u32[]{:S(2)}, u32[]{:S(2)}) collective-permute-start(bf16[128,2048]{1,0:T(8,128)(2,1)} %add_convert_fusion.1.refs_0_), channel_id=1, source_target_pairs={{0,2},{2,0},{1,3},{3,1},{4,6},{6,4},{5,7},{7,5},{8,10},{10,8},{9,1... | collective-permute-start | bytes 1572872 | tf_op jit(solution)/shard_map/ppermute | solution.py:987
  280.7 13.6 %collective-permute-start.31 = (bf16[128,2048]{1,0:T(8,128)(2,1)S(1)}, bf16[128,2048]{1,0:T(8,128)(2,1)S(1)}, u32[]{:S(2)}, u32[]{:S(2)}) collective-permute-start(bf16[128,2048]{1,0:T(8,128)(2,1)S(1)} %get-tuple-element.65.a_ref), channel_id=1, source_target_pairs={{0,2},{2,0},{1,3},{3,1},{4,6},{6,4},{5,7},{7,5},{8,10},{10,8},{9,1... | collective-permute-start | bytes 1572872 | tf_op jit(solution)/shard_map/ppermute | solution.py:974
  282.7 12.2 %collective-permute-start.34 = (bf16[128,2048]{1,0:T(8,128)(2,1)S(1)}, bf16[128,2048]{1,0:T(8,128)(2,1)S(1)}, u32[]{:S(2)}, u32[]{:S(2)}) collective-permute-start(bf16[128,2048]{1,0:T(8,128)(2,1)S(1)} %get-tuple-element.65.a_ref), channel_id=1, source_target_pairs={{0,1},{1,0},{2,3},{3,2},{4,5},{5,4},{6,7},{7,6},{8,9},{9,8},{10,11... | collective-permute-start | bytes 1572872 | tf_op jit(solution)/shard_map/ppermute | solution.py:975
  282.8 14.5 %collective-permute-start.33 = (bf16[2,2,256,256]{3,2,1,0:T(8,128)(2,1)S(1)}, bf16[2,2,256,256]{3,2,1,0:T(8,128)(2,1)S(1)}, u32[]{:S(2)}, u32[]{:S(2)}) collective-permute-start(bf16[2,2,256,256]{3,2,1,0:T(8,128)(2,1)S(1)} %pad_maximum_fusion.4), channel_id=1, source_target_pairs={{0,4},{4,0},{1,5},{5,1},{2,6},{6,2},{3,7},{7,3},{8,12},{12,8},{9,1... | collective-permute-start | bytes 1572872 | tf_op jit(solution)/shard_map/ppermute | solution.py:1271
  294.3 8.8 %collective-permute-start.38 = (f32[2,512]{0,1:T(8,128)S(1)}, f32[2,512]{0,1:T(8,128)S(1)}, u32[]{:S(2)}, u32[]{:S(2)}) collective-permute-start(f32[2,512]{0,1:T(8,128)S(1)} %convert_bitcast_fusion.1), channel_id=1, source_target_pairs={{0,4},{4,0},{1,5},{5,1},{2,6},{6,2},{3,7},{7,3},{8,12},{12,8},{9,1... | collective-permute-start | bytes 12296 | tf_op jit(solution)/shard_map/ppermute | solution.py:1188
  298.9 10.9 %collective-permute-start.35 = (bf16[512,128]{1,0:T(8,128)(2,1)S(1)}, bf16[512,128]{1,0:T(8,128)(2,1)S(1)}, u32[]{:S(2)}, u32[]{:S(2)}) collective-permute-start(bf16[512,128]{1,0:T(8,128)(2,1)S(1)} %get-tuple-element.153), channel_id=1, source_target_pairs={{0,8},{8,16},{16,24},{24,0},{1,9},{9,17},{17,25},{25,1},{2,10},{10... | collective-permute-start | bytes 393224 | tf_op jit(solution)/shard_map/ppermute | solution.py:1109
  320.5 13.2 %collective-permute-start.36 = (bf16[512,128]{1,0:T(8,128)(2,1)S(1)}, bf16[512,128]{1,0:T(8,128)(2,1)S(1)}, u32[]{:S(2)}, u32[]{:S(2)}) collective-permute-start(bf16[512,128]{1,0:T(8,128)(2,1)S(1)} %get-tuple-element.152), channel_id=1, source_target_pairs={{0,16},{8,24},{16,0},{24,8},{1,17},{9,25},{17,1},{25,9},{2,18},{10... | collective-permute-start | bytes 393224 | tf_op jit(solution)/shard_map/ppermute | solution.py:1109
  322.9 10.8 %collective-permute-start.37 = (bf16[512,128]{1,0:T(8,128)(2,1)S(1)}, bf16[512,128]{1,0:T(8,128)(2,1)S(1)}, u32[]{:S(2)}, u32[]{:S(2)}) collective-permute-start(bf16[512,128]{1,0:T(8,128)(2,1)S(1)} %get-tuple-element.151), channel_id=1, source_target_pairs={{0,24},{8,0},{16,8},{24,16},{1,25},{9,1},{17,9},{25,17},{2,26},{10... | collective-permute-start | bytes 393224 | tf_op jit(solution)/shard_map/ppermute | solution.py:1109
  355.7 25.6 %collective-permute-start.39 = (bf16[2048,128]{1,0:T(8,128)(2,1)}, bf16[2048,128]{1,0:T(8,128)(2,1)}, u32[]{:S(2)}, u32[]{:S(2)}) collective-permute-start(bf16[2048,128]{1,0:T(8,128)(2,1)} %get-tuple-element.70), channel_id=1, source_target_pairs={{0,4},{4,0},{1,5},{5,1},{2,6},{6,2},{3,7},{7,3},{8,12},{12,8},{9,1... | collective-permute-start | bytes 1572872 | tf_op jit(solution)/shard_map/ppermute | solution.py:1332
  357.3 24.1 %collective-permute-start.40 = (bf16[2048,128]{1,0:T(8,128)(2,1)}, bf16[2048,128]{1,0:T(8,128)(2,1)}, u32[]{:S(2)}, u32[]{:S(2)}) collective-permute-start(bf16[2048,128]{1,0:T(8,128)(2,1)} %get-tuple-element.72), channel_id=1, source_target_pairs={{0,4},{4,0},{1,5},{5,1},{2,6},{6,2},{3,7},{7,3},{8,12},{12,8},{9,1... | collective-permute-start | bytes 1572872 | tf_op jit(solution)/shard_map/ppermute | solution.py:1332
  357.9 23.5 %collective-permute-start.43 = (f32[1,2048]{1,0:T(1,128)S(1)}, f32[1,2048]{1,0:T(1,128)S(1)}, u32[]{:S(2)}, u32[]{:S(2)}) collective-permute-start(f32[1,2048]{1,0:T(1,128)S(1)} %get-tuple-element.75), channel_id=1, source_target_pairs={{0,4},{4,0},{1,5},{5,1},{2,6},{6,2},{3,7},{7,3},{8,12},{12,8},{9,1... | collective-permute-start | bytes 24584 | tf_op jit(solution)/shard_map/ppermute | solution.py:1335
  409.2 42.3 %all-to-all-start.2 = ((bf16[4,512,384]{2,1,0:T(8,128)(2,1)}), bf16[4,512,384]{2,1,0:T(8,128)(2,1)}, u32[]{:S(2)}, u32[]{:S(2)}) async-start(bf16[4,512,384]{2,1,0:T(8,128)(2,1)} %bitcast.300), calls=%async_computation.3 | async-start | bytes 3145728 | tf_op jit(solution)/shard_map/all_to_all | solution.py:1159
  413.7 89.5 %reduce-scatter.8.cloned.1.call-start = ((), (), s32[]{:S(2)}) async-start(), calls=%async_computation.10 | async-start | bytes 2621440 | tf_op jit(solution)/shard_map/reduce_scatter | solution.py:1401
  427.0 24.4 %collective-permute-start.50 = (bf16[4,256,384]{2,1,0:T(8,128)(2,1)}, bf16[4,256,384]{2,1,0:T(8,128)(2,1)}, u32[]{:S(2)}, u32[]{:S(2)}) collective-permute-start(bf16[4,256,384]{2,1,0:T(8,128)(2,1)} %get-tuple-element.134), channel_id=1, source_target_pairs={{0,4},{4,0},{1,5},{5,1},{2,6},{6,2},{3,7},{7,3},{8,12},{12,8},{9,1... | collective-permute-start | bytes 2359304 | tf_op jit(solution)/shard_map/ppermute | solution.py:1389
  439.6 8.8 %collective-permute-start.53 = (f32[8,2048]{1,0:T(8,128)S(1)}, f32[8,2048]{1,0:T(8,128)S(1)}, u32[]{:S(2)}, u32[]{:S(2)}) collective-permute-start(f32[8,2048]{1,0:T(8,128)S(1)} %add.289), channel_id=1, source_target_pairs={{0,4},{4,0},{1,5},{5,1},{2,6},{6,2},{3,7},{7,3},{8,12},{12,8},{9,1... | collective-permute-start | bytes 196616 | tf_op jit(solution)/shard_map/ppermute | solution.py:1371
  460.7 9.5 %collective-permute-start.55 = (f32[8,2048]{1,0:T(8,128)S(1)}, f32[8,2048]{1,0:T(8,128)S(1)}, u32[]{:S(2)}, u32[]{:S(2)}) collective-permute-start(f32[8,2048]{1,0:T(8,128)S(1)} %add.291), channel_id=1, source_target_pairs={{0,16},{8,24},{16,0},{24,8},{1,17},{9,25},{17,1},{25,9},{2,18},{10... | collective-permute-start | bytes 196616 | tf_op jit(solution)/shard_map/ppermute | solution.py:1000
  462.8 28.4 %collective-permute-start.60 = (bf16[4,256,256]{2,1,0:T(8,128)(2,1)}, bf16[4,256,256]{2,1,0:T(8,128)(2,1)}, u32[]{:S(2)}, u32[]{:S(2)}) collective-permute-start(bf16[4,256,256]{2,1,0:T(8,128)(2,1)} %dynamic-slice_bitcast_fusion.2), channel_id=1, source_target_pairs={{0,4},{4,0},{1,5},{5,1},{2,6},{6,2},{3,7},{7,3},{8,12},{12,8},{9,1... | collective-permute-start | bytes 1572872 | tf_op jit(solution)/shard_map/ppermute | solution.py:1042
  479.1 16.2 %collective-permute-start.57 = (bf16[128,2048]{1,0:T(8,128)(2,1)}, bf16[128,2048]{1,0:T(8,128)(2,1)}, u32[]{:S(2)}, u32[]{:S(2)}) collective-permute-start(bf16[128,2048]{1,0:T(8,128)(2,1)} %get-tuple-element.84), channel_id=1, source_target_pairs={{0,1},{1,0},{2,3},{3,2},{4,5},{5,4},{6,7},{7,6},{8,9},{9,8},{10,11... | collective-permute-start | bytes 1572872 | tf_op jit(solution)/shard_map/ppermute | solution.py:985
  486.9 29.7 %all-to-all-start.3 = ((bf16[4,256,384]{2,1,0:T(8,128)(2,1)}), bf16[4,256,384]{2,1,0:T(8,128)(2,1)}, u32[]{:S(2)}, u32[]{:S(2)}) async-start(bf16[4,256,384]{2,1,0:T(8,128)(2,1)} %add_rows.1), calls=%async_computation.5 | async-start | bytes 1572864 | tf_op jit(solution)/shard_map/all_to_all | solution.py:1415
  494.9 11.2 %collective-permute-start.56 = (bf16[128,2048]{1,0:T(8,128)(2,1)}, bf16[128,2048]{1,0:T(8,128)(2,1)S(1)}, u32[]{:S(2)}, u32[]{:S(2)}) collective-permute-start(bf16[128,2048]{1,0:T(8,128)(2,1)} %get-tuple-element.83), channel_id=1, source_target_pairs={{0,1},{1,0},{2,3},{3,2},{4,5},{5,4},{6,7},{7,6},{8,9},{9,8},{10,11... | collective-permute-start | bytes 1572872 | tf_op jit(solution)/shard_map/ppermute | solution.py:988
  497.3 14.1 %collective-permute-start.58 = (bf16[128,2048]{1,0:T(8,128)(2,1)}, bf16[128,2048]{1,0:T(8,128)(2,1)S(1)}, u32[]{:S(2)}, u32[]{:S(2)}) collective-permute-start(bf16[128,2048]{1,0:T(8,128)(2,1)} %add_convert_fusion), channel_id=1, source_target_pairs={{0,2},{2,0},{1,3},{3,1},{4,6},{6,4},{5,7},{7,5},{8,10},{10,8},{9,1... | collective-permute-start | bytes 1572872 | tf_op jit(solution)/shard_map/ppermute | solution.py:987
  504.2 15.6 %collective-permute-start.59 = (bf16[4,256,128]{2,1,0:T(8,128)(2,1)S(1)}, bf16[4,256,128]{2,1,0:T(8,128)(2,1)}, u32[]{:S(2)}, u32[]{:S(2)}) collective-permute-start(bf16[4,256,128]{2,1,0:T(8,128)(2,1)S(1)} %dynamic-slice_bitcast_fusion.3), channel_id=1, source_target_pairs={{0,4},{4,0},{1,5},{5,1},{2,6},{6,2},{3,7},{7,3},{8,12},{12,8},{9,1... | collective-permute-start | bytes 786440 | tf_op jit(solution)/shard_map/ppermute | solution.py:1042
  (129 other events, 950.7 us)
Sparse Core Ops, SparseCore 0:
  145.4 80.7 all-gather.1
  250.4 79.4 reduce-scatter.3
  332.3 81.5 reduce-scatter.5
  456.5 46.6 reduce-scatter.7
